TPU v7x, 32 devices: a whole 2x2x4 slice. The times are simulated.
32 devices in a mesh: parts: 2 (over y), ep: 16 (over z, x, core), tp: 1.
Axes of the slice: x: 2, y: 2, z: 4, core: 2. Of those that a mesh axis runs over, the one named last changes fastest.
Arguments:
- tokens: bfloat16 [2048, 3584], P(('parts', 'ep'), 'tp'), parts along dimension 0, may hold values from -6 to 6
- expert_ids: int32 [2048, 8], P(('parts', 'ep')), parts along dimension 0, may hold values from 0 to 15, all different within a row; in each aligned block of 64 rows (0 to 63, 64 to 127, ...) at most 48 rows name the same one
- gate_weights: float32 [2048, 8], P(('parts', 'ep')), parts along dimension 0, may hold values from 0.05 to 1
- w_gate: bfloat16 [16, 3584, 1024], P(None, 'ep', 'tp'), may hold values from -0.09375 to 0.09375
- w_up: bfloat16 [16, 3584, 1024], P(None, 'ep', 'tp'), may hold values from -0.09375 to 0.09375
- w_down: bfloat16 [16, 1024, 3584], P(None, 'tp', 'ep'), may hold values from -0.1875 to 0.1875
Outputs:
- mixed: bfloat16 [2048, 3584], P(('parts', 'ep'), 'tp'), parts along dimension 0
There are 2 independent parts, one for each index of `parts`. A program takes and returns all parts, laid end to end along the dimension named above; an argument that names none is the same for every part. Nothing has to cross between parts.
Inputs may be any that keep to these rules, and one draw needn't show every extreme that they name: `expert_ids`: each row names 8 different experts; within the rows of one block of 64 rows no expert is named by more than 48 rows, a bound that some block reaches.
All inputs are finite; a program needn't handle non-finite values.
Results may differ from a plain program's by a relative error of at most 0.015.
Values may be sent and summed in bfloat16 or wider, within the bound.
No kernel may reach another device: no remote copies, remote signals or barrier semaphores. Data moves between devices by JAX's collectives and lax.ppermute only.
A program may use at most 128 MiB of HBM per device.

v0:
```python
import jax
import jax.numpy as jnp
from jax import lax
from jax.sharding import PartitionSpec as P


def slots_of(block_ids, experts):
    flat = block_ids.reshape(-1)
    onehot = (flat[:, None] == jnp.arange(experts, dtype=jnp.int32)[None, :]).astype(jnp.int32)
    before = jnp.cumsum(onehot, axis=0) - onehot
    return jnp.sum(before * onehot, axis=1).reshape(block_ids.shape)


def fill_slots(rows, expert_ids, slot, experts, per_expert):
    count, picks = expert_ids.shape
    spread = jnp.broadcast_to(rows[:, None, :], (count, picks, rows.shape[1]))
    empty = jnp.zeros((experts, per_expert, rows.shape[1]), jnp.bfloat16)
    return empty.at[expert_ids, slot].set(spread)


def body(tokens, expert_ids, gate_weights, w_gate, w_up, w_down):
    tok_rows, picks = expert_ids.shape
    experts = w_gate.shape[0]
    per_expert = min(tok_rows, 3 * tok_rows * picks // (2 * experts))
    slot = slots_of(expert_ids, experts)
    features = lax.all_gather(tokens, "tp", axis=1, tiled=True)
    outgoing = fill_slots(features, expert_ids, slot, experts, per_expert)
    arrived = lax.all_to_all(outgoing, "ep", split_axis=0, concat_axis=1, tiled=True)
    gate_owned, up_owned = (
        lax.all_to_all(w_gate, "ep", split_axis=0, concat_axis=1, tiled=True),
        lax.all_to_all(w_up, "ep", split_axis=0, concat_axis=1, tiled=True),
    )
    gate = jnp.einsum("ecd,edf->ecf", arrived, gate_owned, preferred_element_type=jnp.float32)
    up = jnp.einsum("ecd,edf->ecf", arrived, up_owned, preferred_element_type=jnp.float32)
    hidden = (jax.nn.silu(gate) * up).astype(jnp.bfloat16)
    down_owned = lax.all_to_all(w_down, "ep", split_axis=0, concat_axis=2, tiled=True)
    partial_value = jnp.einsum(
        "ecf,efd->ecd", hidden, down_owned, preferred_element_type=jnp.float32
    )
    expert_out = lax.psum_scatter(
        partial_value.astype(jnp.bfloat16), "tp", scatter_dimension=2, tiled=True
    )
    returned = lax.all_to_all(expert_out, "ep", split_axis=1, concat_axis=0, tiled=True)
    picked = returned[expert_ids, slot]
    mixed = jnp.sum(gate_weights[:, :, None] * picked.astype(jnp.float32), axis=1)
    return mixed.astype(jnp.bfloat16)


def solution(mesh):
    placed = (
        P(("parts", "ep"), "tp"),
        P(("parts", "ep"), None),
        P(("parts", "ep"), None),
        P(None, "ep", "tp"),
        P(None, "ep", "tp"),
        P(None, "tp", "ep"),
    )
    return jax.shard_map(
        body, mesh=mesh, in_specs=placed, out_specs=P(("parts", "ep"), "tp"), check_vma=False
    )
```

profile of v0, /device:TPU:15, one launch (start us, length us, event | category | flops | bytes accessed | tf_op | source)
XLA Modules:
  0.0 1043.8 jit_solution(1088820065056620696)
XLA Ops:
  0.0 0.0 copy-start
  0.0 0.8 copy.38
  0.8 0.1 eq.29
  0.9 0.1 eq.25
  1.0 1.2 reduce-window.6
  2.2 0.2 slice_reduce_fusion
  2.4 0.1 fusion.4
  2.5 0.1 reshape.94
  2.6 0.1 copy.41
  2.7 0.7 fusion.6
  3.4 0.1 copy.44
  3.5 0.1 reshape.105
  3.6 0.0 copy-done
  3.6 2.2 broadcast_bitcast_fusion
  5.8 2.9 broadcast_in_dim.6
  8.7 122.5 %scatter_fusion = bf16[16,48,3584]{2,1,0:T(8,128)(2,1)} fusion(bf16[16,48,3584]{2,1,0:T(8,128)(2,1)} %broadcast_in_dim.6, s32[512]{0:T(512)S(1)} %reshape.105, bf16[512,3584]{1,0:T(8,128)(2,1)} %broadcast_bitcast_fusion), kind=kCustom, calls=%fused_computation.1 | custom fusion | bytes 11014144 | tf_op jit(solution)/shard_map/scatter | solution.py:18
  131.2 0.0 slice-start
  131.2 127.2 %all_to_all.54 = bf16[16,48,3584]{2,1,0:T(8,128)(2,1)} all-to-all(bf16[16,48,3584]{2,1,0:T(8,128)(2,1)} %scatter_fusion), channel_id=1, replica_groups=mesh['parts'=2,'ep'=16,'tp'=1] {'ep'}, dimensions={0} | all-to-all | bytes 11010048 | tf_op jit(solution)/shard_map/all_to_all | solution.py:28
  258.5 0.0 slice-start.1
  258.5 165.6 %all_to_all.55 = bf16[16,224,1024]{2,1,0:T(8,128)(2,1)} all-to-all(bf16[16,224,1024]{2,1,0:T(8,128)(2,1)} %param.9), channel_id=1, replica_groups=mesh['parts'=2,'ep'=16,'tp'=1] {'ep'}, dimensions={0} | all-to-all | bytes 14680064 | tf_op jit(solution)/shard_map/all_to_all | solution.py:30
  424.1 0.0 slice-done
  424.1 0.0 slice-done.1
  424.1 165.2 %all_to_all.56 = bf16[16,224,1024]{2,1,0:T(8,128)(2,1)} all-to-all(bf16[16,224,1024]{2,1,0:T(8,128)(2,1)S(1)} %bitcast.61), channel_id=1, replica_groups=mesh['parts'=2,'ep'=16,'tp'=1] {'ep'}, dimensions={0} | all-to-all | bytes 14680064 | tf_op jit(solution)/shard_map/all_to_all | solution.py:31
  589.2 0.0 slice-start.2
  589.2 5.8 all-to-all-start.3
  595.0 0.0 slice-start.3
  595.0 9.9 fusion.10
  604.9 0.0 slice-done.2
  604.9 0.0 copy-done.2
  604.9 0.0 slice-done.3
  604.9 6.2 multiply_convert_fusion
  611.1 143.8 %all-to-all-done.3 = bf16[16,1024,224]{1,2,0:T(8,128)(2,1)} async-done(((bf16[16,1024,224]{1,2,0:T(8,128)(2,1)}), bf16[16,1024,224]{1,2,0:T(8,128)(2,1)}, u32[]{:S(2)}, u32[]{:S(2)}) %all-to-all-start.3) | async-done | bytes 7340064 | tf_op jit(solution)/shard_map/all_to_all | solution.py:36
  754.9 9.3 fusion.1
  764.1 60.7 %copy.51 = bf16[1,768,3584]{2,0,1:T(2,128)(2,1)} copy(bf16[1,768,3584]{2,1,0:T(8,128)(2,1)S(1)} %fusion.1) | data formatting | bytes 11010048 | tf_op jit(solution)/shard_map/convert_element_type | solution.py:41
  824.9 0.5 broadcast.112
  825.4 37.0 %reduce.2 = bf16[768,3584]{1,0:T(8,128)(2,1)} reduce(bf16[768,1,3584]{2,1,0:T(2,128)(2,1)} %bitcast.58, bf16[]{:T(256)} %broadcast.112), dimensions={1}, to_apply=%bitcast.56.reduce_sub_computation | reduce | bytes 11010050
  862.3 12.3 %reshape.113 = bf16[16,2,86016]{2,1,0:T(2,128)(2,1)} reshape(bf16[768,3584]{1,0:T(8,128)(2,1)} %reduce.2) | data formatting | bytes 11010048
  874.7 5.0 all-to-all-start.4
  879.7 0.1 copy.46
  879.8 0.1 reshape.99
  879.9 0.0 copy-done.3
  879.9 0.1 copy.37
  880.0 120.3 %all-to-all-done.4 = bf16[16,2,86016]{2,1,0:T(2,128)(2,1)} async-done(((bf16[16,2,86016]{2,1,0:T(2,128)(2,1)}), bf16[16,2,86016]{2,1,0:T(2,128)(2,1)}, u32[]{:S(2)}, u32[]{:S(2)}) %all-to-all-start.4) | async-done | bytes 5505056 | tf_op jit(solution)/shard_map/all_to_all | solution.py:43
  1000.3 13.6 %reshape.114 = bf16[768,1,3584]{2,1,0:T(2,128)(2,1)} reshape(bf16[16,2,86016]{2,1,0:T(2,128)(2,1)} %all-to-all-done.4) | data formatting | bytes 11010048
  1013.9 7.8 copy.47
  1021.7 16.3 %gather_fusion = bf16[512,3584]{1,0:T(8,128)(2,1)} fusion(bf16[16,48,3584]{2,1,0:T(8,128)(2,1)} %bitcast.57, s32[512]{0:T(512)S(1)} %reshape.99), kind=kCustom, calls=%fused_computation | custom fusion | bytes 7344128 | tf_op jit(solution)/shard_map/gather | solution.py:44
  1038.0 5.8 fusion
  1043.8 0.0 copy-done.1
  (8 shorter events, 0.1 us)
Async XLA Ops:
  0.0 3.6 copy-start
  131.2 292.8 %slice-start = ((s8[7340032]{0:T(1024)(128)(4,1)}), s8[4194304]{0:T(1024)(128)(4,1)S(1)}, s32[]{:S(2)}) async-start(s8[7340032]{0:T(1024)(128)(4,1)} %bitcast.60), calls=%async_computation.5 | async-start | bytes 8388608
  258.5 165.6 %slice-start.1 = ((s8[7340032]{0:T(1024)(128)(4,1)}), s8[3145728]{0:T(1024)(128)(4,1)S(1)}, s32[]{:S(2)}) async-start(s8[7340032]{0:T(1024)(128)(4,1)} %bitcast.60), calls=%async_computation.6 | async-start | bytes 6291456
  589.2 15.6 %slice-start.2 = ((s8[5505024]{0:T(1024)(128)(4,1)}), s8[1310720]{0:T(1024)(128)(4,1)S(1)}, s32[]{:S(2)}) async-start(s8[5505024]{0:T(1024)(128)(4,1)} %bitcast.65), calls=%async_computation.7 | async-start | bytes 2621440
  589.2 165.6 %all-to-all-start.3 = ((bf16[16,1024,224]{1,2,0:T(8,128)(2,1)}), bf16[16,1024,224]{1,2,0:T(8,128)(2,1)}, u32[]{:S(2)}, u32[]{:S(2)}) async-start(bf16[16,1024,224]{1,2,0:T(8,128)(2,1)} %param.11), calls=%async_computation.3 | async-start | bytes 14680064 | tf_op jit(solution)/shard_map/all_to_all | solution.py:36
  595.0 9.9 copy-start.2
  595.0 9.9 slice-start.3
  874.7 5.2 copy-start.3
  874.7 125.6 %all-to-all-start.4 = ((bf16[16,2,86016]{2,1,0:T(2,128)(2,1)}), bf16[16,2,86016]{2,1,0:T(2,128)(2,1)}, u32[]{:S(2)}, u32[]{:S(2)}) async-start(bf16[16,2,86016]{2,1,0:T(2,128)(2,1)} %reshape.113), calls=%async_computation.4 | async-start | bytes 11010048 | tf_op jit(solution)/shard_map/all_to_all | solution.py:43
  1021.7 22.1 %copy-start.1 = (bf16[64,3584]{1,0:T(8,128)(2,1)S(1)}, bf16[64,3584]{1,0:T(8,128)(2,1)}, u32[]{:S(2)}) copy-start(bf16[64,3584]{1,0:T(8,128)(2,1)} %param.6) | copy-start | bytes 1376260
where the time goes:
time: 1050 us; the launch traced here: 1040 us
  blocking collectives  458 us (44%)
  waiting for transfers between devices  264 us (25%)
  local copies, waits for them, and re-layouts  241 us (23%)
  other arithmetic  44.8 us (4%)
  matrix products  25.3 us (2%)
  starting transfers between devices  10.8 us (1%)
    all_to_all x1, blocking collectives, body(): lax.all_to_all(w_gate, 'ep', split_axis=0, concat_axis=1, tiled=True)  166 us
    all_to_all x1, blocking collectives, body(): lax.all_to_all(w_up, 'ep', split_axis=0, concat_axis=1, tiled=True)  165 us
    all_to_all x1, waiting for transfers between devices, body(): lax.all_to_all(w_down, 'ep', split_axis=0, concat_axis=2, tiled=True)  144 us
    all_to_all x1, blocking collectives, body(): lax.all_to_all(outgoing, 'ep', split_axis=0, concat_axis=1, tiled=True)  127 us
    scatter x1, local copies, waits for them, and re-layouts, fill_slots(): return empty.at[expert_ids, slot].set(spread)  123 us
    all_to_all x1, waiting for transfers between devices, body(): lax.all_to_all(expert_out, 'ep', split_axis=1, concat_axis=0, tiled=True)  120 us
    convert_element_type x1, local copies, waits for them, and re-layouts, body(): partial_value.astype(jnp.bfloat16)  60.7 us
    unnamed x3, other arithmetic  37 us
  transfers between devices with their start and end apart: 2, of which 2 were waited for; matrix products, arithmetic and copies ran while one was open for 2% of the time, Pallas kernels for 0%

commit v1 on v0

v1 whole, which is shorter than its diff:
```python
import functools
import math

import jax
import jax.numpy as jnp
from jax import lax
from jax.experimental import pallas as pl
from jax.experimental.pallas import tpu as pltpu
from jax.sharding import PartitionSpec as P

BF16 = jnp.bfloat16
F32 = jnp.float32
TILE = 256
META = 32


def slots_of(block_ids, experts):
    flat = block_ids.reshape(-1)
    onehot = (flat[:, None] == jnp.arange(experts, dtype=jnp.int32)[None, :]).astype(jnp.int32)
    before = jnp.cumsum(onehot, axis=0) - onehot
    return jnp.sum(before * onehot, axis=1).reshape(block_ids.shape)


def fill_slots(rows, expert_ids, slot, experts, per_expert):
    count, picks = expert_ids.shape
    spread = jnp.broadcast_to(rows[:, None, :], (count, picks, rows.shape[1]))
    empty = jnp.zeros((experts, per_expert, rows.shape[1]), BF16)
    return empty.at[expert_ids, slot].set(spread)


def moved_weights(tokens, expert_ids, gate_weights, w_gate, w_up, w_down):
    tok_rows, picks = expert_ids.shape
    experts = w_gate.shape[0]
    per_expert = min(tok_rows, 3 * tok_rows * picks // (2 * experts))
    slot = slots_of(expert_ids, experts)
    features = lax.all_gather(tokens, "tp", axis=1, tiled=True)
    outgoing = fill_slots(features, expert_ids, slot, experts, per_expert)
    arrived = lax.all_to_all(outgoing, "ep", split_axis=0, concat_axis=1, tiled=True)
    gate_owned, up_owned = (
        lax.all_to_all(w_gate, "ep", split_axis=0, concat_axis=1, tiled=True),
        lax.all_to_all(w_up, "ep", split_axis=0, concat_axis=1, tiled=True),
    )
    gate = jnp.einsum("ecd,edf->ecf", arrived, gate_owned, preferred_element_type=F32)
    up = jnp.einsum("ecd,edf->ecf", arrived, up_owned, preferred_element_type=F32)
    hidden = (jax.nn.silu(gate) * up).astype(BF16)
    down_owned = lax.all_to_all(w_down, "ep", split_axis=0, concat_axis=2, tiled=True)
    partial_value = jnp.einsum("ecf,efd->ecd", hidden, down_owned, preferred_element_type=F32)
    expert_out = lax.psum_scatter(
        partial_value.astype(BF16), "tp", scatter_dimension=2, tiled=True
    )
    returned = lax.all_to_all(expert_out, "ep", split_axis=1, concat_axis=0, tiled=True)
    picked = returned[expert_ids, slot]
    mixed = jnp.sum(gate_weights[:, :, None] * picked.astype(F32), axis=1)
    return mixed.astype(BF16)


def dot(a, b, contract):
    return lax.dot_general(a, b, ((contract[0], contract[1]), ((), ())), preferred_element_type=F32)


def order_of(ids, weights, experts):
    names = jnp.arange(experts, dtype=jnp.int32)[:, None, None]
    hit = ids.T[None] == names
    mask = jnp.any(hit, axis=1)
    gates = jnp.sum(jnp.where(hit, weights.T[None], 0.0), axis=1)
    count = jnp.cumsum(mask.astype(jnp.int32), axis=1)
    total = count[:, -1]
    ends = jnp.cumsum(total)
    place = jnp.where(mask, count - 1 + (ends - total)[:, None], -1)
    base = jnp.concatenate([jnp.zeros((1,), jnp.int32), ends])
    return place, gates, base


def visits_of(base, rows, tile):
    experts = base.shape[0] - 1
    start, end = base[:-1], base[1:]
    first = start // tile
    count = jnp.where(end > start, (end - 1) // tile - first + 1, 0)
    upto = jnp.cumsum(count)
    number = jnp.minimum(jnp.arange(rows // tile + experts - 1, dtype=jnp.int32), upto[-1] - 1)
    expert = jnp.sum((upto[None, :] <= number[:, None]).astype(jnp.int32), axis=1)
    pick = expert[:, None] == jnp.arange(experts, dtype=jnp.int32)[None, :]
    tiles = number + jnp.sum(jnp.where(pick, (first - upto + count)[None, :], 0), axis=1)
    return tiles, expert, upto[-1:]


def spans_of(base, rows, tile):
    low = jnp.arange(rows // tile, dtype=jnp.int32)[:, None] * tile
    return (
        jnp.sum((base[None, 1:] <= low).astype(jnp.int32), axis=1),
        jnp.sum((base[None, :-1] < low + tile).astype(jnp.int32), axis=1),
    )


def match_of(row0, low, high, place_ref, tile):
    tokens = place_ref.shape[1]
    row = row0 + lax.broadcasted_iota(jnp.int32, (tile, 1), 0)

    def add(e, found):
        return jnp.where(place_ref[pl.ds(e, 1), :] == row, e, found)

    return lax.fori_loop(low, high, add, jnp.full((tile, tokens), -1, jnp.int32))


def sort_kernel(tile, low, high, place_ref, own_ref, other_ref, own_out, other_out):
    i = pl.program_id(0)
    match = match_of(i * tile, low[i], high[i], place_ref, tile)
    onehot = jnp.where(match >= 0, 1.0, 0.0).astype(BF16)
    own_out[...] = dot(onehot, own_ref[...], ((1,), (0,))).astype(BF16)
    other_out[...] = dot(onehot, other_ref[...], ((1,), (0,))).astype(BF16)


def sort_rows(spans, place, own, other, rows):
    experts, tokens = place.shape
    width = own.shape[1]
    whole = lambda i, *_: (0, 0)
    block = pl.BlockSpec((TILE, width), lambda i, *_: (i, 0))
    return pl.pallas_call(
        functools.partial(sort_kernel, TILE),
        grid_spec=pltpu.PrefetchScalarGridSpec(
            num_scalar_prefetch=2,
            grid=(rows // TILE,),
            in_specs=[
                pl.BlockSpec((experts, tokens), whole),
                pl.BlockSpec((tokens, width), whole),
                pl.BlockSpec((tokens, width), whole),
            ],
            out_specs=[block, block],
        ),
        out_shape=[jax.ShapeDtypeStruct((rows, width), BF16)] * 2,
        compiler_params=pltpu.CompilerParams(vmem_limit_bytes=48 << 20),
        cost_estimate=pl.CostEstimate(
            flops=4 * rows * tokens * width, bytes_accessed=4 * rows * width, transcendentals=0
        ),
        name="sort_rows",
    )(*spans, place, own, other)


def partial_kernel(
    tile, tiles, experts, total, base, core, own_ref, other_ref,
    gate_own, gate_other, up_own, up_other, gate_out, up_out,
):
    v = pl.program_id(0)

    @pl.when(v < total[0])
    def _():
        e = experts[v]
        row = tiles[v] * tile + lax.broadcasted_iota(jnp.int32, (tile, 1), 0)
        mine = (row >= base[e]) & (row < base[e + 1])
        for near, far, out in ((gate_own, gate_other, gate_out), (up_own, up_other, up_out)):
            value = dot(own_ref[...], near[...], ((1,), (0,)))
            value += dot(other_ref[...], far[...], ((1,), (0,)))
            out[...] = jnp.where(mine, value, out[...].astype(F32)).astype(BF16)


def partial_sums(visits, base, core, own, other, gate_own, gate_other, up_own, up_other):
    rows, width = own.shape
    half = gate_other.shape[2]
    tile_block = pl.BlockSpec((TILE, width), lambda v, t, e, *_: (t[v], 0))
    near = pl.BlockSpec((None, width, half), lambda v, t, e, n, b, c: (e[v], 0, c[0]))
    far = pl.BlockSpec((None, width, half), lambda v, t, e, *_: (e[v], 0, 0))
    out = pl.BlockSpec((TILE, half), lambda v, t, e, *_: (t[v], 0))
    return pl.pallas_call(
        functools.partial(partial_kernel, TILE),
        grid_spec=pltpu.PrefetchScalarGridSpec(
            num_scalar_prefetch=5,
            grid=(visits[0].shape[0],),
            in_specs=[tile_block, tile_block, near, far, near, far],
            out_specs=[out, out],
        ),
        out_shape=[jax.ShapeDtypeStruct((rows, half), BF16)] * 2,
        compiler_params=pltpu.CompilerParams(vmem_limit_bytes=48 << 20),
        cost_estimate=pl.CostEstimate(
            flops=8 * rows * width * half, bytes_accessed=8 * rows * half, transcendentals=0
        ),
        name="partial_sums",
    )(*visits, base, core, own, other, gate_own, gate_other, up_own, up_other)


def down_kernel(
    tile, tiles, experts, total, base, core, low, high, hidden_ref, near, far, place_ref, gates_ref,
    own_out, other_out, own_acc, other_acc,
):
    v = pl.program_id(0)
    m = tiles[v]

    @pl.when(v == 0)
    def _():
        own_out[...] = jnp.zeros_like(own_out)
        other_out[...] = jnp.zeros_like(other_out)

    @pl.when(v < total[0])
    def _():
        e = experts[v]
        row = m * tile + lax.broadcasted_iota(jnp.int32, (tile, 1), 0)
        mine = (row >= base[e]) & (row < base[e + 1])
        for weight, acc in ((near, own_acc), (far, other_acc)):
            value = dot(hidden_ref[...], weight[...], ((1,), (1,)))
            acc[...] = jnp.where(mine, value, acc[...])

    final = jnp.where(v + 1 < total[0], tiles[jnp.minimum(v + 1, total[0] - 1)] != m, v + 1 == total[0])

    @pl.when(final)
    def _():
        row = m * tile + lax.broadcasted_iota(jnp.int32, (tile, 1), 0)

        def add(e, found):
            return jnp.where(place_ref[pl.ds(e, 1), :] == row, gates_ref[pl.ds(e, 1), :], found)

        tokens = place_ref.shape[1]
        found = lax.fori_loop(low[m], high[m], add, jnp.zeros((tile, tokens), F32))
        scale = jnp.sum(found, axis=1, keepdims=True)
        onehot = jnp.where(found != 0.0, 1.0, 0.0).astype(BF16)
        for acc, out in ((own_acc, own_out), (other_acc, other_out)):
            scaled = (acc[...] * scale).astype(BF16)
            out[...] += dot(onehot, scaled, ((0,), (0,)))


def down_and_mix(visits, base, core, spans, hidden, down_own, down_other, place, gates):
    rows, half = hidden.shape
    width = down_own.shape[1]
    experts, tokens = place.shape
    whole = lambda v, *_: (0, 0)
    out = pl.BlockSpec((tokens, width), whole)
    return pl.pallas_call(
        functools.partial(down_kernel, TILE),
        grid_spec=pltpu.PrefetchScalarGridSpec(
            num_scalar_prefetch=7,
            grid=(visits[0].shape[0],),
            in_specs=[
                pl.BlockSpec((TILE, half), lambda v, t, e, *_: (t[v], 0)),
                pl.BlockSpec((None, width, half), lambda v, t, e, n, b, c, *_: (e[v], 0, c[0])),
                pl.BlockSpec((None, width, half), lambda v, t, e, *_: (e[v], 0, 0)),
                pl.BlockSpec((experts, tokens), whole),
                pl.BlockSpec((experts, tokens), whole),
            ],
            out_specs=[out, out],
            scratch_shapes=[pltpu.VMEM((TILE, width), F32)] * 2,
        ),
        out_shape=[jax.ShapeDtypeStruct((tokens, width), F32)] * 2,
        compiler_params=pltpu.CompilerParams(vmem_limit_bytes=48 << 20),
        cost_estimate=pl.CostEstimate(
            flops=4 * rows * width * half, bytes_accessed=2 * rows * half, transcendentals=0
        ),
        name="down_and_mix",
    )(*visits, base, core, *spans, hidden, down_own, down_other, place, gates)


def fixed_weights(size, tokens, expert_ids, gate_weights, w_gate, w_up, w_down):
    count, picks = expert_ids.shape
    experts, width, hidden_units = w_gate.shape
    half = hidden_units // 2
    rows = size * count * picks
    chips = size // 2
    core = lax.axis_index("ep") % 2
    pairs = [(i, i ^ 1) for i in range(size)]
    same_core = [[2 * c + k for c in range(chips)] for k in range(2)]
    w_down = jnp.swapaxes(w_down, 1, 2)

    def swap_halves(w):
        return lax.ppermute(lax.dynamic_slice_in_dim(w, (1 - core) * half, half, 2), "ep", pairs)

    high = lax.reduce_precision(gate_weights, 8, 7)
    rest = gate_weights - high
    middle = lax.reduce_precision(rest, 8, 7)
    note = jnp.concatenate(
        [expert_ids.astype(F32), high, middle, lax.reduce_precision(rest - middle, 8, 7)], axis=1
    ).astype(BF16)
    parcels = jnp.concatenate(
        [
            tokens.reshape(count, size, width).swapaxes(0, 1),
            jnp.broadcast_to(note[None], (size,) + note.shape),
        ],
        axis=2,
    )
    arrived = lax.all_to_all(parcels, "ep", split_axis=0, concat_axis=0, tiled=True)
    arrived = arrived.reshape(size * count, width + 4 * picks)
    own = arrived[:, :width]
    other = lax.ppermute(own, "ep", pairs)
    note = arrived[:, width:].astype(F32)
    ids = note[:, :picks].astype(jnp.int32)
    weights = note[:, picks : 2 * picks] + (note[:, 2 * picks : 3 * picks] + note[:, 3 * picks :])

    gate_other, up_other, down_other = swap_halves(w_gate), swap_halves(w_up), swap_halves(w_down)

    place, gates, base = order_of(ids, weights, experts)
    visits = visits_of(base, rows, TILE)
    spans = spans_of(base, rows, TILE)
    which = core.astype(jnp.int32).reshape(1)
    own, other = sort_rows(spans, place, own, other, rows)
    gate, up = partial_sums(visits, base, which, own, other, w_gate, gate_other, w_up, up_other)
    gate = lax.psum_scatter(gate, "ep", scatter_dimension=0, axis_index_groups=same_core, tiled=True)
    up = lax.psum_scatter(up, "ep", scatter_dimension=0, axis_index_groups=same_core, tiled=True)
    hidden = (jax.nn.silu(gate.astype(F32)) * up.astype(F32)).astype(BF16)
    hidden = lax.all_gather(hidden, "ep", axis=0, axis_index_groups=same_core, tiled=True)
    mine, theirs = down_and_mix(
        visits, base, which, spans, hidden, w_down, down_other, place, gates
    )
    mixed = (mine + lax.ppermute(theirs, "ep", pairs)).astype(BF16)
    mixed = lax.all_to_all(
        mixed.reshape(size, count, width), "ep", split_axis=0, concat_axis=0, tiled=True
    )
    return mixed.swapaxes(0, 1).reshape(count, size * width)


def solution(mesh):
    size, inner = mesh.shape["ep"], mesh.shape["tp"]

    def body(tokens, expert_ids, gate_weights, w_gate, w_up, w_down):
        rows = size * math.prod(expert_ids.shape)
        sums = rows * w_gate.shape[2]
        even = size % 4 == 0 and rows % (size * TILE) == 0 and w_gate.shape[2] % 256 == 0
        args = (tokens, expert_ids, gate_weights, w_gate, w_up, w_down)
        if inner == 1 and even and sums <= 3 * math.prod(w_gate.shape):
            return fixed_weights(size, *args)
        return moved_weights(*args)

    placed = (
        P(("parts", "ep"), "tp"),
        P(("parts", "ep"), None),
        P(("parts", "ep"), None),
        P(None, "ep", "tp"),
        P(None, "ep", "tp"),
        P(None, "tp", "ep"),
    )
    return jax.shard_map(
        body, mesh=mesh, in_specs=placed, out_specs=P(("parts", "ep"), "tp"), check_vma=False
    )
```

time: 1050 us -> 646 us (0.62)
  blocking collectives: 458 us -> 19.5 us
  local copies, waits for them, and re-layouts: 241 us -> 21.7 us
  waiting for transfers between devices: 264 us -> 425 us
  Pallas kernels: 0 us -> 141 us
  other arithmetic: 44.8 us -> 12.1 us
  matrix products: 25.3 us -> 0 us
  between operations: 0.12 us -> 13.9 us
    all_to_all x3 -> x1, blocking collectives: 458 us -> 19.5 us  [fixed_weights(): lax.all_to_all(mixed.reshape(size, count, width), 'ep', split_axis=0, con...]
    reduce_scatter x0 -> x2, waiting for transfers between devices: none -> 298 us  [the longest x1 152 us: fixed_weights(): lax.psum_scatter(up, 'ep', scatter_dimension=0, axis_index_groups=same_co...]
    all_to_all x2 -> x1, waiting for transfers between devices: 264 us -> 5.36 us  [fixed_weights(): lax.all_to_all(parcels, 'ep', split_axis=0, concat_axis=0, tiled=True)]
    pallas_call x0 -> x3, Pallas kernels: none -> 141 us  [the longest x1 64.9 us: down_and_mix(): pl.pallas_call(functools.partial(down_kernel, TILE), grid_spec=pltpu.Pref...]
    scatter x1 -> x0, local copies, waits for them, and re-layouts: 123 us -> none  [fill_slots(): return empty.at[expert_ids, slot].set(spread)]
    all_gather x0 -> x1, waiting for transfers between devices: none -> 111 us  [fixed_weights(): lax.all_gather(hidden, 'ep', axis=0, axis_index_groups=same_core, tiled=T...]
    convert_element_type x1 -> x0, local copies, waits for them, and re-layouts: 60.7 us -> none  [body(): partial_value.astype(jnp.bfloat16)]
    unnamed x3 -> x1, other arithmetic: 37 us -> 0.01 us
  transfers between devices with their start and end apart: 2 -> 9, of which waited for: 2 -> 7; matrix products, arithmetic and copies ran while one was open for 2% -> 3% of each run, Pallas kernels for 0% -> 5%
where the time goes in v1:
time: 646 us; the launch traced here: 643 us
  waiting for transfers between devices  425 us (66%)
  Pallas kernels  141 us (22%)
  local copies, waits for them, and re-layouts  21.7 us (3%)
  blocking collectives  19.5 us (3%)
  between operations  13.9 us (2%)
  other arithmetic  12.1 us (2%)
  starting transfers between devices  9.6 us (1%)
    reduce_scatter x1, waiting for transfers between devices, fixed_weights(): lax.psum_scatter(up, 'ep', scatter_dimension=0, axis_index_groups=same_co...  152 us
    reduce_scatter x1, waiting for transfers between devices, fixed_weights(): lax.psum_scatter(gate, 'ep', scatter_dimension=0, axis_index_groups=same_...  146 us
    all_gather x1, waiting for transfers between devices, fixed_weights(): lax.all_gather(hidden, 'ep', axis=0, axis_index_groups=same_core, tiled=T...  111 us
    pallas_call x1, Pallas kernels, down_and_mix(): pl.pallas_call(functools.partial(down_kernel, TILE), grid_spec=pltpu.Pref...  64.9 us
    pallas_call x1, Pallas kernels, partial_sums(): pl.pallas_call(functools.partial(partial_kernel, TILE), grid_spec=pltpu.P...  43.6 us
    pallas_call x1, Pallas kernels, sort_rows(): pl.pallas_call(functools.partial(sort_kernel, TILE), grid_spec=pltpu.Pref...  32.5 us
    all_to_all x1, blocking collectives, fixed_weights(): lax.all_to_all(mixed.reshape(size, count, width), 'ep', split_axis=0, con...  19.5 us
  transfers between devices with their start and end apart: 9, of which 7 were waited for; matrix products, arithmetic and copies ran while one was open for 3% of the time, Pallas kernels for 5%

profile of v1, /device:TPU:15, one launch (start us, length us, event | category | flops | bytes accessed | tf_op | source)
XLA Modules:
  0.0 642.5 jit_solution(13290419327511922252)
XLA Ops:
  6.5 0.7 reduce-precision_convert_fusion.1
  7.2 0.7 convert_convert_fusion
  7.9 0.1 copy.34
  8.0 1.8 reshape.89
  9.8 0.2 copy.49
  10.0 1.0 pad_maximum_fusion
  11.0 6.6 %all-to-all-start = ((bf16[16,64,256]{2,1,0:T(8,128)(2,1)}), bf16[16,64,256]{2,1,0:T(8,128)(2,1)S(1)}, u32[]{:S(2)}, u32[]{:S(2)}) async-start(bf16[16,64,256]{2,1,0:T(8,128)(2,1)} %pad_maximum_fusion), calls=%async_computation | async-start | bytes 1048576 | tf_op jit(solution)/shard_map/all_to_all | solution.py:276
  17.6 4.4 constant_dynamic-slice_fusion.1
  22.0 0.4 collective-permute-start.1
  22.3 0.8 copy-done.1
  23.1 2.3 constant_dynamic-slice_fusion
  25.4 0.4 collective-permute-start.2
  25.7 5.4 all-to-all-done
  31.1 0.1 slice_convert_fusion.1
  31.3 0.5 fusion.6
  31.7 0.2 copy.35
  31.9 0.2 fusion.8
  32.1 4.5 reduce-window.14
  36.7 0.1 copy.36
  36.9 0.1 broadcast_add_fusion
  37.2 0.2 subtract_reduce_fusion
  37.6 0.5 slice.55
  38.1 0.1 reduce.1
  38.2 0.3 collective-permute-start
  39.1 0.1 convert_reduce_fusion.2.experts
  39.5 0.7 collective-permute-done.other_ref
  40.2 32.5 %sort_rows.1 = (bf16[8192,224]{1,0:T(8,128)(2,1)S(1)}, bf16[8192,224]{1,0:T(8,128)(2,1)}) custom-call(s32[32]{0:T(128)S(1)} %get-tuple-element.28.low, s32[32]{0:T(128)S(1)} %get-tuple-element.27.high, s32[16,1024]{1,0:T(8,128)S(1)} %add_select_fusion.place_ref, bf16[1024,224]{1,0:T(8,128)(2,1)S(1)} %bitcast.30, ...), custom_call_target="tpu_custom_call" | custom-call | flops 7516192768 | bytes 7340032 | tf_op jit(solution)/shard_map/sort_rows/pallas_call | solution.py:118
  72.7 2.0 copy-done
  74.7 43.6 %partial_sums.1 = (bf16[8192,512]{1,0:T(8,128)(2,1)}, bf16[8192,512]{1,0:T(8,128)(2,1)}) custom-call(s32[47]{0:T(128)S(1)} %fusion.11.tiles, s32[47]{0:T(128)S(1)} %convert_reduce_fusion.2.experts, s32[1]{0:T(128)} %bitcast.6.total, s32[17]{0:T(128)S(1)} %pad_add_fusion.base, s32[1]{0:T(128)} %bitcast.7.core, bf16[8192,224]{1,0:T(8,128)(2,1)} %copy-done, ...), custom_call_target="tpu_custom_call" | custom-call | flops 7516192768 | bytes 33554432 | tf_op jit(solution)/shard_map/partial_sums/pallas_call | solution.py:163
  118.3 0.7 reduce-scatter.5.cloned.1.call-update
  119.1 146.3 %reduce-scatter.3.cloned.1.call-done = bf16[1024,512]{1,0:T(8,128)(2,1)} async-done(((bf16[8192,512]{1,0:T(8,128)(2,1)}), bf16[1024,512]{1,0:T(8,128)(2,1)}) %reduce-scatter.3.cloned.1.call-update) | async-done | bytes 1048592 | tf_op jit(solution)/shard_map/reduce_scatter | solution.py:292
  265.4 152.1 %reduce-scatter.5.cloned.1.call-done = bf16[1024,512]{1,0:T(8,128)(2,1)} async-done(((bf16[8192,512]{1,0:T(8,128)(2,1)}), bf16[1024,512]{1,0:T(8,128)(2,1)}) %reduce-scatter.5.cloned.1.call-update) | async-done | bytes 1048592 | tf_op jit(solution)/shard_map/reduce_scatter | solution.py:293
  417.5 3.2 fusion.4
  420.8 4.2 dynamic-slice_bitcast_fusion
  425.0 0.9 collective-permute-start.3
  425.8 0.2 copy.39
  426.0 0.2 select_reduce_fusion.gates_ref
  426.2 6.0 collective-permute-done.3.far
  432.2 111.0 %all-gather.2.cloned.1.call-done.hidden_ref = bf16[8192,512]{1,0:T(8,128)(2,1)} async-done(((bf16[1024,512]{1,0:T(8,128)(2,1)}), bf16[8192,512]{1,0:T(8,128)(2,1)}) %all-gather.2.cloned.1.call-update) | async-done | bytes 8388624 | tf_op jit(solution)/shard_map/all_gather | solution.py:295
  543.2 64.9 %down_and_mix.1 = (f32[1024,224]{1,0:T(8,128)S(1)}, f32[1024,224]{1,0:T(8,128)S(1)}) custom-call(s32[47]{0:T(128)S(1)} %fusion.11.tiles, s32[47]{0:T(128)S(1)} %convert_reduce_fusion.2.experts, s32[1]{0:T(128)} %bitcast.6.total, s32[17]{0:T(128)S(1)} %pad_add_fusion.base, s32[1]{0:T(128)} %bitcast.7.core, s32[32]{0:T(128)S(1)} %get-tuple-element.28.low, ...), custom_call_target="tpu_custom_call" | custom-call | flops 3758096384 | bytes 8388608 | tf_op jit(solution)/shard_map/down_and_mix/pallas_call | solution.py:225
  608.1 1.3 copy.40
  609.4 1.1 collective-permute-start.4
  610.4 2.4 collective-permute-done.4
  612.9 1.5 copy.41
  614.4 0.2 add_convert_fusion
  614.6 19.5 %all_to_all.10 = bf16[16,64,224]{2,1,0:T(8,128)(2,1)S(1)} all-to-all(bf16[16,64,224]{2,1,0:T(8,128)(2,1)S(1)} %bitcast.32), channel_id=1, replica_groups=mesh['parts'=2,'ep'=16,'tp'=1] {'ep'}, dimensions={0} | all-to-all | bytes 917504 | tf_op jit(solution)/shard_map/all_to_all | solution.py:300
  634.1 0.3 copy.42
  634.4 1.6 reshape.96
  (32 shorter events, 1.0 us)
Async XLA Ops:
  11.0 20.1 %all-to-all-start = ((bf16[16,64,256]{2,1,0:T(8,128)(2,1)}), bf16[16,64,256]{2,1,0:T(8,128)(2,1)S(1)}, u32[]{:S(2)}, u32[]{:S(2)}) async-start(bf16[16,64,256]{2,1,0:T(8,128)(2,1)} %pad_maximum_fusion), calls=%async_computation | async-start | bytes 1048576 | tf_op jit(solution)/shard_map/all_to_all | solution.py:276
  17.5 247.9 %reduce-scatter.3.cloned.1.call-start = ((), (), s32[]{:S(2)}) async-start(), calls=%async_computation.4 | async-start | bytes 9437184 | tf_op jit(solution)/shard_map/reduce_scatter | solution.py:292
  17.6 5.5 copy-start.1
  22.0 52.7 %collective-permute-start.1 = (bf16[16,224,512]{2,1,0:T(8,128)(2,1)}, bf16[16,224,512]{2,1,0:T(8,128)(2,1)}, u32[]{:S(2)}, u32[]{:S(2)}) collective-permute-start(bf16[16,224,512]{2,1,0:T(8,128)(2,1)} %constant_dynamic-slice_fusion.1), channel_id=1, source_target_pairs={{0,1},{1,0},{2,3},{3,2},{4,5},{5,4},{6,7},{7,6},{8,9},{9,8},{10,11... | collective-permute-start | bytes 11010056 | tf_op jit(solution)/shard_map/ppermute | solution.py:261
  25.4 49.3 %collective-permute-start.2 = (bf16[16,224,512]{2,1,0:T(8,128)(2,1)}, bf16[16,224,512]{2,1,0:T(8,128)(2,1)}, u32[]{:S(2)}, u32[]{:S(2)}) collective-permute-start(bf16[16,224,512]{2,1,0:T(8,128)(2,1)} %constant_dynamic-slice_fusion), channel_id=1, source_target_pairs={{0,1},{1,0},{2,3},{3,2},{4,5},{5,4},{6,7},{7,6},{8,9},{9,8},{10,11... | collective-permute-start | bytes 11010056 | tf_op jit(solution)/shard_map/ppermute | solution.py:261
  38.2 2.0 collective-permute-start
  72.7 2.0 copy-start
  118.3 299.3 %reduce-scatter.5.cloned.1.call-start = ((), (), s32[]{:S(2)}) async-start(), calls=%async_computation.5 | async-start | bytes 9437184 | tf_op jit(solution)/shard_map/reduce_scatter | solution.py:293
  119.0 424.2 %all-gather.2.cloned.1.call-start = ((), (), s32[]{:S(2)}) async-start(), calls=%async_computation.6 | async-start | bytes 9437184 | tf_op jit(solution)/shard_map/all_gather | solution.py:295
  425.0 7.2 %collective-permute-start.3 = (bf16[16,224,512]{2,1,0:T(8,128)(2,1)}, bf16[16,224,512]{2,1,0:T(8,128)(2,1)}, u32[]{:S(2)}, u32[]{:S(2)}) collective-permute-start(bf16[16,224,512]{2,1,0:T(8,128)(2,1)} %dynamic-slice_bitcast_fusion), channel_id=1, source_target_pairs={{0,1},{1,0},{2,3},{3,2},{4,5},{5,4},{6,7},{7,6},{8,9},{9,8},{10,11... | collective-permute-start | bytes 11010056 | tf_op jit(solution)/shard_map/ppermute | solution.py:261
  609.4 3.5 collective-permute-start.4
Sparse Core Ops, SparseCore 0:
  118.4 146.9 reduce-scatter.2
  269.5 148.0 reduce-scatter.4
  420.9 122.3 all-gather.1

commit v2 on v0

v2 whole, which is shorter than its diff:
```python
import functools
import math

import jax
import jax.numpy as jnp
from jax import lax
from jax.experimental import pallas as pl
from jax.experimental.pallas import tpu as pltpu
from jax.sharding import PartitionSpec as P

BF16 = jnp.bfloat16
F32 = jnp.float32
TILE = 256
BLOCK = 1024
LANES = 256


def slots_of(block_ids, experts):
    flat = block_ids.reshape(-1)
    onehot = (flat[:, None] == jnp.arange(experts, dtype=jnp.int32)[None, :]).astype(jnp.int32)
    before = jnp.cumsum(onehot, axis=0) - onehot
    return jnp.sum(before * onehot, axis=1).reshape(block_ids.shape)


def fill_slots(rows, expert_ids, slot, experts, per_expert):
    count, picks = expert_ids.shape
    spread = jnp.broadcast_to(rows[:, None, :], (count, picks, rows.shape[1]))
    empty = jnp.zeros((experts, per_expert, rows.shape[1]), BF16)
    return empty.at[expert_ids, slot].set(spread)


def moved_weights(tokens, expert_ids, gate_weights, w_gate, w_up, w_down):
    tok_rows, picks = expert_ids.shape
    experts = w_gate.shape[0]
    per_expert = min(tok_rows, 3 * tok_rows * picks // (2 * experts))
    slot = slots_of(expert_ids, experts)
    features = lax.all_gather(tokens, "tp", axis=1, tiled=True)
    outgoing = fill_slots(features, expert_ids, slot, experts, per_expert)
    arrived = lax.all_to_all(outgoing, "ep", split_axis=0, concat_axis=1, tiled=True)
    gate_owned, up_owned = (
        lax.all_to_all(w_gate, "ep", split_axis=0, concat_axis=1, tiled=True),
        lax.all_to_all(w_up, "ep", split_axis=0, concat_axis=1, tiled=True),
    )
    gate = jnp.einsum("ecd,edf->ecf", arrived, gate_owned, preferred_element_type=F32)
    up = jnp.einsum("ecd,edf->ecf", arrived, up_owned, preferred_element_type=F32)
    hidden = (jax.nn.silu(gate) * up).astype(BF16)
    down_owned = lax.all_to_all(w_down, "ep", split_axis=0, concat_axis=2, tiled=True)
    partial_value = jnp.einsum("ecf,efd->ecd", hidden, down_owned, preferred_element_type=F32)
    expert_out = lax.psum_scatter(
        partial_value.astype(BF16), "tp", scatter_dimension=2, tiled=True
    )
    returned = lax.all_to_all(expert_out, "ep", split_axis=1, concat_axis=0, tiled=True)
    picked = returned[expert_ids, slot]
    mixed = jnp.sum(gate_weights[:, :, None] * picked.astype(F32), axis=1)
    return mixed.astype(BF16)


def dot(a, b, contract):
    return lax.dot_general(a, b, ((contract[0], contract[1]), ((), ())), preferred_element_type=F32)


def order_of(ids, weights, experts):
    names = jnp.arange(experts, dtype=jnp.int32)
    mask = jnp.any(ids.T[None] == names[:, None, None], axis=1)
    gates = jnp.sum(jnp.where(ids[:, :, None] == names, weights[:, :, None], 0.0), axis=1)
    count = jnp.cumsum(mask.astype(jnp.int32), axis=1)
    total = count[:, -1]
    ends = jnp.cumsum(total)
    place = jnp.where(mask, count - 1 + (ends - total)[:, None], -1)
    base = jnp.concatenate([jnp.zeros((1,), jnp.int32), ends])
    return place, gates, base


def spans_of(base, rows):
    low = jnp.arange(rows // TILE, dtype=jnp.int32)[:, None] * TILE
    return (
        jnp.sum((base[None, 1:] <= low).astype(jnp.int32), axis=1),
        jnp.sum((base[None, :-1] < low + TILE).astype(jnp.int32), axis=1),
    )


def split3(value):
    high = lax.reduce_precision(value, 8, 7)
    middle = lax.reduce_precision(value - high, 8, 7)
    return high, middle, lax.reduce_precision(value - high - middle, 8, 7)


def onehot_of(place_ref, row0, low, high):
    tokens = place_ref.shape[1]
    number = lax.broadcasted_iota(jnp.int32, (TILE, tokens), 0).astype(F32).astype(BF16)

    def add(e, found):
        away = place_ref[pl.ds(e, 1), :] - row0
        away = jnp.where((away >= 0) & (away < TILE), away, -1).astype(F32).astype(BF16)
        return jnp.where(number == away, jnp.ones((), BF16), found)

    return lax.fori_loop(low, high, add, jnp.zeros((TILE, tokens), BF16))


def mine_of(base, e, row0):
    row = row0 + lax.broadcasted_iota(jnp.int32, (TILE, 1), 0)
    return (row >= base[e]) & (row < base[e + 1])


def sort_kernel(low, high, base, place_ref, gates_ref, *refs):
    slices, (out, scale_out) = refs[:-2], refs[-2:]
    experts = place_ref.shape[0]
    lane = lax.broadcasted_iota(jnp.int32, (TILE, scale_out.shape[1]), 1)

    @pl.loop(0, BLOCK // TILE)
    def _(part):
        i = pl.program_id(0) * (BLOCK // TILE) + part
        row0 = i * TILE
        here = pl.ds(pl.multiple_of(part * TILE, TILE), TILE)
        onehot = onehot_of(place_ref, row0, low[i], high[i])
        for k, ref in enumerate(slices):
            out[here, k * LANES : (k + 1) * LANES] = dot(onehot, ref[...], ((1,), (0,))).astype(BF16)
        gates = dot(onehot, gates_ref[...], ((1,), (0,)))
        name = lax.fori_loop(
            low[i],
            high[i],
            lambda e, name: jnp.where(mine_of(base, e, row0), e, name),
            jnp.zeros((TILE, 1), jnp.int32),
        )
        kept = (lane == name) | (lane == name + experts) | (lane == name + 2 * experts)
        scale = jnp.sum(jnp.where(kept, gates, 0.0), axis=1, keepdims=True)
        scale_out[here, :] = jnp.broadcast_to(scale, lane.shape)


def sort_rows(spans, base, place, gates, slices, rows, units):
    experts, tokens = place.shape
    whole = lambda i, *_: (0, 0)
    width = len(slices) * LANES
    return pl.pallas_call(
        sort_kernel,
        grid_spec=pltpu.PrefetchScalarGridSpec(
            num_scalar_prefetch=3,
            grid=(rows // BLOCK,),
            in_specs=[
                pl.BlockSpec((experts, tokens), whole),
                pl.BlockSpec((tokens, units), whole),
            ]
            + [pl.BlockSpec((tokens, LANES), whole)] * len(slices),
            out_specs=[
                pl.BlockSpec((BLOCK, width), lambda i, *_: (i, 0)),
                pl.BlockSpec((BLOCK, units), lambda i, *_: (i, 0)),
            ],
        ),
        out_shape=[
            jax.ShapeDtypeStruct((rows, width), BF16),
            jax.ShapeDtypeStruct((rows, units), F32),
        ],
        compiler_params=pltpu.CompilerParams(vmem_limit_bytes=48 << 20),
        cost_estimate=pl.CostEstimate(
            flops=2 * rows * tokens * width, bytes_accessed=4 * rows * width, transcendentals=0
        ),
        name="sort_rows",
    )(*spans, base, place, gates, *slices)


def partial_kernel(low, high, base, rows_ref, *refs):
    weights, out = refs[:-1], refs[-1]
    width = weights[0].shape[1]

    @pl.loop(0, BLOCK // TILE)
    def _(part):
        i = pl.program_id(0) * (BLOCK // TILE) + part
        here = pl.ds(pl.multiple_of(part * TILE, TILE), TILE)

        def add(e, kept):
            value = kept
            total = 0.0
            for k, weight in enumerate(weights):
                total += dot(rows_ref[here, k * LANES : k * LANES + width], weight[e], ((1,), (0,)))
            return jnp.where(mine_of(base, e, i * TILE), total, value)

        out[here, :] = lax.fori_loop(
            low[i], high[i], add, jnp.zeros((TILE, out.shape[1]), F32)
        ).astype(BF16)


def partial_sums(spans, base, rows_in, weights):
    rows = rows_in.shape[0]
    experts, width, units = weights[0].shape
    return pl.pallas_call(
        partial_kernel,
        grid_spec=pltpu.PrefetchScalarGridSpec(
            num_scalar_prefetch=3,
            grid=(rows // BLOCK,),
            in_specs=[pl.BlockSpec((BLOCK, rows_in.shape[1]), lambda i, *_: (i, 0))]
            + [pl.BlockSpec((experts, width, units), lambda i, *_: (0, 0, 0))] * len(weights),
            out_specs=pl.BlockSpec((BLOCK, units), lambda i, *_: (i, 0)),
        ),
        out_shape=jax.ShapeDtypeStruct((rows, units), BF16),
        compiler_params=pltpu.CompilerParams(vmem_limit_bytes=48 << 20),
        cost_estimate=pl.CostEstimate(
            flops=2 * rows * rows_in.shape[1] * units,
            bytes_accessed=2 * rows * rows_in.shape[1],
            transcendentals=0,
        ),
        name="partial_sums",
    )(*spans, base, rows_in, *weights)


def down_kernel(low, high, base, place_ref, *refs):
    count = len(refs) // 2 - 1
    hidden, weights = refs[:2], refs[2 : 2 + 4]
    out, onehot_ref, value_ref = refs[6:]
    width = weights[0].shape[1]

    @pl.when(pl.program_id(0) == 0)
    def _():
        out[...] = jnp.zeros_like(out)
        value_ref[...] = jnp.zeros_like(value_ref)

    @pl.loop(0, BLOCK // TILE)
    def _(part):
        i = pl.program_id(0) * (BLOCK // TILE) + part
        here = pl.ds(pl.multiple_of(part * TILE, TILE), TILE)
        units = jnp.concatenate([hidden[0][here, :], hidden[1][here, :]], axis=1)
        onehot_ref[here, :] = onehot_of(place_ref, i * TILE, low[i], high[i])
        for k, weight in enumerate(weights):
            value_ref[here, k * LANES : k * LANES + width] = lax.fori_loop(
                low[i],
                high[i],
                lambda e, kept: jnp.where(
                    mine_of(base, e, i * TILE), dot(units, weight[e], ((1,), (1,))), kept
                ),
                jnp.zeros((TILE, width), F32),
            ).astype(BF16)

    out[...] += dot(onehot_ref[...], value_ref[...], ((0,), (0,)))


def down_and_mix(spans, base, place, hidden, weights):
    rows, units = hidden[0].shape
    experts, tokens = place.shape
    width = len(weights) * LANES
    block = pl.BlockSpec((BLOCK, units), lambda i, *_: (i, 0))
    return pl.pallas_call(
        down_kernel,
        grid_spec=pltpu.PrefetchScalarGridSpec(
            num_scalar_prefetch=3,
            grid=(rows // BLOCK,),
            in_specs=[pl.BlockSpec((experts, tokens), lambda i, *_: (0, 0)), block, block]
            + [pl.BlockSpec(weights[0].shape, lambda i, *_: (0, 0, 0))] * len(weights),
            out_specs=pl.BlockSpec((tokens, width), lambda i, *_: (0, 0)),
            scratch_shapes=[pltpu.VMEM((BLOCK, tokens), BF16), pltpu.VMEM((BLOCK, width), BF16)],
        ),
        out_shape=jax.ShapeDtypeStruct((tokens, width), F32),
        compiler_params=pltpu.CompilerParams(vmem_limit_bytes=52 << 20),
        cost_estimate=pl.CostEstimate(
            flops=4 * rows * width * units, bytes_accessed=4 * rows * units, transcendentals=0
        ),
        name="down_and_mix",
    )(*spans, base, place, *hidden, *weights)


def links_of(step, pieces, places, down):
    pairs = []
    for place in range(places):
        to = place - 1 if down else place + 1
        hop = places - 1 - place if down else place
        if 0 <= to < places and 0 <= step - hop < pieces:
            pairs += [(4 * place + k, 4 * to + k) for k in range(4)]
    return pairs


def sum_flow(take, pieces, places, place, down):
    hop = places - 1 - place if down else place
    sums, got = [], None
    for step in range(pieces + places - 1):
        piece = take(jnp.clip(step - hop, 0, pieces - 1))
        if got is not None:
            piece = (piece.astype(F32) + got.astype(F32)).astype(BF16)
        if step >= places - 1:
            sums.append(piece)
        if step < pieces + places - 2:
            got = lax.ppermute(piece, "ep", links_of(step, pieces, places, down))
    return sums


def copy_flow(chunks, places, place, down):
    hop = places - 1 - place if down else place
    pieces, held, got = len(chunks), [], None
    for step in range(pieces + places - 1):
        piece = chunks[min(step, pieces - 1)]
        if got is not None:
            piece = jnp.where(hop == 0, piece, got)
        held.append(piece)
        if step < pieces + places - 2:
            got = lax.ppermute(piece, "ep", links_of(step, pieces, places, down))
    size = chunks[0].shape[0]
    return lax.dynamic_slice_in_dim(jnp.concatenate(held, axis=0), hop * size, pieces * size, 0)


def fixed_weights(size, tokens, expert_ids, gate_weights, w_gate, w_up, w_down):
    count, picks = expert_ids.shape
    experts, width, hidden_units = w_gate.shape
    quarter = hidden_units // 4
    units = quarter // 2
    rows = size * count * picks
    places = size // 4
    me, plane = lax.axis_index("ep"), lax.axis_index("parts")
    core, place_on_line = me % 2, me // 4
    w_down = jnp.swapaxes(w_down, 1, 2)

    twins = [(i, i ^ 1) for i in range(size)]
    cross = [
        (p * size + i, p * size + (i ^ 2 ^ p)) for p in range(2) for i in range(size)
    ]
    to_twin = lambda value: lax.ppermute(value, "ep", twins)
    to_cross = lambda value: lax.ppermute(value, ("parts", "ep"), cross)
    to_plane = lambda value: lax.ppermute(value, "parts", [(0, 1), (1, 0)])
    my_quarter = me % 4
    twin_quarter = my_quarter ^ 1
    cross_quarter = my_quarter ^ 2 ^ plane

    def gate_up(f):
        def cut(q, e0, e1):
            at = q * quarter + f * units
            return jnp.concatenate(
                [lax.dynamic_slice_in_dim(w[e0:e1], at, units, 2) for w in (w_gate, w_up)], axis=2
            )
        return cut

    def down(q, e0, e1):
        return lax.dynamic_slice_in_dim(w_down[e0:e1], q * quarter, quarter, 2)

    note = jnp.concatenate([expert_ids.astype(F32), *split3(gate_weights)], axis=1).astype(BF16)
    fill = LANES - width - note.shape[1]
    parcels = jnp.concatenate(
        [
            tokens.reshape(count, size, width).swapaxes(0, 1),
            jnp.broadcast_to(jnp.pad(note, ((0, 0), (0, fill)))[None], (size, count, LANES - width)),
        ],
        axis=2,
    )
    own = lax.all_to_all(parcels, "ep", split_axis=0, concat_axis=0, tiled=True)
    own = own.reshape(size * count, LANES)
    far = to_cross(own)
    slices = [own, to_twin(own), far, to_twin(far)]
    note = own[:, width : width + 4 * picks].astype(F32)
    ids = note[:, :picks].astype(jnp.int32)
    weights = note[:, picks : 2 * picks] + (note[:, 2 * picks : 3 * picks] + note[:, 3 * picks :])
    place, gates, base = order_of(ids, weights, experts)
    spans = spans_of(base, rows)
    gates = jnp.concatenate(split3(gates), axis=1).astype(BF16)
    gates = jnp.pad(gates, ((0, 0), (0, units - gates.shape[1])))

    half = experts // 2
    last = None
    held = []
    for cut in (gate_up(0), gate_up(1), down):
        across, beside = [], []
        for e0 in (0, half):
            piece = cut(cross_quarter, e0, e0 + half)
            if last is not None:
                piece, _ = lax.optimization_barrier((piece, last))
            last = to_cross(piece)
            across.append(last)
            beside.append(to_plane(last))
        held.append(
            [
                cut(my_quarter, 0, experts),
                to_twin(cut(twin_quarter, 0, experts)),
                jnp.concatenate(across, axis=0),
                jnp.concatenate(beside, axis=0),
            ]
        )

    sorted_rows, scale = sort_rows(spans, base, place, gates, slices, rows, units)
    hidden = []
    chunks, streams = 4, 2
    side = rows // 2
    size_of = side // (chunks * streams)
    for f in range(2):
        sums = partial_sums(spans, base, sorted_rows, held[f])
        sides = []
        for is_down in (True, False):
            first_row = 0 if is_down else side
            flows = [
                sum_flow(
                    lambda k, m=m: lax.dynamic_slice_in_dim(
                        sums, first_row + (k * streams + m) * size_of, size_of, 0
                    ),
                    chunks, places, place_on_line, is_down,
                )
                for m in range(streams)
            ]
            ready = []
            for k in range(chunks):
                total = jnp.concatenate([flow[k] for flow in flows], axis=0).astype(F32)
                at = first_row + k * streams * size_of
                gate, up = total[:, :units], total[:, units:]
                ready.append(
                    (jax.nn.silu(gate) * up * scale[at : at + streams * size_of]).astype(BF16)
                )
            sides.append(copy_flow(ready, places, place_on_line, not is_down))
        hidden.append(jnp.concatenate(sides, axis=0))

    mixed = down_and_mix(spans, base, place, hidden, held[2])
    mine, twin, far, far_twin = (mixed[:, k * LANES : k * LANES + width] for k in range(4))
    moved = to_twin(jnp.concatenate([far_twin, twin], axis=0).astype(BF16)).astype(F32)
    tokens_all = size * count
    far = to_cross((far + moved[:tokens_all]).astype(BF16)).astype(F32)
    mixed = (mine + moved[tokens_all:] + far).astype(BF16)
    mixed = lax.all_to_all(
        mixed.reshape(size, count, width), "ep", split_axis=0, concat_axis=0, tiled=True
    )
    return mixed.swapaxes(0, 1).reshape(count, size * width)


def solution(mesh):
    size, inner = mesh.shape["ep"], mesh.shape["tp"]

    def body(tokens, expert_ids, gate_weights, w_gate, w_up, w_down):
        rows = size * math.prod(expert_ids.shape)
        sums = rows * w_gate.shape[2]
        experts, width, units = w_gate.shape
        even = (
            size % 4 == 0
            and size > 4
            and mesh.shape["parts"] == 2
            and rows % (2 * BLOCK) == 0
            and units % 1024 == 0
            and experts % 2 == 0
            and 3 * experts <= units // 8
            and width + 4 * expert_ids.shape[1] <= LANES
        )
        args = (tokens, expert_ids, gate_weights, w_gate, w_up, w_down)
        if inner == 1 and even and sums <= 3 * math.prod(w_gate.shape):
            return fixed_weights(size, *args)
        return moved_weights(*args)

    placed = (
        P(("parts", "ep"), "tp"),
        P(("parts", "ep"), None),
        P(("parts", "ep"), None),
        P(None, "ep", "tp"),
        P(None, "ep", "tp"),
        P(None, "tp", "ep"),
    )
    return jax.shard_map(
        body, mesh=mesh, in_specs=placed, out_specs=P(("parts", "ep"), "tp"), check_vma=False
    )
```

time: 1050 us -> 628 us (0.60)
  blocking collectives: 458 us -> 23.1 us
  local copies, waits for them, and re-layouts: 241 us -> 60.4 us
  starting transfers between devices: 10.8 us -> 188 us
  Pallas kernels: 0 us -> 167 us
  waiting for transfers between devices: 264 us -> 122 us
  matrix products: 25.3 us -> 0 us
  other arithmetic: 44.8 us -> 60.1 us
    all_to_all x3 -> x1, blocking collectives: 458 us -> 23.1 us  [fixed_weights(): lax.all_to_all(mixed.reshape(size, count, width), 'ep', split_axis=0, con...]
    all_to_all x2 -> x1, waiting for transfers between devices: 264 us -> 0.01 us  [fixed_weights(): own = lax.all_to_all(parcels, 'ep', split_axis=0, concat_axis=0, tiled=True)]
    ppermute x0 -> x92, starting transfers between devices: none -> 182 us  [the longest x48 94.3 us: sum_flow(): got = lax.ppermute(piece, 'ep', links_of(step, pieces, places, down))]
    pallas_call x0 -> x4, Pallas kernels: none -> 167 us  [the longest x1 82.7 us: down_and_mix(): pl.pallas_call(down_kernel, grid_spec=pltpu.PrefetchScalarGridSpec(num_sc...]
    scatter x1 -> x0, local copies, waits for them, and re-layouts: 123 us -> none  [fill_slots(): return empty.at[expert_ids, slot].set(spread)]
    ppermute x0 -> x92, waiting for transfers between devices: none -> 122 us  [the longest x48 40 us: sum_flow(): got = lax.ppermute(piece, 'ep', links_of(step, pieces, places, down))]
    convert_element_type x1, local copies, waits for them, and re-layouts: 60.7 us -> 1.81 us  [fixed_weights(): ids = note[:, :picks].astype(jnp.int32)]
    unnamed x22 -> x36, local copies, waits for them, and re-layouts: 35.2 us -> 2.47 us
  transfers between devices with their start and end apart: 2 -> 93, of which waited for: 2 -> 28; matrix products, arithmetic and copies ran while one was open for 2% -> 17% of each run, Pallas kernels for 0% -> 10%
where the time goes in v2:
time: 628 us; the launch traced here: 622 us
  starting transfers between devices  188 us (30%)
  Pallas kernels  167 us (27%)
  waiting for transfers between devices  122 us (19%)
  local copies, waits for them, and re-layouts  60.4 us (10%)
  other arithmetic  60.1 us (10%)
  blocking collectives  23.1 us (4%)
    ppermute x48, starting transfers between devices, sum_flow(): got = lax.ppermute(piece, 'ep', links_of(step, pieces, places, down))  94.3 us
    pallas_call x1, Pallas kernels, down_and_mix(): pl.pallas_call(down_kernel, grid_spec=pltpu.PrefetchScalarGridSpec(num_sc...  82.7 us
    ppermute x24, starting transfers between devices, copy_flow(): got = lax.ppermute(piece, 'ep', links_of(step, pieces, places, down))  53.3 us
    pallas_call x1, Pallas kernels, sort_rows(): pl.pallas_call(sort_kernel, grid_spec=pltpu.PrefetchScalarGridSpec(num_sc...  44.2 us
    ppermute x48, waiting for transfers between devices, sum_flow(): got = lax.ppermute(piece, 'ep', links_of(step, pieces, places, down))  40 us
    pallas_call x2, Pallas kernels, partial_sums(): pl.pallas_call(partial_kernel, grid_spec=pltpu.PrefetchScalarGridSpec(num...  40 us
    ppermute x8, waiting for transfers between devices, fixed_weights(): to_cross = lambda value: lax.ppermute(value, ('parts', 'ep'), cross)  38.5 us
    all_to_all x1, blocking collectives, fixed_weights(): lax.all_to_all(mixed.reshape(size, count, width), 'ep', split_axis=0, con...  23.1 us
  transfers between devices with their start and end apart: 93, of which 28 were waited for; matrix products, arithmetic and copies ran while one was open for 17% of the time, Pallas kernels for 10%

profile of v2, /device:TPU:15, one launch (start us, length us, event | category | flops | bytes accessed | tf_op | source)
XLA Modules:
  0.0 622.2 jit_solution(3309472705460492487)
XLA Ops:
  4.4 6.6 %all-to-all-start = ((bf16[16,64,256]{2,1,0:T(8,128)(2,1)}), bf16[16,64,256]{2,1,0:T(8,128)(2,1)S(1)}, u32[]{:S(2)}, u32[]{:S(2)}) async-start(bf16[16,64,256]{2,1,0:T(8,128)(2,1)} %pad_maximum_fusion.17), calls=%async_computation | async-start | bytes 1048576 | tf_op jit(solution)/shard_map/all_to_all | solution.py:339
  11.0 7.2 %fusion.68 = (bf16[8,224,1024]{2,1,0:T(8,128)(2,1)}, bf16[8,224,1024]{2,1,0:T(8,128)(2,1)}) fusion(bf16[16,224,1024]{2,1,0:T(8,128)(2,1)} %param.10), kind=kLoop, calls=%fused_computation.252 | loop fusion | bytes 14680064 | tf_op jit(solution)/shard_map/slice | solution.py:323
  18.2 7.3 %fusion.67 = (bf16[8,224,1024]{2,1,0:T(8,128)(2,1)}, bf16[8,224,1024]{2,1,0:T(8,128)(2,1)}) fusion(bf16[16,224,1024]{2,1,0:T(8,128)(2,1)} %param.9), kind=kLoop, calls=%fused_computation.251 | loop fusion | bytes 14680064 | tf_op jit(solution)/shard_map/slice | solution.py:323
  28.1 2.6 constant_dynamic-slice_fusion.9
  32.3 5.4 constant_dynamic-slice_fusion.12
  44.2 10.2 %collective-permute-done.4 = bf16[8,224,256]{2,1,0:T(8,128)(2,1)} collective-permute-done((bf16[8,224,256]{2,1,0:T(8,128)(2,1)}, bf16[8,224,256]{2,1,0:T(8,128)(2,1)}, u32[]{:S(2)}, u32[]{:S(2)}) %collective-permute-start.4) | collective-permute-done | bytes 917536 | tf_op jit(solution)/shard_map/ppermute | solution.py:313
  60.8 4.5 reduce-window.10
  73.8 14.4 %collective-permute-done.1.refs_2_ = bf16[1024,256]{1,0:T(8,128)(2,1)S(1)} collective-permute-done((bf16[1024,256]{1,0:T(8,128)(2,1)S(1)}, bf16[1024,256]{1,0:T(8,128)(2,1)S(1)}, u32[]{:S(2)}, u32[]{:S(2)}) %collective-permute-start.1) | collective-permute-done | bytes 524320 | tf_op jit(solution)/shard_map/ppermute | solution.py:313
  94.7 44.2 %sort_rows.1 = (bf16[8192,1024]{1,0:T(8,128)(2,1)}, f32[8192,128]{1,0:T(8,128)}) custom-call(s32[32]{0:T(128)S(1)} %get-tuple-element.179.low, s32[32]{0:T(128)S(1)} %get-tuple-element.178.high, s32[17]{0:T(128)S(1)} %pad_add_fusion.base, s32[16,1024]{1,0:T(8,128)S(1)} %add_select_fusion.place_ref, bf16[1024,128]{1,0:T(8,128)(2,1)S(1)} %pad.4.gates_ref, ...), custom_call_target="tpu_custom_call" | custom-call | flops 17179869184 | bytes 33554432 | tf_op jit(solution)/shard_map/sort_rows/pallas_call | solution.py:134
  141.5 20.0 %partial_sums.2 = bf16[8192,256]{1,0:T(8,128)(2,1)} custom-call(s32[32]{0:T(128)S(1)} %get-tuple-element.179.low, s32[32]{0:T(128)S(1)} %get-tuple-element.178.high, s32[17]{0:T(128)S(1)} %pad_add_fusion.base, bf16[8192,1024]{1,0:T(8,128)(2,1)} %get-tuple-element.12.rows_ref, bf16[16,224,256]{2,1,0:T(8,128)(2,1)S(1)} %pad_maximum_fusion.2.refs_0_, ...), custom_call_target="tpu_custom_call" | custom-call | flops 4294967296 | bytes 16777216 | tf_op jit(solution)/shard_map/partial_sums/pallas_call | solution.py:185
  167.9 7.4 %fusion.66 = (bf16[8,224,1024]{2,1,0:T(8,128)(2,1)}, bf16[8,224,1024]{2,1,0:T(8,128)(2,1)}) fusion(bf16[16,224,1024]{2,1,0:T(8,128)(2,1)} %bitcast.29), kind=kLoop, calls=%fused_computation.250 | loop fusion | bytes 14680064 | tf_op jit(solution)/shard_map/slice | solution.py:328
  178.8 4.7 collective-permute-done.9
  191.2 5.6 collective-permute-done.10
  203.0 5.5 collective-permute-start.27
  212.2 4.0 collective-permute-start.13
  218.4 3.7 dynamic-slice_bitcast_fusion
  234.1 2.7 collective-permute-done.31
  236.8 4.4 collective-permute-start.86
  243.4 17.6 %collective-permute-done.48 = bf16[8,224,256]{2,1,0:T(8,128)(2,1)S(1)} collective-permute-done((bf16[8,224,256]{2,1,0:T(8,128)(2,1)}, bf16[8,224,256]{2,1,0:T(8,128)(2,1)S(1)}, u32[]{:S(2)}, u32[]{:S(2)}) %collective-permute-start.48) | collective-permute-done | bytes 917536 | tf_op jit(solution)/shard_map/ppermute | solution.py:314
  266.2 20.0 %partial_sums.3 = bf16[8192,256]{1,0:T(8,128)(2,1)} custom-call(s32[32]{0:T(128)S(1)} %get-tuple-element.179.low, s32[32]{0:T(128)S(1)} %get-tuple-element.178.high, s32[17]{0:T(128)S(1)} %pad_add_fusion.base, bf16[8192,1024]{1,0:T(8,128)(2,1)} %get-tuple-element.12.rows_ref, bf16[16,224,256]{2,1,0:T(8,128)(2,1)S(1)} %pad_maximum_fusion.6.refs_0_, ...), custom_call_target="tpu_custom_call" | custom-call | flops 4294967296 | bytes 16777216 | tf_op jit(solution)/shard_map/partial_sums/pallas_call | solution.py:185
  288.5 3.6 collective-permute-start.17
  294.1 3.4 collective-permute-start.35
  303.2 4.9 collective-permute-start.87
  309.6 6.1 collective-permute-done.50
  326.2 5.6 collective-permute-done.21
  333.5 4.0 collective-permute-start.68
  339.6 3.4 collective-permute-start.54
  345.0 2.7 pad_maximum_fusion.10.refs_4_
  348.0 3.4 collective-permute-start.69
  358.9 2.9 collective-permute-start.73
  364.8 8.2 %collective-permute-start.85 = (bf16[16,224,256]{2,1,0:T(8,128)(2,1)S(1)}, bf16[16,224,256]{2,1,0:T(8,128)(2,1)S(1)}, u32[]{:S(2)}, u32[]{:S(2)}) collective-permute-start(bf16[16,224,256]{2,1,0:T(8,128)(2,1)S(1)} %copy-done.11), channel_id=1, source_target_pairs={{0,1},{1,0},{2,3},{3,2},{4,5},{5,4},{6,7},{7,6},{8,9},{9,8},{10,11... | collective-permute-start | bytes 5505032 | tf_op jit(solution)/shard_map/ppermute | solution.py:312
  376.8 4.0 collective-permute-start.58
  382.9 3.4 collective-permute-start.76
  406.6 3.7 collective-permute-start.63
  417.0 5.6 collective-permute-start.64
  425.1 4.1 collective-permute-start.19
  430.7 4.0 collective-permute-start.65
  440.9 2.8 collective-permute-start.81
  446.1 3.3 collective-permute-done.81
  449.8 4.1 collective-permute-start.82
  456.0 4.0 collective-permute-done.82
  460.2 4.1 collective-permute-start.83
  465.9 4.0 collective-permute-done.83
  472.9 4.8 collective-permute-done.84
  482.3 82.7 %down_and_mix.1 = f32[1024,1024]{1,0:T(8,128)} custom-call(s32[32]{0:T(128)S(1)} %get-tuple-element.179.low, s32[32]{0:T(128)S(1)} %get-tuple-element.178.high, s32[17]{0:T(128)S(1)} %pad_add_fusion.base, s32[16,1024]{1,0:T(8,128)S(1)} %add_select_fusion.place_ref, bf16[8192,128]{1,0:T(8,128)(2,1)} %pad_maximum_fusion.refs_0_, ...), custom_call_target="tpu_custom_call" | custom-call | flops 4294967296 | bytes 4194304 | tf_op jit(solution)/shard_map/down_and_mix/pallas_call | solution.py:240
  568.3 9.2 %collective-permute-start.90 = (bf16[2048,224]{0,1:T(8,128)(2,1)S(1)}, bf16[2048,224]{0,1:T(8,128)(2,1)S(1)}, u32[]{:S(2)}, u32[]{:S(2)}) collective-permute-start(bf16[2048,224]{0,1:T(8,128)(2,1)S(1)} %copy.36), channel_id=1, source_target_pairs={{0,1},{1,0},{2,3},{3,2},{4,5},{5,4},{6,7},{7,6},{8,9},{9,8},{10,11... | collective-permute-start | bytes 2752520 | tf_op jit(solution)/shard_map/ppermute | solution.py:312
  581.8 13.9 %collective-permute-done.91 = bf16[1024,224]{1,0:T(8,128)(2,1)S(1)} collective-permute-done((bf16[1024,224]{1,0:T(8,128)(2,1)S(1)}, bf16[1024,224]{1,0:T(8,128)(2,1)S(1)}, u32[]{:S(2)}, u32[]{:S(2)}) %collective-permute-start.91) | collective-permute-done | bytes 458784 | tf_op jit(solution)/shard_map/ppermute | solution.py:313
  597.1 23.1 %all_to_all.10 = bf16[16,64,224]{2,1,0:T(8,128)(2,1)S(1)} all-to-all(bf16[16,64,224]{2,1,0:T(8,128)(2,1)S(1)} %bitcast.32), channel_id=1, replica_groups=mesh['parts'=2,'ep'=16,'tp'=1] {'ep'}, dimensions={0} | all-to-all | bytes 917504 | tf_op jit(solution)/shard_map/all_to_all | solution.py:408
  (308 shorter events, 193.7 us)
Async XLA Ops:
  4.4 50.5 %all-to-all-start = ((bf16[16,64,256]{2,1,0:T(8,128)(2,1)}), bf16[16,64,256]{2,1,0:T(8,128)(2,1)S(1)}, u32[]{:S(2)}, u32[]{:S(2)}) async-start(bf16[16,64,256]{2,1,0:T(8,128)(2,1)} %pad_maximum_fusion.17), calls=%async_computation | async-start | bytes 1048576 | tf_op jit(solution)/shard_map/all_to_all | solution.py:339
  31.8 22.6 %collective-permute-start.4 = (bf16[8,224,256]{2,1,0:T(8,128)(2,1)}, bf16[8,224,256]{2,1,0:T(8,128)(2,1)}, u32[]{:S(2)}, u32[]{:S(2)}) collective-permute-start(bf16[8,224,256]{2,1,0:T(8,128)(2,1)} %pad_maximum_fusion.13), channel_id=1, source_target_pairs={{0,2},{1,3},{2,0},{3,1},{4,6},{5,7},{6,4},{7,5},{8,10},{9,11},{10,... | collective-permute-start | bytes 2752520 | tf_op jit(solution)/shard_map/ppermute | solution.py:313
  39.2 102.3 %collective-permute-start.3 = (bf16[16,224,256]{2,1,0:T(8,128)(2,1)}, bf16[16,224,256]{2,1,0:T(8,128)(2,1)}, u32[]{:S(2)}, u32[]{:S(2)}) collective-permute-start(bf16[16,224,256]{2,1,0:T(8,128)(2,1)} %pad_maximum_fusion.3), channel_id=1, source_target_pairs={{0,1},{1,0},{2,3},{3,2},{4,5},{5,4},{6,7},{7,6},{8,9},{9,8},{10,11... | collective-permute-start | bytes 5505032 | tf_op jit(solution)/shard_map/ppermute | solution.py:312
  54.4 38.5 %collective-permute-start.5 = (bf16[8,224,256]{2,1,0:T(8,128)(2,1)}, bf16[8,224,256]{2,1,0:T(8,128)(2,1)}, u32[]{:S(2)}, u32[]{:S(2)}) collective-permute-start(bf16[8,224,256]{2,1,0:T(8,128)(2,1)} %pad_maximum_fusion.14), channel_id=1, source_target_pairs={{0,2},{1,3},{2,0},{3,1},{4,6},{5,7},{6,4},{7,5},{8,10},{9,11},{10,... | collective-permute-start | bytes 2752520 | tf_op jit(solution)/shard_map/ppermute | solution.py:313
  55.0 83.9 %collective-permute-start.6 = (bf16[8,224,256]{2,1,0:T(8,128)(2,1)}, bf16[8,224,256]{2,1,0:T(8,128)(2,1)}, u32[]{:S(2)}, u32[]{:S(2)}) collective-permute-start(bf16[8,224,256]{2,1,0:T(8,128)(2,1)} %collective-permute-done.4), channel_id=1, source_target_pairs={{0,16},{16,0},{1,17},{17,1},{2,18},{18,2},{3,19},{19,3},{4,20},{20... | collective-permute-start | bytes 2752520 | tf_op jit(solution)/shard_map/ppermute | solution.py:314
  55.1 33.1 %collective-permute-start.1 = (bf16[1024,256]{1,0:T(8,128)(2,1)S(1)}, bf16[1024,256]{1,0:T(8,128)(2,1)S(1)}, u32[]{:S(2)}, u32[]{:S(2)}) collective-permute-start(bf16[1024,256]{1,0:T(8,128)(2,1)S(1)} %bitcast.25), channel_id=1, source_target_pairs={{0,2},{1,3},{2,0},{3,1},{4,6},{5,7},{6,4},{7,5},{8,10},{9,11},{10,... | collective-permute-start | bytes 1572872 | tf_op jit(solution)/shard_map/ppermute | solution.py:313
  57.2 37.4 %collective-permute-start = (bf16[1024,256]{1,0:T(8,128)(2,1)S(1)}, bf16[1024,256]{1,0:T(8,128)(2,1)S(1)}, u32[]{:S(2)}, u32[]{:S(2)}) collective-permute-start(bf16[1024,256]{1,0:T(8,128)(2,1)S(1)} %bitcast.26), channel_id=1, source_target_pairs={{0,1},{1,0},{2,3},{3,2},{4,5},{5,4},{6,7},{7,6},{8,9},{9,8},{10,11... | collective-permute-start | bytes 1572872 | tf_op jit(solution)/shard_map/ppermute | solution.py:312
  92.9 45.9 %collective-permute-start.7 = (bf16[8,224,256]{2,1,0:T(8,128)(2,1)}, bf16[8,224,256]{2,1,0:T(8,128)(2,1)S(1)}, u32[]{:S(2)}, u32[]{:S(2)}) collective-permute-start(bf16[8,224,256]{2,1,0:T(8,128)(2,1)} %collective-permute-done.5), channel_id=1, source_target_pairs={{0,16},{16,0},{1,17},{17,1},{2,18},{18,2},{3,19},{19,3},{4,20},{20... | collective-permute-start | bytes 2752520 | tf_op jit(solution)/shard_map/ppermute | solution.py:314
  165.1 23.9 %collective-permute-start.45 = (bf16[8,224,256]{2,1,0:T(8,128)(2,1)S(1)}, bf16[8,224,256]{2,1,0:T(8,128)(2,1)S(1)}, u32[]{:S(2)}, u32[]{:S(2)}) collective-permute-start(bf16[8,224,256]{2,1,0:T(8,128)(2,1)S(1)} %pad_maximum_fusion.15), channel_id=1, source_target_pairs={{0,2},{1,3},{2,0},{3,1},{4,6},{5,7},{6,4},{7,5},{8,10},{9,11},{10,... | collective-permute-start | bytes 2752520 | tf_op jit(solution)/shard_map/ppermute | solution.py:313
  166.6 16.9 %collective-permute-start.9 = (bf16[512,256]{1,0:T(8,128)(2,1)S(1)}, bf16[512,256]{1,0:T(8,128)(2,1)S(1)}, u32[]{:S(2)}, u32[]{:S(2)}) collective-permute-start(bf16[512,256]{1,0:T(8,128)(2,1)S(1)} %add_convert_fusion.47), channel_id=1, source_target_pairs={{8,4},{9,5},{10,6},{11,7},{12,8},{13,9},{14,10},{15,11},{24,20},{2... | collective-permute-start | bytes 786440 | tf_op jit(solution)/shard_map/ppermute | solution.py:279
  175.3 15.2 %collective-permute-start.11 = (bf16[512,256]{1,0:T(8,128)(2,1)S(1)}, bf16[512,256]{1,0:T(8,128)(2,1)S(1)}, u32[]{:S(2)}, u32[]{:S(2)}) collective-permute-start(bf16[512,256]{1,0:T(8,128)(2,1)S(1)} %copy-done.13), channel_id=1, source_target_pairs={{12,8},{13,9},{14,10},{15,11},{28,24},{29,25},{30,26},{31,27}} | collective-permute-start | bytes 786440 | tf_op jit(solution)/shard_map/ppermute | solution.py:279
  176.2 14.7 %collective-permute-start.26 = (bf16[512,256]{1,0:T(8,128)(2,1)S(1)}, bf16[512,256]{1,0:T(8,128)(2,1)S(1)}, u32[]{:S(2)}, u32[]{:S(2)}) collective-permute-start(bf16[512,256]{1,0:T(8,128)(2,1)S(1)} %get-tuple-element.152), channel_id=1, source_target_pairs={{0,4},{1,5},{2,6},{3,7},{16,20},{17,21},{18,22},{19,23}} | collective-permute-start | bytes 786440 | tf_op jit(solution)/shard_map/ppermute | solution.py:279
  177.5 13.8 %collective-permute-start.29 = (bf16[512,256]{1,0:T(8,128)(2,1)S(1)}, bf16[512,256]{1,0:T(8,128)(2,1)S(1)}, u32[]{:S(2)}, u32[]{:S(2)}) collective-permute-start(bf16[512,256]{1,0:T(8,128)(2,1)S(1)} %get-tuple-element.151), channel_id=1, source_target_pairs={{0,4},{1,5},{2,6},{3,7},{16,20},{17,21},{18,22},{19,23}} | collective-permute-start | bytes 786440 | tf_op jit(solution)/shard_map/ppermute | solution.py:279
  184.5 12.3 %collective-permute-start.10 = (bf16[512,256]{1,0:T(8,128)(2,1)S(1)}, bf16[512,256]{1,0:T(8,128)(2,1)S(1)}, u32[]{:S(2)}, u32[]{:S(2)}) collective-permute-start(bf16[512,256]{1,0:T(8,128)(2,1)S(1)} %add_convert_fusion.46), channel_id=1, source_target_pairs={{4,0},{5,1},{6,2},{7,3},{8,4},{9,5},{10,6},{11,7},{12,8},{13,9},{1... | collective-permute-start | bytes 786440 | tf_op jit(solution)/shard_map/ppermute | solution.py:279
  189.0 75.3 %collective-permute-start.44 = (bf16[16,224,256]{2,1,0:T(8,128)(2,1)}, bf16[16,224,256]{2,1,0:T(8,128)(2,1)}, u32[]{:S(2)}, u32[]{:S(2)}) collective-permute-start(bf16[16,224,256]{2,1,0:T(8,128)(2,1)} %pad_maximum_fusion.7), channel_id=1, source_target_pairs={{0,1},{1,0},{2,3},{3,2},{4,5},{5,4},{6,7},{7,6},{8,9},{9,8},{10,11... | collective-permute-start | bytes 5505032 | tf_op jit(solution)/shard_map/ppermute | solution.py:312
  190.6 31.5 %collective-permute-start.46 = (bf16[8,224,256]{2,1,0:T(8,128)(2,1)}, bf16[8,224,256]{2,1,0:T(8,128)(2,1)}, u32[]{:S(2)}, u32[]{:S(2)}) collective-permute-start(bf16[8,224,256]{2,1,0:T(8,128)(2,1)} %pad_maximum_fusion.16), channel_id=1, source_target_pairs={{0,2},{1,3},{2,0},{3,1},{4,6},{5,7},{6,4},{7,5},{8,10},{9,11},{10,... | collective-permute-start | bytes 2752520 | tf_op jit(solution)/shard_map/ppermute | solution.py:313
  203.0 19.8 %collective-permute-start.27 = (bf16[512,256]{1,0:T(8,128)(2,1)}, bf16[512,256]{1,0:T(8,128)(2,1)S(1)}, u32[]{:S(2)}, u32[]{:S(2)}) collective-permute-start(bf16[512,256]{1,0:T(8,128)(2,1)} %get-tuple-element.148), channel_id=1, source_target_pairs={{0,4},{1,5},{2,6},{3,7},{4,8},{5,9},{6,10},{7,11},{16,20},{17,21},... | collective-permute-start | bytes 786440 | tf_op jit(solution)/shard_map/ppermute | solution.py:279
  208.4 15.1 %collective-permute-start.30 = (bf16[512,256]{1,0:T(8,128)(2,1)}, bf16[512,256]{1,0:T(8,128)(2,1)}, u32[]{:S(2)}, u32[]{:S(2)}) collective-permute-start(bf16[512,256]{1,0:T(8,128)(2,1)} %get-tuple-element.147), channel_id=1, source_target_pairs={{0,4},{1,5},{2,6},{3,7},{4,8},{5,9},{6,10},{7,11},{16,20},{17,21},... | collective-permute-start | bytes 786440 | tf_op jit(solution)/shard_map/ppermute | solution.py:279
  222.1 19.4 %collective-permute-start.47 = (bf16[8,224,256]{2,1,0:T(8,128)(2,1)S(1)}, bf16[8,224,256]{2,1,0:T(8,128)(2,1)S(1)}, u32[]{:S(2)}, u32[]{:S(2)}) collective-permute-start(bf16[8,224,256]{2,1,0:T(8,128)(2,1)S(1)} %collective-permute-done.45), channel_id=1, source_target_pairs={{0,16},{16,0},{1,17},{17,1},{2,18},{18,2},{3,19},{19,3},{4,20},{20... | collective-permute-start | bytes 2752520 | tf_op jit(solution)/shard_map/ppermute | solution.py:314
  222.8 38.2 %collective-permute-start.48 = (bf16[8,224,256]{2,1,0:T(8,128)(2,1)}, bf16[8,224,256]{2,1,0:T(8,128)(2,1)S(1)}, u32[]{:S(2)}, u32[]{:S(2)}) collective-permute-start(bf16[8,224,256]{2,1,0:T(8,128)(2,1)} %collective-permute-done.46), channel_id=1, source_target_pairs={{0,16},{16,0},{1,17},{17,1},{2,18},{18,2},{3,19},{19,3},{4,20},{20... | collective-permute-start | bytes 2752520 | tf_op jit(solution)/shard_map/ppermute | solution.py:314
  232.2 56.0 %collective-permute-start.14 = (bf16[512,256]{1,0:T(8,128)(2,1)S(1)}, bf16[512,256]{1,0:T(8,128)(2,1)S(1)}, u32[]{:S(2)}, u32[]{:S(2)}) collective-permute-start(bf16[512,256]{1,0:T(8,128)(2,1)S(1)} %get-tuple-element.146), channel_id=1, source_target_pairs={{4,0},{5,1},{6,2},{7,3},{8,4},{9,5},{10,6},{11,7},{12,8},{13,9},{1... | collective-permute-start | bytes 786440 | tf_op jit(solution)/shard_map/ppermute | solution.py:279
  236.8 50.7 %collective-permute-start.86 = (bf16[8,224,256]{2,1,0:T(8,128)(2,1)}, bf16[8,224,256]{2,1,0:T(8,128)(2,1)}, u32[]{:S(2)}, u32[]{:S(2)}) collective-permute-start(bf16[8,224,256]{2,1,0:T(8,128)(2,1)} %constant_dynamic-slice_fusion.1), channel_id=1, source_target_pairs={{0,2},{1,3},{2,0},{3,1},{4,6},{5,7},{6,4},{7,5},{8,10},{9,11},{10,... | collective-permute-start | bytes 2752520 | tf_op jit(solution)/shard_map/ppermute | solution.py:313
  241.4 46.8 %collective-permute-start.15 = (bf16[512,256]{1,0:T(8,128)(2,1)S(1)}, bf16[512,256]{1,0:T(8,128)(2,1)S(1)}, u32[]{:S(2)}, u32[]{:S(2)}) collective-permute-start(bf16[512,256]{1,0:T(8,128)(2,1)S(1)} %get-tuple-element.154), channel_id=1, source_target_pairs={{4,0},{5,1},{6,2},{7,3},{8,4},{9,5},{10,6},{11,7},{12,8},{13,9},{1... | collective-permute-start | bytes 786440 | tf_op jit(solution)/shard_map/ppermute | solution.py:279
  261.0 27.2 %collective-permute-start.32 = (bf16[512,256]{1,0:T(8,128)(2,1)S(1)}, bf16[512,256]{1,0:T(8,128)(2,1)S(1)}, u32[]{:S(2)}, u32[]{:S(2)}) collective-permute-start(bf16[512,256]{1,0:T(8,128)(2,1)S(1)} %get-tuple-element.157), channel_id=1, source_target_pairs={{0,4},{1,5},{2,6},{3,7},{4,8},{5,9},{6,10},{7,11},{8,12},{9,13},{1... | collective-permute-start | bytes 786440 | tf_op jit(solution)/shard_map/ppermute | solution.py:279
  264.3 23.9 %collective-permute-start.33 = (bf16[512,256]{1,0:T(8,128)(2,1)S(1)}, bf16[512,256]{1,0:T(8,128)(2,1)S(1)}, u32[]{:S(2)}, u32[]{:S(2)}) collective-permute-start(bf16[512,256]{1,0:T(8,128)(2,1)S(1)} %get-tuple-element.158), channel_id=1, source_target_pairs={{0,4},{1,5},{2,6},{3,7},{4,8},{5,9},{6,10},{7,11},{8,12},{9,13},{1... | collective-permute-start | bytes 786440 | tf_op jit(solution)/shard_map/ppermute | solution.py:279
  287.5 12.2 %collective-permute-start.49 = (bf16[512,256]{1,0:T(8,128)(2,1)S(1)}, bf16[512,256]{1,0:T(8,128)(2,1)S(1)}, u32[]{:S(2)}, u32[]{:S(2)}) collective-permute-start(bf16[512,256]{1,0:T(8,128)(2,1)S(1)} %get-tuple-element.118), channel_id=1, source_target_pairs={{12,8},{13,9},{14,10},{15,11},{28,24},{29,25},{30,26},{31,27}} | collective-permute-start | bytes 786440 | tf_op jit(solution)/shard_map/ppermute | solution.py:279
  288.5 12.0 %collective-permute-start.17 = (bf16[512,256]{1,0:T(8,128)(2,1)S(1)}, bf16[512,256]{1,0:T(8,128)(2,1)S(1)}, u32[]{:S(2)}, u32[]{:S(2)}) collective-permute-start(bf16[512,256]{1,0:T(8,128)(2,1)S(1)} %get-tuple-element.142), channel_id=1, source_target_pairs={{4,0},{5,1},{6,2},{7,3},{8,4},{9,5},{10,6},{11,7},{20,16},{21,17},... | collective-permute-start | bytes 786440 | tf_op jit(solution)/shard_map/ppermute | solution.py:279
  299.7 18.1 %collective-permute-start.52 = (bf16[512,256]{1,0:T(8,128)(2,1)S(1)}, bf16[512,256]{1,0:T(8,128)(2,1)S(1)}, u32[]{:S(2)}, u32[]{:S(2)}) collective-permute-start(bf16[512,256]{1,0:T(8,128)(2,1)S(1)} %get-tuple-element.121), channel_id=1, source_target_pairs={{12,8},{13,9},{14,10},{15,11},{28,24},{29,25},{30,26},{31,27}} | collective-permute-start | bytes 786440 | tf_op jit(solution)/shard_map/ppermute | solution.py:279
  300.5 18.7 %collective-permute-start.67 = (bf16[512,256]{1,0:T(8,128)(2,1)S(1)}, bf16[512,256]{1,0:T(8,128)(2,1)S(1)}, u32[]{:S(2)}, u32[]{:S(2)}) collective-permute-start(bf16[512,256]{1,0:T(8,128)(2,1)S(1)} %get-tuple-element.120), channel_id=1, source_target_pairs={{0,4},{1,5},{2,6},{3,7},{16,20},{17,21},{18,22},{19,23}} | collective-permute-start | bytes 786440 | tf_op jit(solution)/shard_map/ppermute | solution.py:279
  301.8 18.7 %collective-permute-start.70 = (bf16[512,256]{1,0:T(8,128)(2,1)S(1)}, bf16[512,256]{1,0:T(8,128)(2,1)S(1)}, u32[]{:S(2)}, u32[]{:S(2)}) collective-permute-start(bf16[512,256]{1,0:T(8,128)(2,1)S(1)} %get-tuple-element.119), channel_id=1, source_target_pairs={{0,4},{1,5},{2,6},{3,7},{16,20},{17,21},{18,22},{19,23}} | collective-permute-start | bytes 786440 | tf_op jit(solution)/shard_map/ppermute | solution.py:279
  303.2 39.9 %collective-permute-start.87 = (bf16[8,224,256]{2,1,0:T(8,128)(2,1)S(1)}, bf16[8,224,256]{2,1,0:T(8,128)(2,1)S(1)}, u32[]{:S(2)}, u32[]{:S(2)}) collective-permute-start(bf16[8,224,256]{2,1,0:T(8,128)(2,1)S(1)} %copy-done.12), channel_id=1, source_target_pairs={{0,2},{1,3},{2,0},{3,1},{4,6},{5,7},{6,4},{7,5},{8,10},{9,11},{10,... | collective-permute-start | bytes 2752520 | tf_op jit(solution)/shard_map/ppermute | solution.py:313
  319.2 12.6 %collective-permute-start.21 = (bf16[512,256]{1,0:T(8,128)(2,1)S(1)}, bf16[512,256]{1,0:T(8,128)(2,1)S(1)}, u32[]{:S(2)}, u32[]{:S(2)}) collective-permute-start(bf16[512,256]{1,0:T(8,128)(2,1)S(1)} %get-tuple-element.141), channel_id=1, source_target_pairs={{4,0},{5,1},{6,2},{7,3},{20,16},{21,17},{22,18},{23,19}} | collective-permute-start | bytes 786440 | tf_op jit(solution)/shard_map/ppermute | solution.py:279
  320.5 12.6 %collective-permute-start.38 = (bf16[512,256]{1,0:T(8,128)(2,1)S(1)}, bf16[512,256]{1,0:T(8,128)(2,1)S(1)}, u32[]{:S(2)}, u32[]{:S(2)}) collective-permute-start(bf16[512,256]{1,0:T(8,128)(2,1)S(1)} %get-tuple-element.140), channel_id=1, source_target_pairs={{8,12},{9,13},{10,14},{11,15},{24,28},{25,29},{26,30},{27,31}} | collective-permute-start | bytes 786440 | tf_op jit(solution)/shard_map/ppermute | solution.py:279
  326.2 35.6 %collective-permute-start.88 = (bf16[8,224,256]{2,1,0:T(8,128)(2,1)}, bf16[8,224,256]{2,1,0:T(8,128)(2,1)S(1)}, u32[]{:S(2)}, u32[]{:S(2)}) collective-permute-start(bf16[8,224,256]{2,1,0:T(8,128)(2,1)} %collective-permute-done.86), channel_id=1, source_target_pairs={{0,16},{16,0},{1,17},{17,1},{2,18},{18,2},{3,19},{19,3},{4,20},{20... | collective-permute-start | bytes 2752520 | tf_op jit(solution)/shard_map/ppermute | solution.py:314
  333.5 14.2 %collective-permute-start.68 = (bf16[512,256]{1,0:T(8,128)(2,1)S(1)}, bf16[512,256]{1,0:T(8,128)(2,1)S(1)}, u32[]{:S(2)}, u32[]{:S(2)}) collective-permute-start(bf16[512,256]{1,0:T(8,128)(2,1)S(1)} %get-tuple-element.116), channel_id=1, source_target_pairs={{0,4},{1,5},{2,6},{3,7},{4,8},{5,9},{6,10},{7,11},{16,20},{17,21},... | collective-permute-start | bytes 786440 | tf_op jit(solution)/shard_map/ppermute | solution.py:279
  343.0 31.4 %collective-permute-start.55 = (bf16[512,256]{1,0:T(8,128)(2,1)S(1)}, bf16[512,256]{1,0:T(8,128)(2,1)S(1)}, u32[]{:S(2)}, u32[]{:S(2)}) collective-permute-start(bf16[512,256]{1,0:T(8,128)(2,1)S(1)} %get-tuple-element.114), channel_id=1, source_target_pairs={{4,0},{5,1},{6,2},{7,3},{8,4},{9,5},{10,6},{11,7},{12,8},{13,9},{1... | collective-permute-start | bytes 786440 | tf_op jit(solution)/shard_map/ppermute | solution.py:279
  347.7 17.1 %collective-permute-start.89 = (bf16[8,224,256]{2,1,0:T(8,128)(2,1)S(1)}, bf16[8,224,256]{2,1,0:T(8,128)(2,1)S(1)}, u32[]{:S(2)}, u32[]{:S(2)}) collective-permute-start(bf16[8,224,256]{2,1,0:T(8,128)(2,1)S(1)} %collective-permute-done.87), channel_id=1, source_target_pairs={{0,16},{16,0},{1,17},{17,1},{2,18},{18,2},{3,19},{19,3},{4,20},{20... | collective-permute-start | bytes 2752520 | tf_op jit(solution)/shard_map/ppermute | solution.py:314
  355.4 19.8 %collective-permute-start.56 = (bf16[512,256]{1,0:T(8,128)(2,1)S(1)}, bf16[512,256]{1,0:T(8,128)(2,1)S(1)}, u32[]{:S(2)}, u32[]{:S(2)}) collective-permute-start(bf16[512,256]{1,0:T(8,128)(2,1)S(1)} %get-tuple-element.122), channel_id=1, source_target_pairs={{4,0},{5,1},{6,2},{7,3},{8,4},{9,5},{10,6},{11,7},{12,8},{13,9},{1... | collective-permute-start | bytes 786440 | tf_op jit(solution)/shard_map/ppermute | solution.py:279
  358.9 17.6 %collective-permute-start.73 = (bf16[512,256]{1,0:T(8,128)(2,1)S(1)}, bf16[512,256]{1,0:T(8,128)(2,1)S(1)}, u32[]{:S(2)}, u32[]{:S(2)}) collective-permute-start(bf16[512,256]{1,0:T(8,128)(2,1)S(1)} %get-tuple-element.132), channel_id=1, source_target_pairs={{0,4},{1,5},{2,6},{3,7},{4,8},{5,9},{6,10},{7,11},{8,12},{9,13},{1... | collective-permute-start | bytes 786440 | tf_op jit(solution)/shard_map/ppermute | solution.py:279
  361.8 14.7 %collective-permute-start.74 = (bf16[512,256]{1,0:T(8,128)(2,1)S(1)}, bf16[512,256]{1,0:T(8,128)(2,1)S(1)}, u32[]{:S(2)}, u32[]{:S(2)}) collective-permute-start(bf16[512,256]{1,0:T(8,128)(2,1)S(1)} %get-tuple-element.133), channel_id=1, source_target_pairs={{0,4},{1,5},{2,6},{3,7},{4,8},{5,9},{6,10},{7,11},{8,12},{9,13},{1... | collective-permute-start | bytes 786440 | tf_op jit(solution)/shard_map/ppermute | solution.py:279
  364.8 116.2 %collective-permute-start.85 = (bf16[16,224,256]{2,1,0:T(8,128)(2,1)S(1)}, bf16[16,224,256]{2,1,0:T(8,128)(2,1)S(1)}, u32[]{:S(2)}, u32[]{:S(2)}) collective-permute-start(bf16[16,224,256]{2,1,0:T(8,128)(2,1)S(1)} %copy-done.11), channel_id=1, source_target_pairs={{0,1},{1,0},{2,3},{3,2},{4,5},{5,4},{6,7},{7,6},{8,9},{9,8},{10,11... | collective-permute-start | bytes 5505032 | tf_op jit(solution)/shard_map/ppermute | solution.py:312
  376.8 11.9 %collective-permute-start.58 = (bf16[512,256]{1,0:T(8,128)(2,1)S(1)}, bf16[512,256]{1,0:T(8,128)(2,1)S(1)}, u32[]{:S(2)}, u32[]{:S(2)}) collective-permute-start(bf16[512,256]{1,0:T(8,128)(2,1)S(1)} %get-tuple-element.108), channel_id=1, source_target_pairs={{4,0},{5,1},{6,2},{7,3},{8,4},{9,5},{10,6},{11,7},{20,16},{21,17},... | collective-permute-start | bytes 786440 | tf_op jit(solution)/shard_map/ppermute | solution.py:279
  417.0 13.5 %collective-permute-start.64 = (bf16[1024,128]{1,0:T(8,128)(2,1)S(1)}, bf16[1024,128]{1,0:T(8,128)(2,1)S(1)}, u32[]{:S(2)}, u32[]{:S(2)}) collective-permute-start(bf16[1024,128]{1,0:T(8,128)(2,1)S(1)} %get-tuple-element.26), channel_id=1, source_target_pairs={{0,4},{1,5},{2,6},{3,7},{4,8},{5,9},{6,10},{7,11},{8,12},{9,13},{1... | collective-permute-start | bytes 786440 | tf_op jit(solution)/shard_map/ppermute | solution.py:292
  422.6 12.1 %collective-permute-start.41 = (bf16[1024,128]{1,0:T(8,128)(2,1)S(1)}, bf16[1024,128]{1,0:T(8,128)(2,1)S(1)}, u32[]{:S(2)}, u32[]{:S(2)}) collective-permute-start(bf16[1024,128]{1,0:T(8,128)(2,1)S(1)} %get-tuple-element.92), channel_id=1, source_target_pairs={{4,0},{5,1},{6,2},{7,3},{8,4},{9,5},{10,6},{11,7},{12,8},{13,9},{1... | collective-permute-start | bytes 786440 | tf_op jit(solution)/shard_map/ppermute | solution.py:292
  430.7 13.1 %collective-permute-start.65 = (bf16[1024,128]{1,0:T(8,128)(2,1)S(1)}, bf16[1024,128]{1,0:T(8,128)(2,1)S(1)}, u32[]{:S(2)}, u32[]{:S(2)}) collective-permute-start(bf16[1024,128]{1,0:T(8,128)(2,1)S(1)} %get-tuple-element.24), channel_id=1, source_target_pairs={{4,8},{5,9},{6,10},{7,11},{8,12},{9,13},{10,14},{11,15},{20,24},{2... | collective-permute-start | bytes 786440 | tf_op jit(solution)/shard_map/ppermute | solution.py:292
  443.9 11.9 %collective-permute-start.66 = (bf16[1024,128]{1,0:T(8,128)(2,1)S(1)}, bf16[1024,128]{1,0:T(8,128)(2,1)S(1)}, u32[]{:S(2)}, u32[]{:S(2)}) collective-permute-start(bf16[1024,128]{1,0:T(8,128)(2,1)S(1)} %get-tuple-element.22), channel_id=1, source_target_pairs={{8,12},{9,13},{10,14},{11,15},{24,28},{25,29},{26,30},{27,31}} | collective-permute-start | bytes 786440 | tf_op jit(solution)/shard_map/ppermute | solution.py:292
  444.7 19.6 %collective-permute-start.43 = (bf16[1024,128]{1,0:T(8,128)(2,1)S(1)}, bf16[1024,128]{1,0:T(8,128)(2,1)S(1)}, u32[]{:S(2)}, u32[]{:S(2)}) collective-permute-start(bf16[1024,128]{1,0:T(8,128)(2,1)S(1)} %get-tuple-element.61), channel_id=1, source_target_pairs={{4,0},{5,1},{6,2},{7,3},{20,16},{21,17},{22,18},{23,19}} | collective-permute-start | bytes 786440 | tf_op jit(solution)/shard_map/ppermute | solution.py:292
  581.7 14.0 %collective-permute-start.91 = (bf16[1024,224]{1,0:T(8,128)(2,1)S(1)}, bf16[1024,224]{1,0:T(8,128)(2,1)S(1)}, u32[]{:S(2)}, u32[]{:S(2)}) collective-permute-start(bf16[1024,224]{1,0:T(8,128)(2,1)S(1)} %fusion), channel_id=1, source_target_pairs={{0,2},{1,3},{2,0},{3,1},{4,6},{5,7},{6,4},{7,5},{8,10},{9,11},{10,... | collective-permute-start | bytes 1376264 | tf_op jit(solution)/shard_map/ppermute | solution.py:313
  (62 other events, 545.8 us)

commit v3 on v0

v3 whole, which is shorter than its diff:
```python
import functools
import math

import jax
import jax.numpy as jnp
from jax import lax
from jax.experimental import pallas as pl
from jax.experimental.pallas import tpu as pltpu
from jax.sharding import PartitionSpec as P

BF16 = jnp.bfloat16
F32 = jnp.float32
TILE = 256
BLOCK = 1024
LANES = 256
UNITS = 128


def slots_of(block_ids, experts):
    flat = block_ids.reshape(-1)
    onehot = (flat[:, None] == jnp.arange(experts, dtype=jnp.int32)[None, :]).astype(jnp.int32)
    before = jnp.cumsum(onehot, axis=0) - onehot
    return jnp.sum(before * onehot, axis=1).reshape(block_ids.shape)


def fill_slots(rows, expert_ids, slot, experts, per_expert):
    count, picks = expert_ids.shape
    spread = jnp.broadcast_to(rows[:, None, :], (count, picks, rows.shape[1]))
    empty = jnp.zeros((experts, per_expert, rows.shape[1]), BF16)
    return empty.at[expert_ids, slot].set(spread)


def moved_weights(tokens, expert_ids, gate_weights, w_gate, w_up, w_down):
    tok_rows, picks = expert_ids.shape
    experts = w_gate.shape[0]
    per_expert = min(tok_rows, 3 * tok_rows * picks // (2 * experts))
    slot = slots_of(expert_ids, experts)
    features = lax.all_gather(tokens, "tp", axis=1, tiled=True)
    outgoing = fill_slots(features, expert_ids, slot, experts, per_expert)
    arrived = lax.all_to_all(outgoing, "ep", split_axis=0, concat_axis=1, tiled=True)
    gate_owned, up_owned = (
        lax.all_to_all(w_gate, "ep", split_axis=0, concat_axis=1, tiled=True),
        lax.all_to_all(w_up, "ep", split_axis=0, concat_axis=1, tiled=True),
    )
    gate = jnp.einsum("ecd,edf->ecf", arrived, gate_owned, preferred_element_type=F32)
    up = jnp.einsum("ecd,edf->ecf", arrived, up_owned, preferred_element_type=F32)
    hidden = (jax.nn.silu(gate) * up).astype(BF16)
    down_owned = lax.all_to_all(w_down, "ep", split_axis=0, concat_axis=2, tiled=True)
    partial_value = jnp.einsum("ecf,efd->ecd", hidden, down_owned, preferred_element_type=F32)
    expert_out = lax.psum_scatter(
        partial_value.astype(BF16), "tp", scatter_dimension=2, tiled=True
    )
    returned = lax.all_to_all(expert_out, "ep", split_axis=1, concat_axis=0, tiled=True)
    picked = returned[expert_ids, slot]
    mixed = jnp.sum(gate_weights[:, :, None] * picked.astype(F32), axis=1)
    return mixed.astype(BF16)


def dot(a, b, contract):
    return lax.dot_general(a, b, ((contract[0], contract[1]), ((), ())), preferred_element_type=F32)


def params(mib=48):
    return pltpu.CompilerParams(vmem_limit_bytes=mib << 20)


def cost(flops, moved):
    return pl.CostEstimate(flops=flops, bytes_accessed=moved, transcendentals=0)


def split3(value):
    high = lax.reduce_precision(value, 8, 7)
    middle = lax.reduce_precision(value - high, 8, 7)
    return high, middle, lax.reduce_precision(value - high - middle, 8, 7)


def order_kernel(width, picks, experts, note_ref, place_out, across_out, gates_out, base_out):
    tokens = note_ref.shape[0]
    note = note_ref[...].astype(F32)
    lane = lax.broadcasted_iota(jnp.int32, (tokens, UNITS), 1)
    name = jnp.where(lane < 3 * experts, lane % experts, -1).astype(F32)
    gates = jnp.zeros((tokens, UNITS), F32)
    for k in range(picks):
        one = note[:, width + k : width + k + 1]
        weight = (
            note[:, width + picks + k : width + picks + k + 1]
            + note[:, width + 2 * picks + k : width + 2 * picks + k + 1]
            + note[:, width + 3 * picks + k : width + 3 * picks + k + 1]
        )
        gates = jnp.where(name == one, weight, gates)
    mask = jnp.where((gates != 0.0) & (lane < experts), 1.0, 0.0)
    high = gates.astype(BF16)
    middle = (gates - high.astype(F32)).astype(BF16)
    rest = (gates - high.astype(F32) - middle.astype(F32)).astype(BF16)
    gates_out[...] = jnp.where(
        lane < experts,
        high.astype(F32),
        jnp.where(lane < 2 * experts, middle.astype(F32), rest.astype(F32)),
    ).astype(BF16)
    row = lax.broadcasted_iota(jnp.int32, (tokens, tokens), 0)
    column = lax.broadcasted_iota(jnp.int32, (tokens, tokens), 1)
    upto = jnp.where(column <= row, 1.0, 0.0).astype(BF16)
    count = dot(upto, mask.astype(BF16), ((1,), (0,)))
    total = jnp.broadcast_to(count[tokens - 1 : tokens, :], (8, UNITS))
    large = jnp.floor(total * (1.0 / 128.0))
    row = lax.broadcasted_iota(jnp.int32, (UNITS, UNITS), 0)
    column = lax.broadcasted_iota(jnp.int32, (UNITS, UNITS), 1)
    before = jnp.where(row < column, 1.0, 0.0).astype(BF16)
    base = 128.0 * dot(large.astype(BF16), before, ((1,), (0,)))
    base += dot((total - 128.0 * large).astype(BF16), before, ((1,), (0,)))
    base_out[...] = base.astype(jnp.int32)
    place = jnp.where(mask > 0.0, count - 1.0 + base[0:1, :], -1.0)
    place_out[...] = place.astype(jnp.int32)
    across_out[...] = place.T.astype(jnp.int32)


def order_of(note, width, picks, experts):
    tokens = note.shape[0]
    return pl.pallas_call(
        functools.partial(order_kernel, width, picks, experts),
        out_shape=[
            jax.ShapeDtypeStruct((tokens, UNITS), jnp.int32),
            jax.ShapeDtypeStruct((UNITS, tokens), jnp.int32),
            jax.ShapeDtypeStruct((tokens, UNITS), BF16),
            jax.ShapeDtypeStruct((8, UNITS), jnp.int32),
        ],
        compiler_params=params(),
        cost_estimate=cost(2 * tokens * tokens * UNITS, 4 * tokens * tokens),
        name="order",
    )(note)


def spans_of(base, rows):
    low = jnp.arange(rows // TILE, dtype=jnp.int32)[:, None] * TILE
    return (
        jnp.sum((base[None, 1:] <= low).astype(jnp.int32), axis=1),
        jnp.sum((base[None, :-1] < low + TILE).astype(jnp.int32), axis=1),
    )


def mine_of(base, e, row0):
    row = row0 + lax.broadcasted_iota(jnp.int32, (TILE, 1), 0)
    return (row >= base[e]) & (row < base[e + 1])


def sort_kernel(experts, low, high, base, across_ref, gates_ref, *refs):
    slices, (out, scale_out, onehot_ref, name_ref) = refs[:-4], refs[-4:]
    tokens = onehot_ref.shape[1]
    number = lax.broadcasted_iota(jnp.int32, (TILE, 128), 0).astype(F32).astype(BF16)

    @pl.loop(0, BLOCK // TILE)
    def _(part):
        i = pl.program_id(0) * (BLOCK // TILE) + part
        row0 = i * TILE
        here = pl.ds(pl.multiple_of(part * TILE, TILE), TILE)
        for c in range(tokens // 128):

            def add(e, found):
                away = across_ref[e][c : c + 1, :] - row0
                away = jnp.where((away >= 0) & (away < TILE), away, -1).astype(F32).astype(BF16)
                return jnp.where(number == away, jnp.ones((), BF16), found)

            onehot_ref[here, c * 128 : (c + 1) * 128] = lax.fori_loop(
                low[i], high[i], add, jnp.zeros((TILE, 128), BF16)
            )
        name_ref[here, :] = lax.fori_loop(
            low[i],
            high[i],
            lambda e, name: jnp.where(mine_of(base, e, row0), e, name),
            jnp.zeros((TILE, UNITS), jnp.int32),
        )

    onehot = onehot_ref[...]
    for k, ref in enumerate(slices):
        out[:, k * LANES : (k + 1) * LANES] = dot(onehot, ref[...], ((1,), (0,))).astype(BF16)
    gates = dot(onehot, gates_ref[...], ((1,), (0,)))
    lane = lax.broadcasted_iota(jnp.int32, (BLOCK, UNITS), 1)
    name = name_ref[...]
    kept = (lane == name) | (lane == name + experts) | (lane == name + 2 * experts)
    scale = jnp.sum(jnp.where(kept, gates, 0.0), axis=1, keepdims=True)
    scale_out[...] = jnp.broadcast_to(scale, lane.shape)


def sort_rows(spans, base, across, gates, slices, rows, experts):
    tokens = gates.shape[0]
    across = across[:experts].reshape(experts, tokens // 128, 128)
    whole = lambda i, *_: (0, 0)
    width = len(slices) * LANES
    return pl.pallas_call(
        functools.partial(sort_kernel, experts),
        grid_spec=pltpu.PrefetchScalarGridSpec(
            num_scalar_prefetch=3,
            grid=(rows // BLOCK,),
            in_specs=[
                pl.BlockSpec(across.shape, lambda i, *_: (0, 0, 0)),
                pl.BlockSpec((tokens, UNITS), whole),
            ]
            + [pl.BlockSpec((tokens, LANES), whole)] * len(slices),
            out_specs=[
                pl.BlockSpec((BLOCK, width), lambda i, *_: (i, 0)),
                pl.BlockSpec((BLOCK, UNITS), lambda i, *_: (i, 0)),
            ],
            scratch_shapes=[
                pltpu.VMEM((BLOCK, tokens), BF16),
                pltpu.VMEM((BLOCK, UNITS), jnp.int32),
            ],
        ),
        out_shape=[
            jax.ShapeDtypeStruct((rows, width), BF16),
            jax.ShapeDtypeStruct((rows, UNITS), F32),
        ],
        compiler_params=params(),
        cost_estimate=cost(2 * rows * tokens * width, 4 * rows * width),
        name="sort_rows",
    )(*spans, base, across, gates, *slices)


def partial_kernel(low, high, base, quarter, rows_ref, *refs):
    pairs, out = [refs[j : j + 2] for j in range(0, 8, 2)], refs[-1]
    width = pairs[0][0].shape[1]

    @pl.loop(0, BLOCK // TILE)
    def _(part):
        i = pl.program_id(0) * (BLOCK // TILE) + part
        here = pl.ds(pl.multiple_of(part * TILE, TILE), TILE)

        def add(e, kept):
            total = 0.0
            for k, pair in enumerate(pairs):
                weight = jnp.concatenate([pair[0][e], pair[1][e]], axis=1)
                rows = rows_ref[here, k * LANES : k * LANES + width]
                total += dot(rows, weight, ((1,), (0,)))
            return jnp.where(mine_of(base, e, i * TILE), total, kept)

        out[here, :] = lax.fori_loop(
            low[i], high[i], add, jnp.zeros((TILE, out.shape[1]), F32)
        ).astype(BF16)


def partial_sums(f, spans, base, quarter, rows_in, w_gate, w_up, pieces):
    rows = rows_in.shape[0]
    experts, width, _ = w_gate.shape
    own = pl.BlockSpec((experts, width, UNITS), lambda i, lo, hi, b, q: (0, 0, 2 * q[0] + f))
    block = pl.BlockSpec((experts, width, UNITS), lambda i, *_: (0, 0, 0))
    return pl.pallas_call(
        partial_kernel,
        grid_spec=pltpu.PrefetchScalarGridSpec(
            num_scalar_prefetch=4,
            grid=(rows // BLOCK,),
            in_specs=[pl.BlockSpec((BLOCK, rows_in.shape[1]), lambda i, *_: (i, 0)), own, own]
            + [block] * len(pieces),
            out_specs=pl.BlockSpec((BLOCK, 2 * UNITS), lambda i, *_: (i, 0)),
        ),
        out_shape=jax.ShapeDtypeStruct((rows, 2 * UNITS), BF16),
        compiler_params=params(),
        cost_estimate=cost(4 * rows * rows_in.shape[1] * UNITS, 2 * rows * rows_in.shape[1]),
        name="partial_sums",
    )(*spans, base, quarter, rows_in, w_gate, w_up, *pieces)


def down_kernel(low, high, base, quarter, place_ref, hidden0, hidden1, own_ref, *refs):
    pairs, (out, onehot_ref, value_ref) = [refs[j : j + 2] for j in range(0, 6, 2)], refs[6:]
    width = own_ref.shape[1]
    tokens = place_ref.shape[1]
    lane = lax.broadcasted_iota(jnp.int32, (tokens, 128), 1)

    @pl.when(pl.program_id(0) == 0)
    def _():
        out[...] = jnp.zeros_like(out)
        value_ref[...] = jnp.zeros_like(value_ref)

    for part in range(BLOCK // TILE):
        i = pl.program_id(0) * (BLOCK // TILE) + part
        here = slice(part * TILE, (part + 1) * TILE)
        units = jnp.concatenate([hidden0[here, :], hidden1[here, :]], axis=1)
        onehot_ref[:, here] = jnp.zeros((tokens, TILE), BF16)

        @pl.loop(low[i], high[i])
        def _(e):
            mine = mine_of(base, e, i * TILE)
            for k in range(4):
                weight = own_ref[e]
                if k:
                    weight = jnp.concatenate([pairs[k - 1][0][e], pairs[k - 1][1][e]], axis=1)
                value = dot(units, weight, ((1,), (1,)))
                at = slice(k * LANES, k * LANES + width)
                value_ref[here, at] = jnp.where(
                    mine, value, value_ref[here, at].astype(F32)
                ).astype(BF16)
            place = place_ref[e] - i * TILE
            for c in range(TILE // 128):
                at = slice(part * TILE + c * 128, part * TILE + (c + 1) * 128)
                hit = jnp.where(place == lane + c * 128, 1.0, 0.0).astype(BF16)
                onehot_ref[:, at] += hit

    out[...] += dot(onehot_ref[...], value_ref[...], ((1,), (0,)))


def down_and_mix(spans, base, quarter, place, hidden, w_down, pieces):
    rows = hidden[0].shape[0]
    experts, width, _ = w_down.shape
    tokens = place.shape[1]
    block = pl.BlockSpec((BLOCK, UNITS), lambda i, *_: (i, 0))
    own = pl.BlockSpec((experts, width, 2 * UNITS), lambda i, lo, hi, b, q: (0, 0, q[0]))
    return pl.pallas_call(
        down_kernel,
        grid_spec=pltpu.PrefetchScalarGridSpec(
            num_scalar_prefetch=4,
            grid=(rows // BLOCK,),
            in_specs=[
                pl.BlockSpec((experts, tokens, 128), lambda i, *_: (0, 0, 0)),
                block,
                block,
                own,
            ]
            + [pl.BlockSpec((experts, width, UNITS), lambda i, *_: (0, 0, 0))] * len(pieces),
            out_specs=pl.BlockSpec((tokens, 4 * LANES), lambda i, *_: (0, 0)),
            scratch_shapes=[
                pltpu.VMEM((tokens, BLOCK), BF16),
                pltpu.VMEM((BLOCK, 4 * LANES), BF16),
            ],
        ),
        out_shape=jax.ShapeDtypeStruct((tokens, 4 * LANES), F32),
        compiler_params=params(56),
        cost_estimate=cost(8 * rows * tokens * LANES, 16 * rows * UNITS),
        name="down_and_mix",
    )(*spans, base, quarter, place, *hidden, w_down, *pieces)


def fixed_weights(size, tokens, expert_ids, gate_weights, w_gate, w_up, w_down):
    count, picks = expert_ids.shape
    experts, width, hidden_units = w_gate.shape
    quarter = hidden_units // 4
    rows = size * count * picks
    places = size // 4
    me, plane = lax.axis_index("ep"), lax.axis_index("parts")
    w_down = jnp.swapaxes(w_down, 1, 2)

    twins = [(i, i ^ 1) for i in range(size)]
    cross = [(p * size + i, p * size + (i ^ 2 ^ p)) for p in range(2) for i in range(size)]
    to_twin = lambda value: lax.ppermute(value, "ep", twins)
    to_cross = lambda value: lax.ppermute(value, ("parts", "ep"), cross)
    to_plane = lambda value: lax.ppermute(value, "parts", [(0, 1), (1, 0)])
    line = [[4 * p + k for p in range(places)] for k in range(4)]
    my_quarter = me % 4
    twin_quarter = my_quarter ^ 1
    cross_quarter = my_quarter ^ 2 ^ plane

    note = jnp.concatenate([expert_ids.astype(F32), *split3(gate_weights)], axis=1).astype(BF16)
    fill = LANES - width - note.shape[1]
    parcels = jnp.concatenate(
        [
            tokens.reshape(count, size, width).swapaxes(0, 1),
            jnp.broadcast_to(jnp.pad(note, ((0, 0), (0, fill)))[None], (size, count, LANES - width)),
        ],
        axis=2,
    )
    own = lax.all_to_all(parcels, "ep", split_axis=0, concat_axis=0, tiled=True)
    own = own.reshape(size * count, LANES)
    far = to_cross(own)
    slices = [own, to_twin(own), far, to_twin(far)]
    place, across, gates, base = order_of(own, width, picks, experts)
    base = base[0, : experts + 1]
    spans = spans_of(base, rows)
    which = my_quarter.astype(jnp.int32).reshape(1)

    def cut(w, q, f):
        return lax.dynamic_slice_in_dim(w, q * quarter + f * UNITS, UNITS, 2)

    last = []
    held = []
    for f, w in ((0, w_gate), (0, w_up), (1, w_gate), (1, w_up), (0, w_down), (1, w_down)):
        piece = cut(w, cross_quarter, f)
        if last:
            piece = lax.optimization_barrier((piece, *last))[0]
        across_x = to_cross(piece)
        last = [across_x, far]
        held.append((to_twin(cut(w, twin_quarter, f)), across_x, to_plane(across_x)))
    weave = lambda pair: [piece for both in zip(*pair) for piece in both]

    sorted_rows, scale = sort_rows(spans, base, across, gates, slices, rows, experts)
    scale = lax.dynamic_slice_in_dim(scale, (me // 4) * (rows // places), rows // places, 0)
    hidden = []
    for f in range(2):
        pieces = weave(held[2 * f : 2 * f + 2])
        sums = partial_sums(f, spans, base, which, sorted_rows, w_gate, w_up, pieces)
        sums = lax.psum_scatter(
            sums, "ep", scatter_dimension=0, axis_index_groups=line, tiled=True
        ).astype(F32)
        units = (jax.nn.silu(sums[:, :UNITS]) * sums[:, UNITS:] * scale).astype(BF16)
        hidden.append(lax.all_gather(units, "ep", axis=0, axis_index_groups=line, tiled=True))

    place = jnp.broadcast_to(across[:experts, :, None], (experts, size * count, 128))
    mixed = down_and_mix(spans, base, which, place, hidden, w_down, weave(held[4:]))
    mine, twin, far, far_twin = (mixed[:, k * LANES : k * LANES + width] for k in range(4))
    moved = to_twin(jnp.concatenate([far_twin, twin], axis=0).astype(BF16)).astype(F32)
    tokens_all = size * count
    far = to_cross((far + moved[:tokens_all]).astype(BF16)).astype(F32)
    mixed = (mine + moved[tokens_all:] + far).astype(BF16)
    mixed = lax.all_to_all(
        mixed.reshape(size, count, width), "ep", split_axis=0, concat_axis=0, tiled=True
    )
    return mixed.swapaxes(0, 1).reshape(count, size * width)


def solution(mesh):
    size, inner = mesh.shape["ep"], mesh.shape["tp"]

    def body(tokens, expert_ids, gate_weights, w_gate, w_up, w_down):
        rows = size * math.prod(expert_ids.shape)
        sums = rows * w_gate.shape[2]
        experts, width, units = w_gate.shape
        even = (
            size % 4 == 0
            and size > 4
            and mesh.shape["parts"] == 2
            and rows % (2 * BLOCK) == 0
            and units == 8 * UNITS
            and 3 * experts <= UNITS
            and size * math.prod(expert_ids.shape[:1]) % 128 == 0
            and width + 4 * expert_ids.shape[1] <= LANES
        )
        args = (tokens, expert_ids, gate_weights, w_gate, w_up, w_down)
        if inner == 1 and even and sums <= 3 * math.prod(w_gate.shape):
            return fixed_weights(size, *args)
        return moved_weights(*args)

    placed = (
        P(("parts", "ep"), "tp"),
        P(("parts", "ep"), None),
        P(("parts", "ep"), None),
        P(None, "ep", "tp"),
        P(None, "ep", "tp"),
        P(None, "tp", "ep"),
    )
    return jax.shard_map(
        body, mesh=mesh, in_specs=placed, out_specs=P(("parts", "ep"), "tp"), check_vma=False
    )
```

time: 1050 us -> 519 us (0.49)
  blocking collectives: 458 us -> 18.9 us
  local copies, waits for them, and re-layouts: 241 us -> 22 us
  Pallas kernels: 0 us -> 143 us
  other arithmetic: 44.8 us -> 13.8 us
  matrix products: 25.3 us -> 0 us
  waiting for transfers between devices: 264 us -> 289 us
  between operations: 0.12 us -> 13.4 us
    all_to_all x3 -> x1, blocking collectives: 458 us -> 18.9 us  [fixed_weights(): lax.all_to_all(mixed.reshape(size, count, width), 'ep', split_axis=0, con...]
    all_to_all x2 -> x1, waiting for transfers between devices: 264 us -> 9.53 us  [fixed_weights(): own = lax.all_to_all(parcels, 'ep', split_axis=0, concat_axis=0, tiled=True)]
    ppermute x0 -> x23, waiting for transfers between devices: none -> 184 us  [the longest x8 139 us: fixed_weights(): to_cross = lambda value: lax.ppermute(value, ('parts', 'ep'), cross)]
    pallas_call x0 -> x5, Pallas kernels: none -> 143 us  [the longest x1 61.2 us: down_and_mix(): pl.pallas_call(down_kernel, grid_spec=pltpu.PrefetchScalarGridSpec(num_sc...]
    scatter x1 -> x0, local copies, waits for them, and re-layouts: 123 us -> none  [fill_slots(): return empty.at[expert_ids, slot].set(spread)]
    reduce_scatter x0 -> x2, waiting for transfers between devices: none -> 74.5 us  [fixed_weights(): lax.psum_scatter(sums, 'ep', scatter_dimension=0, axis_index_groups=line,...]
    convert_element_type x1 -> x0, local copies, waits for them, and re-layouts: 60.7 us -> none  [body(): partial_value.astype(jnp.bfloat16)]
    unnamed x3 -> x0, other arithmetic: 37 us -> none
  transfers between devices with their start and end apart: 2 -> 28, of which waited for: 2 -> 15; matrix products, arithmetic and copies ran while one was open for 2% -> 2% of each run, Pallas kernels for 0% -> 12%
where the time goes in v3:
time: 519 us; the launch traced here: 516 us
  waiting for transfers between devices  289 us (56%)
  Pallas kernels  143 us (28%)
  local copies, waits for them, and re-layouts  22 us (4%)
  blocking collectives  18.9 us (4%)
  starting transfers between devices  16.5 us (3%)
  other arithmetic  13.8 us (3%)
  between operations  13.4 us (3%)
    ppermute x8, waiting for transfers between devices, fixed_weights(): to_cross = lambda value: lax.ppermute(value, ('parts', 'ep'), cross)  139 us
    reduce_scatter x2, waiting for transfers between devices, fixed_weights(): lax.psum_scatter(sums, 'ep', scatter_dimension=0, axis_index_groups=line,...  74.5 us
    pallas_call x1, Pallas kernels, down_and_mix(): pl.pallas_call(down_kernel, grid_spec=pltpu.PrefetchScalarGridSpec(num_sc...  61.2 us
    ppermute x6, waiting for transfers between devices, fixed_weights(): to_plane = lambda value: lax.ppermute(value, 'parts', [(0, 1), (1, 0)])  42.5 us
    pallas_call x2, Pallas kernels, partial_sums(): pl.pallas_call(partial_kernel, grid_spec=pltpu.PrefetchScalarGridSpec(num...  39.9 us
    pallas_call x1, Pallas kernels, sort_rows(): pl.pallas_call(functools.partial(sort_kernel, experts), grid_spec=pltpu.P...  38.4 us
    all_gather x2, waiting for transfers between devices, fixed_weights(): lax.all_gather(units, 'ep', axis=0, axis_index_groups=line, tiled=True)  20.3 us
    all_to_all x1, blocking collectives, fixed_weights(): lax.all_to_all(mixed.reshape(size, count, width), 'ep', split_axis=0, con...  18.9 us
  transfers between devices with their start and end apart: 28, of which 15 were waited for; matrix products, arithmetic and copies ran while one was open for 2% of the time, Pallas kernels for 12%

profile of v3, /device:TPU:15, one launch (start us, length us, event | category | flops | bytes accessed | tf_op | source)
XLA Modules:
  0.0 516.4 jit_solution(8893496205511893913)
XLA Ops:
  6.5 0.7 reduce-precision_convert_fusion.1
  7.2 0.7 convert_convert_fusion
  8.0 1.8 reshape.60
  10.0 1.0 pad_maximum_fusion.1
  11.0 6.6 %all-to-all-start = ((bf16[16,64,256]{2,1,0:T(8,128)(2,1)}), bf16[16,64,256]{2,1,0:T(8,128)(2,1)S(1)}, u32[]{:S(2)}, u32[]{:S(2)}) async-start(bf16[16,64,256]{2,1,0:T(8,128)(2,1)} %pad_maximum_fusion.1), calls=%async_computation | async-start | bytes 1048576 | tf_op jit(solution)/shard_map/all_to_all | solution.py:358
  17.6 3.7 constant_dynamic-slice_fusion.1
  21.4 0.5 collective-permute-start.5
  21.9 9.5 %all-to-all-done = bf16[16,64,256]{2,1,0:T(8,128)(2,1)S(1)} async-done(((bf16[16,64,256]{2,1,0:T(8,128)(2,1)}), bf16[16,64,256]{2,1,0:T(8,128)(2,1)S(1)}, u32[]{:S(2)}, u32[]{:S(2)}) %all-to-all-start) | async-done | bytes 524320 | tf_op jit(solution)/shard_map/all_to_all | solution.py:358
  31.7 0.8 collective-permute-start.3
  32.5 3.3 constant_dynamic-slice_fusion
  35.7 10.9 %collective-permute-done.5.refs_4_ = bf16[16,224,128]{2,1,0:T(8,128)(2,1)S(1)} collective-permute-done((bf16[16,224,128]{2,1,0:T(8,128)(2,1)}, bf16[16,224,128]{2,1,0:T(8,128)(2,1)S(1)}, u32[]{:S(2)}, u32[]{:S(2)}) %collective-permute-start.5) | collective-permute-done | bytes 917536 | tf_op jit(solution)/shard_map/ppermute | solution.py:342
  46.6 11.2 %collective-permute-done.1.refs_2_ = bf16[1024,256]{1,0:T(8,128)(2,1)S(1)} collective-permute-done((bf16[1024,256]{1,0:T(8,128)(2,1)S(1)}, bf16[1024,256]{1,0:T(8,128)(2,1)S(1)}, u32[]{:S(2)}, u32[]{:S(2)}) %collective-permute-start.1) | collective-permute-done | bytes 524320 | tf_op jit(solution)/shard_map/ppermute | solution.py:342
  57.8 0.8 collective-permute-start.6
  58.8 3.6 order.1
  63.3 17.2 %collective-permute-done.6.refs_5_ = bf16[16,224,128]{2,1,0:T(8,128)(2,1)S(1)} collective-permute-done((bf16[16,224,128]{2,1,0:T(8,128)(2,1)S(1)}, bf16[16,224,128]{2,1,0:T(8,128)(2,1)S(1)}, u32[]{:S(2)}, u32[]{:S(2)}) %collective-permute-start.6) | collective-permute-done | bytes 917536 | tf_op jit(solution)/shard_map/ppermute | solution.py:342
  80.5 38.4 %sort_rows.1 = (bf16[8192,1024]{1,0:T(8,128)(2,1)}, f32[8192,128]{1,0:T(8,128)}) custom-call(s32[32]{0:T(128)S(1)} %get-tuple-element.49.low, s32[32]{0:T(128)S(1)} %get-tuple-element.48.high, s32[17]{0:T(128)S(1)} %slice_bitcast_fusion.base, s32[16,8,128]{2,1,0:T(8,128)S(1)} %bitcast.29, bf16[1024,128]{1,0:T(8,128)(2,1)S(1)} %get-tuple-element.17.gates_ref, ...), custom_call_target="tpu_custom_call" | custom-call | flops 17179869184 | bytes 33554432 | tf_op jit(solution)/shard_map/sort_rows/pallas_call | solution.py:189
  118.9 19.9 %partial_sums.2 = bf16[8192,256]{1,0:T(8,128)(2,1)} custom-call(s32[32]{0:T(128)S(1)} %get-tuple-element.49.low, s32[32]{0:T(128)S(1)} %get-tuple-element.48.high, s32[17]{0:T(128)S(1)} %slice_bitcast_fusion.base, s32[1]{0:T(128)} %bitcast.5.quarter, bf16[8192,1024]{1,0:T(8,128)(2,1)} %get-tuple-element.18.rows_ref, bf16[16,224,1024]{2,1,0:T(8,128)(2,1)} %refs_0_.3, ...), custom_call_target="tpu_custom_call" | custom-call | flops 4294967296 | bytes 16777216 | tf_op jit(solution)/shard_map/partial_sums/pallas_call | solution.py:245
  138.9 0.8 collective-permute-start.11
  139.7 22.4 %collective-permute-done.11.refs_4_ = bf16[16,224,128]{2,1,0:T(8,128)(2,1)S(1)} collective-permute-done((bf16[16,224,128]{2,1,0:T(8,128)(2,1)}, bf16[16,224,128]{2,1,0:T(8,128)(2,1)S(1)}, u32[]{:S(2)}, u32[]{:S(2)}) %collective-permute-start.11) | collective-permute-done | bytes 917536 | tf_op jit(solution)/shard_map/ppermute | solution.py:342
  162.8 1.4 collective-permute-start.13
  164.2 20.6 %collective-permute-done.12.refs_5_ = bf16[16,224,128]{2,1,0:T(8,128)(2,1)S(1)} collective-permute-done((bf16[16,224,128]{2,1,0:T(8,128)(2,1)}, bf16[16,224,128]{2,1,0:T(8,128)(2,1)S(1)}, u32[]{:S(2)}, u32[]{:S(2)}) %collective-permute-start.12) | collective-permute-done | bytes 917536 | tf_op jit(solution)/shard_map/ppermute | solution.py:342
  184.8 22.2 %collective-permute-done.14.refs_7_ = bf16[16,224,128]{2,1,0:T(8,128)(2,1)S(1)} collective-permute-done((bf16[16,224,128]{2,1,0:T(8,128)(2,1)S(1)}, bf16[16,224,128]{2,1,0:T(8,128)(2,1)S(1)}, u32[]{:S(2)}, u32[]{:S(2)}) %collective-permute-start.14) | collective-permute-done | bytes 917536 | tf_op jit(solution)/shard_map/ppermute | solution.py:343
  207.0 20.0 %partial_sums.3 = bf16[8192,256]{1,0:T(8,128)(2,1)} custom-call(s32[32]{0:T(128)S(1)} %get-tuple-element.49.low, s32[32]{0:T(128)S(1)} %get-tuple-element.48.high, s32[17]{0:T(128)S(1)} %slice_bitcast_fusion.base, s32[1]{0:T(128)} %bitcast.5.quarter, bf16[8192,1024]{1,0:T(8,128)(2,1)} %get-tuple-element.18.rows_ref, bf16[16,224,1024]{2,1,0:T(8,128)(2,1)} %refs_0_.3, ...), custom_call_target="tpu_custom_call" | custom-call | flops 4294967296 | bytes 16777216 | tf_op jit(solution)/shard_map/partial_sums/pallas_call | solution.py:245
  227.1 1.4 convert_element_type.42
  228.5 74.5 %reduce-scatter.5.cloned.1.call-done = bf16[2048,256]{1,0:T(8,128)(2,1)} async-done(((bf16[8192,256]{1,0:T(8,128)(2,1)}), bf16[2048,256]{1,0:T(8,128)(2,1)}) %reduce-scatter.5.cloned.1.call-update) | async-done | bytes 1048592 | tf_op jit(solution)/shard_map/reduce_scatter | solution.py:387
  303.0 1.4 convert_element_type.44
  304.4 3.0 fusion.4
  307.9 2.4 dynamic-slice_bitcast_fusion
  310.3 0.8 collective-permute-start.17
  311.1 22.0 %collective-permute-done.17.refs_2_ = bf16[16,224,128]{2,1,0:T(8,128)(2,1)S(1)} collective-permute-done((bf16[16,224,128]{2,1,0:T(8,128)(2,1)S(1)}, bf16[16,224,128]{2,1,0:T(8,128)(2,1)S(1)}, u32[]{:S(2)}, u32[]{:S(2)}) %collective-permute-start.17) | collective-permute-done | bytes 917536 | tf_op jit(solution)/shard_map/ppermute | solution.py:342
  333.2 0.5 collective-permute-start.18
  334.2 21.6 %collective-permute-done.18.refs_3_ = bf16[16,224,128]{2,1,0:T(8,128)(2,1)S(1)} collective-permute-done((bf16[16,224,128]{2,1,0:T(8,128)(2,1)S(1)}, bf16[16,224,128]{2,1,0:T(8,128)(2,1)S(1)}, u32[]{:S(2)}, u32[]{:S(2)}) %collective-permute-start.18) | collective-permute-done | bytes 917536 | tf_op jit(solution)/shard_map/ppermute | solution.py:342
  356.1 0.7 copy-done.6
  356.8 0.9 copy-done.7
  357.8 20.1 %collective-permute-done.20.refs_5_ = bf16[16,224,128]{2,1,0:T(8,128)(2,1)} collective-permute-done((bf16[16,224,128]{2,1,0:T(8,128)(2,1)S(1)}, bf16[16,224,128]{2,1,0:T(8,128)(2,1)}, u32[]{:S(2)}, u32[]{:S(2)}) %collective-permute-start.20) | collective-permute-done | bytes 917536 | tf_op jit(solution)/shard_map/ppermute | solution.py:343
  377.8 20.3 %all-gather.5.cloned.1.call-done.hidden1 = bf16[8192,128]{1,0:T(8,128)(2,1)} async-done(((bf16[2048,128]{1,0:T(8,128)(2,1)}), bf16[8192,128]{1,0:T(8,128)(2,1)}) %all-gather.5.cloned.1.call-update) | async-done | bytes 2097168 | tf_op jit(solution)/shard_map/all_gather | solution.py:391
  398.1 5.9 %broadcast_in_dim.5.place_ref = s32[16,1024,128]{2,1,0:T(8,128)} broadcast(s32[16,1024]{1,0:T(8,128)S(1)} %get-tuple-element.42), dimensions={0,1} | broadcast | bytes 8454144 | tf_op jit(solution)/shard_map/broadcast_in_dim | solution.py:393
  404.0 61.2 %down_and_mix.1 = f32[1024,1024]{1,0:T(8,128)} custom-call(s32[32]{0:T(128)} %copy-done.1, s32[32]{0:T(128)} %copy-done, s32[17]{0:T(128)} %copy-done.2, s32[1]{0:T(128)} %bitcast.5.quarter, s32[16,1024,128]{2,1,0:T(8,128)} %broadcast_in_dim.5.place_ref, bf16[8192,128]{1,0:T(8,128)(2,1)} %all-gather.3.cloned.1.call-done.hidden0, ...), custom_call_target="tpu_custom_call" | custom-call | flops 17179869184 | bytes 16777216 | tf_op jit(solution)/shard_map/down_and_mix/pallas_call | solution.py:305
  465.2 2.5 convert.22
  467.9 0.5 copy.17
  468.5 1.1 collective-permute-start.21
  469.5 2.1 collective-permute-done.21
  472.3 1.4 fusion
  473.7 0.5 collective-permute-start.22
  474.2 13.5 %collective-permute-done.22 = bf16[1024,224]{1,0:T(8,128)(2,1)S(1)} collective-permute-done((bf16[1024,224]{1,0:T(8,128)(2,1)S(1)}, bf16[1024,224]{1,0:T(8,128)(2,1)S(1)}, u32[]{:S(2)}, u32[]{:S(2)}) %collective-permute-start.22) | collective-permute-done | bytes 458784 | tf_op jit(solution)/shard_map/ppermute | solution.py:342
  487.6 1.4 fusion.2
  489.1 18.9 %all_to_all.10 = bf16[16,64,224]{2,1,0:T(8,128)(2,1)S(1)} all-to-all(bf16[16,64,224]{2,1,0:T(8,128)(2,1)S(1)} %bitcast.32), channel_id=1, replica_groups=mesh['parts'=2,'ep'=16,'tp'=1] {'ep'}, dimensions={0} | all-to-all | bytes 917504 | tf_op jit(solution)/shard_map/all_to_all | solution.py:400
  508.2 1.6 reshape.65
  (66 shorter events, 5.2 us)
Async XLA Ops:
  11.0 20.4 %all-to-all-start = ((bf16[16,64,256]{2,1,0:T(8,128)(2,1)}), bf16[16,64,256]{2,1,0:T(8,128)(2,1)S(1)}, u32[]{:S(2)}, u32[]{:S(2)}) async-start(bf16[16,64,256]{2,1,0:T(8,128)(2,1)} %pad_maximum_fusion.1), calls=%async_computation | async-start | bytes 1048576 | tf_op jit(solution)/shard_map/all_to_all | solution.py:358
  17.6 209.5 %reduce-scatter.3.cloned.1.call-start = ((), (), s32[]{:S(2)}) async-start(), calls=%async_computation.4 | async-start | bytes 5242880 | tf_op jit(solution)/shard_map/reduce_scatter | solution.py:387
  21.4 25.3 %collective-permute-start.5 = (bf16[16,224,128]{2,1,0:T(8,128)(2,1)}, bf16[16,224,128]{2,1,0:T(8,128)(2,1)S(1)}, u32[]{:S(2)}, u32[]{:S(2)}) collective-permute-start(bf16[16,224,128]{2,1,0:T(8,128)(2,1)} %get-tuple-element.35), channel_id=1, source_target_pairs={{0,2},{1,3},{2,0},{3,1},{4,6},{5,7},{6,4},{7,5},{8,10},{9,11},{10,... | collective-permute-start | bytes 2752520 | tf_op jit(solution)/shard_map/ppermute | solution.py:342
  31.4 26.4 %collective-permute-start.1 = (bf16[1024,256]{1,0:T(8,128)(2,1)S(1)}, bf16[1024,256]{1,0:T(8,128)(2,1)S(1)}, u32[]{:S(2)}, u32[]{:S(2)}) collective-permute-start(bf16[1024,256]{1,0:T(8,128)(2,1)S(1)} %bitcast.25), channel_id=1, source_target_pairs={{0,2},{1,3},{2,0},{3,1},{4,6},{5,7},{6,4},{7,5},{8,10},{9,11},{10,... | collective-permute-start | bytes 1572872 | tf_op jit(solution)/shard_map/ppermute | solution.py:342
  31.7 87.1 %collective-permute-start.3 = (bf16[16,224,128]{2,1,0:T(8,128)(2,1)}, bf16[16,224,128]{2,1,0:T(8,128)(2,1)S(1)}, u32[]{:S(2)}, u32[]{:S(2)}) collective-permute-start(bf16[16,224,128]{2,1,0:T(8,128)(2,1)} %get-tuple-element.36), channel_id=1, source_target_pairs={{0,1},{1,0},{2,3},{3,2},{4,5},{5,4},{6,7},{7,6},{8,9},{9,8},{10,11... | collective-permute-start | bytes 2752520 | tf_op jit(solution)/shard_map/ppermute | solution.py:341
  35.7 83.1 %collective-permute-start.4 = (bf16[16,224,128]{2,1,0:T(8,128)(2,1)S(1)}, bf16[16,224,128]{2,1,0:T(8,128)(2,1)S(1)}, u32[]{:S(2)}, u32[]{:S(2)}) collective-permute-start(bf16[16,224,128]{2,1,0:T(8,128)(2,1)S(1)} %get-tuple-element.32), channel_id=1, source_target_pairs={{0,1},{1,0},{2,3},{3,2},{4,5},{5,4},{6,7},{7,6},{8,9},{9,8},{10,11... | collective-permute-start | bytes 2752520 | tf_op jit(solution)/shard_map/ppermute | solution.py:341
  57.8 22.7 %collective-permute-start.6 = (bf16[16,224,128]{2,1,0:T(8,128)(2,1)S(1)}, bf16[16,224,128]{2,1,0:T(8,128)(2,1)S(1)}, u32[]{:S(2)}, u32[]{:S(2)}) collective-permute-start(bf16[16,224,128]{2,1,0:T(8,128)(2,1)S(1)} %get-tuple-element.19), channel_id=1, source_target_pairs={{0,2},{1,3},{2,0},{3,1},{4,6},{5,7},{6,4},{7,5},{8,10},{9,11},{10,... | collective-permute-start | bytes 2752520 | tf_op jit(solution)/shard_map/ppermute | solution.py:342
  58.7 4.4 collective-permute-start
  62.4 18.1 %collective-permute-start.2 = (bf16[1024,256]{1,0:T(8,128)(2,1)S(1)}, bf16[1024,256]{1,0:T(8,128)(2,1)S(1)}, u32[]{:S(2)}, u32[]{:S(2)}) collective-permute-start(bf16[1024,256]{1,0:T(8,128)(2,1)S(1)} %collective-permute-done.1.refs_2_), channel_id=1, source_target_pairs={{0,1},{1,0},{2,3},{3,2},{4,5},{5,4},{6,7},{7,6},{8,9},{9,8},{10,11... | collective-permute-start | bytes 1572872 | tf_op jit(solution)/shard_map/ppermute | solution.py:341
  63.0 144.0 %copy-start = (s32[32]{0:T(128)}, s32[32]{0:T(128)S(1)}, u32[]{:S(2)}) copy-start(s32[32]{0:T(128)S(1)} %get-tuple-element.48.high) | copy-start | bytes 388
  63.0 144.0 %copy-start.1 = (s32[32]{0:T(128)}, s32[32]{0:T(128)S(1)}, u32[]{:S(2)}) copy-start(s32[32]{0:T(128)S(1)} %get-tuple-element.49.low) | copy-start | bytes 388
  63.1 143.9 %copy-start.2 = (s32[17]{0:T(128)}, s32[17]{0:T(128)S(1)}, u32[]{:S(2)}) copy-start(s32[17]{0:T(128)S(1)} %slice_bitcast_fusion.base) | copy-start | bytes 208
  63.1 55.8 %collective-permute-start.7 = (bf16[16,224,128]{2,1,0:T(8,128)(2,1)S(1)}, bf16[16,224,128]{2,1,0:T(8,128)(2,1)S(1)}, u32[]{:S(2)}, u32[]{:S(2)}) collective-permute-start(bf16[16,224,128]{2,1,0:T(8,128)(2,1)S(1)} %collective-permute-done.5.refs_4_), channel_id=1, source_target_pairs={{0,16},{16,0},{1,17},{17,1},{2,18},{18,2},{3,19},{19,3},{4,20},{20... | collective-permute-start | bytes 2752520 | tf_op jit(solution)/shard_map/ppermute | solution.py:343
  80.5 38.4 %collective-permute-start.8 = (bf16[16,224,128]{2,1,0:T(8,128)(2,1)S(1)}, bf16[16,224,128]{2,1,0:T(8,128)(2,1)S(1)}, u32[]{:S(2)}, u32[]{:S(2)}) collective-permute-start(bf16[16,224,128]{2,1,0:T(8,128)(2,1)S(1)} %collective-permute-done.6.refs_5_), channel_id=1, source_target_pairs={{0,16},{16,0},{1,17},{17,1},{2,18},{18,2},{3,19},{19,3},{4,20},{20... | collective-permute-start | bytes 2752520 | tf_op jit(solution)/shard_map/ppermute | solution.py:343
  138.8 164.1 %reduce-scatter.5.cloned.1.call-start = ((), (), s32[]{:S(2)}) async-start(), calls=%async_computation.6 | async-start | bytes 5242880 | tf_op jit(solution)/shard_map/reduce_scatter | solution.py:387
  138.9 23.2 %collective-permute-start.11 = (bf16[16,224,128]{2,1,0:T(8,128)(2,1)}, bf16[16,224,128]{2,1,0:T(8,128)(2,1)S(1)}, u32[]{:S(2)}, u32[]{:S(2)}) collective-permute-start(bf16[16,224,128]{2,1,0:T(8,128)(2,1)} %get-tuple-element.21), channel_id=1, source_target_pairs={{0,2},{1,3},{2,0},{3,1},{4,6},{5,7},{6,4},{7,5},{8,10},{9,11},{10,... | collective-permute-start | bytes 2752520 | tf_op jit(solution)/shard_map/ppermute | solution.py:342
  162.1 22.7 %collective-permute-start.12 = (bf16[16,224,128]{2,1,0:T(8,128)(2,1)}, bf16[16,224,128]{2,1,0:T(8,128)(2,1)S(1)}, u32[]{:S(2)}, u32[]{:S(2)}) collective-permute-start(bf16[16,224,128]{2,1,0:T(8,128)(2,1)} %get-tuple-element.22), channel_id=1, source_target_pairs={{0,2},{1,3},{2,0},{3,1},{4,6},{5,7},{6,4},{7,5},{8,10},{9,11},{10,... | collective-permute-start | bytes 2752520 | tf_op jit(solution)/shard_map/ppermute | solution.py:342
  162.3 22.5 %collective-permute-start.10 = (bf16[16,224,128]{2,1,0:T(8,128)(2,1)S(1)}, bf16[16,224,128]{2,1,0:T(8,128)(2,1)S(1)}, u32[]{:S(2)}, u32[]{:S(2)}) collective-permute-start(bf16[16,224,128]{2,1,0:T(8,128)(2,1)S(1)} %get-tuple-element.30), channel_id=1, source_target_pairs={{0,1},{1,0},{2,3},{3,2},{4,5},{5,4},{6,7},{7,6},{8,9},{9,8},{10,11... | collective-permute-start | bytes 2752520 | tf_op jit(solution)/shard_map/ppermute | solution.py:341
  162.8 22.0 %collective-permute-start.9 = (bf16[16,224,128]{2,1,0:T(8,128)(2,1)S(1)}, bf16[16,224,128]{2,1,0:T(8,128)(2,1)S(1)}, u32[]{:S(2)}, u32[]{:S(2)}) collective-permute-start(bf16[16,224,128]{2,1,0:T(8,128)(2,1)S(1)} %get-tuple-element.34), channel_id=1, source_target_pairs={{0,1},{1,0},{2,3},{3,2},{4,5},{5,4},{6,7},{7,6},{8,9},{9,8},{10,11... | collective-permute-start | bytes 2752520 | tf_op jit(solution)/shard_map/ppermute | solution.py:341
  162.8 22.0 %collective-permute-start.13 = (bf16[16,224,128]{2,1,0:T(8,128)(2,1)S(1)}, bf16[16,224,128]{2,1,0:T(8,128)(2,1)S(1)}, u32[]{:S(2)}, u32[]{:S(2)}) collective-permute-start(bf16[16,224,128]{2,1,0:T(8,128)(2,1)S(1)} %collective-permute-done.11.refs_4_), channel_id=1, source_target_pairs={{0,16},{16,0},{1,17},{17,1},{2,18},{18,2},{3,19},{19,3},{4,20},{20... | collective-permute-start | bytes 2752520 | tf_op jit(solution)/shard_map/ppermute | solution.py:343
  184.8 22.2 %collective-permute-start.14 = (bf16[16,224,128]{2,1,0:T(8,128)(2,1)S(1)}, bf16[16,224,128]{2,1,0:T(8,128)(2,1)S(1)}, u32[]{:S(2)}, u32[]{:S(2)}) collective-permute-start(bf16[16,224,128]{2,1,0:T(8,128)(2,1)S(1)} %collective-permute-done.12.refs_5_), channel_id=1, source_target_pairs={{0,16},{16,0},{1,17},{17,1},{2,18},{18,2},{3,19},{19,3},{4,20},{20... | collective-permute-start | bytes 2752520 | tf_op jit(solution)/shard_map/ppermute | solution.py:343
  227.0 150.8 %all-gather.3.cloned.1.call-start = ((), (), s32[]{:S(2)}) async-start(), calls=%async_computation.5 | async-start | bytes 2621440 | tf_op jit(solution)/shard_map/all_gather | solution.py:391
  307.3 90.8 %all-gather.5.cloned.1.call-start = ((), (), s32[]{:S(2)}) async-start(), calls=%async_computation.7 | async-start | bytes 2621440 | tf_op jit(solution)/shard_map/all_gather | solution.py:391
  310.3 22.9 %collective-permute-start.17 = (bf16[16,224,128]{2,1,0:T(8,128)(2,1)S(1)}, bf16[16,224,128]{2,1,0:T(8,128)(2,1)S(1)}, u32[]{:S(2)}, u32[]{:S(2)}) collective-permute-start(bf16[16,224,128]{2,1,0:T(8,128)(2,1)S(1)} %get-tuple-element.23), channel_id=1, source_target_pairs={{0,2},{1,3},{2,0},{3,1},{4,6},{5,7},{6,4},{7,5},{8,10},{9,11},{10,... | collective-permute-start | bytes 2752520 | tf_op jit(solution)/shard_map/ppermute | solution.py:342
  333.2 70.8 %copy-start.3 = (bf16[16,224,128]{2,1,0:T(8,128)(2,1)}, bf16[16,224,128]{2,1,0:T(8,128)(2,1)S(1)}, u32[]{:S(2)}) copy-start(bf16[16,224,128]{2,1,0:T(8,128)(2,1)S(1)} %collective-permute-done.17.refs_2_) | copy-start | bytes 2752516
  333.2 22.7 %collective-permute-start.18 = (bf16[16,224,128]{2,1,0:T(8,128)(2,1)S(1)}, bf16[16,224,128]{2,1,0:T(8,128)(2,1)S(1)}, u32[]{:S(2)}, u32[]{:S(2)}) collective-permute-start(bf16[16,224,128]{2,1,0:T(8,128)(2,1)S(1)} %get-tuple-element.24), channel_id=1, source_target_pairs={{0,2},{1,3},{2,0},{3,1},{4,6},{5,7},{6,4},{7,5},{8,10},{9,11},{10,... | collective-permute-start | bytes 2752520 | tf_op jit(solution)/shard_map/ppermute | solution.py:342
  333.7 22.1 %collective-permute-start.15 = (bf16[16,224,128]{2,1,0:T(8,128)(2,1)S(1)}, bf16[16,224,128]{2,1,0:T(8,128)(2,1)S(1)}, u32[]{:S(2)}, u32[]{:S(2)}) collective-permute-start(bf16[16,224,128]{2,1,0:T(8,128)(2,1)S(1)} %get-tuple-element.27), channel_id=1, source_target_pairs={{0,1},{1,0},{2,3},{3,2},{4,5},{5,4},{6,7},{7,6},{8,9},{9,8},{10,11... | collective-permute-start | bytes 2752520 | tf_op jit(solution)/shard_map/ppermute | solution.py:341
  333.8 22.0 %collective-permute-start.16 = (bf16[16,224,128]{2,1,0:T(8,128)(2,1)S(1)}, bf16[16,224,128]{2,1,0:T(8,128)(2,1)S(1)}, u32[]{:S(2)}, u32[]{:S(2)}) collective-permute-start(bf16[16,224,128]{2,1,0:T(8,128)(2,1)S(1)} %get-tuple-element.26), channel_id=1, source_target_pairs={{0,1},{1,0},{2,3},{3,2},{4,5},{5,4},{6,7},{7,6},{8,9},{9,8},{10,11... | collective-permute-start | bytes 2752520 | tf_op jit(solution)/shard_map/ppermute | solution.py:341
  334.2 21.9 %collective-permute-start.19 = (bf16[16,224,128]{2,1,0:T(8,128)(2,1)S(1)}, bf16[16,224,128]{2,1,0:T(8,128)(2,1)S(1)}, u32[]{:S(2)}, u32[]{:S(2)}) collective-permute-start(bf16[16,224,128]{2,1,0:T(8,128)(2,1)S(1)} %collective-permute-done.17.refs_2_), channel_id=1, source_target_pairs={{0,16},{16,0},{1,17},{17,1},{2,18},{18,2},{3,19},{19,3},{4,20},{20... | collective-permute-start | bytes 2752520 | tf_op jit(solution)/shard_map/ppermute | solution.py:343
  355.8 48.2 %copy-start.4 = (bf16[16,224,128]{2,1,0:T(8,128)(2,1)}, bf16[16,224,128]{2,1,0:T(8,128)(2,1)S(1)}, u32[]{:S(2)}) copy-start(bf16[16,224,128]{2,1,0:T(8,128)(2,1)S(1)} %collective-permute-done.18.refs_3_) | copy-start | bytes 2752516
  355.8 22.0 %collective-permute-start.20 = (bf16[16,224,128]{2,1,0:T(8,128)(2,1)S(1)}, bf16[16,224,128]{2,1,0:T(8,128)(2,1)}, u32[]{:S(2)}, u32[]{:S(2)}) collective-permute-start(bf16[16,224,128]{2,1,0:T(8,128)(2,1)S(1)} %collective-permute-done.18.refs_3_), channel_id=1, source_target_pairs={{0,16},{16,0},{1,17},{17,1},{2,18},{18,2},{3,19},{19,3},{4,20},{20... | collective-permute-start | bytes 2752520 | tf_op jit(solution)/shard_map/ppermute | solution.py:343
  355.8 48.2 %copy-start.5 = (bf16[16,224,128]{2,1,0:T(8,128)(2,1)}, bf16[16,224,128]{2,1,0:T(8,128)(2,1)S(1)}, u32[]{:S(2)}) copy-start(bf16[16,224,128]{2,1,0:T(8,128)(2,1)S(1)} %collective-permute-done.15.refs_0_) | copy-start | bytes 2752516
  355.9 1.0 copy-start.6
  356.8 0.9 copy-start.7
  468.5 3.2 collective-permute-start.21
  473.7 14.0 %collective-permute-start.22 = (bf16[1024,224]{1,0:T(8,128)(2,1)S(1)}, bf16[1024,224]{1,0:T(8,128)(2,1)S(1)}, u32[]{:S(2)}, u32[]{:S(2)}) collective-permute-start(bf16[1024,224]{1,0:T(8,128)(2,1)S(1)} %fusion), channel_id=1, source_target_pairs={{0,2},{1,3},{2,0},{3,1},{4,6},{5,7},{6,4},{7,5},{8,10},{9,11},{10,... | collective-permute-start | bytes 1376264 | tf_op jit(solution)/shard_map/ppermute | solution.py:342
Sparse Core Ops, SparseCore 0:
  139.0 76.6 reduce-scatter.2
  227.1 75.7 reduce-scatter.4
  307.5 44.5 all-gather.2
  353.4 44.6 all-gather.4

commit v4 on v3

--- a/solution.py
+++ b/solution.py
@@ -147,28 +147,23 @@
     slices, (out, scale_out, onehot_ref, name_ref) = refs[:-4], refs[-4:]
     tokens = onehot_ref.shape[1]
     number = lax.broadcasted_iota(jnp.int32, (TILE, 128), 0).astype(F32).astype(BF16)
+    onehot_ref[...] = jnp.zeros_like(onehot_ref)
 
     @pl.loop(0, BLOCK // TILE)
     def _(part):
         i = pl.program_id(0) * (BLOCK // TILE) + part
         row0 = i * TILE
         here = pl.ds(pl.multiple_of(part * TILE, TILE), TILE)
-        for c in range(tokens // 128):
-
-            def add(e, found):
-                away = across_ref[e][c : c + 1, :] - row0
-                away = jnp.where((away >= 0) & (away < TILE), away, -1).astype(F32).astype(BF16)
-                return jnp.where(number == away, jnp.ones((), BF16), found)
-
-            onehot_ref[here, c * 128 : (c + 1) * 128] = lax.fori_loop(
-                low[i], high[i], add, jnp.zeros((TILE, 128), BF16)
-            )
-        name_ref[here, :] = lax.fori_loop(
-            low[i],
-            high[i],
-            lambda e, name: jnp.where(mine_of(base, e, row0), e, name),
-            jnp.zeros((TILE, UNITS), jnp.int32),
-        )
+
+        @pl.loop(low[i], high[i])
+        def _(e):
+            away = across_ref[e] - row0
+            away = jnp.where((away >= 0) & (away < TILE), away, -1).astype(F32)
+            for c in range(tokens // 128):
+                at = slice(c * 128, (c + 1) * 128)
+                hit = number == away[c : c + 1, :].astype(BF16)
+                onehot_ref[here, at] = jnp.where(hit, jnp.ones((), BF16), onehot_ref[here, at])
+            name_ref[here, :] = jnp.where(mine_of(base, e, row0), e, name_ref[here, :])
 
     onehot = onehot_ref[...]
     for k, ref in enumerate(slices):
@@ -199,23 +194,76 @@
             out_specs=[
                 pl.BlockSpec((BLOCK, width), lambda i, *_: (i, 0)),
                 pl.BlockSpec((BLOCK, UNITS), lambda i, *_: (i, 0)),
+                pl.BlockSpec((BLOCK, tokens), lambda i, *_: (i, 0)),
             ],
-            scratch_shapes=[
-                pltpu.VMEM((BLOCK, tokens), BF16),
-                pltpu.VMEM((BLOCK, UNITS), jnp.int32),
-            ],
+            scratch_shapes=[pltpu.VMEM((BLOCK, UNITS), jnp.int32)],
         ),
         out_shape=[
             jax.ShapeDtypeStruct((rows, width), BF16),
             jax.ShapeDtypeStruct((rows, UNITS), F32),
+            jax.ShapeDtypeStruct((rows, tokens), BF16),
         ],
         compiler_params=params(),
-        cost_estimate=cost(2 * rows * tokens * width, 4 * rows * width),
+        cost_estimate=cost(2 * rows * tokens * width, 8 * rows * width),
         name="sort_rows",
     )(*spans, base, across, gates, *slices)
 
 
-def partial_kernel(low, high, base, quarter, rows_ref, *refs):
+def sort_more_kernel(onehot_ref, *refs):
+    for k, ref in enumerate(refs[:-1]):
+        at = slice(k * LANES, (k + 1) * LANES)
+        refs[-1][:, at] = dot(onehot_ref[...], ref[...], ((1,), (0,))).astype(BF16)
+
+
+def sort_more(onehot, slices):
+    rows, tokens = onehot.shape
+    width = len(slices) * LANES
+    return pl.pallas_call(
+        sort_more_kernel,
+        grid=(rows // BLOCK,),
+        in_specs=[pl.BlockSpec((BLOCK, tokens), lambda i: (i, 0))]
+        + [pl.BlockSpec((tokens, LANES), lambda i: (0, 0))] * len(slices),
+        out_specs=pl.BlockSpec((BLOCK, width), lambda i: (i, 0)),
+        out_shape=jax.ShapeDtypeStruct((rows, width), BF16),
+        compiler_params=params(),
+        cost_estimate=cost(2 * rows * tokens * width, 8 * rows * width),
+        name="sort_more",
+    )(onehot, *slices)
+
+
+def scatter_kernel(low, high, place_ref, onehot_ref):
+    tokens = place_ref.shape[1]
+    lane = lax.broadcasted_iota(jnp.int32, (tokens, 128), 1)
+    onehot_ref[...] = jnp.zeros_like(onehot_ref)
+    for part in range(BLOCK // TILE):
+        i = pl.program_id(0) * (BLOCK // TILE) + part
+
+        @pl.loop(low[i], high[i])
+        def _(e):
+            place = place_ref[e] - i * TILE
+            for c in range(TILE // 128):
+                at = slice(part * TILE + c * 128, part * TILE + (c + 1) * 128)
+                onehot_ref[:, at] += jnp.where(place == lane + c * 128, 1.0, 0.0).astype(BF16)
+
+
+def scatter_rows(spans, place, rows):
+    tokens = place.shape[1]
+    return pl.pallas_call(
+        scatter_kernel,
+        grid_spec=pltpu.PrefetchScalarGridSpec(
+            num_scalar_prefetch=2,
+            grid=(rows // BLOCK,),
+            in_specs=[pl.BlockSpec(place.shape, lambda i, *_: (0, 0, 0))],
+            out_specs=pl.BlockSpec((tokens, BLOCK), lambda i, *_: (0, i)),
+        ),
+        out_shape=jax.ShapeDtypeStruct((tokens, rows), BF16),
+        compiler_params=params(),
+        cost_estimate=cost(rows * tokens, 2 * rows * tokens),
+        name="scatter_rows",
+    )(*spans, place)
+
+
+def partial_kernel(low, high, base, quarter, near_ref, far_ref, *refs):
     pairs, out = [refs[j : j + 2] for j in range(0, 8, 2)], refs[-1]
     width = pairs[0][0].shape[1]
 
@@ -228,7 +276,8 @@
             total = 0.0
             for k, pair in enumerate(pairs):
                 weight = jnp.concatenate([pair[0][e], pair[1][e]], axis=1)
-                rows = rows_ref[here, k * LANES : k * LANES + width]
+                rows_ref, at = (near_ref, far_ref)[k // 2], k % 2 * LANES
+                rows = rows_ref[here, at : at + width]
                 total += dot(rows, weight, ((1,), (0,)))
             return jnp.where(mine_of(base, e, i * TILE), total, kept)
 
@@ -237,8 +286,8 @@
         ).astype(BF16)
 
 
-def partial_sums(f, spans, base, quarter, rows_in, w_gate, w_up, pieces):
-    rows = rows_in.shape[0]
+def partial_sums(f, spans, base, quarter, near, far, w_gate, w_up, pieces):
+    rows = near.shape[0]
     experts, width, _ = w_gate.shape
     own = pl.BlockSpec((experts, width, UNITS), lambda i, lo, hi, b, q: (0, 0, 2 * q[0] + f))
     block = pl.BlockSpec((experts, width, UNITS), lambda i, *_: (0, 0, 0))
@@ -247,84 +296,85 @@
         grid_spec=pltpu.PrefetchScalarGridSpec(
             num_scalar_prefetch=4,
             grid=(rows // BLOCK,),
-            in_specs=[pl.BlockSpec((BLOCK, rows_in.shape[1]), lambda i, *_: (i, 0)), own, own]
+            in_specs=[pl.BlockSpec((BLOCK, 2 * LANES), lambda i, *_: (i, 0))] * 2 + [own] * 2
             + [block] * len(pieces),
             out_specs=pl.BlockSpec((BLOCK, 2 * UNITS), lambda i, *_: (i, 0)),
         ),
         out_shape=jax.ShapeDtypeStruct((rows, 2 * UNITS), BF16),
         compiler_params=params(),
-        cost_estimate=cost(4 * rows * rows_in.shape[1] * UNITS, 2 * rows * rows_in.shape[1]),
+        cost_estimate=cost(16 * rows * LANES * UNITS, 8 * rows * LANES),
         name="partial_sums",
-    )(*spans, base, quarter, rows_in, w_gate, w_up, *pieces)
-
-
-def down_kernel(low, high, base, quarter, place_ref, hidden0, hidden1, own_ref, *refs):
-    pairs, (out, onehot_ref, value_ref) = [refs[j : j + 2] for j in range(0, 6, 2)], refs[6:]
-    width = own_ref.shape[1]
-    tokens = place_ref.shape[1]
-    lane = lax.broadcasted_iota(jnp.int32, (tokens, 128), 1)
-
-    @pl.when(pl.program_id(0) == 0)
+    )(*spans, base, quarter, near, far, w_gate, w_up, *pieces)
+
+
+def down_kernel(near, half, low, high, base, quarter, onehot_ref, hidden, start, *refs):
+    weights, (out, total_ref, value_ref) = refs[:-3], refs[-3:]
+    count = out.shape[1] // LANES
+    width = weights[0].shape[1]
+    j = pl.program_id(0)
+
+    @pl.when(j == 0)
     def _():
-        out[...] = jnp.zeros_like(out)
+        total_ref[...] = jnp.zeros_like(total_ref) if start is None else start[...]
         value_ref[...] = jnp.zeros_like(value_ref)
 
     for part in range(BLOCK // TILE):
-        i = pl.program_id(0) * (BLOCK // TILE) + part
+        i = (2 * j + half) * (BLOCK // TILE) + part
         here = slice(part * TILE, (part + 1) * TILE)
-        units = jnp.concatenate([hidden0[here, :], hidden1[here, :]], axis=1)
-        onehot_ref[:, here] = jnp.zeros((tokens, TILE), BF16)
+        units = hidden[here, :]
 
         @pl.loop(low[i], high[i])
         def _(e):
             mine = mine_of(base, e, i * TILE)
-            for k in range(4):
-                weight = own_ref[e]
-                if k:
-                    weight = jnp.concatenate([pairs[k - 1][0][e], pairs[k - 1][1][e]], axis=1)
+            rest = list(weights)
+            for k in range(count):
+                first = rest.pop(0)
+                weight = first[e]
+                if not (near and k == 0):
+                    weight = jnp.concatenate([weight, rest.pop(0)[e]], axis=1)
                 value = dot(units, weight, ((1,), (1,)))
                 at = slice(k * LANES, k * LANES + width)
                 value_ref[here, at] = jnp.where(
                     mine, value, value_ref[here, at].astype(F32)
                 ).astype(BF16)
-            place = place_ref[e] - i * TILE
-            for c in range(TILE // 128):
-                at = slice(part * TILE + c * 128, part * TILE + (c + 1) * 128)
-                hit = jnp.where(place == lane + c * 128, 1.0, 0.0).astype(BF16)
-                onehot_ref[:, at] += hit
-
-    out[...] += dot(onehot_ref[...], value_ref[...], ((1,), (0,)))
-
-
-def down_and_mix(spans, base, quarter, place, hidden, w_down, pieces):
-    rows = hidden[0].shape[0]
-    experts, width, _ = w_down.shape
-    tokens = place.shape[1]
-    block = pl.BlockSpec((BLOCK, UNITS), lambda i, *_: (i, 0))
-    own = pl.BlockSpec((experts, width, 2 * UNITS), lambda i, lo, hi, b, q: (0, 0, q[0]))
+
+    total_ref[...] += dot(onehot_ref[...], value_ref[...], ((1,), (0,)))
+
+    @pl.when(j == pl.num_programs(0) - 1)
+    def _():
+        out[...] = total_ref[...].astype(out.dtype)
+
+
+def down_and_mix(near, half, spans, base, quarter, onehot, hidden, start, weights, count, dtype):
+    rows, units = hidden.shape
+    experts, width, _ = weights[0].shape
+    tokens = onehot.shape[0]
+    block = pl.BlockSpec((BLOCK, units), lambda j, *_: (j, 0))
+    own = pl.BlockSpec((experts, width, units), lambda j, lo, hi, b, q: (0, 0, q[0]))
+    piece = pl.BlockSpec((experts, width, UNITS), lambda j, *_: (0, 0, 0))
+    whole = pl.BlockSpec((tokens, count * LANES), lambda j, *_: (0, 0))
+    kernel = functools.partial(down_kernel, near, half)
+    if start is None:
+        kernel = lambda *refs: down_kernel(near, half, *refs[:6], None, *refs[6:])
     return pl.pallas_call(
-        down_kernel,
+        kernel,
         grid_spec=pltpu.PrefetchScalarGridSpec(
             num_scalar_prefetch=4,
             grid=(rows // BLOCK,),
-            in_specs=[
-                pl.BlockSpec((experts, tokens, 128), lambda i, *_: (0, 0, 0)),
-                block,
-                block,
-                own,
-            ]
-            + [pl.BlockSpec((experts, width, UNITS), lambda i, *_: (0, 0, 0))] * len(pieces),
-            out_specs=pl.BlockSpec((tokens, 4 * LANES), lambda i, *_: (0, 0)),
+            in_specs=[pl.BlockSpec((tokens, BLOCK), lambda j, *_: (0, 2 * j + half)), block]
+            + ([] if start is None else [whole])
+            + ([own] + [piece] * (len(weights) - 1) if near else [piece] * len(weights)),
+            out_specs=whole,
             scratch_shapes=[
-                pltpu.VMEM((tokens, BLOCK), BF16),
-                pltpu.VMEM((BLOCK, 4 * LANES), BF16),
+                pltpu.VMEM((tokens, count * LANES), F32),
+                pltpu.VMEM((BLOCK, count * LANES), BF16),
             ],
         ),
-        out_shape=jax.ShapeDtypeStruct((tokens, 4 * LANES), F32),
+        out_shape=jax.ShapeDtypeStruct((tokens, count * LANES), dtype),
         compiler_params=params(56),
-        cost_estimate=cost(8 * rows * tokens * LANES, 16 * rows * UNITS),
+        cost_estimate=cost(2 * rows * tokens * LANES * count, 2 * rows * tokens),
         name="down_and_mix",
-    )(*spans, base, quarter, place, *hidden, w_down, *pieces)
+    )(*spans, base, quarter, onehot, hidden, *([] if start is None else [start]), *weights)
 
 
 def fixed_weights(size, tokens, expert_ids, gate_weights, w_gate, w_up, w_down):
@@ -367,36 +417,54 @@
     def cut(w, q, f):
         return lax.dynamic_slice_in_dim(w, q * quarter + f * UNITS, UNITS, 2)
 
-    last = []
-    held = []
-    for f, w in ((0, w_gate), (0, w_up), (1, w_gate), (1, w_up), (0, w_down), (1, w_down)):
+    last = ()
+    held, crossed = [], []
+    for n, (f, w) in enumerate(
+        ((0, w_gate), (0, w_up), (1, w_gate), (1, w_up), (0, w_down), (1, w_down))
+    ):
         piece = cut(w, cross_quarter, f)
-        if last:
+        if n:
+            last = (crossed[0],) if n == 1 else (far, crossed[1], crossed[n // 2 * 2 - 1])
             piece = lax.optimization_barrier((piece, *last))[0]
-        across_x = to_cross(piece)
-        last = [across_x, far]
-        held.append((to_twin(cut(w, twin_quarter, f)), across_x, to_plane(across_x)))
+        crossed.append(to_cross(piece))
+        held.append((to_twin(cut(w, twin_quarter, f)), crossed[n], to_plane(crossed[n])))
     weave = lambda pair: [piece for both in zip(*pair) for piece in both]
 
-    sorted_rows, scale = sort_rows(spans, base, across, gates, slices, rows, experts)
+    near_rows, scale, onehot = sort_rows(spans, base, across, gates, slices[:2], rows, experts)
+    far_rows = sort_more(onehot, slices[2:])
     scale = lax.dynamic_slice_in_dim(scale, (me // 4) * (rows // places), rows // places, 0)
-    hidden = []
+    units = []
     for f in range(2):
         pieces = weave(held[2 * f : 2 * f + 2])
-        sums = partial_sums(f, spans, base, which, sorted_rows, w_gate, w_up, pieces)
+        sums = partial_sums(f, spans, base, which, near_rows, far_rows, w_gate, w_up, pieces)
+        later = sums
         sums = lax.psum_scatter(
             sums, "ep", scatter_dimension=0, axis_index_groups=line, tiled=True
         ).astype(F32)
-        units = (jax.nn.silu(sums[:, :UNITS]) * sums[:, UNITS:] * scale).astype(BF16)
-        hidden.append(lax.all_gather(units, "ep", axis=0, axis_index_groups=line, tiled=True))
-
-    place = jnp.broadcast_to(across[:experts, :, None], (experts, size * count, 128))
-    mixed = down_and_mix(spans, base, which, place, hidden, w_down, weave(held[4:]))
-    mine, twin, far, far_twin = (mixed[:, k * LANES : k * LANES + width] for k in range(4))
-    moved = to_twin(jnp.concatenate([far_twin, twin], axis=0).astype(BF16)).astype(F32)
-    tokens_all = size * count
-    far = to_cross((far + moved[:tokens_all]).astype(BF16)).astype(F32)
-    mixed = (mine + moved[tokens_all:] + far).astype(BF16)
+        units.append((jax.nn.silu(sums[:, :UNITS]) * sums[:, UNITS:] * scale).astype(BF16))
+    units = jnp.concatenate(units, axis=1).reshape(-1, BLOCK, 2 * UNITS)
+    hidden = [
+        lax.all_gather(units[half], "ep", axis=0, axis_index_groups=line, tiled=True)
+        for half in range(2)
+    ]
+
+    across = lax.optimization_barrier((across[:experts], later))[0]
+    place = jnp.broadcast_to(across[:, :, None], (experts, size * count, 128))
+    columns = scatter_rows(spans, place, rows)
+    near_weights, far_weights = weave(held[4:])[:2], weave(held[4:])[2:]
+    near_weights = [w_down] + near_weights
+    mix = lambda near, half, start, dtype: down_and_mix(
+        near, half, spans, base, which, columns, hidden[half], start,
+        near_weights if near else far_weights, 2, dtype,
+    )
+    far = mix(False, 1, mix(False, 0, None, F32), BF16)
+    near = mix(True, 0, None, F32)
+    near = mix(True, 1, lax.optimization_barrier((near, far))[0], F32)
+    far, far_twin = far[:, :width], far[:, LANES : LANES + width]
+    far = (far.astype(F32) + to_twin(far_twin).astype(F32)).astype(BF16)
+    far = to_cross(far).astype(F32)
+    twin = to_twin(near[:, LANES : LANES + width].astype(BF16)).astype(F32)
+    mixed = (near[:, :width] + twin + far).astype(BF16)
     mixed = lax.all_to_all(
         mixed.reshape(size, count, width), "ep", split_axis=0, concat_axis=0, tiled=True
     )
@@ -414,7 +482,7 @@
             size % 4 == 0
             and size > 4
             and mesh.shape["parts"] == 2
-            and rows % (2 * BLOCK) == 0
+            and rows == size // 4 * 2 * BLOCK
             and units == 8 * UNITS
             and 3 * experts <= UNITS
             and size * math.prod(expert_ids.shape[:1]) % 128 == 0

time: 519 us -> 496 us (0.956)
  waiting for transfers between devices: 289 us -> 239 us
  Pallas kernels: 143 us -> 170 us
  local copies, waits for them, and re-layouts: 22 us -> 27.8 us
  other arithmetic: 13.8 us -> 8.51 us
    pallas_call x1 -> x6, Pallas kernels: 61.2 us -> 99.4 us  [the longest x4 67.2 us: down_and_mix(): pl.pallas_call(kernel, grid_spec=pltpu.PrefetchScalarGridSpec(num_scalar_...]
    ppermute x6, waiting for transfers between devices: 42.5 us -> 22 us  [fixed_weights(): to_plane = lambda value: lax.ppermute(value, 'parts', [(0, 1), (1, 0)])]
    all_gather x2, waiting for transfers between devices: 20.3 us -> 3.43 us  [fixed_weights(): lax.all_gather(units[half], 'ep', axis=0, axis_index_groups=line, tiled=T...]
    pallas_call x1, Pallas kernels: 38.4 us -> 27.3 us  [sort_rows(): pl.pallas_call(functools.partial(sort_kernel, experts), grid_spec=pltpu.P...]
    all_to_all x1, waiting for transfers between devices: 9.53 us -> 0.89 us  [fixed_weights(): own = lax.all_to_all(parcels, 'ep', split_axis=0, concat_axis=0, tiled=True)]
  transfers between devices with their start and end apart: 28 -> 29, of which waited for: 15 -> 13; matrix products, arithmetic and copies ran while one was open for 2% -> 4% of each run, Pallas kernels for 12% -> 30%
where the time goes in v4:
time: 496 us; the launch traced here: 493 us
  waiting for transfers between devices  239 us (48%)
  Pallas kernels  170 us (34%)
  local copies, waits for them, and re-layouts  27.8 us (6%)
  blocking collectives  18.9 us (4%)
  starting transfers between devices  16 us (3%)
  between operations  13.4 us (3%)
  other arithmetic  8.51 us (2%)
    ppermute x8, waiting for transfers between devices, fixed_weights(): to_cross = lambda value: lax.ppermute(value, ('parts', 'ep'), cross)  134 us
    reduce_scatter x2, waiting for transfers between devices, fixed_weights(): lax.psum_scatter(sums, 'ep', scatter_dimension=0, axis_index_groups=line,...  76.6 us
    pallas_call x4, Pallas kernels, down_and_mix(): pl.pallas_call(kernel, grid_spec=pltpu.PrefetchScalarGridSpec(num_scalar_...  67.2 us
    pallas_call x2, Pallas kernels, partial_sums(): pl.pallas_call(partial_kernel, grid_spec=pltpu.PrefetchScalarGridSpec(num...  39.7 us
    pallas_call x1, Pallas kernels, sort_rows(): pl.pallas_call(functools.partial(sort_kernel, experts), grid_spec=pltpu.P...  27.3 us
    ppermute x6, waiting for transfers between devices, fixed_weights(): to_plane = lambda value: lax.ppermute(value, 'parts', [(0, 1), (1, 0)])  22 us
    all_to_all x1, blocking collectives, fixed_weights(): lax.all_to_all(mixed.reshape(size, count, width), 'ep', split_axis=0, con...  18.9 us
    pallas_call x1, Pallas kernels, scatter_rows(): pl.pallas_call(scatter_kernel, grid_spec=pltpu.PrefetchScalarGridSpec(num...  17 us
  transfers between devices with their start and end apart: 29, of which 13 were waited for; matrix products, arithmetic and copies ran while one was open for 4% of the time, Pallas kernels for 30%

profile of v4, /device:TPU:15, one launch (start us, length us, event | category | flops | bytes accessed | tf_op | source)
XLA Modules:
  0.0 493.4 jit_solution(72705559786311122)
XLA Ops:
  6.5 4.0 constant_dynamic-slice_fusion.1
  10.5 0.8 collective-permute-start.5
  11.5 0.7 reshape.65
  12.4 1.0 pad_maximum_fusion.1
  13.4 6.0 %all-to-all-start = ((bf16[16,64,256]{2,1,0:T(8,128)(2,1)}), bf16[16,64,256]{2,1,0:T(8,128)(2,1)S(1)}, u32[]{:S(2)}, u32[]{:S(2)}) async-start(bf16[16,64,256]{2,1,0:T(8,128)(2,1)} %pad_maximum_fusion.1), calls=%async_computation | async-start | bytes 1048576 | tf_op jit(solution)/shard_map/all_to_all | solution.py:408
  19.9 4.0 constant_dynamic-slice_fusion
  24.1 13.8 %collective-permute-done.5.refs_4_ = bf16[16,224,128]{2,1,0:T(8,128)(2,1)S(1)} collective-permute-done((bf16[16,224,128]{2,1,0:T(8,128)(2,1)}, bf16[16,224,128]{2,1,0:T(8,128)(2,1)S(1)}, u32[]{:S(2)}, u32[]{:S(2)}) %collective-permute-start.5) | collective-permute-done | bytes 917536 | tf_op jit(solution)/shard_map/ppermute | solution.py:392
  38.4 0.9 all-to-all-done
  40.0 3.6 order.1
  44.3 27.3 %collective-permute-done.1.refs_0_ = bf16[1024,256]{1,0:T(8,128)(2,1)S(1)} collective-permute-done((bf16[1024,256]{1,0:T(8,128)(2,1)S(1)}, bf16[1024,256]{1,0:T(8,128)(2,1)S(1)}, u32[]{:S(2)}, u32[]{:S(2)}) %collective-permute-start.1) | collective-permute-done | bytes 524320 | tf_op jit(solution)/shard_map/ppermute | solution.py:392
  72.0 27.3 %sort_rows.1 = (bf16[8192,512]{1,0:T(8,128)(2,1)}, f32[8192,128]{1,0:T(8,128)S(1)}, bf16[8192,1024]{1,0:T(8,128)(2,1)}) custom-call(s32[32]{0:T(128)S(1)} %get-tuple-element.55.low.refs_0_, s32[32]{0:T(128)S(1)} %get-tuple-element.54.high.refs_1_, s32[17]{0:T(128)S(1)} %slice_bitcast_fusion.base.refs_2_, s32[16,8,128]{2,1,0:T(8,128)S(1)} %bitcast.29, ...), custom_call_target="tpu_custom_call" | custom-call | flops 8589934592 | bytes 33554432 | tf_op jit(solution)/shard_map/sort_rows/pallas_call | solution.py:184
  99.3 2.1 copy-done
  101.4 15.2 %sort_more.1.far_ref = bf16[8192,512]{1,0:T(8,128)(2,1)} custom-call(bf16[8192,1024]{1,0:T(8,128)(2,1)} %get-tuple-element.22.onehot_ref, bf16[1024,256]{1,0:T(8,128)(2,1)S(1)} %collective-permute-done.1.refs_0_, bf16[1024,256]{1,0:T(8,128)(2,1)S(1)} %collective-permute-done.2.refs_1_), custom_call_target="tpu_custom_call" | custom-call | flops 8589934592 | bytes 33554432 | tf_op jit(solution)/shard_map/sort_more/pallas_call | solution.py:221
  116.6 19.9 %partial_sums.3 = bf16[8192,256]{1,0:T(8,128)(2,1)} custom-call(s32[32]{0:T(128)S(1)} %get-tuple-element.55.low.refs_0_, s32[32]{0:T(128)S(1)} %get-tuple-element.54.high.refs_1_, s32[17]{0:T(128)S(1)} %slice_bitcast_fusion.base.refs_2_, s32[1]{0:T(128)} %bitcast.5.quarter.refs_3_, bf16[8192,512]{1,0:T(8,128)(2,1)} %get-tuple-element.21.near_ref, ...), custom_call_target="tpu_custom_call" | custom-call | flops 4294967296 | bytes 16777216 | tf_op jit(solution)/shard_map/partial_sums/pallas_call | solution.py:294
  137.0 0.8 copy-done.11
  137.8 0.7 collective-permute-start.7
  139.0 20.9 %collective-permute-done.8.refs_5_ = bf16[16,224,128]{2,1,0:T(8,128)(2,1)S(1)} collective-permute-done((bf16[16,224,128]{2,1,0:T(8,128)(2,1)}, bf16[16,224,128]{2,1,0:T(8,128)(2,1)S(1)}, u32[]{:S(2)}, u32[]{:S(2)}) %collective-permute-start.8) | collective-permute-done | bytes 917536 | tf_op jit(solution)/shard_map/ppermute | solution.py:392
  160.0 19.1 %collective-permute-done.7.refs_4_ = bf16[16,224,128]{2,1,0:T(8,128)(2,1)S(1)} collective-permute-done((bf16[16,224,128]{2,1,0:T(8,128)(2,1)S(1)}, bf16[16,224,128]{2,1,0:T(8,128)(2,1)S(1)}, u32[]{:S(2)}, u32[]{:S(2)}) %collective-permute-start.7) | collective-permute-done | bytes 917536 | tf_op jit(solution)/shard_map/ppermute | solution.py:392
  179.7 1.9 collective-permute-done.10.refs_7_
  181.6 20.1 %collective-permute-done.9.refs_6_ = bf16[16,224,128]{2,1,0:T(8,128)(2,1)S(1)} collective-permute-done((bf16[16,224,128]{2,1,0:T(8,128)(2,1)S(1)}, bf16[16,224,128]{2,1,0:T(8,128)(2,1)S(1)}, u32[]{:S(2)}, u32[]{:S(2)}) %collective-permute-start.9) | collective-permute-done | bytes 917536 | tf_op jit(solution)/shard_map/ppermute | solution.py:393
  201.7 19.8 %partial_sums.2 = bf16[8192,256]{1,0:T(8,128)(2,1)} custom-call(s32[32]{0:T(128)S(1)} %get-tuple-element.55.low.refs_0_, s32[32]{0:T(128)S(1)} %get-tuple-element.54.high.refs_1_, s32[17]{0:T(128)S(1)} %slice_bitcast_fusion.base.refs_2_, s32[1]{0:T(128)} %bitcast.5.quarter.refs_3_, bf16[8192,512]{1,0:T(8,128)(2,1)} %get-tuple-element.21.near_ref, ...), custom_call_target="tpu_custom_call" | custom-call | flops 4294967296 | bytes 16777216 | tf_op jit(solution)/shard_map/partial_sums/pallas_call | solution.py:294
  221.6 1.4 convert_element_type.48
  222.9 76.5 %reduce-scatter.5.cloned.1.call-done = bf16[2048,256]{1,0:T(8,128)(2,1)} async-done(((bf16[8192,256]{1,0:T(8,128)(2,1)}), bf16[2048,256]{1,0:T(8,128)(2,1)}) %reduce-scatter.5.cloned.1.call-update) | async-done | bytes 1048592 | tf_op jit(solution)/shard_map/reduce_scatter | solution.py:441
  299.5 1.4 convert_element_type.50
  300.9 2.0 fusion.3
  302.9 1.1 pad_maximum_fusion
  304.6 3.6 dynamic-slice_bitcast_fusion
  308.2 0.8 collective-permute-start.17
  309.0 1.0 collective-permute-start.18
  310.0 21.3 %collective-permute-done.17.refs_6_.refs_0_ = bf16[16,224,128]{2,1,0:T(8,128)(2,1)S(1)} collective-permute-done((bf16[16,224,128]{2,1,0:T(8,128)(2,1)S(1)}, bf16[16,224,128]{2,1,0:T(8,128)(2,1)S(1)}, u32[]{:S(2)}, u32[]{:S(2)}) %collective-permute-start.17) | collective-permute-done | bytes 917536 | tf_op jit(solution)/shard_map/ppermute | solution.py:392
  331.3 19.5 %collective-permute-done.18.refs_7_.refs_1_ = bf16[16,224,128]{2,1,0:T(8,128)(2,1)S(1)} collective-permute-done((bf16[16,224,128]{2,1,0:T(8,128)(2,1)S(1)}, bf16[16,224,128]{2,1,0:T(8,128)(2,1)S(1)}, u32[]{:S(2)}, u32[]{:S(2)}) %collective-permute-start.18) | collective-permute-done | bytes 917536 | tf_op jit(solution)/shard_map/ppermute | solution.py:392
  351.3 5.8 %broadcast_in_dim.5.place_ref = s32[16,1024,128]{2,1,0:T(8,128)} broadcast(s32[16,1024]{1,0:T(8,128)S(1)} %get-tuple-element.26), dimensions={0,1} | broadcast | bytes 8454144 | tf_op jit(solution)/shard_map/broadcast_in_dim | solution.py:452
  357.1 17.0 %scatter_rows.1.refs_4_.onehot_ref = bf16[1024,8192]{1,0:T(8,128)(2,1)} custom-call(s32[32]{0:T(128)S(1)} %get-tuple-element.55.low.refs_0_, s32[32]{0:T(128)S(1)} %get-tuple-element.54.high.refs_1_, s32[16,1024,128]{2,1,0:T(8,128)} %broadcast_in_dim.5.place_ref), custom_call_target="tpu_custom_call" | custom-call | flops 8388608 | bytes 16777216 | tf_op jit(solution)/shard_map/scatter_rows/pallas_call | solution.py:251
  374.1 0.9 copy-done.9
  375.0 16.4 %down_and_mix.5.start = f32[1024,512]{1,0:T(8,128)} custom-call(s32[32]{0:T(128)} %copy-done.2, s32[32]{0:T(128)} %copy-done.1, s32[17]{0:T(128)} %copy-done.3, s32[1]{0:T(128)} %bitcast.5.quarter.refs_3_, bf16[1024,8192]{1,0:T(8,128)(2,1)} %scatter_rows.1.refs_4_.onehot_ref, bf16[4096,256]{1,0:T(8,128)(2,1)} %all-gather.5.cloned.1.call-done.refs_5_, ...), custom_call_target="tpu_custom_call" | custom-call | flops 4294967296 | bytes 8388608 | tf_op jit(solution)/shard_map/down_and_mix/pallas_call | solution.py:359
  391.4 3.4 all-gather.3.cloned.1.call-done.hidden
  394.9 16.9 %down_and_mix.6 = bf16[1024,512]{1,0:T(8,128)(2,1)} custom-call(s32[32]{0:T(128)} %copy-done.2, s32[32]{0:T(128)} %copy-done.1, s32[17]{0:T(128)} %copy-done.3, s32[1]{0:T(128)} %bitcast.5.quarter.refs_3_, bf16[1024,8192]{1,0:T(8,128)(2,1)} %scatter_rows.1.refs_4_.onehot_ref, bf16[4096,256]{1,0:T(8,128)(2,1)} %all-gather.3.cloned.1.call-done.hidden, ...), custom_call_target="tpu_custom_call" | custom-call | flops 4294967296 | bytes 8388608 | tf_op jit(solution)/shard_map/down_and_mix/pallas_call | solution.py:359
  411.7 1.1 slice.73
  412.8 1.0 collective-permute-start.22
  413.8 0.9 copy-done.5
  415.1 16.4 %down_and_mix.4.start = f32[1024,512]{1,0:T(8,128)} custom-call(s32[32]{0:T(128)} %copy-done.2, s32[32]{0:T(128)} %copy-done.1, s32[17]{0:T(128)} %copy-done.3, s32[1]{0:T(128)} %bitcast.5.quarter.refs_3_, bf16[1024,8192]{1,0:T(8,128)(2,1)} %scatter_rows.1.refs_4_.onehot_ref, bf16[4096,256]{1,0:T(8,128)(2,1)} %all-gather.5.cloned.1.call-done.refs_5_, ...), custom_call_target="tpu_custom_call" | custom-call | flops 4294967296 | bytes 8388608 | tf_op jit(solution)/shard_map/down_and_mix/pallas_call | solution.py:359
  431.5 17.5 %down_and_mix.7 = f32[1024,512]{1,0:T(8,128)} custom-call(s32[32]{0:T(128)} %copy-done.2, s32[32]{0:T(128)} %copy-done.1, s32[17]{0:T(128)} %copy-done.3, s32[1]{0:T(128)} %bitcast.5.quarter.refs_3_, bf16[1024,8192]{1,0:T(8,128)(2,1)} %scatter_rows.1.refs_4_.onehot_ref, bf16[4096,256]{1,0:T(8,128)(2,1)} %all-gather.3.cloned.1.call-done.hidden, ...), custom_call_target="tpu_custom_call" | custom-call | flops 4294967296 | bytes 8388608 | tf_op jit(solution)/shard_map/down_and_mix/pallas_call | solution.py:359
  449.0 1.3 slice.103
  451.2 1.0 collective-permute-done.21
  452.2 12.4 %collective-permute-done.23 = bf16[1024,224]{1,0:T(8,128)(2,1)S(1)} collective-permute-done((bf16[1024,224]{1,0:T(8,128)(2,1)S(1)}, bf16[1024,224]{1,0:T(8,128)(2,1)S(1)}, u32[]{:S(2)}, u32[]{:S(2)}) %collective-permute-start.23) | collective-permute-done | bytes 458784 | tf_op jit(solution)/shard_map/ppermute | solution.py:392
  464.7 1.4 fusion.1
  466.1 18.9 %all_to_all.10 = bf16[16,64,224]{2,1,0:T(8,128)(2,1)S(1)} all-to-all(bf16[16,64,224]{2,1,0:T(8,128)(2,1)S(1)} %bitcast.32), channel_id=1, replica_groups=mesh['parts'=2,'ep'=16,'tp'=1] {'ep'}, dimensions={0} | all-to-all | bytes 917504 | tf_op jit(solution)/shard_map/all_to_all | solution.py:468
  485.2 1.6 reshape.70
  (84 shorter events, 7.5 us)
Async XLA Ops:
  6.5 4.8 copy-start.14
  6.5 4.8 copy-start.13
  6.5 4.9 %copy-start.12 = (bf16[64,3584]{1,0:T(8,128)(2,1)S(1)}, bf16[64,3584]{1,0:T(8,128)(2,1)}, u32[]{:S(2)}) copy-start(bf16[64,3584]{1,0:T(8,128)(2,1)} %param.6) | copy-start | bytes 1376260
  10.5 27.4 %collective-permute-start.5 = (bf16[16,224,128]{2,1,0:T(8,128)(2,1)}, bf16[16,224,128]{2,1,0:T(8,128)(2,1)S(1)}, u32[]{:S(2)}, u32[]{:S(2)}) collective-permute-start(bf16[16,224,128]{2,1,0:T(8,128)(2,1)} %get-tuple-element.40), channel_id=1, source_target_pairs={{0,2},{1,3},{2,0},{3,1},{4,6},{5,7},{6,4},{7,5},{8,10},{9,11},{10,... | collective-permute-start | bytes 2752520 | tf_op jit(solution)/shard_map/ppermute | solution.py:392
  13.4 25.8 %all-to-all-start = ((bf16[16,64,256]{2,1,0:T(8,128)(2,1)}), bf16[16,64,256]{2,1,0:T(8,128)(2,1)S(1)}, u32[]{:S(2)}, u32[]{:S(2)}) async-start(bf16[16,64,256]{2,1,0:T(8,128)(2,1)} %pad_maximum_fusion.1), calls=%async_computation | async-start | bytes 1048576 | tf_op jit(solution)/shard_map/all_to_all | solution.py:408
  19.4 202.1 %reduce-scatter.3.cloned.1.call-start = ((), (), s32[]{:S(2)}) async-start(), calls=%async_computation.4 | async-start | bytes 5242880 | tf_op jit(solution)/shard_map/reduce_scatter | solution.py:441
  19.5 97.1 %collective-permute-start.11 = (bf16[16,224,128]{2,1,0:T(8,128)(2,1)}, bf16[16,224,128]{2,1,0:T(8,128)(2,1)S(1)}, u32[]{:S(2)}, u32[]{:S(2)}) collective-permute-start(bf16[16,224,128]{2,1,0:T(8,128)(2,1)} %get-tuple-element.39), channel_id=1, source_target_pairs={{0,1},{1,0},{2,3},{3,2},{4,5},{5,4},{6,7},{7,6},{8,9},{9,8},{10,11... | collective-permute-start | bytes 2752520 | tf_op jit(solution)/shard_map/ppermute | solution.py:391
  23.9 92.7 %collective-permute-start.12 = (bf16[16,224,128]{2,1,0:T(8,128)(2,1)}, bf16[16,224,128]{2,1,0:T(8,128)(2,1)S(1)}, u32[]{:S(2)}, u32[]{:S(2)}) collective-permute-start(bf16[16,224,128]{2,1,0:T(8,128)(2,1)} %get-tuple-element.35), channel_id=1, source_target_pairs={{0,1},{1,0},{2,3},{3,2},{4,5},{5,4},{6,7},{7,6},{8,9},{9,8},{10,11... | collective-permute-start | bytes 2752520 | tf_op jit(solution)/shard_map/ppermute | solution.py:391
  37.9 34.1 %collective-permute-start.6 = (bf16[16,224,128]{2,1,0:T(8,128)(2,1)}, bf16[16,224,128]{2,1,0:T(8,128)(2,1)}, u32[]{:S(2)}, u32[]{:S(2)}) collective-permute-start(bf16[16,224,128]{2,1,0:T(8,128)(2,1)} %get-tuple-element.23), channel_id=1, source_target_pairs={{0,2},{1,3},{2,0},{3,1},{4,6},{5,7},{6,4},{7,5},{8,10},{9,11},{10,... | collective-permute-start | bytes 2752520 | tf_op jit(solution)/shard_map/ppermute | solution.py:392
  39.3 4.6 collective-permute-start
  39.7 32.0 %collective-permute-start.1 = (bf16[1024,256]{1,0:T(8,128)(2,1)S(1)}, bf16[1024,256]{1,0:T(8,128)(2,1)S(1)}, u32[]{:S(2)}, u32[]{:S(2)}) collective-permute-start(bf16[1024,256]{1,0:T(8,128)(2,1)S(1)} %bitcast.26), channel_id=1, source_target_pairs={{0,2},{1,3},{2,0},{3,1},{4,6},{5,7},{6,4},{7,5},{8,10},{9,11},{10,... | collective-permute-start | bytes 1572872 | tf_op jit(solution)/shard_map/ppermute | solution.py:392
  43.8 313.2 %copy-start.1 = (s32[32]{0:T(128)}, s32[32]{0:T(128)S(1)}, u32[]{:S(2)}) copy-start(s32[32]{0:T(128)S(1)} %get-tuple-element.54.high.refs_1_) | copy-start | bytes 388
  43.8 313.2 %copy-start.2 = (s32[32]{0:T(128)}, s32[32]{0:T(128)S(1)}, u32[]{:S(2)}) copy-start(s32[32]{0:T(128)S(1)} %get-tuple-element.55.low.refs_0_) | copy-start | bytes 388
  43.9 157.8 %copy-start.3 = (s32[17]{0:T(128)}, s32[17]{0:T(128)S(1)}, u32[]{:S(2)}) copy-start(s32[17]{0:T(128)S(1)} %slice_bitcast_fusion.base.refs_2_) | copy-start | bytes 208
  43.9 72.8 %collective-permute-start.13 = (bf16[16,224,128]{2,1,0:T(8,128)(2,1)S(1)}, bf16[16,224,128]{2,1,0:T(8,128)(2,1)S(1)}, u32[]{:S(2)}, u32[]{:S(2)}) collective-permute-start(bf16[16,224,128]{2,1,0:T(8,128)(2,1)S(1)} %collective-permute-done.5.refs_4_), channel_id=1, source_target_pairs={{0,16},{16,0},{1,17},{17,1},{2,18},{18,2},{3,19},{19,3},{4,20},{20... | collective-permute-start | bytes 2752520 | tf_op jit(solution)/shard_map/ppermute | solution.py:393
  71.7 29.8 %collective-permute-start.2 = (bf16[1024,256]{1,0:T(8,128)(2,1)S(1)}, bf16[1024,256]{1,0:T(8,128)(2,1)S(1)}, u32[]{:S(2)}, u32[]{:S(2)}) collective-permute-start(bf16[1024,256]{1,0:T(8,128)(2,1)S(1)} %collective-permute-done.1.refs_0_), channel_id=1, source_target_pairs={{0,1},{1,0},{2,3},{3,2},{4,5},{5,4},{6,7},{7,6},{8,9},{9,8},{10,11... | collective-permute-start | bytes 1572872 | tf_op jit(solution)/shard_map/ppermute | solution.py:391
  72.0 44.6 %collective-permute-start.14 = (bf16[16,224,128]{2,1,0:T(8,128)(2,1)}, bf16[16,224,128]{2,1,0:T(8,128)(2,1)S(1)}, u32[]{:S(2)}, u32[]{:S(2)}) collective-permute-start(bf16[16,224,128]{2,1,0:T(8,128)(2,1)} %collective-permute-done.6.refs_5_), channel_id=1, source_target_pairs={{0,16},{16,0},{1,17},{17,1},{2,18},{18,2},{3,19},{19,3},{4,20},{20... | collective-permute-start | bytes 2752520 | tf_op jit(solution)/shard_map/ppermute | solution.py:393
  99.3 2.1 copy-start
  136.6 1.2 copy-start.11
  136.6 1.9 copy-start.10
  136.6 162.9 %reduce-scatter.5.cloned.1.call-start = ((), (), s32[]{:S(2)}) async-start(), calls=%async_computation.5 | async-start | bytes 5242880 | tf_op jit(solution)/shard_map/reduce_scatter | solution.py:441
  136.7 23.3 %collective-permute-start.8 = (bf16[16,224,128]{2,1,0:T(8,128)(2,1)}, bf16[16,224,128]{2,1,0:T(8,128)(2,1)S(1)}, u32[]{:S(2)}, u32[]{:S(2)}) collective-permute-start(bf16[16,224,128]{2,1,0:T(8,128)(2,1)} %get-tuple-element.25), channel_id=1, source_target_pairs={{0,2},{1,3},{2,0},{3,1},{4,6},{5,7},{6,4},{7,5},{8,10},{9,11},{10,... | collective-permute-start | bytes 2752520 | tf_op jit(solution)/shard_map/ppermute | solution.py:392
  137.8 41.4 %collective-permute-start.7 = (bf16[16,224,128]{2,1,0:T(8,128)(2,1)S(1)}, bf16[16,224,128]{2,1,0:T(8,128)(2,1)S(1)}, u32[]{:S(2)}, u32[]{:S(2)}) collective-permute-start(bf16[16,224,128]{2,1,0:T(8,128)(2,1)S(1)} %copy-done.11), channel_id=1, source_target_pairs={{0,2},{1,3},{2,0},{3,1},{4,6},{5,7},{6,4},{7,5},{8,10},{9,11},{10,... | collective-permute-start | bytes 2752520 | tf_op jit(solution)/shard_map/ppermute | solution.py:392
  138.5 41.2 %collective-permute-start.3 = (bf16[16,224,128]{2,1,0:T(8,128)(2,1)S(1)}, bf16[16,224,128]{2,1,0:T(8,128)(2,1)S(1)}, u32[]{:S(2)}, u32[]{:S(2)}) collective-permute-start(bf16[16,224,128]{2,1,0:T(8,128)(2,1)S(1)} %copy-done.10), channel_id=1, source_target_pairs={{0,1},{1,0},{2,3},{3,2},{4,5},{5,4},{6,7},{7,6},{8,9},{9,8},{10,11... | collective-permute-start | bytes 2752520 | tf_op jit(solution)/shard_map/ppermute | solution.py:391
  138.6 41.0 %collective-permute-start.4 = (bf16[16,224,128]{2,1,0:T(8,128)(2,1)}, bf16[16,224,128]{2,1,0:T(8,128)(2,1)S(1)}, u32[]{:S(2)}, u32[]{:S(2)}) collective-permute-start(bf16[16,224,128]{2,1,0:T(8,128)(2,1)} %get-tuple-element.38), channel_id=1, source_target_pairs={{0,1},{1,0},{2,3},{3,2},{4,5},{5,4},{6,7},{7,6},{8,9},{9,8},{10,11... | collective-permute-start | bytes 2752520 | tf_op jit(solution)/shard_map/ppermute | solution.py:391
  159.9 21.7 %collective-permute-start.10 = (bf16[16,224,128]{2,1,0:T(8,128)(2,1)S(1)}, bf16[16,224,128]{2,1,0:T(8,128)(2,1)S(1)}, u32[]{:S(2)}, u32[]{:S(2)}) collective-permute-start(bf16[16,224,128]{2,1,0:T(8,128)(2,1)S(1)} %collective-permute-done.8.refs_5_), channel_id=1, source_target_pairs={{0,16},{16,0},{1,17},{17,1},{2,18},{18,2},{3,19},{19,3},{4,20},{20... | collective-permute-start | bytes 2752520 | tf_op jit(solution)/shard_map/ppermute | solution.py:393
  179.1 22.5 %collective-permute-start.9 = (bf16[16,224,128]{2,1,0:T(8,128)(2,1)S(1)}, bf16[16,224,128]{2,1,0:T(8,128)(2,1)S(1)}, u32[]{:S(2)}, u32[]{:S(2)}) collective-permute-start(bf16[16,224,128]{2,1,0:T(8,128)(2,1)S(1)} %collective-permute-done.7.refs_4_), channel_id=1, source_target_pairs={{0,16},{16,0},{1,17},{17,1},{2,18},{18,2},{3,19},{19,3},{4,20},{20... | collective-permute-start | bytes 2752520 | tf_op jit(solution)/shard_map/ppermute | solution.py:393
  221.5 153.6 %all-gather.5.cloned.1.call-start = ((), (), s32[]{:S(2)}) async-start(), calls=%async_computation.7 | async-start | bytes 2621440 | tf_op jit(solution)/shard_map/all_gather | solution.py:447
  304.0 90.8 %all-gather.3.cloned.1.call-start = ((), (), s32[]{:S(2)}) async-start(), calls=%async_computation.6 | async-start | bytes 2621440 | tf_op jit(solution)/shard_map/all_gather | solution.py:447
  308.2 23.0 %collective-permute-start.17 = (bf16[16,224,128]{2,1,0:T(8,128)(2,1)S(1)}, bf16[16,224,128]{2,1,0:T(8,128)(2,1)S(1)}, u32[]{:S(2)}, u32[]{:S(2)}) collective-permute-start(bf16[16,224,128]{2,1,0:T(8,128)(2,1)S(1)} %get-tuple-element.28), channel_id=1, source_target_pairs={{0,2},{1,3},{2,0},{3,1},{4,6},{5,7},{6,4},{7,5},{8,10},{9,11},{10,... | collective-permute-start | bytes 2752520 | tf_op jit(solution)/shard_map/ppermute | solution.py:392
  309.0 41.8 %collective-permute-start.18 = (bf16[16,224,128]{2,1,0:T(8,128)(2,1)S(1)}, bf16[16,224,128]{2,1,0:T(8,128)(2,1)S(1)}, u32[]{:S(2)}, u32[]{:S(2)}) collective-permute-start(bf16[16,224,128]{2,1,0:T(8,128)(2,1)S(1)} %get-tuple-element.29), channel_id=1, source_target_pairs={{0,2},{1,3},{2,0},{3,1},{4,6},{5,7},{6,4},{7,5},{8,10},{9,11},{10,... | collective-permute-start | bytes 2752520 | tf_op jit(solution)/shard_map/ppermute | solution.py:392
  331.3 25.8 %copy-start.6 = (bf16[16,224,128]{2,1,0:T(8,128)(2,1)}, bf16[16,224,128]{2,1,0:T(8,128)(2,1)S(1)}, u32[]{:S(2)}) copy-start(bf16[16,224,128]{2,1,0:T(8,128)(2,1)S(1)} %collective-permute-done.17.refs_6_.refs_0_) | copy-start | bytes 2752516
  331.3 42.8 %collective-permute-start.19 = (bf16[16,224,128]{2,1,0:T(8,128)(2,1)S(1)}, bf16[16,224,128]{2,1,0:T(8,128)(2,1)S(1)}, u32[]{:S(2)}, u32[]{:S(2)}) collective-permute-start(bf16[16,224,128]{2,1,0:T(8,128)(2,1)S(1)} %collective-permute-done.17.refs_6_.refs_0_), channel_id=1, source_target_pairs={{0,16},{16,0},{1,17},{17,1},{2,18},{18,2},{3,19},{19,3},{4,20},{20... | collective-permute-start | bytes 2752520 | tf_op jit(solution)/shard_map/ppermute | solution.py:393
  350.8 6.3 %copy-start.8 = (bf16[16,224,128]{2,1,0:T(8,128)(2,1)}, bf16[16,224,128]{2,1,0:T(8,128)(2,1)S(1)}, u32[]{:S(2)}) copy-start(bf16[16,224,128]{2,1,0:T(8,128)(2,1)S(1)} %collective-permute-done.18.refs_7_.refs_1_) | copy-start | bytes 2752516
  350.8 24.2 %collective-permute-start.20 = (bf16[16,224,128]{2,1,0:T(8,128)(2,1)S(1)}, bf16[16,224,128]{2,1,0:T(8,128)(2,1)}, u32[]{:S(2)}, u32[]{:S(2)}) collective-permute-start(bf16[16,224,128]{2,1,0:T(8,128)(2,1)S(1)} %collective-permute-done.18.refs_7_.refs_1_), channel_id=1, source_target_pairs={{0,16},{16,0},{1,17},{17,1},{2,18},{18,2},{3,19},{19,3},{4,20},{20... | collective-permute-start | bytes 2752520 | tf_op jit(solution)/shard_map/ppermute | solution.py:393
  350.8 63.0 %collective-permute-start.15 = (bf16[16,224,128]{2,1,0:T(8,128)(2,1)}, bf16[16,224,128]{2,1,0:T(8,128)(2,1)S(1)}, u32[]{:S(2)}, u32[]{:S(2)}) collective-permute-start(bf16[16,224,128]{2,1,0:T(8,128)(2,1)} %get-tuple-element.33), channel_id=1, source_target_pairs={{0,1},{1,0},{2,3},{3,2},{4,5},{5,4},{6,7},{7,6},{8,9},{9,8},{10,11... | collective-permute-start | bytes 2752520 | tf_op jit(solution)/shard_map/ppermute | solution.py:391
  351.2 62.6 %collective-permute-start.16 = (bf16[16,224,128]{2,1,0:T(8,128)(2,1)}, bf16[16,224,128]{2,1,0:T(8,128)(2,1)S(1)}, u32[]{:S(2)}, u32[]{:S(2)}) collective-permute-start(bf16[16,224,128]{2,1,0:T(8,128)(2,1)} %get-tuple-element.32), channel_id=1, source_target_pairs={{0,1},{1,0},{2,3},{3,2},{4,5},{5,4},{6,7},{7,6},{8,9},{9,8},{10,11... | collective-permute-start | bytes 2752520 | tf_op jit(solution)/shard_map/ppermute | solution.py:391
  374.1 0.9 copy-start.9
  412.8 37.5 %collective-permute-start.22 = (bf16[1024,224]{1,0:T(8,128)(2,1)S(1)}, bf16[1024,224]{1,0:T(8,128)(2,1)S(1)}, u32[]{:S(2)}, u32[]{:S(2)}) collective-permute-start(bf16[1024,224]{1,0:T(8,128)(2,1)S(1)} %slice.73), channel_id=1, source_target_pairs={{0,1},{1,0},{2,3},{3,2},{4,5},{5,4},{6,7},{7,6},{8,9},{9,8},{10,11... | collective-permute-start | bytes 1376264 | tf_op jit(solution)/shard_map/ppermute | solution.py:391
  413.8 1.0 copy-start.5
  413.8 1.2 copy-start.7
  431.5 18.8 %copy-start.4 = (bf16[1024,512]{1,0:T(8,128)(2,1)S(1)}, bf16[1024,512]{1,0:T(8,128)(2,1)}, u32[]{:S(2)}) copy-start(bf16[1024,512]{1,0:T(8,128)(2,1)} %down_and_mix.6) | copy-start | bytes 3145732
  450.3 2.0 collective-permute-start.21
  450.5 14.2 %collective-permute-start.23 = (bf16[1024,224]{1,0:T(8,128)(2,1)S(1)}, bf16[1024,224]{1,0:T(8,128)(2,1)S(1)}, u32[]{:S(2)}, u32[]{:S(2)}) collective-permute-start(bf16[1024,224]{1,0:T(8,128)(2,1)S(1)} %add_convert_fusion), channel_id=1, source_target_pairs={{0,2},{1,3},{2,0},{3,1},{4,6},{5,7},{6,4},{7,5},{8,10},{9,11},{10,... | collective-permute-start | bytes 1376264 | tf_op jit(solution)/shard_map/ppermute | solution.py:392
Sparse Core Ops, SparseCore 0:
  136.7 77.9 reduce-scatter.2
  221.6 77.8 reduce-scatter.4
  304.2 44.5 all-gather.4
  350.2 44.6 all-gather.2

commit v5 on v4

--- a/solution.py
+++ b/solution.py
@@ -407,8 +407,7 @@
     )
     own = lax.all_to_all(parcels, "ep", split_axis=0, concat_axis=0, tiled=True)
     own = own.reshape(size * count, LANES)
-    far = to_cross(own)
-    slices = [own, to_twin(own), far, to_twin(far)]
+    far, near = to_cross(own), [own, to_twin(own)]
     place, across, gates, base = order_of(own, width, picks, experts)
     base = base[0, : experts + 1]
     spans = spans_of(base, rows)
@@ -417,54 +416,63 @@
     def cut(w, q, f):
         return lax.dynamic_slice_in_dim(w, q * quarter + f * UNITS, UNITS, 2)
 
-    last = ()
+    def after(value, *others):
+        return lax.optimization_barrier((value, *others))[0]
+
+    near_rows, scale, onehot = sort_rows(spans, base, across, gates, near, rows, experts)
+    far = after(far, near_rows)
+    far_rows = sort_more(onehot, [far, to_twin(far)])
+    scale = lax.dynamic_slice_in_dim(scale, (me // 4) * (rows // places), rows // places, 0)
+
     held, crossed = [], []
     for n, (f, w) in enumerate(
         ((0, w_gate), (0, w_up), (1, w_gate), (1, w_up), (0, w_down), (1, w_down))
     ):
         piece = cut(w, cross_quarter, f)
         if n:
-            last = (crossed[0],) if n == 1 else (far, crossed[1], crossed[n // 2 * 2 - 1])
-            piece = lax.optimization_barrier((piece, *last))[0]
+            piece = after(piece, crossed[n - 1] if n < 4 else crossed[3])
+        if n == 2:
+            piece = after(piece, far)
         crossed.append(to_cross(piece))
         held.append((to_twin(cut(w, twin_quarter, f)), crossed[n], to_plane(crossed[n])))
     weave = lambda pair: [piece for both in zip(*pair) for piece in both]
 
-    near_rows, scale, onehot = sort_rows(spans, base, across, gates, slices[:2], rows, experts)
-    far_rows = sort_more(onehot, slices[2:])
-    scale = lax.dynamic_slice_in_dim(scale, (me // 4) * (rows // places), rows // places, 0)
-    units = []
+    units, later = [], crossed[2]
     for f in range(2):
         pieces = weave(held[2 * f : 2 * f + 2])
-        sums = partial_sums(f, spans, base, which, near_rows, far_rows, w_gate, w_up, pieces)
-        later = sums
+        far_rows = after(far_rows, later)
+        later = partial_sums(f, spans, base, which, near_rows, far_rows, w_gate, w_up, pieces)
         sums = lax.psum_scatter(
-            sums, "ep", scatter_dimension=0, axis_index_groups=line, tiled=True
+            later, "ep", scatter_dimension=0, axis_index_groups=line, tiled=True
         ).astype(F32)
         units.append((jax.nn.silu(sums[:, :UNITS]) * sums[:, UNITS:] * scale).astype(BF16))
+
+    place = jnp.broadcast_to(
+        after(across[:experts], later)[:, :, None], (experts, size * count, 128)
+    )
+    columns = scatter_rows(spans, place, rows)
+    units, columns, pieces = lax.optimization_barrier((units, columns, weave(held[4:])))
     units = jnp.concatenate(units, axis=1).reshape(-1, BLOCK, 2 * UNITS)
-    hidden = [
+    first, second = (
         lax.all_gather(units[half], "ep", axis=0, axis_index_groups=line, tiled=True)
         for half in range(2)
-    ]
-
-    across = lax.optimization_barrier((across[:experts], later))[0]
-    place = jnp.broadcast_to(across[:, :, None], (experts, size * count, 128))
-    columns = scatter_rows(spans, place, rows)
-    near_weights, far_weights = weave(held[4:])[:2], weave(held[4:])[2:]
-    near_weights = [w_down] + near_weights
-    mix = lambda near, half, start, dtype: down_and_mix(
-        near, half, spans, base, which, columns, hidden[half], start,
-        near_weights if near else far_weights, 2, dtype,
-    )
-    far = mix(False, 1, mix(False, 0, None, F32), BF16)
-    near = mix(True, 0, None, F32)
-    near = mix(True, 1, lax.optimization_barrier((near, far))[0], F32)
+    )
+    far_mix = lambda half, hidden, start, dtype: down_and_mix(
+        False, half, spans, base, which, columns, hidden, start, pieces[2:], 2, dtype
+    )
+    near_mix = lambda half, hidden, start, dtype: down_and_mix(
+        True, half, spans, base, which, columns, hidden, start, [w_down] + pieces[:2], 2, dtype
+    )
+    far, near = far_mix(0, first, None, F32), near_mix(0, first, None, F32)
+    second, far, near = lax.optimization_barrier((second, far, near))
+    far = far_mix(1, second, far, BF16)
     far, far_twin = far[:, :width], far[:, LANES : LANES + width]
     far = (far.astype(F32) + to_twin(far_twin).astype(F32)).astype(BF16)
-    far = to_cross(far).astype(F32)
+    near, far = lax.optimization_barrier((near, far))
+    far = to_cross(far)
+    near = near_mix(1, second, near, F32)
     twin = to_twin(near[:, LANES : LANES + width].astype(BF16)).astype(F32)
-    mixed = (near[:, :width] + twin + far).astype(BF16)
+    mixed = (near[:, :width] + twin + far.astype(F32)).astype(BF16)
     mixed = lax.all_to_all(
         mixed.reshape(size, count, width), "ep", split_axis=0, concat_axis=0, tiled=True
     )

time: 496 us -> 483 us (0.974)
  waiting for transfers between devices: 239 us -> 222 us
    reduce_scatter x2, waiting for transfers between devices: 76.6 us -> 22.8 us  [fixed_weights(): lax.psum_scatter(later, 'ep', scatter_dimension=0, axis_index_groups=line...]
    all_gather x2, waiting for transfers between devices: 3.43 us -> 56.8 us  [fixed_weights(): lax.all_gather(units[half], 'ep', axis=0, axis_index_groups=line, tiled=T...]
    ppermute x8, waiting for transfers between devices: 134 us -> 97.5 us  [fixed_weights(): to_cross = lambda value: lax.ppermute(value, ('parts', 'ep'), cross)]
    ppermute x6, waiting for transfers between devices: 22 us -> 42 us  [fixed_weights(): to_plane = lambda value: lax.ppermute(value, 'parts', [(0, 1), (1, 0)])]
  transfers between devices with their start and end apart: 29 -> 29, of which waited for: 13 -> 15; matrix products, arithmetic and copies ran while one was open for 4% -> 5% of each run, Pallas kernels for 30% -> 24%
where the time goes in v5:
time: 483 us; the launch traced here: 479 us
  waiting for transfers between devices  222 us (46%)
  Pallas kernels  169 us (35%)
  local copies, waits for them, and re-layouts  26.2 us (5%)
  starting transfers between devices  19.9 us (4%)
  blocking collectives  18.8 us (4%)
  between operations  13.4 us (3%)
  other arithmetic  9.73 us (2%)
    ppermute x8, waiting for transfers between devices, fixed_weights(): to_cross = lambda value: lax.ppermute(value, ('parts', 'ep'), cross)  97.5 us
    pallas_call x4, Pallas kernels, down_and_mix(): pl.pallas_call(kernel, grid_spec=pltpu.PrefetchScalarGridSpec(num_scalar_...  67.1 us
    all_gather x2, waiting for transfers between devices, fixed_weights(): lax.all_gather(units[half], 'ep', axis=0, axis_index_groups=line, tiled=T...  56.8 us
    ppermute x6, waiting for transfers between devices, fixed_weights(): to_plane = lambda value: lax.ppermute(value, 'parts', [(0, 1), (1, 0)])  42 us
    pallas_call x2, Pallas kernels, partial_sums(): pl.pallas_call(partial_kernel, grid_spec=pltpu.PrefetchScalarGridSpec(num...  39.2 us
    pallas_call x1, Pallas kernels, sort_rows(): pl.pallas_call(functools.partial(sort_kernel, experts), grid_spec=pltpu.P...  27.3 us
    reduce_scatter x2, waiting for transfers between devices, fixed_weights(): lax.psum_scatter(later, 'ep', scatter_dimension=0, axis_index_groups=line...  22.8 us
    all_to_all x1, blocking collectives, fixed_weights(): lax.all_to_all(mixed.reshape(size, count, width), 'ep', split_axis=0, con...  18.8 us
  transfers between devices with their start and end apart: 29, of which 15 were waited for; matrix products, arithmetic and copies ran while one was open for 5% of the time, Pallas kernels for 24%

profile of v5, /device:TPU:15, one launch (start us, length us, event | category | flops | bytes accessed | tf_op | source)
XLA Modules:
  0.0 478.6 jit_solution(13190380565642697292)
XLA Ops:
  8.0 1.8 reshape.65
  10.0 1.0 pad_maximum_fusion
  11.0 6.6 %all-to-all-start = ((bf16[16,64,256]{2,1,0:T(8,128)(2,1)}), bf16[16,64,256]{2,1,0:T(8,128)(2,1)S(1)}, u32[]{:S(2)}, u32[]{:S(2)}) async-start(bf16[16,64,256]{2,1,0:T(8,128)(2,1)} %pad_maximum_fusion), calls=%async_computation | async-start | bytes 1048576 | tf_op jit(solution)/shard_map/all_to_all | solution.py:408
  17.6 3.8 constant_dynamic-slice_fusion.2
  22.9 2.2 constant_dynamic-slice_fusion
  25.1 21.5 %collective-permute-done.3.refs_4_ = bf16[16,224,128]{2,1,0:T(8,128)(2,1)S(1)} collective-permute-done((bf16[16,224,128]{2,1,0:T(8,128)(2,1)S(1)}, bf16[16,224,128]{2,1,0:T(8,128)(2,1)S(1)}, u32[]{:S(2)}, u32[]{:S(2)}) %collective-permute-start.3) | collective-permute-done | bytes 917536 | tf_op jit(solution)/shard_map/ppermute | solution.py:392
  47.4 3.6 order.1
  51.1 1.2 collective-permute-start.1
  52.9 27.3 %sort_rows.1 = (bf16[8192,512]{1,0:T(8,128)(2,1)}, f32[8192,128]{1,0:T(8,128)S(1)}, bf16[8192,1024]{1,0:T(8,128)(2,1)}) custom-call(s32[32]{0:T(128)S(1)} %get-tuple-element.89.low.refs_0_, s32[32]{0:T(128)S(1)} %get-tuple-element.88.high.refs_1_, s32[17]{0:T(128)S(1)} %slice_bitcast_fusion.base.refs_2_, s32[16,8,128]{2,1,0:T(8,128)S(1)} %bitcast.29, ...), custom_call_target="tpu_custom_call" | custom-call | flops 8589934592 | bytes 33554432 | tf_op jit(solution)/shard_map/sort_rows/pallas_call | solution.py:184
  80.2 2.0 copy-done
  82.4 1.2 collective-permute-start.5
  84.4 1.2 collective-permute-start.9
  85.6 15.3 %sort_more.1.far_ref = bf16[8192,512]{1,0:T(8,128)(2,1)} custom-call(bf16[8192,1024]{1,0:T(8,128)(2,1)} %get-tuple-element.39.onehot_ref, bf16[1024,256]{1,0:T(8,128)(2,1)S(1)} %collective-permute-done.1.refs_0_, bf16[1024,256]{1,0:T(8,128)(2,1)S(1)} %collective-permute-done.2.refs_1_), custom_call_target="tpu_custom_call" | custom-call | flops 8589934592 | bytes 33554432 | tf_op jit(solution)/shard_map/sort_more/pallas_call | solution.py:221
  100.9 4.1 collective-permute-done.5.refs_4_
  106.0 19.7 %collective-permute-done.9.refs_7_ = bf16[16,224,128]{2,1,0:T(8,128)(2,1)S(1)} collective-permute-done((bf16[16,224,128]{2,1,0:T(8,128)(2,1)S(1)}, bf16[16,224,128]{2,1,0:T(8,128)(2,1)S(1)}, u32[]{:S(2)}, u32[]{:S(2)}) %collective-permute-start.9) | collective-permute-done | bytes 917536 | tf_op jit(solution)/shard_map/ppermute | solution.py:393
  125.6 19.6 %partial_sums.2 = bf16[8192,256]{1,0:T(8,128)(2,1)} custom-call(s32[32]{0:T(128)S(1)} %get-tuple-element.89.low.refs_0_, s32[32]{0:T(128)S(1)} %get-tuple-element.88.high.refs_1_, s32[17]{0:T(128)S(1)} %slice_bitcast_fusion.base.refs_2_, s32[1]{0:T(128)} %bitcast.5.quarter.refs_3_, bf16[8192,512]{1,0:T(8,128)(2,1)} %get-tuple-element.38.near_ref, ...), custom_call_target="tpu_custom_call" | custom-call | flops 4294967296 | bytes 16777216 | tf_op jit(solution)/shard_map/partial_sums/pallas_call | solution.py:294
  145.3 1.4 collective-permute-start.12
  147.4 21.0 %collective-permute-done.12.refs_5_ = bf16[16,224,128]{2,1,0:T(8,128)(2,1)S(1)} collective-permute-done((bf16[16,224,128]{2,1,0:T(8,128)(2,1)}, bf16[16,224,128]{2,1,0:T(8,128)(2,1)S(1)}, u32[]{:S(2)}, u32[]{:S(2)}) %collective-permute-start.12) | collective-permute-done | bytes 917536 | tf_op jit(solution)/shard_map/ppermute | solution.py:392
  168.4 0.9 collective-permute-done.13.refs_6_
  169.3 20.5 %collective-permute-done.14.refs_7_ = bf16[16,224,128]{2,1,0:T(8,128)(2,1)S(1)} collective-permute-done((bf16[16,224,128]{2,1,0:T(8,128)(2,1)S(1)}, bf16[16,224,128]{2,1,0:T(8,128)(2,1)S(1)}, u32[]{:S(2)}, u32[]{:S(2)}) %collective-permute-start.14) | collective-permute-done | bytes 917536 | tf_op jit(solution)/shard_map/ppermute | solution.py:393
  189.8 19.6 %partial_sums.3 = bf16[8192,256]{1,0:T(8,128)(2,1)} custom-call(s32[32]{0:T(128)S(1)} %get-tuple-element.89.low.refs_0_, s32[32]{0:T(128)S(1)} %get-tuple-element.88.high.refs_1_, s32[17]{0:T(128)S(1)} %slice_bitcast_fusion.base.refs_2_, s32[1]{0:T(128)} %bitcast.5.quarter.refs_3_, bf16[8192,512]{1,0:T(8,128)(2,1)} %get-tuple-element.38.near_ref, ...), custom_call_target="tpu_custom_call" | custom-call | flops 4294967296 | bytes 16777216 | tf_op jit(solution)/shard_map/partial_sums/pallas_call | solution.py:294
  209.7 3.8 dynamic-slice_bitcast_fusion
  213.5 1.8 collective-permute-start.17
  215.3 1.3 collective-permute-start.15
  216.6 19.4 %collective-permute-done.17.refs_6_.refs_0_ = bf16[16,224,128]{2,1,0:T(8,128)(2,1)} collective-permute-done((bf16[16,224,128]{2,1,0:T(8,128)(2,1)S(1)}, bf16[16,224,128]{2,1,0:T(8,128)(2,1)}, u32[]{:S(2)}, u32[]{:S(2)}) %collective-permute-start.17) | collective-permute-done | bytes 917536 | tf_op jit(solution)/shard_map/ppermute | solution.py:392
  236.0 19.7 %collective-permute-done.18.refs_7_.refs_1_ = bf16[16,224,128]{2,1,0:T(8,128)(2,1)} collective-permute-done((bf16[16,224,128]{2,1,0:T(8,128)(2,1)S(1)}, bf16[16,224,128]{2,1,0:T(8,128)(2,1)}, u32[]{:S(2)}, u32[]{:S(2)}) %collective-permute-start.18) | collective-permute-done | bytes 917536 | tf_op jit(solution)/shard_map/ppermute | solution.py:392
  255.7 5.7 %broadcast_in_dim.5.place_ref = s32[16,1024,128]{2,1,0:T(8,128)} broadcast(s32[16,1024]{1,0:T(8,128)S(1)} %get-tuple-element.48), dimensions={0,1} | broadcast | bytes 8454144 | tf_op jit(solution)/shard_map/broadcast_in_dim | solution.py:450
  261.4 16.4 %scatter_rows.1.refs_4_.onehot_ref = bf16[1024,8192]{1,0:T(8,128)(2,1)} custom-call(s32[32]{0:T(128)S(1)} %get-tuple-element.89.low.refs_0_, s32[32]{0:T(128)S(1)} %get-tuple-element.88.high.refs_1_, s32[16,1024,128]{2,1,0:T(8,128)} %broadcast_in_dim.5.place_ref), custom_call_target="tpu_custom_call" | custom-call | flops 8388608 | bytes 16777216 | tf_op jit(solution)/shard_map/scatter_rows/pallas_call | solution.py:251
  277.8 1.4 convert_element_type.48
  279.2 22.8 %reduce-scatter.5.cloned.1.call-done = bf16[2048,256]{1,0:T(8,128)(2,1)} async-done(((bf16[8192,256]{1,0:T(8,128)(2,1)}), bf16[2048,256]{1,0:T(8,128)(2,1)}) %reduce-scatter.5.cloned.1.call-update) | async-done | bytes 1048592 | tf_op jit(solution)/shard_map/reduce_scatter | solution.py:445
  302.0 1.4 convert_element_type.50
  303.4 2.0 fusion.3
  305.7 1.1 fusion.8
  307.3 44.1 %all-gather.5.cloned.1.call-done.refs_5_ = bf16[4096,256]{1,0:T(8,128)(2,1)} async-done(((bf16[1024,256]{1,0:T(8,128)(2,1)}), bf16[4096,256]{1,0:T(8,128)(2,1)}) %all-gather.5.cloned.1.call-update) | async-done | bytes 2097168 | tf_op jit(solution)/shard_map/all_gather | solution.py:457
  351.4 16.7 %down_and_mix.5.start = f32[1024,512]{1,0:T(8,128)} custom-call(s32[32]{0:T(128)} %copy-done.2, s32[32]{0:T(128)} %copy-done.1, s32[17]{0:T(128)} %copy-done.3, s32[1]{0:T(128)} %bitcast.5.quarter.refs_3_, bf16[1024,8192]{1,0:T(8,128)(2,1)} %scatter_rows.1.refs_4_.onehot_ref, bf16[4096,256]{1,0:T(8,128)(2,1)} %all-gather.5.cloned.1.call-done.refs_5_, ...), custom_call_target="tpu_custom_call" | custom-call | flops 4294967296 | bytes 8388608 | tf_op jit(solution)/shard_map/down_and_mix/pallas_call | solution.py:359
  368.1 16.7 %down_and_mix.4.start = f32[1024,512]{1,0:T(8,128)} custom-call(s32[32]{0:T(128)} %copy-done.2, s32[32]{0:T(128)} %copy-done.1, s32[17]{0:T(128)} %copy-done.3, s32[1]{0:T(128)} %bitcast.5.quarter.refs_3_, bf16[1024,8192]{1,0:T(8,128)(2,1)} %scatter_rows.1.refs_4_.onehot_ref, bf16[4096,256]{1,0:T(8,128)(2,1)} %all-gather.5.cloned.1.call-done.refs_5_, ...), custom_call_target="tpu_custom_call" | custom-call | flops 4294967296 | bytes 8388608 | tf_op jit(solution)/shard_map/down_and_mix/pallas_call | solution.py:359
  384.9 12.7 %all-gather.3.cloned.1.call-done.hidden = bf16[4096,256]{1,0:T(8,128)(2,1)} async-done(((bf16[1024,256]{1,0:T(8,128)(2,1)}), bf16[4096,256]{1,0:T(8,128)(2,1)}) %all-gather.3.cloned.1.call-update) | async-done | bytes 2097168 | tf_op jit(solution)/shard_map/all_gather | solution.py:457
  397.5 16.6 %down_and_mix.6 = bf16[1024,512]{1,0:T(8,128)(2,1)} custom-call(s32[32]{0:T(128)} %copy-done.2, s32[32]{0:T(128)} %copy-done.1, s32[17]{0:T(128)} %copy-done.3, s32[1]{0:T(128)} %bitcast.5.quarter.refs_3_, bf16[1024,8192]{1,0:T(8,128)(2,1)} %scatter_rows.1.refs_4_.onehot_ref, bf16[4096,256]{1,0:T(8,128)(2,1)} %all-gather.3.cloned.1.call-done.hidden, ...), custom_call_target="tpu_custom_call" | custom-call | flops 4294967296 | bytes 8388608 | tf_op jit(solution)/shard_map/down_and_mix/pallas_call | solution.py:359
  414.2 1.1 slice.71
  415.2 1.0 collective-permute-start.21
  416.2 1.5 collective-permute-done.21
  417.8 1.2 add_convert_fusion
  418.9 17.1 %down_and_mix.7 = f32[1024,512]{1,0:T(8,128)} custom-call(s32[32]{0:T(128)} %copy-done.2, s32[32]{0:T(128)} %copy-done.1, s32[17]{0:T(128)} %copy-done.3, s32[1]{0:T(128)} %bitcast.5.quarter.refs_3_, bf16[1024,8192]{1,0:T(8,128)(2,1)} %scatter_rows.1.refs_4_.onehot_ref, bf16[4096,256]{1,0:T(8,128)(2,1)} %all-gather.3.cloned.1.call-done.hidden, ...), custom_call_target="tpu_custom_call" | custom-call | flops 4294967296 | bytes 8388608 | tf_op jit(solution)/shard_map/down_and_mix/pallas_call | solution.py:359
  436.6 1.3 slice.97
  438.1 11.9 %collective-permute-done.23 = bf16[1024,224]{1,0:T(8,128)(2,1)S(1)} collective-permute-done((bf16[1024,224]{1,0:T(8,128)(2,1)S(1)}, bf16[1024,224]{1,0:T(8,128)(2,1)S(1)}, u32[]{:S(2)}, u32[]{:S(2)}) %collective-permute-start.23) | collective-permute-done | bytes 458784 | tf_op jit(solution)/shard_map/ppermute | solution.py:392
  450.0 1.4 fusion.1
  451.3 18.8 %all_to_all.10 = bf16[16,64,224]{2,1,0:T(8,128)(2,1)S(1)} all-to-all(bf16[16,64,224]{2,1,0:T(8,128)(2,1)S(1)} %bitcast.32), channel_id=1, replica_groups=mesh['parts'=2,'ep'=16,'tp'=1] {'ep'}, dimensions={0} | all-to-all | bytes 917504 | tf_op jit(solution)/shard_map/all_to_all | solution.py:476
  470.4 1.6 reshape.70
  (74 shorter events, 9.3 us)
Async XLA Ops:
  11.0 36.4 %all-to-all-start = ((bf16[16,64,256]{2,1,0:T(8,128)(2,1)}), bf16[16,64,256]{2,1,0:T(8,128)(2,1)S(1)}, u32[]{:S(2)}, u32[]{:S(2)}) async-start(bf16[16,64,256]{2,1,0:T(8,128)(2,1)} %pad_maximum_fusion), calls=%async_computation | async-start | bytes 1048576 | tf_op jit(solution)/shard_map/all_to_all | solution.py:408
  17.5 260.3 %reduce-scatter.3.cloned.1.call-start = ((), (), s32[]{:S(2)}) async-start(), calls=%async_computation.4 | async-start | bytes 5242880 | tf_op jit(solution)/shard_map/reduce_scatter | solution.py:445
  17.6 5.2 %copy-start.4 = (bf16[16,224,1024]{2,1,0:T(8,128)(2,1)S(1)}, bf16[16,224,1024]{2,1,0:T(8,128)(2,1)}, u32[]{:S(2)}) copy-start(bf16[16,224,1024]{2,1,0:T(8,128)(2,1)} %refs_1_.3) | copy-start | bytes 22020100
  21.4 25.1 %collective-permute-start.3 = (bf16[16,224,128]{2,1,0:T(8,128)(2,1)S(1)}, bf16[16,224,128]{2,1,0:T(8,128)(2,1)S(1)}, u32[]{:S(2)}, u32[]{:S(2)}) collective-permute-start(bf16[16,224,128]{2,1,0:T(8,128)(2,1)S(1)} %get-tuple-element.75), channel_id=1, source_target_pairs={{0,2},{1,3},{2,0},{3,1},{4,6},{5,7},{6,4},{7,5},{8,10},{9,11},{10,... | collective-permute-start | bytes 2752520 | tf_op jit(solution)/shard_map/ppermute | solution.py:392
  46.6 35.9 %collective-permute-start.4 = (bf16[16,224,128]{2,1,0:T(8,128)(2,1)S(1)}, bf16[16,224,128]{2,1,0:T(8,128)(2,1)S(1)}, u32[]{:S(2)}, u32[]{:S(2)}) collective-permute-start(bf16[16,224,128]{2,1,0:T(8,128)(2,1)S(1)} %get-tuple-element.41), channel_id=1, source_target_pairs={{0,2},{1,3},{2,0},{3,1},{4,6},{5,7},{6,4},{7,5},{8,10},{9,11},{10,... | collective-permute-start | bytes 2752520 | tf_op jit(solution)/shard_map/ppermute | solution.py:392
  51.0 1.9 collective-permute-start
  51.1 31.2 %collective-permute-start.1 = (bf16[1024,256]{1,0:T(8,128)(2,1)S(1)}, bf16[1024,256]{1,0:T(8,128)(2,1)S(1)}, u32[]{:S(2)}, u32[]{:S(2)}) collective-permute-start(bf16[1024,256]{1,0:T(8,128)(2,1)S(1)} %bitcast.27), channel_id=1, source_target_pairs={{0,2},{1,3},{2,0},{3,1},{4,6},{5,7},{6,4},{7,5},{8,10},{9,11},{10,... | collective-permute-start | bytes 1572872 | tf_op jit(solution)/shard_map/ppermute | solution.py:392
  52.5 208.9 %copy-start.1 = (s32[32]{0:T(128)}, s32[32]{0:T(128)S(1)}, u32[]{:S(2)}) copy-start(s32[32]{0:T(128)S(1)} %get-tuple-element.88.high.refs_1_) | copy-start | bytes 388
  52.5 208.9 %copy-start.2 = (s32[32]{0:T(128)}, s32[32]{0:T(128)S(1)}, u32[]{:S(2)}) copy-start(s32[32]{0:T(128)S(1)} %get-tuple-element.89.low.refs_0_) | copy-start | bytes 388
  52.5 137.3 %copy-start.3 = (s32[17]{0:T(128)}, s32[17]{0:T(128)S(1)}, u32[]{:S(2)}) copy-start(s32[17]{0:T(128)S(1)} %slice_bitcast_fusion.base.refs_2_) | copy-start | bytes 208
  52.9 29.5 %copy-start.7 = (bf16[16,224,128]{2,1,0:T(8,128)(2,1)S(1)}, bf16[16,224,128]{2,1,0:T(8,128)(2,1)}, u32[]{:S(2)}) copy-start(bf16[16,224,128]{2,1,0:T(8,128)(2,1)} %get-tuple-element.43) | copy-start | bytes 2752516
  52.9 30.8 %copy-start.6 = (bf16[16,224,128]{2,1,0:T(8,128)(2,1)S(1)}, bf16[16,224,128]{2,1,0:T(8,128)(2,1)}, u32[]{:S(2)}) copy-start(bf16[16,224,128]{2,1,0:T(8,128)(2,1)} %get-tuple-element.74) | copy-start | bytes 2752516
  52.9 30.9 %copy-start.8 = (bf16[16,224,128]{2,1,0:T(8,128)(2,1)S(1)}, bf16[16,224,128]{2,1,0:T(8,128)(2,1)}, u32[]{:S(2)}) copy-start(bf16[16,224,128]{2,1,0:T(8,128)(2,1)} %get-tuple-element.71) | copy-start | bytes 2752516
  80.2 2.1 copy-start
  82.3 2.1 collective-permute-start.2
  82.4 22.6 %collective-permute-start.5 = (bf16[16,224,128]{2,1,0:T(8,128)(2,1)S(1)}, bf16[16,224,128]{2,1,0:T(8,128)(2,1)S(1)}, u32[]{:S(2)}, u32[]{:S(2)}) collective-permute-start(bf16[16,224,128]{2,1,0:T(8,128)(2,1)S(1)} %copy-done.7), channel_id=1, source_target_pairs={{0,2},{1,3},{2,0},{3,1},{4,6},{5,7},{6,4},{7,5},{8,10},{9,11},{10,... | collective-permute-start | bytes 2752520 | tf_op jit(solution)/shard_map/ppermute | solution.py:392
  83.7 21.4 %collective-permute-start.6 = (bf16[16,224,128]{2,1,0:T(8,128)(2,1)S(1)}, bf16[16,224,128]{2,1,0:T(8,128)(2,1)S(1)}, u32[]{:S(2)}, u32[]{:S(2)}) collective-permute-start(bf16[16,224,128]{2,1,0:T(8,128)(2,1)S(1)} %copy-done.6), channel_id=1, source_target_pairs={{0,1},{1,0},{2,3},{3,2},{4,5},{5,4},{6,7},{7,6},{8,9},{9,8},{10,11... | collective-permute-start | bytes 2752520 | tf_op jit(solution)/shard_map/ppermute | solution.py:391
  83.8 21.3 %collective-permute-start.7 = (bf16[16,224,128]{2,1,0:T(8,128)(2,1)S(1)}, bf16[16,224,128]{2,1,0:T(8,128)(2,1)S(1)}, u32[]{:S(2)}, u32[]{:S(2)}) collective-permute-start(bf16[16,224,128]{2,1,0:T(8,128)(2,1)S(1)} %copy-done.8), channel_id=1, source_target_pairs={{0,1},{1,0},{2,3},{3,2},{4,5},{5,4},{6,7},{7,6},{8,9},{9,8},{10,11... | collective-permute-start | bytes 2752520 | tf_op jit(solution)/shard_map/ppermute | solution.py:391
  84.2 21.8 %collective-permute-start.8 = (bf16[16,224,128]{2,1,0:T(8,128)(2,1)S(1)}, bf16[16,224,128]{2,1,0:T(8,128)(2,1)S(1)}, u32[]{:S(2)}, u32[]{:S(2)}) collective-permute-start(bf16[16,224,128]{2,1,0:T(8,128)(2,1)S(1)} %collective-permute-done.3.refs_4_), channel_id=1, source_target_pairs={{0,16},{16,0},{1,17},{17,1},{2,18},{18,2},{3,19},{19,3},{4,20},{20... | collective-permute-start | bytes 2752520 | tf_op jit(solution)/shard_map/ppermute | solution.py:393
  84.4 41.2 %collective-permute-start.9 = (bf16[16,224,128]{2,1,0:T(8,128)(2,1)S(1)}, bf16[16,224,128]{2,1,0:T(8,128)(2,1)S(1)}, u32[]{:S(2)}, u32[]{:S(2)}) collective-permute-start(bf16[16,224,128]{2,1,0:T(8,128)(2,1)S(1)} %collective-permute-done.4.refs_5_), channel_id=1, source_target_pairs={{0,16},{16,0},{1,17},{17,1},{2,18},{18,2},{3,19},{19,3},{4,20},{20... | collective-permute-start | bytes 2752520 | tf_op jit(solution)/shard_map/ppermute | solution.py:393
  145.3 156.8 %reduce-scatter.5.cloned.1.call-start = ((), (), s32[]{:S(2)}) async-start(), calls=%async_computation.5 | async-start | bytes 5242880 | tf_op jit(solution)/shard_map/reduce_scatter | solution.py:445
  145.3 23.1 %collective-permute-start.12 = (bf16[16,224,128]{2,1,0:T(8,128)(2,1)}, bf16[16,224,128]{2,1,0:T(8,128)(2,1)S(1)}, u32[]{:S(2)}, u32[]{:S(2)}) collective-permute-start(bf16[16,224,128]{2,1,0:T(8,128)(2,1)} %get-tuple-element.47), channel_id=1, source_target_pairs={{0,2},{1,3},{2,0},{3,1},{4,6},{5,7},{6,4},{7,5},{8,10},{9,11},{10,... | collective-permute-start | bytes 2752520 | tf_op jit(solution)/shard_map/ppermute | solution.py:392
  146.7 21.6 %collective-permute-start.10 = (bf16[16,224,128]{2,1,0:T(8,128)(2,1)}, bf16[16,224,128]{2,1,0:T(8,128)(2,1)S(1)}, u32[]{:S(2)}, u32[]{:S(2)}) collective-permute-start(bf16[16,224,128]{2,1,0:T(8,128)(2,1)} %get-tuple-element.73), channel_id=1, source_target_pairs={{0,1},{1,0},{2,3},{3,2},{4,5},{5,4},{6,7},{7,6},{8,9},{9,8},{10,11... | collective-permute-start | bytes 2752520 | tf_op jit(solution)/shard_map/ppermute | solution.py:391
  146.7 21.6 %collective-permute-start.11 = (bf16[16,224,128]{2,1,0:T(8,128)(2,1)}, bf16[16,224,128]{2,1,0:T(8,128)(2,1)S(1)}, u32[]{:S(2)}, u32[]{:S(2)}) collective-permute-start(bf16[16,224,128]{2,1,0:T(8,128)(2,1)} %get-tuple-element.70), channel_id=1, source_target_pairs={{0,1},{1,0},{2,3},{3,2},{4,5},{5,4},{6,7},{7,6},{8,9},{9,8},{10,11... | collective-permute-start | bytes 2752520 | tf_op jit(solution)/shard_map/ppermute | solution.py:391
  147.2 22.1 %collective-permute-start.13 = (bf16[16,224,128]{2,1,0:T(8,128)(2,1)S(1)}, bf16[16,224,128]{2,1,0:T(8,128)(2,1)S(1)}, u32[]{:S(2)}, u32[]{:S(2)}) collective-permute-start(bf16[16,224,128]{2,1,0:T(8,128)(2,1)S(1)} %collective-permute-done.5.refs_4_), channel_id=1, source_target_pairs={{0,16},{16,0},{1,17},{17,1},{2,18},{18,2},{3,19},{19,3},{4,20},{20... | collective-permute-start | bytes 2752520 | tf_op jit(solution)/shard_map/ppermute | solution.py:393
  168.4 21.4 %collective-permute-start.14 = (bf16[16,224,128]{2,1,0:T(8,128)(2,1)S(1)}, bf16[16,224,128]{2,1,0:T(8,128)(2,1)S(1)}, u32[]{:S(2)}, u32[]{:S(2)}) collective-permute-start(bf16[16,224,128]{2,1,0:T(8,128)(2,1)S(1)} %collective-permute-done.12.refs_5_), channel_id=1, source_target_pairs={{0,16},{16,0},{1,17},{17,1},{2,18},{18,2},{3,19},{19,3},{4,20},{20... | collective-permute-start | bytes 2752520 | tf_op jit(solution)/shard_map/ppermute | solution.py:393
  209.5 142.0 %all-gather.5.cloned.1.call-start = ((), (), s32[]{:S(2)}) async-start(), calls=%async_computation.7 | async-start | bytes 2621440 | tf_op jit(solution)/shard_map/all_gather | solution.py:457
  213.5 22.5 %collective-permute-start.17 = (bf16[16,224,128]{2,1,0:T(8,128)(2,1)S(1)}, bf16[16,224,128]{2,1,0:T(8,128)(2,1)}, u32[]{:S(2)}, u32[]{:S(2)}) collective-permute-start(bf16[16,224,128]{2,1,0:T(8,128)(2,1)S(1)} %get-tuple-element.49), channel_id=1, source_target_pairs={{0,2},{1,3},{2,0},{3,1},{4,6},{5,7},{6,4},{7,5},{8,10},{9,11},{10,... | collective-permute-start | bytes 2752520 | tf_op jit(solution)/shard_map/ppermute | solution.py:392
  215.3 40.4 %collective-permute-start.18 = (bf16[16,224,128]{2,1,0:T(8,128)(2,1)S(1)}, bf16[16,224,128]{2,1,0:T(8,128)(2,1)}, u32[]{:S(2)}, u32[]{:S(2)}) collective-permute-start(bf16[16,224,128]{2,1,0:T(8,128)(2,1)S(1)} %get-tuple-element.50), channel_id=1, source_target_pairs={{0,2},{1,3},{2,0},{3,1},{4,6},{5,7},{6,4},{7,5},{8,10},{9,11},{10,... | collective-permute-start | bytes 2752520 | tf_op jit(solution)/shard_map/ppermute | solution.py:392
  215.3 90.1 %collective-permute-start.15 = (bf16[16,224,128]{2,1,0:T(8,128)(2,1)}, bf16[16,224,128]{2,1,0:T(8,128)(2,1)S(1)}, u32[]{:S(2)}, u32[]{:S(2)}) collective-permute-start(bf16[16,224,128]{2,1,0:T(8,128)(2,1)} %get-tuple-element.68), channel_id=1, source_target_pairs={{0,1},{1,0},{2,3},{3,2},{4,5},{5,4},{6,7},{7,6},{8,9},{9,8},{10,11... | collective-permute-start | bytes 2752520 | tf_op jit(solution)/shard_map/ppermute | solution.py:391
  216.6 88.8 %collective-permute-start.16 = (bf16[16,224,128]{2,1,0:T(8,128)(2,1)}, bf16[16,224,128]{2,1,0:T(8,128)(2,1)}, u32[]{:S(2)}, u32[]{:S(2)}) collective-permute-start(bf16[16,224,128]{2,1,0:T(8,128)(2,1)} %get-tuple-element.67), channel_id=1, source_target_pairs={{0,1},{1,0},{2,3},{3,2},{4,5},{5,4},{6,7},{7,6},{8,9},{9,8},{10,11... | collective-permute-start | bytes 2752520 | tf_op jit(solution)/shard_map/ppermute | solution.py:391
  236.0 69.4 %collective-permute-start.19 = (bf16[16,224,128]{2,1,0:T(8,128)(2,1)}, bf16[16,224,128]{2,1,0:T(8,128)(2,1)}, u32[]{:S(2)}, u32[]{:S(2)}) collective-permute-start(bf16[16,224,128]{2,1,0:T(8,128)(2,1)} %collective-permute-done.17.refs_6_.refs_0_), channel_id=1, source_target_pairs={{0,16},{16,0},{1,17},{17,1},{2,18},{18,2},{3,19},{19,3},{4,20},{20... | collective-permute-start | bytes 2752520 | tf_op jit(solution)/shard_map/ppermute | solution.py:393
  255.7 49.8 %collective-permute-start.20 = (bf16[16,224,128]{2,1,0:T(8,128)(2,1)}, bf16[16,224,128]{2,1,0:T(8,128)(2,1)}, u32[]{:S(2)}, u32[]{:S(2)}) collective-permute-start(bf16[16,224,128]{2,1,0:T(8,128)(2,1)} %collective-permute-done.18.refs_7_.refs_1_), channel_id=1, source_target_pairs={{0,16},{16,0},{1,17},{17,1},{2,18},{18,2},{3,19},{19,3},{4,20},{20... | collective-permute-start | bytes 2752520 | tf_op jit(solution)/shard_map/ppermute | solution.py:393
  305.4 46.0 %copy-start.5 = (bf16[16,224,128]{2,1,0:T(8,128)(2,1)}, bf16[16,224,128]{2,1,0:T(8,128)(2,1)S(1)}, u32[]{:S(2)}) copy-start(bf16[16,224,128]{2,1,0:T(8,128)(2,1)S(1)} %collective-permute-done.15.refs_7_.refs_1_) | copy-start | bytes 2752516
  306.8 90.8 %all-gather.3.cloned.1.call-start = ((), (), s32[]{:S(2)}) async-start(), calls=%async_computation.6 | async-start | bytes 2621440 | tf_op jit(solution)/shard_map/all_gather | solution.py:457
  415.2 2.5 collective-permute-start.21
  436.0 13.9 %collective-permute-start.23 = (bf16[1024,224]{1,0:T(8,128)(2,1)S(1)}, bf16[1024,224]{1,0:T(8,128)(2,1)S(1)}, u32[]{:S(2)}, u32[]{:S(2)}) collective-permute-start(bf16[1024,224]{1,0:T(8,128)(2,1)S(1)} %add_convert_fusion), channel_id=1, source_target_pairs={{0,2},{1,3},{2,0},{3,1},{4,6},{5,7},{6,4},{7,5},{8,10},{9,11},{10,... | collective-permute-start | bytes 1376264 | tf_op jit(solution)/shard_map/ppermute | solution.py:392
  437.9 12.1 %collective-permute-start.22 = (bf16[1024,224]{1,0:T(8,128)(2,1)S(1)}, bf16[1024,224]{1,0:T(8,128)(2,1)S(1)}, u32[]{:S(2)}, u32[]{:S(2)}) collective-permute-start(bf16[1024,224]{1,0:T(8,128)(2,1)S(1)} %slice.97), channel_id=1, source_target_pairs={{0,1},{1,0},{2,3},{3,2},{4,5},{5,4},{6,7},{7,6},{8,9},{9,8},{10,11... | collective-permute-start | bytes 1376264 | tf_op jit(solution)/shard_map/ppermute | solution.py:391
Sparse Core Ops, SparseCore 0:
  145.4 76.9 reduce-scatter.2
  224.7 77.2 reduce-scatter.4
  306.9 44.5 all-gather.4
  352.9 44.6 all-gather.2

commit v6 on v5

--- a/solution.py
+++ b/solution.py
@@ -65,7 +65,7 @@
 
 
 def cost(flops, moved):
-    return pl.CostEstimate(flops=flops, bytes_accessed=moved, transcendentals=0)
+    return pl.CostEstimate(flops=4 * flops, bytes_accessed=4 * moved, transcendentals=0)
 
 
 def split3(value):
@@ -307,10 +307,9 @@
     )(*spans, base, quarter, near, far, w_gate, w_up, *pieces)
 
 
-def down_kernel(near, half, low, high, base, quarter, onehot_ref, hidden, start, *refs):
+def down_kernel(half, low, high, base, onehot_ref, hidden, start, *refs):
     weights, (out, total_ref, value_ref) = refs[:-3], refs[-3:]
-    count = out.shape[1] // LANES
-    width = weights[0].shape[1]
+    width = weights[0].shape[2]
     j = pl.program_id(0)
 
     @pl.when(j == 0)
@@ -326,13 +325,8 @@
         @pl.loop(low[i], high[i])
         def _(e):
             mine = mine_of(base, e, i * TILE)
-            rest = list(weights)
-            for k in range(count):
-                first = rest.pop(0)
-                weight = first[e]
-                if not (near and k == 0):
-                    weight = jnp.concatenate([weight, rest.pop(0)[e]], axis=1)
-                value = dot(units, weight, ((1,), (1,)))
+            for k, weight in enumerate(weights):
+                value = dot(units, weight[e], ((1,), (0,)))
                 at = slice(k * LANES, k * LANES + width)
                 value_ref[here, at] = jnp.where(
                     mine, value, value_ref[here, at].astype(F32)
@@ -345,25 +339,22 @@
         out[...] = total_ref[...].astype(out.dtype)
 
 
-def down_and_mix(near, half, spans, base, quarter, onehot, hidden, start, weights, count, dtype):
+def down_and_mix(half, spans, base, onehot, hidden, start, weights, dtype):
     rows, units = hidden.shape
-    experts, width, _ = weights[0].shape
-    tokens = onehot.shape[0]
+    count, tokens = len(weights), onehot.shape[0]
     block = pl.BlockSpec((BLOCK, units), lambda j, *_: (j, 0))
-    own = pl.BlockSpec((experts, width, units), lambda j, lo, hi, b, q: (0, 0, q[0]))
-    piece = pl.BlockSpec((experts, width, UNITS), lambda j, *_: (0, 0, 0))
     whole = pl.BlockSpec((tokens, count * LANES), lambda j, *_: (0, 0))
-    kernel = functools.partial(down_kernel, near, half)
+    kernel = functools.partial(down_kernel, half)
     if start is None:
-        kernel = lambda *refs: down_kernel(near, half, *refs[:6], None, *refs[6:])
+        kernel = lambda *refs: down_kernel(half, *refs[:5], None, *refs[5:])
     return pl.pallas_call(
         kernel,
         grid_spec=pltpu.PrefetchScalarGridSpec(
-            num_scalar_prefetch=4,
+            num_scalar_prefetch=3,
             grid=(rows // BLOCK,),
             in_specs=[pl.BlockSpec((tokens, BLOCK), lambda j, *_: (0, 2 * j + half)), block]
             + ([] if start is None else [whole])
-            + ([own] + [piece] * (len(weights) - 1) if near else [piece] * len(weights)),
+            + [pl.BlockSpec(w.shape, lambda j, *_: (0, 0, 0)) for w in weights],
             out_specs=whole,
             scratch_shapes=[
                 pltpu.VMEM((tokens, count * LANES), F32),
@@ -374,7 +365,7 @@
         compiler_params=params(56),
         cost_estimate=cost(2 * rows * tokens * LANES * count, 2 * rows * tokens),
         name="down_and_mix",
-    )(*spans, base, quarter, onehot, hidden, *([] if start is None else [start]), *weights)
+    )(*spans, base, onehot, hidden, *([] if start is None else [start]), *weights)
 
 
 def fixed_weights(size, tokens, expert_ids, gate_weights, w_gate, w_up, w_down):
@@ -389,12 +380,15 @@
     twins = [(i, i ^ 1) for i in range(size)]
     cross = [(p * size + i, p * size + (i ^ 2 ^ p)) for p in range(2) for i in range(size)]
     to_twin = lambda value: lax.ppermute(value, "ep", twins)
+    other = [(p * size + i, p * size + (i ^ 3 ^ p)) for p in range(2) for i in range(size)]
     to_cross = lambda value: lax.ppermute(value, ("parts", "ep"), cross)
+    to_other = lambda value: lax.ppermute(value, ("parts", "ep"), other)
     to_plane = lambda value: lax.ppermute(value, "parts", [(0, 1), (1, 0)])
     line = [[4 * p + k for p in range(places)] for k in range(4)]
     my_quarter = me % 4
     twin_quarter = my_quarter ^ 1
     cross_quarter = my_quarter ^ 2 ^ plane
+    other_quarter = cross_quarter ^ 1
 
     note = jnp.concatenate([expert_ids.astype(F32), *split3(gate_weights)], axis=1).astype(BF16)
     fill = LANES - width - note.shape[1]
@@ -429,18 +423,16 @@
         ((0, w_gate), (0, w_up), (1, w_gate), (1, w_up), (0, w_down), (1, w_down))
     ):
         piece = cut(w, cross_quarter, f)
-        if n:
-            piece = after(piece, crossed[n - 1] if n < 4 else crossed[3])
-        if n == 2:
-            piece = after(piece, far)
+        if n > 1:
+            piece = after(piece, far_rows, crossed[n - 1], *[pieces[2] for pieces in held[:2]])
         crossed.append(to_cross(piece))
-        held.append((to_twin(cut(w, twin_quarter, f)), crossed[n], to_plane(crossed[n])))
+        beside = to_plane(crossed[n]) if n > 1 else to_other(cut(w, other_quarter, f))
+        held.append((to_twin(cut(w, twin_quarter, f)), crossed[n], beside))
     weave = lambda pair: [piece for both in zip(*pair) for piece in both]
 
-    units, later = [], crossed[2]
+    units = []
     for f in range(2):
         pieces = weave(held[2 * f : 2 * f + 2])
-        far_rows = after(far_rows, later)
         later = partial_sums(f, spans, base, which, near_rows, far_rows, w_gate, w_up, pieces)
         sums = lax.psum_scatter(
             later, "ep", scatter_dimension=0, axis_index_groups=line, tiled=True
@@ -451,17 +443,26 @@
         after(across[:experts], later)[:, :, None], (experts, size * count, 128)
     )
     columns = scatter_rows(spans, place, rows)
-    units, columns, pieces = lax.optimization_barrier((units, columns, weave(held[4:])))
+    turned = weave(held[4:])
+    turned = [
+        jnp.concatenate([jnp.swapaxes(piece, 1, 2) for piece in turned[k : k + 2]], axis=1)
+        for k in (0, 2, 4)
+    ]
+    turned = [
+        jnp.swapaxes(lax.dynamic_slice_in_dim(w_down, my_quarter * quarter, quarter, 2), 1, 2)
+    ] + turned
+    turned = after(turned, later)
+    units, columns, turned = lax.optimization_barrier((units, columns, turned))
     units = jnp.concatenate(units, axis=1).reshape(-1, BLOCK, 2 * UNITS)
     first, second = (
         lax.all_gather(units[half], "ep", axis=0, axis_index_groups=line, tiled=True)
         for half in range(2)
     )
     far_mix = lambda half, hidden, start, dtype: down_and_mix(
-        False, half, spans, base, which, columns, hidden, start, pieces[2:], 2, dtype
+        half, spans, base, columns, hidden, start, turned[2:], dtype
     )
     near_mix = lambda half, hidden, start, dtype: down_and_mix(
-        True, half, spans, base, which, columns, hidden, start, [w_down] + pieces[:2], 2, dtype
+        half, spans, base, columns, hidden, start, turned[:2], dtype
     )
     far, near = far_mix(0, first, None, F32), near_mix(0, first, None, F32)
     second, far, near = lax.optimization_barrier((second, far, near))
@@ -471,7 +472,8 @@
     near, far = lax.optimization_barrier((near, far))
     far = to_cross(far)
     near = near_mix(1, second, near, F32)
-    twin = to_twin(near[:, LANES : LANES + width].astype(BF16)).astype(F32)
+    twin = near[:, LANES : LANES + width].astype(BF16)
+    twin = to_twin(after(twin, far)).astype(F32)
     mixed = (near[:, :width] + twin + far.astype(F32)).astype(BF16)
     mixed = lax.all_to_all(
         mixed.reshape(size, count, width), "ep", split_axis=0, concat_axis=0, tiled=True

time: 483 us -> 494 us (1.023)
  local copies, waits for them, and re-layouts: 26.2 us -> 36.5 us
  other arithmetic: 9.73 us -> 15.1 us
    ppermute x0 -> x2, waiting for transfers between devices: none -> 23.3 us  [fixed_weights(): to_other = lambda value: lax.ppermute(value, ('parts', 'ep'), other)]
    reduce_scatter x2, waiting for transfers between devices: 22.8 us -> 0.02 us  [fixed_weights(): lax.psum_scatter(later, 'ep', scatter_dimension=0, axis_index_groups=line...]
    ppermute x6 -> x4, waiting for transfers between devices: 42 us -> 22.5 us  [fixed_weights(): to_plane = lambda value: lax.ppermute(value, 'parts', [(0, 1), (1, 0)])]
    all_to_all x1, waiting for transfers between devices: 0.01 us -> 9.34 us  [fixed_weights(): own = lax.all_to_all(parcels, 'ep', split_axis=0, concat_axis=0, tiled=True)]
    ppermute x8, waiting for transfers between devices: 97.5 us -> 107 us  [fixed_weights(): to_cross = lambda value: lax.ppermute(value, ('parts', 'ep'), cross)]
    ppermute x0 -> x6, local copies, waits for them, and re-layouts: none -> 7.78 us  [the longest x2 2.91 us: fixed_weights(): to_plane = lambda value: lax.ppermute(value, 'parts', [(0, 1), (1, 0)])]
    concatenate x0 -> x3, other arithmetic: none -> 5.38 us  [fixed_weights(): jnp.concatenate([jnp.swapaxes(piece, 1, 2) for piece in turned[k:k + 2]],...]
  transfers between devices with their start and end apart: 29 -> 29, of which waited for: 15 -> 15; matrix products, arithmetic and copies ran while one was open for 5% -> 8% of each run, Pallas kernels for 24% -> 27%
where the time goes in v6:
time: 494 us; the launch traced here: 492 us
  waiting for transfers between devices  223 us (45%)
  Pallas kernels  167 us (34%)
  local copies, waits for them, and re-layouts  36.5 us (7%)
  blocking collectives  19.1 us (4%)
  starting transfers between devices  16.7 us (3%)
  other arithmetic  15.1 us (3%)
  between operations  13.4 us (3%)
    ppermute x8, waiting for transfers between devices, fixed_weights(): to_cross = lambda value: lax.ppermute(value, ('parts', 'ep'), cross)  107 us
    pallas_call x4, Pallas kernels, down_and_mix(): pl.pallas_call(kernel, grid_spec=pltpu.PrefetchScalarGridSpec(num_scalar_...  65.4 us
    all_gather x2, waiting for transfers between devices, fixed_weights(): lax.all_gather(units[half], 'ep', axis=0, axis_index_groups=line, tiled=T...  57.2 us
    pallas_call x2, Pallas kernels, partial_sums(): pl.pallas_call(partial_kernel, grid_spec=pltpu.PrefetchScalarGridSpec(num...  39.2 us
    pallas_call x1, Pallas kernels, sort_rows(): pl.pallas_call(functools.partial(sort_kernel, experts), grid_spec=pltpu.P...  27.3 us
    ppermute x2, waiting for transfers between devices, fixed_weights(): to_other = lambda value: lax.ppermute(value, ('parts', 'ep'), other)  23.3 us
    ppermute x4, waiting for transfers between devices, fixed_weights(): to_plane = lambda value: lax.ppermute(value, 'parts', [(0, 1), (1, 0)])  22.5 us
    all_to_all x1, blocking collectives, fixed_weights(): lax.all_to_all(mixed.reshape(size, count, width), 'ep', split_axis=0, con...  19.1 us
  transfers between devices with their start and end apart: 29, of which 15 were waited for; matrix products, arithmetic and copies ran while one was open for 8% of the time, Pallas kernels for 27%

profile of v6, /device:TPU:15, one launch (start us, length us, event | category | flops | bytes accessed | tf_op | source)
XLA Modules:
  0.0 491.6 jit_solution(17572044854245703973)
XLA Ops:
  8.0 1.8 reshape.65
  11.0 6.6 %all-to-all-start = ((bf16[16,64,256]{2,1,0:T(8,128)(2,1)}), bf16[16,64,256]{2,1,0:T(8,128)(2,1)S(1)}, u32[]{:S(2)}, u32[]{:S(2)}) async-start(bf16[16,64,256]{2,1,0:T(8,128)(2,1)} %pad_maximum_fusion.3), calls=%async_computation | async-start | bytes 1048576 | tf_op jit(solution)/shard_map/all_to_all | solution.py:402
  17.6 3.9 constant_dynamic-slice_fusion.1
  22.1 9.3 %all-to-all-done = bf16[16,64,256]{2,1,0:T(8,128)(2,1)S(1)} async-done(((bf16[16,64,256]{2,1,0:T(8,128)(2,1)}), bf16[16,64,256]{2,1,0:T(8,128)(2,1)S(1)}, u32[]{:S(2)}, u32[]{:S(2)}) %all-to-all-start) | async-done | bytes 524320 | tf_op jit(solution)/shard_map/all_to_all | solution.py:402
  31.4 3.6 order.1
  37.0 27.3 %sort_rows.1 = (bf16[8192,512]{1,0:T(8,128)(2,1)}, f32[8192,128]{1,0:T(8,128)S(1)}, bf16[8192,1024]{1,0:T(8,128)(2,1)}) custom-call(s32[32]{0:T(128)S(1)} %get-tuple-element.89.low.refs_0_, s32[32]{0:T(128)S(1)} %get-tuple-element.88.high.refs_1_, s32[17]{0:T(128)S(1)} %slice_bitcast_fusion.base.refs_2_, s32[16,8,128]{2,1,0:T(8,128)S(1)} %bitcast.34, ...), custom_call_target="tpu_custom_call" | custom-call | flops 34359738368 | bytes 134217728 | tf_op jit(solution)/shard_map/sort_rows/pallas_call | solution.py:184
  64.5 3.3 constant_dynamic-slice_fusion.2
  71.0 15.3 %sort_more.1.far_ref = bf16[8192,512]{1,0:T(8,128)(2,1)} custom-call(bf16[8192,1024]{1,0:T(8,128)(2,1)} %get-tuple-element.38.onehot_ref, bf16[1024,256]{1,0:T(8,128)(2,1)S(1)} %collective-permute-done.1.refs_0_, bf16[1024,256]{1,0:T(8,128)(2,1)S(1)} %collective-permute-done.2.refs_1_), custom_call_target="tpu_custom_call" | custom-call | flops 34359738368 | bytes 134217728 | tf_op jit(solution)/shard_map/sort_more/pallas_call | solution.py:221
  86.2 3.7 collective-permute-done.7.refs_6_
  89.9 19.7 %collective-permute-done.8.refs_7_ = bf16[16,224,128]{2,1,0:T(8,128)(2,1)S(1)} collective-permute-done((bf16[16,224,128]{2,1,0:T(8,128)(2,1)}, bf16[16,224,128]{2,1,0:T(8,128)(2,1)S(1)}, u32[]{:S(2)}, u32[]{:S(2)}) %collective-permute-start.8) | collective-permute-done | bytes 917536 | tf_op jit(solution)/shard_map/ppermute | solution.py:385
  109.6 19.8 %collective-permute-done.5.refs_4_ = bf16[16,224,128]{2,1,0:T(8,128)(2,1)S(1)} collective-permute-done((bf16[16,224,128]{2,1,0:T(8,128)(2,1)}, bf16[16,224,128]{2,1,0:T(8,128)(2,1)S(1)}, u32[]{:S(2)}, u32[]{:S(2)}) %collective-permute-start.5) | collective-permute-done | bytes 917536 | tf_op jit(solution)/shard_map/ppermute | solution.py:384
  129.4 19.7 %partial_sums.2 = bf16[8192,256]{1,0:T(8,128)(2,1)} custom-call(s32[32]{0:T(128)S(1)} %get-tuple-element.89.low.refs_0_, s32[32]{0:T(128)S(1)} %get-tuple-element.88.high.refs_1_, s32[17]{0:T(128)S(1)} %slice_bitcast_fusion.base.refs_2_, s32[1]{0:T(128)} %bitcast.5.quarter, bf16[8192,512]{1,0:T(8,128)(2,1)} %get-tuple-element.37.near_ref, ...), custom_call_target="tpu_custom_call" | custom-call | flops 17179869184 | bytes 67108864 | tf_op jit(solution)/shard_map/partial_sums/pallas_call | solution.py:294
  150.0 22.1 %collective-permute-done.11.refs_4_ = bf16[16,224,128]{2,1,0:T(8,128)(2,1)S(1)} collective-permute-done((bf16[16,224,128]{2,1,0:T(8,128)(2,1)}, bf16[16,224,128]{2,1,0:T(8,128)(2,1)S(1)}, u32[]{:S(2)}, u32[]{:S(2)}) %collective-permute-start.11) | collective-permute-done | bytes 917536 | tf_op jit(solution)/shard_map/ppermute | solution.py:384
  173.1 21.2 %collective-permute-done.12.refs_5_ = bf16[16,224,128]{2,1,0:T(8,128)(2,1)S(1)} collective-permute-done((bf16[16,224,128]{2,1,0:T(8,128)(2,1)S(1)}, bf16[16,224,128]{2,1,0:T(8,128)(2,1)S(1)}, u32[]{:S(2)}, u32[]{:S(2)}) %collective-permute-start.12) | collective-permute-done | bytes 917536 | tf_op jit(solution)/shard_map/ppermute | solution.py:384
  194.6 22.2 %collective-permute-done.14.refs_7_ = bf16[16,224,128]{2,1,0:T(8,128)(2,1)S(1)} collective-permute-done((bf16[16,224,128]{2,1,0:T(8,128)(2,1)S(1)}, bf16[16,224,128]{2,1,0:T(8,128)(2,1)S(1)}, u32[]{:S(2)}, u32[]{:S(2)}) %collective-permute-start.14) | collective-permute-done | bytes 917536 | tf_op jit(solution)/shard_map/ppermute | solution.py:386
  216.8 19.6 %partial_sums.3 = bf16[8192,256]{1,0:T(8,128)(2,1)} custom-call(s32[32]{0:T(128)S(1)} %get-tuple-element.89.low.refs_0_, s32[32]{0:T(128)S(1)} %get-tuple-element.88.high.refs_1_, s32[17]{0:T(128)S(1)} %slice_bitcast_fusion.base.refs_2_, s32[1]{0:T(128)} %bitcast.5.quarter, bf16[8192,512]{1,0:T(8,128)(2,1)} %get-tuple-element.37.near_ref, ...), custom_call_target="tpu_custom_call" | custom-call | flops 17179869184 | bytes 67108864 | tf_op jit(solution)/shard_map/partial_sums/pallas_call | solution.py:294
  236.6 3.6 dynamic-slice_bitcast_fusion.1
  240.8 22.0 %collective-permute-done.17 = bf16[16,224,128]{2,1,0:T(8,128)(2,1)} collective-permute-done((bf16[16,224,128]{2,1,0:T(8,128)(2,1)S(1)}, bf16[16,224,128]{2,1,0:T(8,128)(2,1)}, u32[]{:S(2)}, u32[]{:S(2)}) %collective-permute-start.17) | collective-permute-done | bytes 917536 | tf_op jit(solution)/shard_map/ppermute | solution.py:384
  263.7 21.6 %collective-permute-done.18 = bf16[16,224,128]{2,1,0:T(8,128)(2,1)} collective-permute-done((bf16[16,224,128]{2,1,0:T(8,128)(2,1)S(1)}, bf16[16,224,128]{2,1,0:T(8,128)(2,1)}, u32[]{:S(2)}, u32[]{:S(2)}) %collective-permute-start.18) | collective-permute-done | bytes 917536 | tf_op jit(solution)/shard_map/ppermute | solution.py:384
  285.3 1.6 constant_dynamic-slice_fusion
  287.0 2.8 copy.35.refs_5_.refs_0_
  289.8 1.5 copy.29
  291.8 1.8 pad_maximum_fusion.refs_6_.refs_1_
  293.6 1.5 copy.30
  295.1 5.7 %broadcast_in_dim.5.place_ref = s32[16,1024,128]{2,1,0:T(8,128)} broadcast(s32[16,1024]{1,0:T(8,128)S(1)} %get-tuple-element.43), dimensions={0,1} | broadcast | bytes 8454144 | tf_op jit(solution)/shard_map/broadcast_in_dim | solution.py:442
  300.8 16.5 %scatter_rows.1.refs_3_.onehot_ref = bf16[1024,8192]{1,0:T(8,128)(2,1)} custom-call(s32[32]{0:T(128)S(1)} %get-tuple-element.89.low.refs_0_, s32[32]{0:T(128)S(1)} %get-tuple-element.88.high.refs_1_, s32[16,1024,128]{2,1,0:T(8,128)} %broadcast_in_dim.5.place_ref), custom_call_target="tpu_custom_call" | custom-call | flops 33554432 | bytes 67108864 | tf_op jit(solution)/shard_map/scatter_rows/pallas_call | solution.py:251
  317.3 1.5 copy.31
  318.8 1.5 copy.32
  320.3 1.8 pad_maximum_fusion.1.refs_5_.refs_0_
  322.1 1.5 copy.33
  323.5 1.7 pad_maximum_fusion.2.refs_6_.refs_1_
  325.3 1.4 convert_element_type.48
  326.7 1.4 convert_element_type.50
  328.1 2.0 fusion.3
  331.9 43.1 %all-gather.5.cloned.1.call-done.refs_4_ = bf16[4096,256]{1,0:T(8,128)(2,1)} async-done(((bf16[1024,256]{1,0:T(8,128)(2,1)}), bf16[4096,256]{1,0:T(8,128)(2,1)}) %all-gather.5.cloned.1.call-update) | async-done | bytes 2097168 | tf_op jit(solution)/shard_map/all_gather | solution.py:458
  375.1 16.2 %down_and_mix.4.start = f32[1024,512]{1,0:T(8,128)} custom-call(s32[32]{0:T(128)} %copy-done.2, s32[32]{0:T(128)} %copy-done.1, s32[17]{0:T(128)} %copy-done.3, bf16[1024,8192]{1,0:T(8,128)(2,1)} %scatter_rows.1.refs_3_.onehot_ref, bf16[4096,256]{1,0:T(8,128)(2,1)} %all-gather.5.cloned.1.call-done.refs_4_, ...), custom_call_target="tpu_custom_call" | custom-call | flops 17179869184 | bytes 33554432 | tf_op jit(solution)/shard_map/down_and_mix/pallas_call | solution.py:350
  391.3 16.3 %down_and_mix.5.start = f32[1024,512]{1,0:T(8,128)} custom-call(s32[32]{0:T(128)} %copy-done.2, s32[32]{0:T(128)} %copy-done.1, s32[17]{0:T(128)} %copy-done.3, bf16[1024,8192]{1,0:T(8,128)(2,1)} %scatter_rows.1.refs_3_.onehot_ref, bf16[4096,256]{1,0:T(8,128)(2,1)} %all-gather.5.cloned.1.call-done.refs_4_, bf16[16,256,224]{2,1,0:T(8,128)(2,1)} %copy.35.refs_5_.refs_0_, ...), custom_call_target="tpu_custom_call" | custom-call | flops 17179869184 | bytes 33554432 | tf_op jit(solution)/shard_map/down_and_mix/pallas_call | solution.py:350
  407.6 14.1 %all-gather.3.cloned.1.call-done.hidden = bf16[4096,256]{1,0:T(8,128)(2,1)} async-done(((bf16[1024,256]{1,0:T(8,128)(2,1)}), bf16[4096,256]{1,0:T(8,128)(2,1)}) %all-gather.3.cloned.1.call-update) | async-done | bytes 2097168 | tf_op jit(solution)/shard_map/all_gather | solution.py:458
  421.7 16.2 %down_and_mix.6 = bf16[1024,512]{1,0:T(8,128)(2,1)} custom-call(s32[32]{0:T(128)} %copy-done.2, s32[32]{0:T(128)} %copy-done.1, s32[17]{0:T(128)} %copy-done.3, bf16[1024,8192]{1,0:T(8,128)(2,1)} %scatter_rows.1.refs_3_.onehot_ref, bf16[4096,256]{1,0:T(8,128)(2,1)} %all-gather.3.cloned.1.call-done.hidden, f32[1024,512]{1,0:T(8,128)} %down_and_mix.4.start, ...), custom_call_target="tpu_custom_call" | custom-call | flops 17179869184 | bytes 33554432 | tf_op jit(solution)/shard_map/down_and_mix/pallas_call | solution.py:350
  437.9 1.1 slice.71
  439.9 1.5 collective-permute-done.21
  441.4 1.2 add_convert_fusion
  442.8 16.6 %down_and_mix.7 = f32[1024,512]{1,0:T(8,128)} custom-call(s32[32]{0:T(128)} %copy-done.2, s32[32]{0:T(128)} %copy-done.1, s32[17]{0:T(128)} %copy-done.3, bf16[1024,8192]{1,0:T(8,128)(2,1)} %scatter_rows.1.refs_3_.onehot_ref, bf16[4096,256]{1,0:T(8,128)(2,1)} %all-gather.3.cloned.1.call-done.hidden, f32[1024,512]{1,0:T(8,128)} %down_and_mix.5.start, ...), custom_call_target="tpu_custom_call" | custom-call | flops 17179869184 | bytes 33554432 | tf_op jit(solution)/shard_map/down_and_mix/pallas_call | solution.py:350
  459.4 1.3 slice.97
  461.0 1.6 collective-permute-done.23
  462.7 1.4 fusion.1
  464.0 19.1 %all_to_all.10 = bf16[16,64,224]{2,1,0:T(8,128)(2,1)S(1)} all-to-all(bf16[16,64,224]{2,1,0:T(8,128)(2,1)S(1)} %bitcast.43), channel_id=1, replica_groups=mesh['parts'=2,'ep'=16,'tp'=1] {'ep'}, dimensions={0} | all-to-all | bytes 917504 | tf_op jit(solution)/shard_map/all_to_all | solution.py:478
  483.5 1.6 reshape.70
  (82 shorter events, 16.4 us)
Async XLA Ops:
  11.0 20.4 %all-to-all-start = ((bf16[16,64,256]{2,1,0:T(8,128)(2,1)}), bf16[16,64,256]{2,1,0:T(8,128)(2,1)S(1)}, u32[]{:S(2)}, u32[]{:S(2)}) async-start(bf16[16,64,256]{2,1,0:T(8,128)(2,1)} %pad_maximum_fusion.3), calls=%async_computation | async-start | bytes 1048576 | tf_op jit(solution)/shard_map/all_to_all | solution.py:402
  17.5 307.7 %reduce-scatter.3.cloned.1.call-start = ((), (), s32[]{:S(2)}) async-start(), calls=%async_computation.4 | async-start | bytes 5242880 | tf_op jit(solution)/shard_map/reduce_scatter | solution.py:437
  21.5 48.4 %collective-permute-start.6 = (bf16[16,224,128]{2,1,0:T(8,128)(2,1)}, bf16[16,224,128]{2,1,0:T(8,128)(2,1)S(1)}, u32[]{:S(2)}, u32[]{:S(2)}) collective-permute-start(bf16[16,224,128]{2,1,0:T(8,128)(2,1)} %get-tuple-element.70), channel_id=1, source_target_pairs={{0,2},{1,3},{2,0},{3,1},{4,6},{5,7},{6,4},{7,5},{8,10},{9,11},{10,... | collective-permute-start | bytes 2752520 | tf_op jit(solution)/shard_map/ppermute | solution.py:384
  31.4 33.1 %slice-start = ((s8[7340032]{0:T(1024)(128)(4,1)}), s8[4194304]{0:T(1024)(128)(4,1)S(1)}, s32[]{:S(2)}) async-start(s8[7340032]{0:T(1024)(128)(4,1)} %bitcast.41), calls=%async_computation.8 | async-start | bytes 8388608
  35.0 1.9 collective-permute-start
  35.0 29.3 %collective-permute-start.1 = (bf16[1024,256]{1,0:T(8,128)(2,1)S(1)}, bf16[1024,256]{1,0:T(8,128)(2,1)S(1)}, u32[]{:S(2)}, u32[]{:S(2)}) collective-permute-start(bf16[1024,256]{1,0:T(8,128)(2,1)S(1)} %bitcast.32), channel_id=1, source_target_pairs={{0,2},{1,3},{2,0},{3,1},{4,6},{5,7},{6,4},{7,5},{8,10},{9,11},{10,... | collective-permute-start | bytes 1572872 | tf_op jit(solution)/shard_map/ppermute | solution.py:384
  36.3 264.5 %copy-start.1 = (s32[32]{0:T(128)}, s32[32]{0:T(128)S(1)}, u32[]{:S(2)}) copy-start(s32[32]{0:T(128)S(1)} %get-tuple-element.88.high.refs_1_) | copy-start | bytes 388
  36.3 264.5 %copy-start.2 = (s32[32]{0:T(128)}, s32[32]{0:T(128)S(1)}, u32[]{:S(2)}) copy-start(s32[32]{0:T(128)S(1)} %get-tuple-element.89.low.refs_0_) | copy-start | bytes 388
  36.3 180.5 %copy-start.3 = (s32[17]{0:T(128)}, s32[17]{0:T(128)S(1)}, u32[]{:S(2)}) copy-start(s32[17]{0:T(128)S(1)} %slice_bitcast_fusion.base.refs_2_) | copy-start | bytes 208
  37.0 27.6 %slice-start.1 = ((s8[7340032]{0:T(1024)(128)(4,1)}), s8[3145728]{0:T(1024)(128)(4,1)S(1)}, s32[]{:S(2)}) async-start(s8[7340032]{0:T(1024)(128)(4,1)} %bitcast.41), calls=%async_computation.9 | async-start | bytes 6291456
  64.3 3.5 copy-start
  64.3 5.6 %collective-permute-start.2 = (bf16[1024,256]{1,0:T(8,128)(2,1)S(1)}, bf16[1024,256]{1,0:T(8,128)(2,1)S(1)}, u32[]{:S(2)}, u32[]{:S(2)}) collective-permute-start(bf16[1024,256]{1,0:T(8,128)(2,1)S(1)} %collective-permute-done.1.refs_0_), channel_id=1, source_target_pairs={{0,1},{1,0},{2,3},{3,2},{4,5},{5,4},{6,7},{7,6},{8,9},{9,8},{10,11... | collective-permute-start | bytes 1572872 | tf_op jit(solution)/shard_map/ppermute | solution.py:382
  67.8 22.1 %collective-permute-start.7 = (bf16[16,224,128]{2,1,0:T(8,128)(2,1)}, bf16[16,224,128]{2,1,0:T(8,128)(2,1)S(1)}, u32[]{:S(2)}, u32[]{:S(2)}) collective-permute-start(bf16[16,224,128]{2,1,0:T(8,128)(2,1)} %get-tuple-element.74), channel_id=1, source_target_pairs={{0,3},{1,2},{2,1},{3,0},{4,7},{5,6},{6,5},{7,4},{8,11},{9,10},{10,... | collective-permute-start | bytes 2752520 | tf_op jit(solution)/shard_map/ppermute | solution.py:385
  68.4 41.1 %collective-permute-start.8 = (bf16[16,224,128]{2,1,0:T(8,128)(2,1)}, bf16[16,224,128]{2,1,0:T(8,128)(2,1)S(1)}, u32[]{:S(2)}, u32[]{:S(2)}) collective-permute-start(bf16[16,224,128]{2,1,0:T(8,128)(2,1)} %get-tuple-element.69), channel_id=1, source_target_pairs={{0,3},{1,2},{2,1},{3,0},{4,7},{5,6},{6,5},{7,4},{8,11},{9,10},{10,... | collective-permute-start | bytes 2752520 | tf_op jit(solution)/shard_map/ppermute | solution.py:385
  69.3 40.3 %collective-permute-start.3 = (bf16[16,224,128]{2,1,0:T(8,128)(2,1)}, bf16[16,224,128]{2,1,0:T(8,128)(2,1)S(1)}, u32[]{:S(2)}, u32[]{:S(2)}) collective-permute-start(bf16[16,224,128]{2,1,0:T(8,128)(2,1)} %get-tuple-element.76), channel_id=1, source_target_pairs={{0,1},{1,0},{2,3},{3,2},{4,5},{5,4},{6,7},{7,6},{8,9},{9,8},{10,11... | collective-permute-start | bytes 2752520 | tf_op jit(solution)/shard_map/ppermute | solution.py:382
  69.9 39.7 %collective-permute-start.4 = (bf16[16,224,128]{2,1,0:T(8,128)(2,1)}, bf16[16,224,128]{2,1,0:T(8,128)(2,1)S(1)}, u32[]{:S(2)}, u32[]{:S(2)}) collective-permute-start(bf16[16,224,128]{2,1,0:T(8,128)(2,1)} %get-tuple-element.71), channel_id=1, source_target_pairs={{0,1},{1,0},{2,3},{3,2},{4,5},{5,4},{6,7},{7,6},{8,9},{9,8},{10,11... | collective-permute-start | bytes 2752520 | tf_op jit(solution)/shard_map/ppermute | solution.py:382
  69.9 59.5 %collective-permute-start.5 = (bf16[16,224,128]{2,1,0:T(8,128)(2,1)}, bf16[16,224,128]{2,1,0:T(8,128)(2,1)S(1)}, u32[]{:S(2)}, u32[]{:S(2)}) collective-permute-start(bf16[16,224,128]{2,1,0:T(8,128)(2,1)} %get-tuple-element.75), channel_id=1, source_target_pairs={{0,2},{1,3},{2,0},{3,1},{4,6},{5,7},{6,4},{7,5},{8,10},{9,11},{10,... | collective-permute-start | bytes 2752520 | tf_op jit(solution)/shard_map/ppermute | solution.py:384
  149.1 23.3 %copy-start.4 = (bf16[16,224,128]{2,1,0:T(8,128)(2,1)S(1)}, bf16[16,224,128]{2,1,0:T(8,128)(2,1)}, u32[]{:S(2)}) copy-start(bf16[16,224,128]{2,1,0:T(8,128)(2,1)} %get-tuple-element.73) | copy-start | bytes 2752516
  149.1 177.6 %reduce-scatter.5.cloned.1.call-start = ((), (), s32[]{:S(2)}) async-start(), calls=%async_computation.5 | async-start | bytes 5242880 | tf_op jit(solution)/shard_map/reduce_scatter | solution.py:437
  149.2 22.9 %collective-permute-start.11 = (bf16[16,224,128]{2,1,0:T(8,128)(2,1)}, bf16[16,224,128]{2,1,0:T(8,128)(2,1)S(1)}, u32[]{:S(2)}, u32[]{:S(2)}) collective-permute-start(bf16[16,224,128]{2,1,0:T(8,128)(2,1)} %get-tuple-element.41), channel_id=1, source_target_pairs={{0,2},{1,3},{2,0},{3,1},{4,6},{5,7},{6,4},{7,5},{8,10},{9,11},{10,... | collective-permute-start | bytes 2752520 | tf_op jit(solution)/shard_map/ppermute | solution.py:384
  172.0 22.3 %collective-permute-start.12 = (bf16[16,224,128]{2,1,0:T(8,128)(2,1)S(1)}, bf16[16,224,128]{2,1,0:T(8,128)(2,1)S(1)}, u32[]{:S(2)}, u32[]{:S(2)}) collective-permute-start(bf16[16,224,128]{2,1,0:T(8,128)(2,1)S(1)} %get-tuple-element.42), channel_id=1, source_target_pairs={{0,2},{1,3},{2,0},{3,1},{4,6},{5,7},{6,4},{7,5},{8,10},{9,11},{10,... | collective-permute-start | bytes 2752520 | tf_op jit(solution)/shard_map/ppermute | solution.py:384
  172.4 21.9 %collective-permute-start.9 = (bf16[16,224,128]{2,1,0:T(8,128)(2,1)S(1)}, bf16[16,224,128]{2,1,0:T(8,128)(2,1)S(1)}, u32[]{:S(2)}, u32[]{:S(2)}) collective-permute-start(bf16[16,224,128]{2,1,0:T(8,128)(2,1)S(1)} %copy-done.4), channel_id=1, source_target_pairs={{0,1},{1,0},{2,3},{3,2},{4,5},{5,4},{6,7},{7,6},{8,9},{9,8},{10,11... | collective-permute-start | bytes 2752520 | tf_op jit(solution)/shard_map/ppermute | solution.py:382
  173.1 21.3 %collective-permute-start.10 = (bf16[16,224,128]{2,1,0:T(8,128)(2,1)S(1)}, bf16[16,224,128]{2,1,0:T(8,128)(2,1)S(1)}, u32[]{:S(2)}, u32[]{:S(2)}) collective-permute-start(bf16[16,224,128]{2,1,0:T(8,128)(2,1)S(1)} %get-tuple-element.68), channel_id=1, source_target_pairs={{0,1},{1,0},{2,3},{3,2},{4,5},{5,4},{6,7},{7,6},{8,9},{9,8},{10,11... | collective-permute-start | bytes 2752520 | tf_op jit(solution)/shard_map/ppermute | solution.py:382
  173.1 21.5 %collective-permute-start.13 = (bf16[16,224,128]{2,1,0:T(8,128)(2,1)S(1)}, bf16[16,224,128]{2,1,0:T(8,128)(2,1)S(1)}, u32[]{:S(2)}, u32[]{:S(2)}) collective-permute-start(bf16[16,224,128]{2,1,0:T(8,128)(2,1)S(1)} %collective-permute-done.11.refs_4_), channel_id=1, source_target_pairs={{0,16},{16,0},{1,17},{17,1},{2,18},{18,2},{3,19},{19,3},{4,20},{20... | collective-permute-start | bytes 2752520 | tf_op jit(solution)/shard_map/ppermute | solution.py:386
  194.3 22.5 %collective-permute-start.14 = (bf16[16,224,128]{2,1,0:T(8,128)(2,1)S(1)}, bf16[16,224,128]{2,1,0:T(8,128)(2,1)S(1)}, u32[]{:S(2)}, u32[]{:S(2)}) collective-permute-start(bf16[16,224,128]{2,1,0:T(8,128)(2,1)S(1)} %collective-permute-done.12.refs_5_), channel_id=1, source_target_pairs={{0,16},{16,0},{1,17},{17,1},{2,18},{18,2},{3,19},{19,3},{4,20},{20... | collective-permute-start | bytes 2752520 | tf_op jit(solution)/shard_map/ppermute | solution.py:386
  236.4 138.7 %all-gather.5.cloned.1.call-start = ((), (), s32[]{:S(2)}) async-start(), calls=%async_computation.7 | async-start | bytes 2621440 | tf_op jit(solution)/shard_map/all_gather | solution.py:458
  240.2 22.7 %collective-permute-start.17 = (bf16[16,224,128]{2,1,0:T(8,128)(2,1)S(1)}, bf16[16,224,128]{2,1,0:T(8,128)(2,1)}, u32[]{:S(2)}, u32[]{:S(2)}) collective-permute-start(bf16[16,224,128]{2,1,0:T(8,128)(2,1)S(1)} %get-tuple-element.44), channel_id=1, source_target_pairs={{0,2},{1,3},{2,0},{3,1},{4,6},{5,7},{6,4},{7,5},{8,10},{9,11},{10,... | collective-permute-start | bytes 2752520 | tf_op jit(solution)/shard_map/ppermute | solution.py:384
  262.9 22.4 %collective-permute-start.18 = (bf16[16,224,128]{2,1,0:T(8,128)(2,1)S(1)}, bf16[16,224,128]{2,1,0:T(8,128)(2,1)}, u32[]{:S(2)}, u32[]{:S(2)}) collective-permute-start(bf16[16,224,128]{2,1,0:T(8,128)(2,1)S(1)} %get-tuple-element.45), channel_id=1, source_target_pairs={{0,2},{1,3},{2,0},{3,1},{4,6},{5,7},{6,4},{7,5},{8,10},{9,11},{10,... | collective-permute-start | bytes 2752520 | tf_op jit(solution)/shard_map/ppermute | solution.py:384
  263.2 26.6 %collective-permute-start.16 = (bf16[16,224,128]{2,1,0:T(8,128)(2,1)}, bf16[16,224,128]{2,1,0:T(8,128)(2,1)}, u32[]{:S(2)}, u32[]{:S(2)}) collective-permute-start(bf16[16,224,128]{2,1,0:T(8,128)(2,1)} %get-tuple-element.64), channel_id=1, source_target_pairs={{0,1},{1,0},{2,3},{3,2},{4,5},{5,4},{6,7},{7,6},{8,9},{9,8},{10,11... | collective-permute-start | bytes 2752520 | tf_op jit(solution)/shard_map/ppermute | solution.py:382
  263.7 27.5 %collective-permute-start.15 = (bf16[16,224,128]{2,1,0:T(8,128)(2,1)}, bf16[16,224,128]{2,1,0:T(8,128)(2,1)S(1)}, u32[]{:S(2)}, u32[]{:S(2)}) collective-permute-start(bf16[16,224,128]{2,1,0:T(8,128)(2,1)} %get-tuple-element.65), channel_id=1, source_target_pairs={{0,1},{1,0},{2,3},{3,2},{4,5},{5,4},{6,7},{7,6},{8,9},{9,8},{10,11... | collective-permute-start | bytes 2752520 | tf_op jit(solution)/shard_map/ppermute | solution.py:382
  263.7 55.1 %collective-permute-start.19 = (bf16[16,224,128]{2,1,0:T(8,128)(2,1)}, bf16[16,224,128]{2,1,0:T(8,128)(2,1)}, u32[]{:S(2)}, u32[]{:S(2)}) collective-permute-start(bf16[16,224,128]{2,1,0:T(8,128)(2,1)} %collective-permute-done.17), channel_id=1, source_target_pairs={{0,16},{16,0},{1,17},{17,1},{2,18},{18,2},{3,19},{19,3},{4,20},{20... | collective-permute-start | bytes 2752520 | tf_op jit(solution)/shard_map/ppermute | solution.py:386
  285.3 36.7 %collective-permute-start.20 = (bf16[16,224,128]{2,1,0:T(8,128)(2,1)}, bf16[16,224,128]{2,1,0:T(8,128)(2,1)}, u32[]{:S(2)}, u32[]{:S(2)}) collective-permute-start(bf16[16,224,128]{2,1,0:T(8,128)(2,1)} %collective-permute-done.18), channel_id=1, source_target_pairs={{0,16},{16,0},{1,17},{17,1},{2,18},{18,2},{3,19},{19,3},{4,20},{20... | collective-permute-start | bytes 2752520 | tf_op jit(solution)/shard_map/ppermute | solution.py:386
  331.4 90.3 %all-gather.3.cloned.1.call-start = ((), (), s32[]{:S(2)}) async-start(), calls=%async_computation.6 | async-start | bytes 2621440 | tf_op jit(solution)/shard_map/all_gather | solution.py:458
  439.0 2.4 collective-permute-start.21
  442.6 18.1 %collective-permute-start.22 = (bf16[1024,224]{1,0:T(8,128)(2,1)S(1)}, bf16[1024,224]{1,0:T(8,128)(2,1)S(1)}, u32[]{:S(2)}, u32[]{:S(2)}) collective-permute-start(bf16[1024,224]{1,0:T(8,128)(2,1)S(1)} %add_convert_fusion), channel_id=1, source_target_pairs={{0,2},{1,3},{2,0},{3,1},{4,6},{5,7},{6,4},{7,5},{8,10},{9,11},{10,... | collective-permute-start | bytes 1376264 | tf_op jit(solution)/shard_map/ppermute | solution.py:384
  460.7 2.0 collective-permute-start.23
Sparse Core Ops, SparseCore 0:
  149.2 76.1 reduce-scatter.2
  236.5 76.0 reduce-scatter.4
  331.5 43.5 all-gather.4
  376.5 45.1 all-gather.2

commit v7 on v6

--- a/solution.py
+++ b/solution.py
@@ -65,7 +65,7 @@
 
 
 def cost(flops, moved):
-    return pl.CostEstimate(flops=4 * flops, bytes_accessed=4 * moved, transcendentals=0)
+    return pl.CostEstimate(flops=flops, bytes_accessed=moved, transcendentals=0)
 
 
 def split3(value):
@@ -264,8 +264,8 @@
 
 
 def partial_kernel(low, high, base, quarter, near_ref, far_ref, *refs):
-    pairs, out = [refs[j : j + 2] for j in range(0, 8, 2)], refs[-1]
-    width = pairs[0][0].shape[1]
+    own, stacked, out = refs[:2], refs[2:-1], refs[-1]
+    experts, width, _ = own[0].shape
 
     @pl.loop(0, BLOCK // TILE)
     def _(part):
@@ -274,8 +274,10 @@
 
         def add(e, kept):
             total = 0.0
-            for k, pair in enumerate(pairs):
-                weight = jnp.concatenate([pair[0][e], pair[1][e]], axis=1)
+            for k in range(4):
+                pair = stacked[k - 1] if k else own
+                pair = [pair[e], pair[experts + e]] if k else [pair[0][e], pair[1][e]]
+                weight = jnp.concatenate(pair, axis=1)
                 rows_ref, at = (near_ref, far_ref)[k // 2], k % 2 * LANES
                 rows = rows_ref[here, at : at + width]
                 total += dot(rows, weight, ((1,), (0,)))
@@ -290,7 +292,7 @@
     rows = near.shape[0]
     experts, width, _ = w_gate.shape
     own = pl.BlockSpec((experts, width, UNITS), lambda i, lo, hi, b, q: (0, 0, 2 * q[0] + f))
-    block = pl.BlockSpec((experts, width, UNITS), lambda i, *_: (0, 0, 0))
+    block = pl.BlockSpec((2 * experts, width, UNITS), lambda i, *_: (0, 0, 0))
     return pl.pallas_call(
         partial_kernel,
         grid_spec=pltpu.PrefetchScalarGridSpec(
@@ -309,7 +311,7 @@
 
 def down_kernel(half, low, high, base, onehot_ref, hidden, start, *refs):
     weights, (out, total_ref, value_ref) = refs[:-3], refs[-3:]
-    width = weights[0].shape[2]
+    width = weights[0].shape[1]
     j = pl.program_id(0)
 
     @pl.when(j == 0)
@@ -326,7 +328,7 @@
         def _(e):
             mine = mine_of(base, e, i * TILE)
             for k, weight in enumerate(weights):
-                value = dot(units, weight[e], ((1,), (0,)))
+                value = dot(units, weight[e], ((1,), (1,)))
                 at = slice(k * LANES, k * LANES + width)
                 value_ref[here, at] = jnp.where(
                     mine, value, value_ref[here, at].astype(F32)
@@ -407,8 +409,13 @@
     spans = spans_of(base, rows)
     which = my_quarter.astype(jnp.int32).reshape(1)
 
-    def cut(w, q, f):
-        return lax.dynamic_slice_in_dim(w, q * quarter + f * UNITS, UNITS, 2)
+    def cut(n, q):
+        if n == 2:
+            return lax.dynamic_slice_in_dim(w_down, q * quarter, quarter, 2)
+        at = q * quarter + n * UNITS
+        return jnp.concatenate(
+            [lax.dynamic_slice_in_dim(w, at, UNITS, 2) for w in (w_gate, w_up)], axis=0
+        )
 
     def after(value, *others):
         return lax.optimization_barrier((value, *others))[0]
@@ -418,22 +425,18 @@
     far_rows = sort_more(onehot, [far, to_twin(far)])
     scale = lax.dynamic_slice_in_dim(scale, (me // 4) * (rows // places), rows // places, 0)
 
-    held, crossed = [], []
-    for n, (f, w) in enumerate(
-        ((0, w_gate), (0, w_up), (1, w_gate), (1, w_up), (0, w_down), (1, w_down))
-    ):
-        piece = cut(w, cross_quarter, f)
-        if n > 1:
-            piece = after(piece, far_rows, crossed[n - 1], *[pieces[2] for pieces in held[:2]])
-        crossed.append(to_cross(piece))
-        beside = to_plane(crossed[n]) if n > 1 else to_other(cut(w, other_quarter, f))
-        held.append((to_twin(cut(w, twin_quarter, f)), crossed[n], beside))
-    weave = lambda pair: [piece for both in zip(*pair) for piece in both]
+    held = []
+    for n in range(3):
+        piece = cut(n, cross_quarter)
+        if n:
+            piece = after(piece, far_rows, *held[-1][1:])
+        across_x = to_cross(piece)
+        beside = to_plane(across_x) if n else to_other(cut(n, other_quarter))
+        held.append((to_twin(cut(n, twin_quarter)), across_x, beside))
 
     units = []
     for f in range(2):
-        pieces = weave(held[2 * f : 2 * f + 2])
-        later = partial_sums(f, spans, base, which, near_rows, far_rows, w_gate, w_up, pieces)
+        later = partial_sums(f, spans, base, which, near_rows, far_rows, w_gate, w_up, held[f])
         sums = lax.psum_scatter(
             later, "ep", scatter_dimension=0, axis_index_groups=line, tiled=True
         ).astype(F32)
@@ -443,26 +446,18 @@
         after(across[:experts], later)[:, :, None], (experts, size * count, 128)
     )
     columns = scatter_rows(spans, place, rows)
-    turned = weave(held[4:])
-    turned = [
-        jnp.concatenate([jnp.swapaxes(piece, 1, 2) for piece in turned[k : k + 2]], axis=1)
-        for k in (0, 2, 4)
-    ]
-    turned = [
-        jnp.swapaxes(lax.dynamic_slice_in_dim(w_down, my_quarter * quarter, quarter, 2), 1, 2)
-    ] + turned
-    turned = after(turned, later)
-    units, columns, turned = lax.optimization_barrier((units, columns, turned))
+    pieces = [after(cut(2, my_quarter), later), *held[2]]
+    units, columns, pieces = lax.optimization_barrier((units, columns, pieces))
     units = jnp.concatenate(units, axis=1).reshape(-1, BLOCK, 2 * UNITS)
     first, second = (
         lax.all_gather(units[half], "ep", axis=0, axis_index_groups=line, tiled=True)
         for half in range(2)
     )
     far_mix = lambda half, hidden, start, dtype: down_and_mix(
-        half, spans, base, columns, hidden, start, turned[2:], dtype
+        half, spans, base, columns, hidden, start, pieces[2:], dtype
     )
     near_mix = lambda half, hidden, start, dtype: down_and_mix(
-        half, spans, base, columns, hidden, start, turned[:2], dtype
+        half, spans, base, columns, hidden, start, pieces[:2], dtype
     )
     far, near = far_mix(0, first, None, F32), near_mix(0, first, None, F32)
     second, far, near = lax.optimization_barrier((second, far, near))

time: 494 us -> 518 us (1.049)
  waiting for transfers between devices: 223 us -> 258 us
  local copies, waits for them, and re-layouts: 36.5 us -> 27 us
    ppermute x8 -> x5, waiting for transfers between devices: 107 us -> 138 us  [fixed_weights(): to_cross = lambda value: lax.ppermute(value, ('parts', 'ep'), cross)]
    ppermute x4 -> x2, waiting for transfers between devices: 22.5 us -> 49.9 us  [fixed_weights(): to_plane = lambda value: lax.ppermute(value, 'parts', [(0, 1), (1, 0)])]
    ppermute x2 -> x1, waiting for transfers between devices: 23.3 us -> 0.01 us  [fixed_weights(): to_other = lambda value: lax.ppermute(value, ('parts', 'ep'), other)]
    all_to_all x1, waiting for transfers between devices: 9.34 us -> 0.91 us  [fixed_weights(): own = lax.all_to_all(parcels, 'ep', split_axis=0, concat_axis=0, tiled=True)]
    ppermute x6 -> x0, local copies, waits for them, and re-layouts: 7.78 us -> none  [the longest x2 2.91 us: fixed_weights(): to_plane = lambda value: lax.ppermute(value, 'parts', [(0, 1), (1, 0)])]
    reduce_scatter x2, waiting for transfers between devices: 0.02 us -> 6.2 us  [fixed_weights(): lax.psum_scatter(later, 'ep', scatter_dimension=0, axis_index_groups=line...]
    dynamic_slice x3 -> x2, local copies, waits for them, and re-layouts: 10.8 us -> 11.4 us  [the longest x1 6.5 us: cut(): lax.dynamic_slice_in_dim(w, at, UNITS, 2)]
  transfers between devices with their start and end apart: 29 -> 20, of which waited for: 15 -> 13; matrix products, arithmetic and copies ran while one was open for 8% -> 5% of each run, Pallas kernels for 27% -> 26%
where the time goes in v7:
time: 518 us; the launch traced here: 516 us
  waiting for transfers between devices  258 us (50%)
  Pallas kernels  170 us (33%)
  local copies, waits for them, and re-layouts  27 us (5%)
  blocking collectives  18.9 us (4%)
  other arithmetic  14.3 us (3%)
  starting transfers between devices  13.7 us (3%)
  between operations  13.4 us (3%)
    ppermute x5, waiting for transfers between devices, fixed_weights(): to_cross = lambda value: lax.ppermute(value, ('parts', 'ep'), cross)  138 us
    pallas_call x4, Pallas kernels, down_and_mix(): pl.pallas_call(kernel, grid_spec=pltpu.PrefetchScalarGridSpec(num_scalar_...  67.1 us
    all_gather x2, waiting for transfers between devices, fixed_weights(): lax.all_gather(units[half], 'ep', axis=0, axis_index_groups=line, tiled=T...  57.5 us
    ppermute x2, waiting for transfers between devices, fixed_weights(): to_plane = lambda value: lax.ppermute(value, 'parts', [(0, 1), (1, 0)])  49.9 us
    pallas_call x2, Pallas kernels, partial_sums(): pl.pallas_call(partial_kernel, grid_spec=pltpu.PrefetchScalarGridSpec(num...  40.4 us
    pallas_call x1, Pallas kernels, sort_rows(): pl.pallas_call(functools.partial(sort_kernel, experts), grid_spec=pltpu.P...  27.3 us
    all_to_all x1, blocking collectives, fixed_weights(): lax.all_to_all(mixed.reshape(size, count, width), 'ep', split_axis=0, con...  18.9 us
    pallas_call x1, Pallas kernels, scatter_rows(): pl.pallas_call(scatter_kernel, grid_spec=pltpu.PrefetchScalarGridSpec(num...  16.4 us
  transfers between devices with their start and end apart: 20, of which 13 were waited for; matrix products, arithmetic and copies ran while one was open for 5% of the time, Pallas kernels for 26%

profile of v7, /device:TPU:15, one launch (start us, length us, event | category | flops | bytes accessed | tf_op | source)
XLA Modules:
  0.0 515.8 jit_solution(9274554677944313804)
XLA Ops:
  6.5 0.7 reduce-precision_convert_fusion.1
  7.2 0.7 convert_convert_fusion
  8.0 1.8 reshape.65
  10.0 1.0 pad_maximum_fusion.5
  11.0 6.6 %all-to-all-start = ((bf16[16,64,256]{2,1,0:T(8,128)(2,1)}), bf16[16,64,256]{2,1,0:T(8,128)(2,1)S(1)}, u32[]{:S(2)}, u32[]{:S(2)}) async-start(bf16[16,64,256]{2,1,0:T(8,128)(2,1)} %pad_maximum_fusion.5), calls=%async_computation | async-start | bytes 1048576 | tf_op jit(solution)/shard_map/all_to_all | solution.py:404
  17.6 6.5 %constant_dynamic-slice_fusion = (bf16[16,224,128]{2,1,0:T(8,128)(2,1)}, bf16[16,224,128]{2,1,0:T(8,128)(2,1)S(1)}, bf16[16,224,128]{2,1,0:T(8,128)(2,1)S(1)}, b...) fusion(bf16[16,224,1024]{2,1,0:T(8,128)(2,1)} %refs_1_.3, ...), kind=kLoop, calls=%fused_computation.33 | loop fusion | bytes 18350100 | tf_op jit(solution)/shard_map/dynamic_slice | solution.py:417
  24.1 1.4 pad_maximum_fusion.1
  26.1 1.4 pad_maximum_fusion.2
  27.5 1.2 collective-permute-start.5
  28.6 1.4 pad_maximum_fusion
  30.5 0.9 all-to-all-done
  31.4 3.6 order.1
  35.1 1.0 collective-permute-start.1
  37.0 27.3 %sort_rows.1 = (bf16[8192,512]{1,0:T(8,128)(2,1)}, f32[8192,128]{1,0:T(8,128)S(1)}, bf16[8192,1024]{1,0:T(8,128)(2,1)}) custom-call(s32[32]{0:T(128)S(1)} %get-tuple-element.78.low.refs_0_, s32[32]{0:T(128)S(1)} %get-tuple-element.77.high.refs_1_, s32[17]{0:T(128)S(1)} %slice_bitcast_fusion.base.refs_2_, s32[16,8,128]{2,1,0:T(8,128)S(1)} %bitcast.26, ...), custom_call_target="tpu_custom_call" | custom-call | flops 8589934592 | bytes 33554432 | tf_op jit(solution)/shard_map/sort_rows/pallas_call | solution.py:184
  64.3 55.0 %collective-permute-done.1.refs_0_ = bf16[1024,256]{1,0:T(8,128)(2,1)S(1)} collective-permute-done((bf16[1024,256]{1,0:T(8,128)(2,1)S(1)}, bf16[1024,256]{1,0:T(8,128)(2,1)S(1)}, u32[]{:S(2)}, u32[]{:S(2)}) %collective-permute-start.1) | collective-permute-done | bytes 524320 | tf_op jit(solution)/shard_map/ppermute | solution.py:386
  119.7 1.5 collective-permute-done.2.refs_1_
  121.3 15.2 %sort_more.1.far_ref = bf16[8192,512]{1,0:T(8,128)(2,1)} custom-call(bf16[8192,1024]{1,0:T(8,128)(2,1)} %get-tuple-element.33.onehot_ref, bf16[1024,256]{1,0:T(8,128)(2,1)S(1)} %collective-permute-done.1.refs_0_, bf16[1024,256]{1,0:T(8,128)(2,1)S(1)} %collective-permute-done.2.refs_1_), custom_call_target="tpu_custom_call" | custom-call | flops 8589934592 | bytes 33554432 | tf_op jit(solution)/shard_map/sort_more/pallas_call | solution.py:221
  136.5 20.8 %partial_sums.2 = bf16[8192,256]{1,0:T(8,128)(2,1)} custom-call(s32[32]{0:T(128)S(1)} %get-tuple-element.78.low.refs_0_, s32[32]{0:T(128)S(1)} %get-tuple-element.77.high.refs_1_, s32[17]{0:T(128)S(1)} %slice_bitcast_fusion.base.refs_2_, s32[1]{0:T(128)} %bitcast.5.quarter, bf16[8192,512]{1,0:T(8,128)(2,1)} %get-tuple-element.32.near_ref, ...), custom_call_target="tpu_custom_call" | custom-call | flops 4294967296 | bytes 16777216 | tf_op jit(solution)/shard_map/partial_sums/pallas_call | solution.py:296
  157.4 1.1 copy-done.5
  159.1 0.8 copy-done.4
  160.5 40.8 %collective-permute-done.7.refs_3_ = bf16[32,224,128]{2,1,0:T(8,128)(2,1)S(1)} collective-permute-done((bf16[32,224,128]{2,1,0:T(8,128)(2,1)S(1)}, bf16[32,224,128]{2,1,0:T(8,128)(2,1)S(1)}, u32[]{:S(2)}, u32[]{:S(2)}) %collective-permute-start.7) | collective-permute-done | bytes 1835040 | tf_op jit(solution)/shard_map/ppermute | solution.py:386
  201.4 41.7 %collective-permute-done.8.refs_4_ = bf16[32,224,128]{2,1,0:T(8,128)(2,1)S(1)} collective-permute-done((bf16[32,224,128]{2,1,0:T(8,128)(2,1)S(1)}, bf16[32,224,128]{2,1,0:T(8,128)(2,1)S(1)}, u32[]{:S(2)}, u32[]{:S(2)}) %collective-permute-start.8) | collective-permute-done | bytes 1835040 | tf_op jit(solution)/shard_map/ppermute | solution.py:388
  243.1 19.6 %partial_sums.3 = bf16[8192,256]{1,0:T(8,128)(2,1)} custom-call(s32[32]{0:T(128)S(1)} %get-tuple-element.78.low.refs_0_, s32[32]{0:T(128)S(1)} %get-tuple-element.77.high.refs_1_, s32[17]{0:T(128)S(1)} %slice_bitcast_fusion.base.refs_2_, s32[1]{0:T(128)} %bitcast.5.quarter, bf16[8192,512]{1,0:T(8,128)(2,1)} %get-tuple-element.32.near_ref, ...), custom_call_target="tpu_custom_call" | custom-call | flops 4294967296 | bytes 16777216 | tf_op jit(solution)/shard_map/partial_sums/pallas_call | solution.py:296
  263.0 4.9 dynamic-slice_bitcast_fusion
  268.6 41.9 %collective-permute-done.10.refs_5_.refs_0_ = bf16[16,224,256]{2,1,0:T(8,128)(2,1)} collective-permute-done((bf16[16,224,256]{2,1,0:T(8,128)(2,1)S(1)}, bf16[16,224,256]{2,1,0:T(8,128)(2,1)}, u32[]{:S(2)}, u32[]{:S(2)}) %collective-permute-start.10) | collective-permute-done | bytes 1835040 | tf_op jit(solution)/shard_map/ppermute | solution.py:386
  310.5 5.7 %broadcast_in_dim.5.place_ref = s32[16,1024,128]{2,1,0:T(8,128)} broadcast(s32[16,1024]{1,0:T(8,128)S(1)} %get-tuple-element.37), dimensions={0,1} | broadcast | bytes 8454144 | tf_op jit(solution)/shard_map/broadcast_in_dim | solution.py:445
  316.2 16.4 %scatter_rows.1.refs_3_.onehot_ref = bf16[1024,8192]{1,0:T(8,128)(2,1)} custom-call(s32[32]{0:T(128)S(1)} %get-tuple-element.78.low.refs_0_, s32[32]{0:T(128)S(1)} %get-tuple-element.77.high.refs_1_, s32[16,1024,128]{2,1,0:T(8,128)} %broadcast_in_dim.5.place_ref), custom_call_target="tpu_custom_call" | custom-call | flops 8388608 | bytes 16777216 | tf_op jit(solution)/shard_map/scatter_rows/pallas_call | solution.py:251
  332.7 1.4 convert_element_type.48
  334.1 6.2 %reduce-scatter.5.cloned.1.call-done = bf16[2048,256]{1,0:T(8,128)(2,1)} async-done(((bf16[8192,256]{1,0:T(8,128)(2,1)}), bf16[2048,256]{1,0:T(8,128)(2,1)}) %reduce-scatter.5.cloned.1.call-update) | async-done | bytes 1048592 | tf_op jit(solution)/shard_map/reduce_scatter | solution.py:440
  340.2 1.4 convert_element_type.50
  341.6 2.0 fusion.3
  343.6 8.3 %collective-permute-done.11.refs_6_.refs_1_ = bf16[16,224,256]{2,1,0:T(8,128)(2,1)} collective-permute-done((bf16[16,224,256]{2,1,0:T(8,128)(2,1)}, bf16[16,224,256]{2,1,0:T(8,128)(2,1)}, u32[]{:S(2)}, u32[]{:S(2)}) %collective-permute-start.11) | collective-permute-done | bytes 1835040 | tf_op jit(solution)/shard_map/ppermute | solution.py:388
  352.1 1.1 fusion.8
  353.8 44.8 %all-gather.5.cloned.1.call-done.refs_4_ = bf16[4096,256]{1,0:T(8,128)(2,1)} async-done(((bf16[1024,256]{1,0:T(8,128)(2,1)}), bf16[4096,256]{1,0:T(8,128)(2,1)}) %all-gather.5.cloned.1.call-update) | async-done | bytes 2097168 | tf_op jit(solution)/shard_map/all_gather | solution.py:453
  398.6 16.7 %down_and_mix.4.start = f32[1024,512]{1,0:T(8,128)} custom-call(s32[32]{0:T(128)} %copy-done.2, s32[32]{0:T(128)} %copy-done.1, s32[17]{0:T(128)} %copy-done.3, bf16[1024,8192]{1,0:T(8,128)(2,1)} %scatter_rows.1.refs_3_.onehot_ref, bf16[4096,256]{1,0:T(8,128)(2,1)} %all-gather.5.cloned.1.call-done.refs_4_, ...), custom_call_target="tpu_custom_call" | custom-call | flops 4294967296 | bytes 8388608 | tf_op jit(solution)/shard_map/down_and_mix/pallas_call | solution.py:352
  415.3 16.7 %down_and_mix.5.start = f32[1024,512]{1,0:T(8,128)} custom-call(s32[32]{0:T(128)} %copy-done.2, s32[32]{0:T(128)} %copy-done.1, s32[17]{0:T(128)} %copy-done.3, bf16[1024,8192]{1,0:T(8,128)(2,1)} %scatter_rows.1.refs_3_.onehot_ref, bf16[4096,256]{1,0:T(8,128)(2,1)} %all-gather.5.cloned.1.call-done.refs_4_, ...), custom_call_target="tpu_custom_call" | custom-call | flops 4294967296 | bytes 8388608 | tf_op jit(solution)/shard_map/down_and_mix/pallas_call | solution.py:352
  432.0 12.7 %all-gather.3.cloned.1.call-done.hidden = bf16[4096,256]{1,0:T(8,128)(2,1)} async-done(((bf16[1024,256]{1,0:T(8,128)(2,1)}), bf16[4096,256]{1,0:T(8,128)(2,1)}) %all-gather.3.cloned.1.call-update) | async-done | bytes 2097168 | tf_op jit(solution)/shard_map/all_gather | solution.py:453
  444.7 16.6 %down_and_mix.6 = bf16[1024,512]{1,0:T(8,128)(2,1)} custom-call(s32[32]{0:T(128)} %copy-done.2, s32[32]{0:T(128)} %copy-done.1, s32[17]{0:T(128)} %copy-done.3, bf16[1024,8192]{1,0:T(8,128)(2,1)} %scatter_rows.1.refs_3_.onehot_ref, bf16[4096,256]{1,0:T(8,128)(2,1)} %all-gather.3.cloned.1.call-done.hidden, f32[1024,512]{1,0:T(8,128)} %down_and_mix.4.start, ...), custom_call_target="tpu_custom_call" | custom-call | flops 4294967296 | bytes 8388608 | tf_op jit(solution)/shard_map/down_and_mix/pallas_call | solution.py:352
  461.3 1.1 slice.71
  462.4 1.0 collective-permute-start.12
  463.4 1.5 collective-permute-done.12
  465.0 1.2 add_convert_fusion
  466.7 17.1 %down_and_mix.7 = f32[1024,512]{1,0:T(8,128)} custom-call(s32[32]{0:T(128)} %copy-done.2, s32[32]{0:T(128)} %copy-done.1, s32[17]{0:T(128)} %copy-done.3, bf16[1024,8192]{1,0:T(8,128)(2,1)} %scatter_rows.1.refs_3_.onehot_ref, bf16[4096,256]{1,0:T(8,128)(2,1)} %all-gather.3.cloned.1.call-done.hidden, f32[1024,512]{1,0:T(8,128)} %down_and_mix.5.start, ...), custom_call_target="tpu_custom_call" | custom-call | flops 4294967296 | bytes 8388608 | tf_op jit(solution)/shard_map/down_and_mix/pallas_call | solution.py:352
  483.8 1.3 slice.97
  485.3 1.8 collective-permute-done.14
  487.1 1.4 fusion.1
  488.5 18.9 %all_to_all.10 = bf16[16,64,224]{2,1,0:T(8,128)(2,1)S(1)} all-to-all(bf16[16,64,224]{2,1,0:T(8,128)(2,1)S(1)} %bitcast.27), channel_id=1, replica_groups=mesh['parts'=2,'ep'=16,'tp'=1] {'ep'}, dimensions={0} | all-to-all | bytes 917504 | tf_op jit(solution)/shard_map/all_to_all | solution.py:473
  507.7 1.6 reshape.70
  (56 shorter events, 6.8 us)
Async XLA Ops:
  11.0 20.4 %all-to-all-start = ((bf16[16,64,256]{2,1,0:T(8,128)(2,1)}), bf16[16,64,256]{2,1,0:T(8,128)(2,1)S(1)}, u32[]{:S(2)}, u32[]{:S(2)}) async-start(bf16[16,64,256]{2,1,0:T(8,128)(2,1)} %pad_maximum_fusion.5), calls=%async_computation | async-start | bytes 1048576 | tf_op jit(solution)/shard_map/all_to_all | solution.py:404
  17.6 315.1 %reduce-scatter.3.cloned.1.call-start = ((), (), s32[]{:S(2)}) async-start(), calls=%async_computation.4 | async-start | bytes 5242880 | tf_op jit(solution)/shard_map/reduce_scatter | solution.py:440
  25.5 110.9 %collective-permute-start.4 = (bf16[32,224,128]{2,1,0:T(8,128)(2,1)}, bf16[32,224,128]{2,1,0:T(8,128)(2,1)S(1)}, u32[]{:S(2)}, u32[]{:S(2)}) collective-permute-start(bf16[32,224,128]{2,1,0:T(8,128)(2,1)} %pad_maximum_fusion.1), channel_id=1, source_target_pairs={{0,2},{1,3},{2,0},{3,1},{4,6},{5,7},{6,4},{7,5},{8,10},{9,11},{10,... | collective-permute-start | bytes 5505032 | tf_op jit(solution)/shard_map/ppermute | solution.py:386
  27.5 109.0 %collective-permute-start.5 = (bf16[32,224,128]{2,1,0:T(8,128)(2,1)}, bf16[32,224,128]{2,1,0:T(8,128)(2,1)}, u32[]{:S(2)}, u32[]{:S(2)}) collective-permute-start(bf16[32,224,128]{2,1,0:T(8,128)(2,1)} %pad_maximum_fusion.2), channel_id=1, source_target_pairs={{0,3},{1,2},{2,1},{3,0},{4,7},{5,6},{6,5},{7,4},{8,11},{9,10},{10,... | collective-permute-start | bytes 5505032 | tf_op jit(solution)/shard_map/ppermute | solution.py:387
  30.1 106.4 %collective-permute-start.3 = (bf16[32,224,128]{2,1,0:T(8,128)(2,1)}, bf16[32,224,128]{2,1,0:T(8,128)(2,1)}, u32[]{:S(2)}, u32[]{:S(2)}) collective-permute-start(bf16[32,224,128]{2,1,0:T(8,128)(2,1)} %pad_maximum_fusion), channel_id=1, source_target_pairs={{0,1},{1,0},{2,3},{3,2},{4,5},{5,4},{6,7},{7,6},{8,9},{9,8},{10,11... | collective-permute-start | bytes 5505032 | tf_op jit(solution)/shard_map/ppermute | solution.py:384
  35.1 1.9 collective-permute-start
  35.1 84.2 %collective-permute-start.1 = (bf16[1024,256]{1,0:T(8,128)(2,1)S(1)}, bf16[1024,256]{1,0:T(8,128)(2,1)S(1)}, u32[]{:S(2)}, u32[]{:S(2)}) collective-permute-start(bf16[1024,256]{1,0:T(8,128)(2,1)S(1)} %bitcast.24), channel_id=1, source_target_pairs={{0,2},{1,3},{2,0},{3,1},{4,6},{5,7},{6,4},{7,5},{8,10},{9,11},{10,... | collective-permute-start | bytes 1572872 | tf_op jit(solution)/shard_map/ppermute | solution.py:386
  36.3 279.9 %copy-start.1 = (s32[32]{0:T(128)}, s32[32]{0:T(128)S(1)}, u32[]{:S(2)}) copy-start(s32[32]{0:T(128)S(1)} %get-tuple-element.77.high.refs_1_) | copy-start | bytes 388
  36.3 279.9 %copy-start.2 = (s32[32]{0:T(128)}, s32[32]{0:T(128)S(1)}, u32[]{:S(2)}) copy-start(s32[32]{0:T(128)S(1)} %get-tuple-element.78.low.refs_0_) | copy-start | bytes 388
  36.3 206.7 %copy-start.3 = (s32[17]{0:T(128)}, s32[17]{0:T(128)S(1)}, u32[]{:S(2)}) copy-start(s32[17]{0:T(128)S(1)} %slice_bitcast_fusion.base.refs_2_) | copy-start | bytes 208
  64.3 72.2 %copy-start = (f32[8192,128]{1,0:T(8,128)}, f32[8192,128]{1,0:T(8,128)S(1)}, u32[]{:S(2)}) copy-start(f32[8192,128]{1,0:T(8,128)S(1)} %get-tuple-element.35) | copy-start | bytes 12582916
  119.3 1.9 collective-permute-start.2
  157.3 1.2 copy-start.5
  157.3 1.5 copy-start.6
  157.3 182.9 %reduce-scatter.5.cloned.1.call-start = ((), (), s32[]{:S(2)}) async-start(), calls=%async_computation.5 | async-start | bytes 5242880 | tf_op jit(solution)/shard_map/reduce_scatter | solution.py:440
  158.7 1.2 copy-start.4
  158.9 42.5 %collective-permute-start.7 = (bf16[32,224,128]{2,1,0:T(8,128)(2,1)S(1)}, bf16[32,224,128]{2,1,0:T(8,128)(2,1)S(1)}, u32[]{:S(2)}, u32[]{:S(2)}) collective-permute-start(bf16[32,224,128]{2,1,0:T(8,128)(2,1)S(1)} %pad_maximum_fusion.4), channel_id=1, source_target_pairs={{0,2},{1,3},{2,0},{3,1},{4,6},{5,7},{6,4},{7,5},{8,10},{9,11},{10,... | collective-permute-start | bytes 5505032 | tf_op jit(solution)/shard_map/ppermute | solution.py:386
  160.1 41.3 %collective-permute-start.6 = (bf16[32,224,128]{2,1,0:T(8,128)(2,1)S(1)}, bf16[32,224,128]{2,1,0:T(8,128)(2,1)S(1)}, u32[]{:S(2)}, u32[]{:S(2)}) collective-permute-start(bf16[32,224,128]{2,1,0:T(8,128)(2,1)S(1)} %pad_maximum_fusion.3), channel_id=1, source_target_pairs={{0,1},{1,0},{2,3},{3,2},{4,5},{5,4},{6,7},{7,6},{8,9},{9,8},{10,11... | collective-permute-start | bytes 5505032 | tf_op jit(solution)/shard_map/ppermute | solution.py:384
  201.4 41.7 %collective-permute-start.8 = (bf16[32,224,128]{2,1,0:T(8,128)(2,1)S(1)}, bf16[32,224,128]{2,1,0:T(8,128)(2,1)S(1)}, u32[]{:S(2)}, u32[]{:S(2)}) collective-permute-start(bf16[32,224,128]{2,1,0:T(8,128)(2,1)S(1)} %collective-permute-done.7.refs_3_), channel_id=1, source_target_pairs={{0,16},{16,0},{1,17},{17,1},{2,18},{18,2},{3,19},{19,3},{4,20},{20... | collective-permute-start | bytes 5505032 | tf_op jit(solution)/shard_map/ppermute | solution.py:388
  262.7 135.9 %all-gather.5.cloned.1.call-start = ((), (), s32[]{:S(2)}) async-start(), calls=%async_computation.7 | async-start | bytes 2621440 | tf_op jit(solution)/shard_map/all_gather | solution.py:453
  267.8 42.6 %collective-permute-start.10 = (bf16[16,224,256]{2,1,0:T(8,128)(2,1)S(1)}, bf16[16,224,256]{2,1,0:T(8,128)(2,1)}, u32[]{:S(2)}, u32[]{:S(2)}) collective-permute-start(bf16[16,224,256]{2,1,0:T(8,128)(2,1)S(1)} %get-tuple-element.39), channel_id=1, source_target_pairs={{0,2},{1,3},{2,0},{3,1},{4,6},{5,7},{6,4},{7,5},{8,10},{9,11},{10,... | collective-permute-start | bytes 5505032 | tf_op jit(solution)/shard_map/ppermute | solution.py:386
  268.4 75.2 %collective-permute-start.9 = (bf16[16,224,256]{2,1,0:T(8,128)(2,1)}, bf16[16,224,256]{2,1,0:T(8,128)(2,1)}, u32[]{:S(2)}, u32[]{:S(2)}) collective-permute-start(bf16[16,224,256]{2,1,0:T(8,128)(2,1)} %get-tuple-element.55), channel_id=1, source_target_pairs={{0,1},{1,0},{2,3},{3,2},{4,5},{5,4},{6,7},{7,6},{8,9},{9,8},{10,11... | collective-permute-start | bytes 5505032 | tf_op jit(solution)/shard_map/ppermute | solution.py:384
  310.5 41.4 %collective-permute-start.11 = (bf16[16,224,256]{2,1,0:T(8,128)(2,1)}, bf16[16,224,256]{2,1,0:T(8,128)(2,1)}, u32[]{:S(2)}, u32[]{:S(2)}) collective-permute-start(bf16[16,224,256]{2,1,0:T(8,128)(2,1)} %collective-permute-done.10.refs_5_.refs_0_), channel_id=1, source_target_pairs={{0,16},{16,0},{1,17},{17,1},{2,18},{18,2},{3,19},{19,3},{4,20},{20... | collective-permute-start | bytes 5505032 | tf_op jit(solution)/shard_map/ppermute | solution.py:388
  353.2 91.5 %all-gather.3.cloned.1.call-start = ((), (), s32[]{:S(2)}) async-start(), calls=%async_computation.6 | async-start | bytes 2621440 | tf_op jit(solution)/shard_map/all_gather | solution.py:453
  462.4 2.5 collective-permute-start.12
  466.1 19.0 %collective-permute-start.13 = (bf16[1024,224]{1,0:T(8,128)(2,1)S(1)}, bf16[1024,224]{1,0:T(8,128)(2,1)S(1)}, u32[]{:S(2)}, u32[]{:S(2)}) collective-permute-start(bf16[1024,224]{1,0:T(8,128)(2,1)S(1)} %add_convert_fusion), channel_id=1, source_target_pairs={{0,2},{1,3},{2,0},{3,1},{4,6},{5,7},{6,4},{7,5},{8,10},{9,11},{10,... | collective-permute-start | bytes 1376264 | tf_op jit(solution)/shard_map/ppermute | solution.py:386
  485.1 2.0 collective-permute-start.14
Sparse Core Ops, SparseCore 0:
  157.4 77.0 reduce-scatter.2
  262.8 77.3 reduce-scatter.4
  353.3 45.2 all-gather.4
  400.0 44.6 all-gather.2

commit v8 on v7

--- a/solution.py
+++ b/solution.py
@@ -382,15 +382,12 @@
     twins = [(i, i ^ 1) for i in range(size)]
     cross = [(p * size + i, p * size + (i ^ 2 ^ p)) for p in range(2) for i in range(size)]
     to_twin = lambda value: lax.ppermute(value, "ep", twins)
-    other = [(p * size + i, p * size + (i ^ 3 ^ p)) for p in range(2) for i in range(size)]
     to_cross = lambda value: lax.ppermute(value, ("parts", "ep"), cross)
-    to_other = lambda value: lax.ppermute(value, ("parts", "ep"), other)
     to_plane = lambda value: lax.ppermute(value, "parts", [(0, 1), (1, 0)])
     line = [[4 * p + k for p in range(places)] for k in range(4)]
     my_quarter = me % 4
     twin_quarter = my_quarter ^ 1
     cross_quarter = my_quarter ^ 2 ^ plane
-    other_quarter = cross_quarter ^ 1
 
     note = jnp.concatenate([expert_ids.astype(F32), *split3(gate_weights)], axis=1).astype(BF16)
     fill = LANES - width - note.shape[1]
@@ -425,28 +422,34 @@
     far_rows = sort_more(onehot, [far, to_twin(far)])
     scale = lax.dynamic_slice_in_dim(scale, (me // 4) * (rows // places), rows // places, 0)
 
-    held = []
-    for n in range(3):
-        piece = cut(n, cross_quarter)
-        if n:
-            piece = after(piece, far_rows, *held[-1][1:])
-        across_x = to_cross(piece)
-        beside = to_plane(across_x) if n else to_other(cut(n, other_quarter))
-        held.append((to_twin(cut(n, twin_quarter)), across_x, beside))
-
-    units = []
-    for f in range(2):
-        later = partial_sums(f, spans, base, which, near_rows, far_rows, w_gate, w_up, held[f])
+    def fetch(n, *first):
+        return to_cross(after(cut(n, cross_quarter), *first) if first else cut(n, cross_quarter))
+
+    def group(n, across_x, *first):
+        return (to_twin(cut(n, twin_quarter)), across_x, to_plane(after(across_x, *first)))
+
+    def sums_of(f, held, *first):
+        rows_in = after(far_rows, *first)
+        return partial_sums(f, spans, base, which, near_rows, rows_in, w_gate, w_up, held)
+
+    def units_of(sums):
         sums = lax.psum_scatter(
-            later, "ep", scatter_dimension=0, axis_index_groups=line, tiled=True
+            sums, "ep", scatter_dimension=0, axis_index_groups=line, tiled=True
         ).astype(F32)
-        units.append((jax.nn.silu(sums[:, :UNITS]) * sums[:, UNITS:] * scale).astype(BF16))
+        return (jax.nn.silu(sums[:, :UNITS]) * sums[:, UNITS:] * scale).astype(BF16)
+
+    second = fetch(1, far)
+    third = fetch(2, second)
+    sums = sums_of(0, group(0, fetch(0), near_rows), second)
+    later = sums_of(1, group(1, second, far_rows), sums, third)
+    units = [units_of(sums), units_of(later)]
+    held = group(2, third, later)
 
     place = jnp.broadcast_to(
         after(across[:experts], later)[:, :, None], (experts, size * count, 128)
     )
     columns = scatter_rows(spans, place, rows)
-    pieces = [after(cut(2, my_quarter), later), *held[2]]
+    pieces = [after(cut(2, my_quarter), later), *held]
     units, columns, pieces = lax.optimization_barrier((units, columns, pieces))
     units = jnp.concatenate(units, axis=1).reshape(-1, BLOCK, 2 * UNITS)
     first, second = (

time: 518 us -> 471 us (0.909)
  waiting for transfers between devices: 258 us -> 207 us
    ppermute x5, waiting for transfers between devices: 138 us -> 80 us  [fixed_weights(): to_cross = lambda value: lax.ppermute(value, ('parts', 'ep'), cross)]
    reduce_scatter x2, waiting for transfers between devices: 6.2 us -> 62.1 us  [units_of(): lax.psum_scatter(sums, 'ep', scatter_dimension=0, axis_index_groups=line,...]
    ppermute x2 -> x3, waiting for transfers between devices: 49.9 us -> 0.01 us  [fixed_weights(): to_plane = lambda value: lax.ppermute(value, 'parts', [(0, 1), (1, 0)])]
  transfers between devices with their start and end apart: 20 -> 20, of which waited for: 13 -> 10; matrix products, arithmetic and copies ran while one was open for 5% -> 6% of each run, Pallas kernels for 26% -> 29%
where the time goes in v8:
time: 471 us; the launch traced here: 466 us
  waiting for transfers between devices  207 us (44%)
  Pallas kernels  170 us (36%)
  local copies, waits for them, and re-layouts  27.6 us (6%)
  blocking collectives  18.9 us (4%)
  other arithmetic  15.4 us (3%)
  between operations  13.4 us (3%)
  starting transfers between devices  13.3 us (3%)
    ppermute x5, waiting for transfers between devices, fixed_weights(): to_cross = lambda value: lax.ppermute(value, ('parts', 'ep'), cross)  80 us
    pallas_call x4, Pallas kernels, down_and_mix(): pl.pallas_call(kernel, grid_spec=pltpu.PrefetchScalarGridSpec(num_scalar_...  67.1 us
    reduce_scatter x2, waiting for transfers between devices, units_of(): lax.psum_scatter(sums, 'ep', scatter_dimension=0, axis_index_groups=line,...  62.1 us
    all_gather x2, waiting for transfers between devices, fixed_weights(): lax.all_gather(units[half], 'ep', axis=0, axis_index_groups=line, tiled=T...  55.7 us
    pallas_call x2, Pallas kernels, partial_sums(): pl.pallas_call(partial_kernel, grid_spec=pltpu.PrefetchScalarGridSpec(num...  40 us
    pallas_call x1, Pallas kernels, sort_rows(): pl.pallas_call(functools.partial(sort_kernel, experts), grid_spec=pltpu.P...  27.3 us
    all_to_all x1, blocking collectives, fixed_weights(): lax.all_to_all(mixed.reshape(size, count, width), 'ep', split_axis=0, con...  18.9 us
    pallas_call x1, Pallas kernels, scatter_rows(): pl.pallas_call(scatter_kernel, grid_spec=pltpu.PrefetchScalarGridSpec(num...  16.5 us
  transfers between devices with their start and end apart: 20, of which 10 were waited for; matrix products, arithmetic and copies ran while one was open for 6% of the time, Pallas kernels for 29%

profile of v8, /device:TPU:15, one launch (start us, length us, event | category | flops | bytes accessed | tf_op | source)
XLA Modules:
  0.0 465.8 jit_solution(1520978526960891699)
XLA Ops:
  6.5 0.7 reduce-precision_convert_fusion.1
  8.0 1.8 reshape.65
  10.0 1.0 pad_maximum_fusion.4
  11.0 6.6 %all-to-all-start = ((bf16[16,64,256]{2,1,0:T(8,128)(2,1)}), bf16[16,64,256]{2,1,0:T(8,128)(2,1)S(1)}, u32[]{:S(2)}, u32[]{:S(2)}) async-start(bf16[16,64,256]{2,1,0:T(8,128)(2,1)} %pad_maximum_fusion.4), calls=%async_computation | async-start | bytes 1048576 | tf_op jit(solution)/shard_map/all_to_all | solution.py:401
  17.6 4.8 %constant_dynamic-slice_fusion = (bf16[16,224,128]{2,1,0:T(8,128)(2,1)S(1)}, bf16[16,224,128]{2,1,0:T(8,128)(2,1)S(1)}, bf16[16,224,128]{2,1,0:T(8,128)(2,1)S(1)...) fusion(bf16[16,224,1024]{2,1,0:T(8,128)(2,1)} %refs_1_.3, ...), kind=kLoop, calls=%fused_computation.32 | loop fusion | bytes 14680080 | tf_op jit(solution)/shard_map/dynamic_slice | solution.py:414
  22.4 1.4 pad_maximum_fusion.1
  24.2 1.4 pad_maximum_fusion.2
  25.9 1.4 pad_maximum_fusion
  27.3 4.2 all-to-all-done
  31.5 0.9 collective-permute-start.1
  32.5 3.6 order.1
  36.4 27.3 %sort_rows.1 = (bf16[8192,512]{1,0:T(8,128)(2,1)}, f32[8192,128]{1,0:T(8,128)S(1)}, bf16[8192,1024]{1,0:T(8,128)(2,1)}) custom-call(s32[32]{0:T(128)S(1)} %get-tuple-element.86.low.refs_0_, s32[32]{0:T(128)S(1)} %get-tuple-element.85.high.refs_1_, s32[17]{0:T(128)S(1)} %slice_bitcast_fusion.base.refs_2_, s32[16,8,128]{2,1,0:T(8,128)S(1)} %bitcast.26, ...), custom_call_target="tpu_custom_call" | custom-call | flops 8589934592 | bytes 33554432 | tf_op jit(solution)/shard_map/sort_rows/pallas_call | solution.py:184
  63.7 2.0 copy-done.2
  65.7 14.2 %collective-permute-done.1.refs_0_ = bf16[1024,256]{1,0:T(8,128)(2,1)S(1)} collective-permute-done((bf16[1024,256]{1,0:T(8,128)(2,1)S(1)}, bf16[1024,256]{1,0:T(8,128)(2,1)S(1)}, u32[]{:S(2)}, u32[]{:S(2)}) %collective-permute-start.1) | collective-permute-done | bytes 524320 | tf_op jit(solution)/shard_map/ppermute | solution.py:385
  80.1 1.2 collective-permute-start.2
  81.4 1.5 collective-permute-done.2.refs_1_
  82.9 15.3 %sort_more.1.far_ref = bf16[8192,512]{1,0:T(8,128)(2,1)} custom-call(bf16[8192,1024]{1,0:T(8,128)(2,1)} %get-tuple-element.38.onehot_ref, bf16[1024,256]{1,0:T(8,128)(2,1)S(1)} %collective-permute-done.1.refs_0_, bf16[1024,256]{1,0:T(8,128)(2,1)S(1)} %collective-permute-done.2.refs_1_), custom_call_target="tpu_custom_call" | custom-call | flops 8589934592 | bytes 33554432 | tf_op jit(solution)/shard_map/sort_more/pallas_call | solution.py:221
  98.2 24.0 %collective-permute-done.3.refs_3_ = bf16[32,224,128]{2,1,0:T(8,128)(2,1)S(1)} collective-permute-done((bf16[32,224,128]{2,1,0:T(8,128)(2,1)S(1)}, bf16[32,224,128]{2,1,0:T(8,128)(2,1)S(1)}, u32[]{:S(2)}, u32[]{:S(2)}) %collective-permute-start.3) | collective-permute-done | bytes 1835040 | tf_op jit(solution)/shard_map/ppermute | solution.py:385
  122.2 1.3 copy-done
  123.5 20.3 %partial_sums.2 = bf16[8192,256]{1,0:T(8,128)(2,1)} custom-call(s32[32]{0:T(128)S(1)} %get-tuple-element.86.low.refs_0_, s32[32]{0:T(128)S(1)} %get-tuple-element.85.high.refs_1_, s32[17]{0:T(128)S(1)} %slice_bitcast_fusion.base.refs_2_, s32[1]{0:T(128)} %bitcast.5.quarter, bf16[8192,512]{1,0:T(8,128)(2,1)} %get-tuple-element.37.near_ref, ...), custom_call_target="tpu_custom_call" | custom-call | flops 4294967296 | bytes 16777216 | tf_op jit(solution)/shard_map/partial_sums/pallas_call | solution.py:296
  143.9 1.1 copy-done.6
  145.0 1.4 pad_maximum_fusion.3
  146.5 5.1 %dynamic-slice_bitcast_fusion = (bf16[16,224,256]{2,1,0:T(8,128)(2,1)}, bf16[16,224,256]{2,1,0:T(8,128)(2,1)S(1)}, bf16[16,224,256]{2,1,0:T(8,128)(2,1)}) fusion(bf16[16,1024,224]{1,2,0:T(8,128)(2,1)} %param.11, s32[]{:T(128)S(6)} %select_n.37, s32[]{:T(128)S(6)} %select_n.38, s32[]{:T(128)S(6)} %select_n.42), kind=kLoop, calls=%fused_computation.4 | loop fusion | bytes 11010060 | tf_op jit(solution)/shard_map/dynamic_slice | solution.py:411
  152.2 41.8 %collective-permute-done.7.refs_5_.refs_0_ = bf16[16,224,256]{2,1,0:T(8,128)(2,1)} collective-permute-done((bf16[16,224,256]{2,1,0:T(8,128)(2,1)S(1)}, bf16[16,224,256]{2,1,0:T(8,128)(2,1)}, u32[]{:S(2)}, u32[]{:S(2)}) %collective-permute-start.7) | collective-permute-done | bytes 1835040 | tf_op jit(solution)/shard_map/ppermute | solution.py:385
  194.0 19.7 %partial_sums.3 = bf16[8192,256]{1,0:T(8,128)(2,1)} custom-call(s32[32]{0:T(128)S(1)} %get-tuple-element.86.low.refs_0_, s32[32]{0:T(128)S(1)} %get-tuple-element.85.high.refs_1_, s32[17]{0:T(128)S(1)} %slice_bitcast_fusion.base.refs_2_, s32[1]{0:T(128)} %bitcast.5.quarter, bf16[8192,512]{1,0:T(8,128)(2,1)} %get-tuple-element.37.near_ref, ...), custom_call_target="tpu_custom_call" | custom-call | flops 4294967296 | bytes 16777216 | tf_op jit(solution)/shard_map/partial_sums/pallas_call | solution.py:296
  213.9 0.7 collective-permute-start.10
  214.7 5.6 %broadcast_in_dim.5.place_ref = s32[16,1024,128]{2,1,0:T(8,128)} broadcast(s32[16,1024]{1,0:T(8,128)S(1)} %get-tuple-element.47), dimensions={0,1} | broadcast | bytes 8454144 | tf_op jit(solution)/shard_map/broadcast_in_dim | solution.py:448
  220.3 16.5 %scatter_rows.1.refs_3_.onehot_ref = bf16[1024,8192]{1,0:T(8,128)(2,1)} custom-call(s32[32]{0:T(128)S(1)} %get-tuple-element.86.low.refs_0_, s32[32]{0:T(128)S(1)} %get-tuple-element.85.high.refs_1_, s32[16,1024,128]{2,1,0:T(8,128)} %broadcast_in_dim.5.place_ref), custom_call_target="tpu_custom_call" | custom-call | flops 8388608 | bytes 16777216 | tf_op jit(solution)/shard_map/scatter_rows/pallas_call | solution.py:251
  236.8 1.4 convert_element_type.48
  238.2 62.1 %reduce-scatter.5.cloned.1.call-done = bf16[2048,256]{1,0:T(8,128)(2,1)} async-done(((bf16[8192,256]{1,0:T(8,128)(2,1)}), bf16[2048,256]{1,0:T(8,128)(2,1)}) %reduce-scatter.5.cloned.1.call-update) | async-done | bytes 1048592 | tf_op jit(solution)/shard_map/reduce_scatter | solution.py:436
  300.3 1.4 convert_element_type.50
  301.7 2.0 fusion.3
  303.9 1.0 fusion.8
  305.6 44.1 %all-gather.5.cloned.1.call-done.refs_4_ = bf16[4096,256]{1,0:T(8,128)(2,1)} async-done(((bf16[1024,256]{1,0:T(8,128)(2,1)}), bf16[4096,256]{1,0:T(8,128)(2,1)}) %all-gather.5.cloned.1.call-update) | async-done | bytes 2097168 | tf_op jit(solution)/shard_map/all_gather | solution.py:456
  349.7 17.3 %down_and_mix.4.start = f32[1024,512]{1,0:T(8,128)} custom-call(s32[32]{0:T(128)} %copy-done.4, s32[32]{0:T(128)} %copy-done.3, s32[17]{0:T(128)} %copy-done.5, bf16[1024,8192]{1,0:T(8,128)(2,1)} %scatter_rows.1.refs_3_.onehot_ref, bf16[4096,256]{1,0:T(8,128)(2,1)} %all-gather.5.cloned.1.call-done.refs_4_, ...), custom_call_target="tpu_custom_call" | custom-call | flops 4294967296 | bytes 8388608 | tf_op jit(solution)/shard_map/down_and_mix/pallas_call | solution.py:352
  366.9 17.3 %down_and_mix.5.start = f32[1024,512]{1,0:T(8,128)} custom-call(s32[32]{0:T(128)} %copy-done.4, s32[32]{0:T(128)} %copy-done.3, s32[17]{0:T(128)} %copy-done.5, bf16[1024,8192]{1,0:T(8,128)(2,1)} %scatter_rows.1.refs_3_.onehot_ref, bf16[4096,256]{1,0:T(8,128)(2,1)} %all-gather.5.cloned.1.call-done.refs_4_, ...), custom_call_target="tpu_custom_call" | custom-call | flops 4294967296 | bytes 8388608 | tf_op jit(solution)/shard_map/down_and_mix/pallas_call | solution.py:352
  384.2 11.6 %all-gather.3.cloned.1.call-done.hidden = bf16[4096,256]{1,0:T(8,128)(2,1)} async-done(((bf16[1024,256]{1,0:T(8,128)(2,1)}), bf16[4096,256]{1,0:T(8,128)(2,1)}) %all-gather.3.cloned.1.call-update) | async-done | bytes 2097168 | tf_op jit(solution)/shard_map/all_gather | solution.py:456
  395.8 16.1 %down_and_mix.6 = bf16[1024,512]{1,0:T(8,128)(2,1)} custom-call(s32[32]{0:T(128)} %copy-done.4, s32[32]{0:T(128)} %copy-done.3, s32[17]{0:T(128)} %copy-done.5, bf16[1024,8192]{1,0:T(8,128)(2,1)} %scatter_rows.1.refs_3_.onehot_ref, bf16[4096,256]{1,0:T(8,128)(2,1)} %all-gather.3.cloned.1.call-done.hidden, f32[1024,512]{1,0:T(8,128)} %down_and_mix.4.start, ...), custom_call_target="tpu_custom_call" | custom-call | flops 4294967296 | bytes 8388608 | tf_op jit(solution)/shard_map/down_and_mix/pallas_call | solution.py:352
  411.9 1.1 slice.71
  413.0 1.0 collective-permute-start.12
  414.0 1.5 collective-permute-done.12
  415.5 1.2 add_convert_fusion
  417.3 16.5 %down_and_mix.7 = f32[1024,512]{1,0:T(8,128)} custom-call(s32[32]{0:T(128)} %copy-done.4, s32[32]{0:T(128)} %copy-done.3, s32[17]{0:T(128)} %copy-done.5, bf16[1024,8192]{1,0:T(8,128)(2,1)} %scatter_rows.1.refs_3_.onehot_ref, bf16[4096,256]{1,0:T(8,128)(2,1)} %all-gather.3.cloned.1.call-done.hidden, f32[1024,512]{1,0:T(8,128)} %down_and_mix.5.start, ...), custom_call_target="tpu_custom_call" | custom-call | flops 4294967296 | bytes 8388608 | tf_op jit(solution)/shard_map/down_and_mix/pallas_call | solution.py:352
  433.8 1.3 slice.97
  435.3 1.8 collective-permute-done.14
  437.0 1.4 fusion.1
  438.4 18.9 %all_to_all.10 = bf16[16,64,224]{2,1,0:T(8,128)(2,1)S(1)} all-to-all(bf16[16,64,224]{2,1,0:T(8,128)(2,1)S(1)} %bitcast.27), channel_id=1, replica_groups=mesh['parts'=2,'ep'=16,'tp'=1] {'ep'}, dimensions={0} | all-to-all | bytes 917504 | tf_op jit(solution)/shard_map/all_to_all | solution.py:476
  457.6 1.6 reshape.70
  (57 shorter events, 5.2 us)
Async XLA Ops:
  11.0 20.5 %all-to-all-start = ((bf16[16,64,256]{2,1,0:T(8,128)(2,1)}), bf16[16,64,256]{2,1,0:T(8,128)(2,1)S(1)}, u32[]{:S(2)}, u32[]{:S(2)}) async-start(bf16[16,64,256]{2,1,0:T(8,128)(2,1)} %pad_maximum_fusion.4), calls=%async_computation | async-start | bytes 1048576 | tf_op jit(solution)/shard_map/all_to_all | solution.py:401
  17.5 219.3 %reduce-scatter.3.cloned.1.call-start = ((), (), s32[]{:S(2)}) async-start(), calls=%async_computation.4 | async-start | bytes 5242880 | tf_op jit(solution)/shard_map/reduce_scatter | solution.py:436
  23.8 98.4 %collective-permute-start.4 = (bf16[32,224,128]{2,1,0:T(8,128)(2,1)}, bf16[32,224,128]{2,1,0:T(8,128)(2,1)S(1)}, u32[]{:S(2)}, u32[]{:S(2)}) collective-permute-start(bf16[32,224,128]{2,1,0:T(8,128)(2,1)} %pad_maximum_fusion.1), channel_id=1, source_target_pairs={{0,1},{1,0},{2,3},{3,2},{4,5},{5,4},{6,7},{7,6},{8,9},{9,8},{10,11... | collective-permute-start | bytes 5505032 | tf_op jit(solution)/shard_map/ppermute | solution.py:384
  25.6 54.6 %collective-permute-start.5 = (bf16[32,224,128]{2,1,0:T(8,128)(2,1)}, bf16[32,224,128]{2,1,0:T(8,128)(2,1)}, u32[]{:S(2)}, u32[]{:S(2)}) collective-permute-start(bf16[32,224,128]{2,1,0:T(8,128)(2,1)} %pad_maximum_fusion.2), channel_id=1, source_target_pairs={{0,2},{1,3},{2,0},{3,1},{4,6},{5,7},{6,4},{7,5},{8,10},{9,11},{10,... | collective-permute-start | bytes 5505032 | tf_op jit(solution)/shard_map/ppermute | solution.py:385
  31.5 4.8 %collective-permute-start = (bf16[1024,256]{1,0:T(8,128)(2,1)S(1)}, bf16[1024,256]{1,0:T(8,128)(2,1)S(1)}, u32[]{:S(2)}, u32[]{:S(2)}) collective-permute-start(bf16[1024,256]{1,0:T(8,128)(2,1)S(1)} %bitcast.22), channel_id=1, source_target_pairs={{0,1},{1,0},{2,3},{3,2},{4,5},{5,4},{6,7},{7,6},{8,9},{9,8},{10,11... | collective-permute-start | bytes 1572872 | tf_op jit(solution)/shard_map/ppermute | solution.py:384
  31.5 48.3 %collective-permute-start.1 = (bf16[1024,256]{1,0:T(8,128)(2,1)S(1)}, bf16[1024,256]{1,0:T(8,128)(2,1)S(1)}, u32[]{:S(2)}, u32[]{:S(2)}) collective-permute-start(bf16[1024,256]{1,0:T(8,128)(2,1)S(1)} %bitcast.23), channel_id=1, source_target_pairs={{0,2},{1,3},{2,0},{3,1},{4,6},{5,7},{6,4},{7,5},{8,10},{9,11},{10,... | collective-permute-start | bytes 1572872 | tf_op jit(solution)/shard_map/ppermute | solution.py:385
  36.3 184.0 %copy-start.3 = (s32[32]{0:T(128)}, s32[32]{0:T(128)S(1)}, u32[]{:S(2)}) copy-start(s32[32]{0:T(128)S(1)} %get-tuple-element.85.high.refs_1_) | copy-start | bytes 388
  36.3 184.0 %copy-start.4 = (s32[32]{0:T(128)}, s32[32]{0:T(128)S(1)}, u32[]{:S(2)}) copy-start(s32[32]{0:T(128)S(1)} %get-tuple-element.86.low.refs_0_) | copy-start | bytes 388
  36.3 157.6 %copy-start.5 = (s32[17]{0:T(128)}, s32[17]{0:T(128)S(1)}, u32[]{:S(2)}) copy-start(s32[17]{0:T(128)S(1)} %slice_bitcast_fusion.base.refs_2_) | copy-start | bytes 208
  36.3 43.5 %copy-start.7 = (bf16[32,224,128]{2,1,0:T(8,128)(2,1)S(1)}, bf16[32,224,128]{2,1,0:T(8,128)(2,1)}, u32[]{:S(2)}) copy-start(bf16[32,224,128]{2,1,0:T(8,128)(2,1)} %pad_maximum_fusion) | copy-start | bytes 5505028
  63.7 2.0 copy-start.2
  79.9 42.3 %collective-permute-start.3 = (bf16[32,224,128]{2,1,0:T(8,128)(2,1)S(1)}, bf16[32,224,128]{2,1,0:T(8,128)(2,1)S(1)}, u32[]{:S(2)}, u32[]{:S(2)}) collective-permute-start(bf16[32,224,128]{2,1,0:T(8,128)(2,1)S(1)} %copy-done.7), channel_id=1, source_target_pairs={{0,2},{1,3},{2,0},{3,1},{4,6},{5,7},{6,4},{7,5},{8,10},{9,11},{10,... | collective-permute-start | bytes 5505032 | tf_op jit(solution)/shard_map/ppermute | solution.py:385
  80.1 43.4 %collective-permute-start.6 = (bf16[32,224,128]{2,1,0:T(8,128)(2,1)}, bf16[32,224,128]{2,1,0:T(8,128)(2,1)S(1)}, u32[]{:S(2)}, u32[]{:S(2)}) collective-permute-start(bf16[32,224,128]{2,1,0:T(8,128)(2,1)} %collective-permute-done.5.refs_3_), channel_id=1, source_target_pairs={{0,16},{16,0},{1,17},{17,1},{2,18},{18,2},{3,19},{19,3},{4,20},{20... | collective-permute-start | bytes 5505032 | tf_op jit(solution)/shard_map/ppermute | solution.py:386
  80.1 2.8 collective-permute-start.2
  122.2 1.3 copy-start
  143.8 1.2 copy-start.6
  143.8 156.5 %reduce-scatter.5.cloned.1.call-start = ((), (), s32[]{:S(2)}) async-start(), calls=%async_computation.5 | async-start | bytes 5242880 | tf_op jit(solution)/shard_map/reduce_scatter | solution.py:436
  146.4 47.6 %collective-permute-start.8 = (bf16[32,224,128]{2,1,0:T(8,128)(2,1)}, bf16[32,224,128]{2,1,0:T(8,128)(2,1)S(1)}, u32[]{:S(2)}, u32[]{:S(2)}) collective-permute-start(bf16[32,224,128]{2,1,0:T(8,128)(2,1)} %pad_maximum_fusion.3), channel_id=1, source_target_pairs={{0,1},{1,0},{2,3},{3,2},{4,5},{5,4},{6,7},{7,6},{8,9},{9,8},{10,11... | collective-permute-start | bytes 5505032 | tf_op jit(solution)/shard_map/ppermute | solution.py:384
  146.5 5.6 %copy-start.1 = (bf16[32,224,128]{2,1,0:T(8,128)(2,1)S(1)}, bf16[32,224,128]{2,1,0:T(8,128)(2,1)}, u32[]{:S(2)}) copy-start(bf16[32,224,128]{2,1,0:T(8,128)(2,1)} %copy-done) | copy-start | bytes 5505028
  151.5 42.4 %collective-permute-start.7 = (bf16[16,224,256]{2,1,0:T(8,128)(2,1)S(1)}, bf16[16,224,256]{2,1,0:T(8,128)(2,1)}, u32[]{:S(2)}, u32[]{:S(2)}) collective-permute-start(bf16[16,224,256]{2,1,0:T(8,128)(2,1)S(1)} %get-tuple-element.44), channel_id=1, source_target_pairs={{0,2},{1,3},{2,0},{3,1},{4,6},{5,7},{6,4},{7,5},{8,10},{9,11},{10,... | collective-permute-start | bytes 5505032 | tf_op jit(solution)/shard_map/ppermute | solution.py:385
  152.1 41.9 %collective-permute-start.9 = (bf16[32,224,128]{2,1,0:T(8,128)(2,1)S(1)}, bf16[32,224,128]{2,1,0:T(8,128)(2,1)S(1)}, u32[]{:S(2)}, u32[]{:S(2)}) collective-permute-start(bf16[32,224,128]{2,1,0:T(8,128)(2,1)S(1)} %copy-done.1), channel_id=1, source_target_pairs={{0,16},{16,0},{1,17},{17,1},{2,18},{18,2},{3,19},{19,3},{4,20},{20... | collective-permute-start | bytes 5505032 | tf_op jit(solution)/shard_map/ppermute | solution.py:386
  213.7 136.0 %all-gather.5.cloned.1.call-start = ((), (), s32[]{:S(2)}) async-start(), calls=%async_computation.7 | async-start | bytes 2621440 | tf_op jit(solution)/shard_map/all_gather | solution.py:456
  213.9 89.7 %collective-permute-start.10 = (bf16[16,224,256]{2,1,0:T(8,128)(2,1)}, bf16[16,224,256]{2,1,0:T(8,128)(2,1)}, u32[]{:S(2)}, u32[]{:S(2)}) collective-permute-start(bf16[16,224,256]{2,1,0:T(8,128)(2,1)} %get-tuple-element.63), channel_id=1, source_target_pairs={{0,1},{1,0},{2,3},{3,2},{4,5},{5,4},{6,7},{7,6},{8,9},{9,8},{10,11... | collective-permute-start | bytes 5505032 | tf_op jit(solution)/shard_map/ppermute | solution.py:384
  214.7 89.0 %collective-permute-start.11 = (bf16[16,224,256]{2,1,0:T(8,128)(2,1)}, bf16[16,224,256]{2,1,0:T(8,128)(2,1)}, u32[]{:S(2)}, u32[]{:S(2)}) collective-permute-start(bf16[16,224,256]{2,1,0:T(8,128)(2,1)} %collective-permute-done.7.refs_5_.refs_0_), channel_id=1, source_target_pairs={{0,16},{16,0},{1,17},{17,1},{2,18},{18,2},{3,19},{19,3},{4,20},{20... | collective-permute-start | bytes 5505032 | tf_op jit(solution)/shard_map/ppermute | solution.py:386
  305.0 90.8 %all-gather.3.cloned.1.call-start = ((), (), s32[]{:S(2)}) async-start(), calls=%async_computation.6 | async-start | bytes 2621440 | tf_op jit(solution)/shard_map/all_gather | solution.py:456
  413.0 2.5 collective-permute-start.12
  416.7 18.4 %collective-permute-start.13 = (bf16[1024,224]{1,0:T(8,128)(2,1)S(1)}, bf16[1024,224]{1,0:T(8,128)(2,1)S(1)}, u32[]{:S(2)}, u32[]{:S(2)}) collective-permute-start(bf16[1024,224]{1,0:T(8,128)(2,1)S(1)} %add_convert_fusion), channel_id=1, source_target_pairs={{0,2},{1,3},{2,0},{3,1},{4,6},{5,7},{6,4},{7,5},{8,10},{9,11},{10,... | collective-permute-start | bytes 1376264 | tf_op jit(solution)/shard_map/ppermute | solution.py:385
  435.1 2.0 collective-permute-start.14
Sparse Core Ops, SparseCore 0:
  144.0 76.6 reduce-scatter.2
  223.0 77.2 reduce-scatter.4
  305.1 44.5 all-gather.4
  351.1 44.6 all-gather.2

commit v9 on v8

--- a/solution.py
+++ b/solution.py
@@ -264,8 +264,8 @@
 
 
 def partial_kernel(low, high, base, quarter, near_ref, far_ref, *refs):
-    own, stacked, out = refs[:2], refs[2:-1], refs[-1]
-    experts, width, _ = own[0].shape
+    pairs, out = [refs[j : j + 2] for j in range(0, 8, 2)], refs[-1]
+    width = pairs[0][0].shape[1]
 
     @pl.loop(0, BLOCK // TILE)
     def _(part):
@@ -274,10 +274,8 @@
 
         def add(e, kept):
             total = 0.0
-            for k in range(4):
-                pair = stacked[k - 1] if k else own
-                pair = [pair[e], pair[experts + e]] if k else [pair[0][e], pair[1][e]]
-                weight = jnp.concatenate(pair, axis=1)
+            for k, pair in enumerate(pairs):
+                weight = jnp.concatenate([pair[0][e], pair[1][e]], axis=1)
                 rows_ref, at = (near_ref, far_ref)[k // 2], k % 2 * LANES
                 rows = rows_ref[here, at : at + width]
                 total += dot(rows, weight, ((1,), (0,)))
@@ -292,7 +290,7 @@
     rows = near.shape[0]
     experts, width, _ = w_gate.shape
     own = pl.BlockSpec((experts, width, UNITS), lambda i, lo, hi, b, q: (0, 0, 2 * q[0] + f))
-    block = pl.BlockSpec((2 * experts, width, UNITS), lambda i, *_: (0, 0, 0))
+    block = pl.BlockSpec((experts, width, UNITS), lambda i, *_: (0, 0, 0))
     return pl.pallas_call(
         partial_kernel,
         grid_spec=pltpu.PrefetchScalarGridSpec(
@@ -309,7 +307,7 @@
     )(*spans, base, quarter, near, far, w_gate, w_up, *pieces)
 
 
-def down_kernel(half, low, high, base, onehot_ref, hidden, start, *refs):
+def down_kernel(low, high, base, block, onehot_ref, up_ref, down_ref, start, *refs):
     weights, (out, total_ref, value_ref) = refs[:-3], refs[-3:]
     width = weights[0].shape[1]
     j = pl.program_id(0)
@@ -319,43 +317,50 @@
         total_ref[...] = jnp.zeros_like(total_ref) if start is None else start[...]
         value_ref[...] = jnp.zeros_like(value_ref)
 
-    for part in range(BLOCK // TILE):
-        i = (2 * j + half) * (BLOCK // TILE) + part
-        here = slice(part * TILE, (part + 1) * TILE)
-        units = hidden[here, :]
-
-        @pl.loop(low[i], high[i])
-        def _(e):
-            mine = mine_of(base, e, i * TILE)
-            for k, weight in enumerate(weights):
-                value = dot(units, weight[e], ((1,), (1,)))
-                at = slice(k * LANES, k * LANES + width)
-                value_ref[here, at] = jnp.where(
-                    mine, value, value_ref[here, at].astype(F32)
-                ).astype(BF16)
-
-    total_ref[...] += dot(onehot_ref[...], value_ref[...], ((1,), (0,)))
+    @pl.when(block[2] != 0)
+    def _():
+        for part in range(BLOCK // TILE):
+            i = (2 * block[0] + j) * (BLOCK // TILE) + part
+            here = slice(part * TILE, (part + 1) * TILE)
+            units = jnp.where(block[1] != 0, up_ref[here, :], down_ref[here, :])
+
+            @pl.loop(low[i], high[i])
+            def _(e):
+                mine = mine_of(base, e, i * TILE)
+                for k, weight in enumerate(weights):
+                    value = dot(units, weight[e], ((1,), (1,)))
+                    at = slice(k * LANES, k * LANES + width)
+                    value_ref[here, at] = jnp.where(
+                        mine, value, value_ref[here, at].astype(F32)
+                    ).astype(BF16)
+
+        total_ref[...] += dot(onehot_ref[...], value_ref[...], ((1,), (0,)))
 
     @pl.when(j == pl.num_programs(0) - 1)
     def _():
         out[...] = total_ref[...].astype(out.dtype)
 
 
-def down_and_mix(half, spans, base, onehot, hidden, start, weights, dtype):
-    rows, units = hidden.shape
+def down_and_mix(spans, base, block, onehot, hidden, start, at, weights, dtype):
+    rows, units = hidden[0].shape
     count, tokens = len(weights), onehot.shape[0]
-    block = pl.BlockSpec((BLOCK, units), lambda j, *_: (j, 0))
+    some = pl.BlockSpec((BLOCK, units), lambda j, *_: (j, 0))
     whole = pl.BlockSpec((tokens, count * LANES), lambda j, *_: (0, 0))
-    kernel = functools.partial(down_kernel, half)
+    kernel = down_kernel
     if start is None:
-        kernel = lambda *refs: down_kernel(half, *refs[:5], None, *refs[5:])
+        kernel = lambda *refs: down_kernel(*refs[:7], None, *refs[7:])
     return pl.pallas_call(
         kernel,
         grid_spec=pltpu.PrefetchScalarGridSpec(
-            num_scalar_prefetch=3,
+            num_scalar_prefetch=4,
             grid=(rows // BLOCK,),
-            in_specs=[pl.BlockSpec((tokens, BLOCK), lambda j, *_: (0, 2 * j + half)), block]
-            + ([] if start is None else [whole])
+            in_specs=[
+                pl.BlockSpec((tokens, BLOCK), lambda j, lo, hi, b, k: (0, 2 * k[0] + j)),
+                some,
+                some,
+            ]
+            + [pl.BlockSpec((tokens, count * LANES), lambda j, *_: (0, at // count))]
+            * (start is not None)
             + [pl.BlockSpec(w.shape, lambda j, *_: (0, 0, 0)) for w in weights],
             out_specs=whole,
             scratch_shapes=[
@@ -367,7 +372,7 @@
         compiler_params=params(56),
         cost_estimate=cost(2 * rows * tokens * LANES * count, 2 * rows * tokens),
         name="down_and_mix",
-    )(*spans, base, onehot, hidden, *([] if start is None else [start]), *weights)
+    )(*spans, base, block, onehot, *hidden, *([] if start is None else [start]), *weights)
 
 
 def fixed_weights(size, tokens, expert_ids, gate_weights, w_gate, w_up, w_down):
@@ -407,12 +412,10 @@
     which = my_quarter.astype(jnp.int32).reshape(1)
 
     def cut(n, q):
-        if n == 2:
+        if n == 4:
             return lax.dynamic_slice_in_dim(w_down, q * quarter, quarter, 2)
-        at = q * quarter + n * UNITS
-        return jnp.concatenate(
-            [lax.dynamic_slice_in_dim(w, at, UNITS, 2) for w in (w_gate, w_up)], axis=0
-        )
+        at = q * quarter + n // 2 * UNITS
+        return lax.dynamic_slice_in_dim((w_gate, w_up)[n % 2], at, UNITS, 2)
 
     def after(value, *others):
         return lax.optimization_barrier((value, *others))[0]
@@ -422,14 +425,16 @@
     far_rows = sort_more(onehot, [far, to_twin(far)])
     scale = lax.dynamic_slice_in_dim(scale, (me // 4) * (rows // places), rows // places, 0)
 
-    def fetch(n, *first):
-        return to_cross(after(cut(n, cross_quarter), *first) if first else cut(n, cross_quarter))
-
-    def group(n, across_x, *first):
-        return (to_twin(cut(n, twin_quarter)), across_x, to_plane(after(across_x, *first)))
-
-    def sums_of(f, held, *first):
+    crossed = [to_cross(cut(0, cross_quarter)), to_cross(cut(1, cross_quarter))]
+    for n in range(2, 5):
+        crossed.append(to_cross(after(cut(n, cross_quarter), far, *crossed[2:n])))
+    twin_of = lambda n: to_twin(cut(n, twin_quarter))
+
+    def sums_of(f, *first):
         rows_in = after(far_rows, *first)
+        across_x = crossed[2 * f : 2 * f + 2]
+        beside = [to_plane(after(piece, near_rows)) for piece in across_x]
+        held = [twin_of(2 * f), twin_of(2 * f + 1), *across_x, *beside]
         return partial_sums(f, spans, base, which, near_rows, rows_in, w_gate, w_up, held)
 
     def units_of(sums):
@@ -438,38 +443,59 @@
         ).astype(F32)
         return (jax.nn.silu(sums[:, :UNITS]) * sums[:, UNITS:] * scale).astype(BF16)
 
-    second = fetch(1, far)
-    third = fetch(2, second)
-    sums = sums_of(0, group(0, fetch(0), near_rows), second)
-    later = sums_of(1, group(1, second, far_rows), sums, third)
+    sums = sums_of(0, crossed[2])
+    later = sums_of(1, sums)
     units = [units_of(sums), units_of(later)]
-    held = group(2, third, later)
+    held = [twin_of(4), crossed[4], to_plane(crossed[4])]
 
     place = jnp.broadcast_to(
         after(across[:experts], later)[:, :, None], (experts, size * count, 128)
     )
     columns = scatter_rows(spans, place, rows)
-    pieces = [after(cut(2, my_quarter), later), *held]
+    pieces = [after(cut(4, my_quarter), later), *held]
     units, columns, pieces = lax.optimization_barrier((units, columns, pieces))
-    units = jnp.concatenate(units, axis=1).reshape(-1, BLOCK, 2 * UNITS)
-    first, second = (
-        lax.all_gather(units[half], "ep", axis=0, axis_index_groups=line, tiled=True)
-        for half in range(2)
-    )
-    far_mix = lambda half, hidden, start, dtype: down_and_mix(
-        half, spans, base, columns, hidden, start, pieces[2:], dtype
-    )
-    near_mix = lambda half, hidden, start, dtype: down_and_mix(
-        half, spans, base, columns, hidden, start, pieces[:2], dtype
-    )
-    far, near = far_mix(0, first, None, F32), near_mix(0, first, None, F32)
-    second, far, near = lax.optimization_barrier((second, far, near))
-    far = far_mix(1, second, far, BF16)
+    units = jnp.concatenate(units, axis=1)
+
+    spot = me // 4
+
+    def steps(value, step, up):
+        links = [
+            (4 * p + k, 4 * (p + 1 if up else p - 1) + k)
+            for p in (range(step - 1, places - 1) if up else range(1, places - step + 1))
+            for k in range(4)
+        ]
+        return lax.ppermute(value, "ep", links)
+
+    def mix(flags, hidden, start, at=0, count=4, dtype=F32):
+        block = jnp.stack([jnp.asarray(flag, jnp.int32) for flag in flags])
+        return down_and_mix(
+            spans, base, block, columns, hidden, start, at, pieces[at : at + count], dtype
+        )
+
+    moving = [steps(units, 1, True), steps(units, 1, False)]
+    total, waiting = mix((spot, 1, 1), [units, units], None), []
+    for step in range(1, places):
+        if step == places - 1:
+            for flags, hidden in waiting:
+                total = mix(flags, hidden, total)
+        *hidden, total = lax.optimization_barrier((*moving, total))
+        came_up, came_down = spot >= step, spot < places - step
+        above = jnp.minimum(spot + step, places - 1)
+        flags = (jnp.where(came_up, spot - step, above), came_up, came_up | came_down)
+        if step == places - 1:
+            break
+        moving = [steps(hidden[0], step + 1, True), steps(hidden[1], step + 1, False)]
+        waiting.append((flags, hidden))
+        if 2 * step < places:
+            waiting.append(((above, 0, came_up & came_down), hidden))
+        total = mix(*waiting.pop(0), total)
+    far = mix(flags, hidden, total, 2, 2, BF16)
+    near = after(total, far)
     far, far_twin = far[:, :width], far[:, LANES : LANES + width]
     far = (far.astype(F32) + to_twin(far_twin).astype(F32)).astype(BF16)
     near, far = lax.optimization_barrier((near, far))
     far = to_cross(far)
-    near = near_mix(1, second, near, F32)
+    near = mix(flags, hidden, near, 0, 2)
     twin = near[:, LANES : LANES + width].astype(BF16)
     twin = to_twin(after(twin, far)).astype(F32)
     mixed = (near[:, :width] + twin + far.astype(F32)).astype(BF16)

time: 471 us -> 458 us (0.972)
  waiting for transfers between devices: 207 us -> 164 us
  starting transfers between devices: 13.3 us -> 33.2 us
  Pallas kernels: 170 us -> 183 us
    all_gather x2 -> x0, waiting for transfers between devices: 55.7 us -> none  [fixed_weights(): lax.all_gather(units[half], 'ep', axis=0, axis_index_groups=line, tiled=T...]
    reduce_scatter x2, waiting for transfers between devices: 62.1 us -> 21.1 us  [units_of(): lax.psum_scatter(sums, 'ep', scatter_dimension=0, axis_index_groups=line,...]
    ppermute x3 -> x5, waiting for transfers between devices: 0.01 us -> 40.9 us  [fixed_weights(): to_plane = lambda value: lax.ppermute(value, 'parts', [(0, 1), (1, 0)])]
    pallas_call x4 -> x6, Pallas kernels: 67.1 us -> 81.5 us  [down_and_mix(): pl.pallas_call(kernel, grid_spec=pltpu.PrefetchScalarGridSpec(num_scalar_...]
    ppermute x0 -> x6, starting transfers between devices: none -> 12.8 us  [steps(): return lax.ppermute(value, 'ep', links)]
    ppermute x0 -> x6, waiting for transfers between devices: none -> 10.6 us  [steps(): return lax.ppermute(value, 'ep', links)]
    concatenate x4 -> x0, other arithmetic: 5.61 us -> none  [cut(): jnp.concatenate([lax.dynamic_slice_in_dim(w, at, UNITS, 2) for w in (w_ga...]
    ppermute x5 -> x7, waiting for transfers between devices: 80 us -> 82.4 us  [fixed_weights(): to_cross = lambda value: lax.ppermute(value, ('parts', 'ep'), cross)]
  transfers between devices with their start and end apart: 20 -> 30, of which waited for: 10 -> 18; matrix products, arithmetic and copies ran while one was open for 6% -> 6% of each run, Pallas kernels for 29% -> 35%
where the time goes in v9:
time: 458 us; the launch traced here: 454 us
  Pallas kernels  183 us (40%)
  waiting for transfers between devices  164 us (36%)
  starting transfers between devices  33.2 us (7%)
  local copies, waits for them, and re-layouts  29.8 us (7%)
  blocking collectives  17.6 us (4%)
  between operations  13.8 us (3%)
  other arithmetic  13 us (3%)
    ppermute x7, waiting for transfers between devices, fixed_weights(): to_cross = lambda value: lax.ppermute(value, ('parts', 'ep'), cross)  82.4 us
    pallas_call x6, Pallas kernels, down_and_mix(): pl.pallas_call(kernel, grid_spec=pltpu.PrefetchScalarGridSpec(num_scalar_...  81.5 us
    ppermute x5, waiting for transfers between devices, fixed_weights(): to_plane = lambda value: lax.ppermute(value, 'parts', [(0, 1), (1, 0)])  40.9 us
    pallas_call x2, Pallas kernels, partial_sums(): pl.pallas_call(partial_kernel, grid_spec=pltpu.PrefetchScalarGridSpec(num...  38.6 us
    pallas_call x1, Pallas kernels, sort_rows(): pl.pallas_call(functools.partial(sort_kernel, experts), grid_spec=pltpu.P...  27.2 us
    reduce_scatter x2, waiting for transfers between devices, units_of(): lax.psum_scatter(sums, 'ep', scatter_dimension=0, axis_index_groups=line,...  21.1 us
    all_to_all x1, blocking collectives, fixed_weights(): lax.all_to_all(mixed.reshape(size, count, width), 'ep', split_axis=0, con...  17.6 us
    pallas_call x1, Pallas kernels, scatter_rows(): pl.pallas_call(scatter_kernel, grid_spec=pltpu.PrefetchScalarGridSpec(num...  16.5 us
  transfers between devices with their start and end apart: 30, of which 18 were waited for; matrix products, arithmetic and copies ran while one was open for 6% of the time, Pallas kernels for 35%

profile of v9, /device:TPU:15, one launch (start us, length us, event | category | flops | bytes accessed | tf_op | source)
XLA Modules:
  0.0 454.4 jit_solution(1248829958316308924)
XLA Ops:
  8.0 1.8 reshape.60
  11.0 6.6 %all-to-all-start = ((bf16[16,64,256]{2,1,0:T(8,128)(2,1)}), bf16[16,64,256]{2,1,0:T(8,128)(2,1)S(1)}, u32[]{:S(2)}, u32[]{:S(2)}) async-start(bf16[16,64,256]{2,1,0:T(8,128)(2,1)} %pad_maximum_fusion), calls=%async_computation | async-start | bytes 1048576 | tf_op jit(solution)/shard_map/all_to_all | solution.py:406
  17.6 3.8 constant_dynamic-slice_fusion.2
  22.9 2.6 constant_dynamic-slice_fusion
  26.0 5.5 %all-to-all-done = bf16[16,64,256]{2,1,0:T(8,128)(2,1)S(1)} async-done(((bf16[16,64,256]{2,1,0:T(8,128)(2,1)}), bf16[16,64,256]{2,1,0:T(8,128)(2,1)S(1)}, u32[]{:S(2)}, u32[]{:S(2)}) %all-to-all-start) | async-done | bytes 524320 | tf_op jit(solution)/shard_map/all_to_all | solution.py:406
  31.4 3.6 order.1
  36.9 27.2 %sort_rows.1 = (bf16[8192,512]{1,0:T(8,128)(2,1)}, f32[8192,128]{1,0:T(8,128)S(1)}, bf16[8192,1024]{1,0:T(8,128)(2,1)}) custom-call(s32[32]{0:T(128)S(1)} %get-tuple-element.102.low.refs_0_, s32[32]{0:T(128)S(1)} %get-tuple-element.101.high.refs_1_, s32[17]{0:T(128)S(1)} %slice_bitcast_fusion.base.refs_2_, s32[16,8,128]{2,1,0:T(8,128)S(1)} %bitcast.38, ...), custom_call_target="tpu_custom_call" | custom-call | flops 8589934592 | bytes 33554432 | tf_op jit(solution)/shard_map/sort_rows/pallas_call | solution.py:184
  64.1 2.1 copy-done
  66.2 11.3 %collective-permute-done.1.refs_0_ = bf16[1024,256]{1,0:T(8,128)(2,1)S(1)} collective-permute-done((bf16[1024,256]{1,0:T(8,128)(2,1)S(1)}, bf16[1024,256]{1,0:T(8,128)(2,1)S(1)}, u32[]{:S(2)}, u32[]{:S(2)}) %collective-permute-start.1) | collective-permute-done | bytes 524320 | tf_op jit(solution)/shard_map/ppermute | solution.py:390
  80.5 15.3 %sort_more.1.far_ref = bf16[8192,512]{1,0:T(8,128)(2,1)} custom-call(bf16[8192,1024]{1,0:T(8,128)(2,1)} %get-tuple-element.47.onehot_ref, bf16[1024,256]{1,0:T(8,128)(2,1)S(1)} %collective-permute-done.1.refs_0_, bf16[1024,256]{1,0:T(8,128)(2,1)S(1)} %collective-permute-done.2.refs_1_), custom_call_target="tpu_custom_call" | custom-call | flops 8589934592 | bytes 33554432 | tf_op jit(solution)/shard_map/sort_more/pallas_call | solution.py:221
  95.8 5.0 %collective-permute-done.3.refs_4_ = bf16[16,224,128]{2,1,0:T(8,128)(2,1)S(1)} collective-permute-done((bf16[16,224,128]{2,1,0:T(8,128)(2,1)S(1)}, bf16[16,224,128]{2,1,0:T(8,128)(2,1)S(1)}, u32[]{:S(2)}, u32[]{:S(2)}) %collective-permute-start.3) | collective-permute-done | bytes 917536 | tf_op jit(solution)/shard_map/ppermute | solution.py:390
  100.8 19.4 %collective-permute-done.9.refs_7_ = bf16[16,224,128]{2,1,0:T(8,128)(2,1)S(1)} collective-permute-done((bf16[16,224,128]{2,1,0:T(8,128)(2,1)S(1)}, bf16[16,224,128]{2,1,0:T(8,128)(2,1)S(1)}, u32[]{:S(2)}, u32[]{:S(2)}) %collective-permute-start.9) | collective-permute-done | bytes 917536 | tf_op jit(solution)/shard_map/ppermute | solution.py:391
  120.2 19.3 %partial_sums.2 = bf16[8192,256]{1,0:T(8,128)(2,1)} custom-call(s32[32]{0:T(128)S(1)} %get-tuple-element.102.low.refs_0_, s32[32]{0:T(128)S(1)} %get-tuple-element.101.high.refs_1_, s32[17]{0:T(128)S(1)} %slice_bitcast_fusion.base.refs_2_, s32[1]{0:T(128)} %bitcast.8.quarter, bf16[8192,512]{1,0:T(8,128)(2,1)} %get-tuple-element.46.near_ref, ...), custom_call_target="tpu_custom_call" | custom-call | flops 4294967296 | bytes 16777216 | tf_op jit(solution)/shard_map/partial_sums/pallas_call | solution.py:294
  139.8 2.0 collective-permute-start.12
  142.7 20.3 %collective-permute-done.12.refs_5_ = bf16[16,224,128]{2,1,0:T(8,128)(2,1)S(1)} collective-permute-done((bf16[16,224,128]{2,1,0:T(8,128)(2,1)}, bf16[16,224,128]{2,1,0:T(8,128)(2,1)S(1)}, u32[]{:S(2)}, u32[]{:S(2)}) %collective-permute-start.12) | collective-permute-done | bytes 917536 | tf_op jit(solution)/shard_map/ppermute | solution.py:390
  163.1 1.3 collective-permute-done.13.refs_6_
  164.4 20.1 %collective-permute-done.14.refs_7_ = bf16[16,224,128]{2,1,0:T(8,128)(2,1)S(1)} collective-permute-done((bf16[16,224,128]{2,1,0:T(8,128)(2,1)S(1)}, bf16[16,224,128]{2,1,0:T(8,128)(2,1)S(1)}, u32[]{:S(2)}, u32[]{:S(2)}) %collective-permute-start.14) | collective-permute-done | bytes 917536 | tf_op jit(solution)/shard_map/ppermute | solution.py:391
  184.5 19.3 %partial_sums.3 = bf16[8192,256]{1,0:T(8,128)(2,1)} custom-call(s32[32]{0:T(128)S(1)} %get-tuple-element.102.low.refs_0_, s32[32]{0:T(128)S(1)} %get-tuple-element.101.high.refs_1_, s32[17]{0:T(128)S(1)} %slice_bitcast_fusion.base.refs_2_, s32[1]{0:T(128)} %bitcast.8.quarter, bf16[8192,512]{1,0:T(8,128)(2,1)} %get-tuple-element.46.near_ref, ...), custom_call_target="tpu_custom_call" | custom-call | flops 4294967296 | bytes 16777216 | tf_op jit(solution)/shard_map/partial_sums/pallas_call | solution.py:294
  203.9 4.9 %dynamic-slice_bitcast_fusion = (bf16[16,224,256]{2,1,0:T(8,128)(2,1)S(1)}, bf16[16,224,256]{2,1,0:T(8,128)(2,1)}, bf16[16,224,256]{2,1,0:T(8,128)(2,1)}) fusion(bf16[16,1024,224]{1,2,0:T(8,128)(2,1)} %param.11, s32[]{:T(128)S(6)} %select_n.50, s32[]{:T(128)S(6)} %select_n.53, s32[]{:T(128)S(6)} %select_n.49), kind=kLoop, calls=%fused_computation | loop fusion | bytes 11010060 | tf_op jit(solution)/shard_map/dynamic_slice | solution.py:416
  208.8 1.7 collective-permute-start.16
  210.5 40.3 %collective-permute-done.16.refs_9_.refs_2_.refs_0_ = bf16[16,224,256]{2,1,0:T(8,128)(2,1)} collective-permute-done((bf16[16,224,256]{2,1,0:T(8,128)(2,1)S(1)}, bf16[16,224,256]{2,1,0:T(8,128)(2,1)}, u32[]{:S(2)}, u32[]{:S(2)}) %collective-permute-start.16) | collective-permute-done | bytes 1835040 | tf_op jit(solution)/shard_map/ppermute | solution.py:390
  250.8 5.6 %broadcast_in_dim.5.place_ref = s32[16,1024,128]{2,1,0:T(8,128)} broadcast(s32[16,1024]{1,0:T(8,128)S(1)} %get-tuple-element.58), dimensions={0,1} | broadcast | bytes 8454144 | tf_op jit(solution)/shard_map/broadcast_in_dim | solution.py:451
  256.5 16.5 %scatter_rows.1.refs_4_.onehot_ref = bf16[1024,8192]{1,0:T(8,128)(2,1)} custom-call(s32[32]{0:T(128)S(1)} %get-tuple-element.102.low.refs_0_, s32[32]{0:T(128)S(1)} %get-tuple-element.101.high.refs_1_, s32[16,1024,128]{2,1,0:T(8,128)} %broadcast_in_dim.5.place_ref), custom_call_target="tpu_custom_call" | custom-call | flops 8388608 | bytes 16777216 | tf_op jit(solution)/shard_map/scatter_rows/pallas_call | solution.py:251
  273.0 2.7 convert_element_type.57
  275.7 21.1 %reduce-scatter.5.cloned.1.call-done = bf16[2048,256]{1,0:T(8,128)(2,1)} async-done(((bf16[8192,256]{1,0:T(8,128)(2,1)}), bf16[2048,256]{1,0:T(8,128)(2,1)}) %reduce-scatter.5.cloned.1.call-update) | async-done | bytes 1048592 | tf_op jit(solution)/shard_map/reduce_scatter | solution.py:441
  296.7 1.5 convert_element_type.59
  298.6 2.0 fusion.3
  300.9 3.6 collective-permute-start.18
  304.5 1.9 collective-permute-start.19
  306.9 16.5 %down_and_mix.6.start = f32[1024,1024]{1,0:T(8,128)} custom-call(s32[32]{0:T(128)} %copy-done.2, s32[32]{0:T(128)} %copy-done.1, s32[17]{0:T(128)} %copy-done.3, s32[3]{0:T(128)} %stack.83.refs_3_, bf16[1024,8192]{1,0:T(8,128)(2,1)} %scatter_rows.1.refs_4_.onehot_ref, bf16[2048,256]{1,0:T(8,128)(2,1)} %copy-done.7, bf16[2048,256]{1,0:T(8,128)(2,1)} %copy-done.7, ...), custom_call_target="tpu_custom_call" | custom-call | flops 4294967296 | bytes 4194304 | tf_op jit(solution)/shard_map/down_and_mix/pallas_call | solution.py:352
  323.4 3.6 collective-permute-done.18.up_ref
  327.0 3.3 collective-permute-done.19.down_ref
  330.3 2.1 collective-permute-start.20
  332.4 1.9 collective-permute-start.21
  335.0 17.6 %down_and_mix.7.start = f32[1024,1024]{1,0:T(8,128)} custom-call(s32[32]{0:T(128)} %copy-done.2, s32[32]{0:T(128)} %copy-done.1, s32[17]{0:T(128)} %copy-done.3, s32[3]{0:T(128)} %pad_add_fusion.1.block, bf16[1024,8192]{1,0:T(8,128)(2,1)} %scatter_rows.1.refs_4_.onehot_ref, bf16[2048,256]{1,0:T(8,128)(2,1)} %copy-done.10, ...), custom_call_target="tpu_custom_call" | custom-call | flops 4294967296 | bytes 4194304 | tf_op jit(solution)/shard_map/down_and_mix/pallas_call | solution.py:352
  354.0 3.2 collective-permute-done.21.down_ref
  357.9 2.5 collective-permute-start.23
  361.7 17.7 %down_and_mix.8.start = f32[1024,1024]{1,0:T(8,128)} custom-call(s32[32]{0:T(128)} %copy-done.2, s32[32]{0:T(128)} %copy-done.1, s32[17]{0:T(128)} %copy-done.3, s32[3]{0:T(128)} %pad_add_fusion.3.block, bf16[1024,8192]{1,0:T(8,128)(2,1)} %scatter_rows.1.refs_4_.onehot_ref, bf16[2048,256]{1,0:T(8,128)(2,1)} %copy-done.10, ...), custom_call_target="tpu_custom_call" | custom-call | flops 4294967296 | bytes 4194304 | tf_op jit(solution)/shard_map/down_and_mix/pallas_call | solution.py:352
  379.3 16.9 %down_and_mix.9.start = f32[1024,1024]{1,0:T(8,128)} custom-call(s32[32]{0:T(128)} %copy-done.2, s32[32]{0:T(128)} %copy-done.1, s32[17]{0:T(128)} %copy-done.3, s32[3]{0:T(128)} %get-tuple-element.104.block, bf16[1024,8192]{1,0:T(8,128)(2,1)} %scatter_rows.1.refs_4_.onehot_ref, bf16[2048,256]{1,0:T(8,128)(2,1)} %copy-done.11, ...), custom_call_target="tpu_custom_call" | custom-call | flops 4294967296 | bytes 4194304 | tf_op jit(solution)/shard_map/down_and_mix/pallas_call | solution.py:352
  397.7 6.2 %down_and_mix.10 = bf16[1024,512]{1,0:T(8,128)(2,1)} custom-call(s32[32]{0:T(128)} %copy-done.2, s32[32]{0:T(128)} %copy-done.1, s32[17]{0:T(128)} %copy-done.3, s32[3]{0:T(128)} %get-tuple-element.103.block, bf16[1024,8192]{1,0:T(8,128)(2,1)} %scatter_rows.1.refs_4_.onehot_ref, bf16[2048,256]{1,0:T(8,128)(2,1)} %copy-done.8, bf16[2048,256]{1,0:T(8,128)(2,1)} %copy-done.9, ...), custom_call_target="tpu_custom_call" | custom-call | flops 2147483648 | bytes 4194304 | tf_op jit(solution)/shard_map/down_and_mix/pallas_call | solution.py:352
  405.0 3.1 collective-permute-start.24
  408.1 1.5 collective-permute-done.24
  411.4 6.7 %down_and_mix.11 = f32[1024,512]{1,0:T(8,128)} custom-call(s32[32]{0:T(128)} %copy-done.2, s32[32]{0:T(128)} %copy-done.1, s32[17]{0:T(128)} %copy-done.3, s32[3]{0:T(128)} %get-tuple-element.103.block, bf16[1024,8192]{1,0:T(8,128)(2,1)} %scatter_rows.1.refs_4_.onehot_ref, bf16[2048,256]{1,0:T(8,128)(2,1)} %copy-done.8, bf16[2048,256]{1,0:T(8,128)(2,1)} %copy-done.9, ...), custom_call_target="tpu_custom_call" | custom-call | flops 2147483648 | bytes 4194304 | tf_op jit(solution)/shard_map/down_and_mix/pallas_call | solution.py:352
  419.3 5.4 %collective-permute-done.25 = bf16[1024,224]{1,0:T(8,128)(2,1)S(1)} collective-permute-done((bf16[1024,224]{1,0:T(8,128)(2,1)S(1)}, bf16[1024,224]{1,0:T(8,128)(2,1)S(1)}, u32[]{:S(2)}, u32[]{:S(2)}) %collective-permute-start.25) | collective-permute-done | bytes 458784 | tf_op jit(solution)/shard_map/ppermute | solution.py:390
  425.1 1.5 collective-permute-done.26
  426.7 1.4 fusion.1
  428.0 17.6 %all_to_all.10 = bf16[16,64,224]{2,1,0:T(8,128)(2,1)S(1)} all-to-all(bf16[16,64,224]{2,1,0:T(8,128)(2,1)S(1)} %bitcast.39), channel_id=1, replica_groups=mesh['parts'=2,'ep'=16,'tp'=1] {'ep'}, dimensions={0} | all-to-all | bytes 917504 | tf_op jit(solution)/shard_map/all_to_all | solution.py:502
  446.0 1.6 reshape.65
  (87 shorter events, 21.9 us)
Async XLA Ops:
  11.0 20.4 %all-to-all-start = ((bf16[16,64,256]{2,1,0:T(8,128)(2,1)}), bf16[16,64,256]{2,1,0:T(8,128)(2,1)S(1)}, u32[]{:S(2)}, u32[]{:S(2)}) async-start(bf16[16,64,256]{2,1,0:T(8,128)(2,1)} %pad_maximum_fusion), calls=%async_computation | async-start | bytes 1048576 | tf_op jit(solution)/shard_map/all_to_all | solution.py:406
  17.5 255.4 %reduce-scatter.3.cloned.1.call-start = ((), (), s32[]{:S(2)}) async-start(), calls=%async_computation.4 | async-start | bytes 5242880 | tf_op jit(solution)/shard_map/reduce_scatter | solution.py:441
  17.6 5.2 %copy-start.4 = (bf16[16,224,1024]{2,1,0:T(8,128)(2,1)S(1)}, bf16[16,224,1024]{2,1,0:T(8,128)(2,1)}, u32[]{:S(2)}) copy-start(bf16[16,224,1024]{2,1,0:T(8,128)(2,1)} %refs_1_.3) | copy-start | bytes 22020100
  21.5 56.9 %collective-permute-start.6 = (bf16[16,224,128]{2,1,0:T(8,128)(2,1)S(1)}, bf16[16,224,128]{2,1,0:T(8,128)(2,1)S(1)}, u32[]{:S(2)}, u32[]{:S(2)}) collective-permute-start(bf16[16,224,128]{2,1,0:T(8,128)(2,1)S(1)} %get-tuple-element.89), channel_id=1, source_target_pairs={{0,2},{1,3},{2,0},{3,1},{4,6},{5,7},{6,4},{7,5},{8,10},{9,11},{10,... | collective-permute-start | bytes 2752520 | tf_op jit(solution)/shard_map/ppermute | solution.py:390
  25.4 53.6 %collective-permute-start.7 = (bf16[16,224,128]{2,1,0:T(8,128)(2,1)}, bf16[16,224,128]{2,1,0:T(8,128)(2,1)S(1)}, u32[]{:S(2)}, u32[]{:S(2)}) collective-permute-start(bf16[16,224,128]{2,1,0:T(8,128)(2,1)} %get-tuple-element.86), channel_id=1, source_target_pairs={{0,2},{1,3},{2,0},{3,1},{4,6},{5,7},{6,4},{7,5},{8,10},{9,11},{10,... | collective-permute-start | bytes 2752520 | tf_op jit(solution)/shard_map/ppermute | solution.py:390
  35.0 1.9 collective-permute-start
  35.0 42.4 %collective-permute-start.1 = (bf16[1024,256]{1,0:T(8,128)(2,1)S(1)}, bf16[1024,256]{1,0:T(8,128)(2,1)S(1)}, u32[]{:S(2)}, u32[]{:S(2)}) collective-permute-start(bf16[1024,256]{1,0:T(8,128)(2,1)S(1)} %bitcast.36), channel_id=1, source_target_pairs={{0,2},{1,3},{2,0},{3,1},{4,6},{5,7},{6,4},{7,5},{8,10},{9,11},{10,... | collective-permute-start | bytes 1572872 | tf_op jit(solution)/shard_map/ppermute | solution.py:390
  36.3 220.2 %copy-start.1 = (s32[32]{0:T(128)}, s32[32]{0:T(128)S(1)}, u32[]{:S(2)}) copy-start(s32[32]{0:T(128)S(1)} %get-tuple-element.101.high.refs_1_) | copy-start | bytes 388
  36.3 220.2 %copy-start.2 = (s32[32]{0:T(128)}, s32[32]{0:T(128)S(1)}, u32[]{:S(2)}) copy-start(s32[32]{0:T(128)S(1)} %get-tuple-element.102.low.refs_0_) | copy-start | bytes 388
  36.3 148.2 %copy-start.3 = (s32[17]{0:T(128)}, s32[17]{0:T(128)S(1)}, u32[]{:S(2)}) copy-start(s32[17]{0:T(128)S(1)} %slice_bitcast_fusion.base.refs_2_) | copy-start | bytes 208
  36.9 41.4 %copy-start.12 = (bf16[16,224,128]{2,1,0:T(8,128)(2,1)S(1)}, bf16[16,224,128]{2,1,0:T(8,128)(2,1)}, u32[]{:S(2)}) copy-start(bf16[16,224,128]{2,1,0:T(8,128)(2,1)} %get-tuple-element.49) | copy-start | bytes 2752516
  64.1 2.1 copy-start
  77.5 1.9 collective-permute-start.2
  77.9 22.9 %collective-permute-start.4 = (bf16[16,224,128]{2,1,0:T(8,128)(2,1)}, bf16[16,224,128]{2,1,0:T(8,128)(2,1)S(1)}, u32[]{:S(2)}, u32[]{:S(2)}) collective-permute-start(bf16[16,224,128]{2,1,0:T(8,128)(2,1)} %get-tuple-element.90), channel_id=1, source_target_pairs={{0,1},{1,0},{2,3},{3,2},{4,5},{5,4},{6,7},{7,6},{8,9},{9,8},{10,11... | collective-permute-start | bytes 2752520 | tf_op jit(solution)/shard_map/ppermute | solution.py:389
  78.0 22.8 %collective-permute-start.5 = (bf16[16,224,128]{2,1,0:T(8,128)(2,1)}, bf16[16,224,128]{2,1,0:T(8,128)(2,1)S(1)}, u32[]{:S(2)}, u32[]{:S(2)}) collective-permute-start(bf16[16,224,128]{2,1,0:T(8,128)(2,1)} %get-tuple-element.87), channel_id=1, source_target_pairs={{0,1},{1,0},{2,3},{3,2},{4,5},{5,4},{6,7},{7,6},{8,9},{9,8},{10,11... | collective-permute-start | bytes 2752520 | tf_op jit(solution)/shard_map/ppermute | solution.py:389
  78.4 22.4 %collective-permute-start.3 = (bf16[16,224,128]{2,1,0:T(8,128)(2,1)S(1)}, bf16[16,224,128]{2,1,0:T(8,128)(2,1)S(1)}, u32[]{:S(2)}, u32[]{:S(2)}) collective-permute-start(bf16[16,224,128]{2,1,0:T(8,128)(2,1)S(1)} %copy-done.12), channel_id=1, source_target_pairs={{0,2},{1,3},{2,0},{3,1},{4,6},{5,7},{6,4},{7,5},{8,10},{9,11},{10,... | collective-permute-start | bytes 2752520 | tf_op jit(solution)/shard_map/ppermute | solution.py:390
  79.0 21.8 %collective-permute-start.8 = (bf16[16,224,128]{2,1,0:T(8,128)(2,1)S(1)}, bf16[16,224,128]{2,1,0:T(8,128)(2,1)S(1)}, u32[]{:S(2)}, u32[]{:S(2)}) collective-permute-start(bf16[16,224,128]{2,1,0:T(8,128)(2,1)S(1)} %collective-permute-done.6.refs_4_), channel_id=1, source_target_pairs={{0,16},{16,0},{1,17},{17,1},{2,18},{18,2},{3,19},{19,3},{4,20},{20... | collective-permute-start | bytes 2752520 | tf_op jit(solution)/shard_map/ppermute | solution.py:391
  79.4 40.8 %collective-permute-start.9 = (bf16[16,224,128]{2,1,0:T(8,128)(2,1)S(1)}, bf16[16,224,128]{2,1,0:T(8,128)(2,1)S(1)}, u32[]{:S(2)}, u32[]{:S(2)}) collective-permute-start(bf16[16,224,128]{2,1,0:T(8,128)(2,1)S(1)} %collective-permute-done.7.refs_5_), channel_id=1, source_target_pairs={{0,16},{16,0},{1,17},{17,1},{2,18},{18,2},{3,19},{19,3},{4,20},{20... | collective-permute-start | bytes 2752520 | tf_op jit(solution)/shard_map/ppermute | solution.py:391
  139.5 157.2 %reduce-scatter.5.cloned.1.call-start = ((), (), s32[]{:S(2)}) async-start(), calls=%async_computation.5 | async-start | bytes 5242880 | tf_op jit(solution)/shard_map/reduce_scatter | solution.py:441
  139.8 23.3 %collective-permute-start.12 = (bf16[16,224,128]{2,1,0:T(8,128)(2,1)}, bf16[16,224,128]{2,1,0:T(8,128)(2,1)S(1)}, u32[]{:S(2)}, u32[]{:S(2)}) collective-permute-start(bf16[16,224,128]{2,1,0:T(8,128)(2,1)} %get-tuple-element.55), channel_id=1, source_target_pairs={{0,2},{1,3},{2,0},{3,1},{4,6},{5,7},{6,4},{7,5},{8,10},{9,11},{10,... | collective-permute-start | bytes 2752520 | tf_op jit(solution)/shard_map/ppermute | solution.py:390
  141.8 21.3 %collective-permute-start.10 = (bf16[16,224,128]{2,1,0:T(8,128)(2,1)}, bf16[16,224,128]{2,1,0:T(8,128)(2,1)S(1)}, u32[]{:S(2)}, u32[]{:S(2)}) collective-permute-start(bf16[16,224,128]{2,1,0:T(8,128)(2,1)} %get-tuple-element.88), channel_id=1, source_target_pairs={{0,1},{1,0},{2,3},{3,2},{4,5},{5,4},{6,7},{7,6},{8,9},{9,8},{10,11... | collective-permute-start | bytes 2752520 | tf_op jit(solution)/shard_map/ppermute | solution.py:389
  141.8 21.3 %collective-permute-start.11 = (bf16[16,224,128]{2,1,0:T(8,128)(2,1)}, bf16[16,224,128]{2,1,0:T(8,128)(2,1)S(1)}, u32[]{:S(2)}, u32[]{:S(2)}) collective-permute-start(bf16[16,224,128]{2,1,0:T(8,128)(2,1)} %get-tuple-element.85), channel_id=1, source_target_pairs={{0,1},{1,0},{2,3},{3,2},{4,5},{5,4},{6,7},{7,6},{8,9},{9,8},{10,11... | collective-permute-start | bytes 2752520 | tf_op jit(solution)/shard_map/ppermute | solution.py:389
  142.3 22.1 %collective-permute-start.13 = (bf16[16,224,128]{2,1,0:T(8,128)(2,1)S(1)}, bf16[16,224,128]{2,1,0:T(8,128)(2,1)S(1)}, u32[]{:S(2)}, u32[]{:S(2)}) collective-permute-start(bf16[16,224,128]{2,1,0:T(8,128)(2,1)S(1)} %collective-permute-done.3.refs_4_), channel_id=1, source_target_pairs={{0,16},{16,0},{1,17},{17,1},{2,18},{18,2},{3,19},{19,3},{4,20},{20... | collective-permute-start | bytes 2752520 | tf_op jit(solution)/shard_map/ppermute | solution.py:391
  163.1 21.5 %collective-permute-start.14 = (bf16[16,224,128]{2,1,0:T(8,128)(2,1)S(1)}, bf16[16,224,128]{2,1,0:T(8,128)(2,1)S(1)}, u32[]{:S(2)}, u32[]{:S(2)}) collective-permute-start(bf16[16,224,128]{2,1,0:T(8,128)(2,1)S(1)} %collective-permute-done.12.refs_5_), channel_id=1, source_target_pairs={{0,16},{16,0},{1,17},{17,1},{2,18},{18,2},{3,19},{19,3},{4,20},{20... | collective-permute-start | bytes 2752520 | tf_op jit(solution)/shard_map/ppermute | solution.py:391
  208.8 42.1 %collective-permute-start.16 = (bf16[16,224,256]{2,1,0:T(8,128)(2,1)S(1)}, bf16[16,224,256]{2,1,0:T(8,128)(2,1)}, u32[]{:S(2)}, u32[]{:S(2)}) collective-permute-start(bf16[16,224,256]{2,1,0:T(8,128)(2,1)S(1)} %get-tuple-element.60), channel_id=1, source_target_pairs={{0,2},{1,3},{2,0},{3,1},{4,6},{5,7},{6,4},{7,5},{8,10},{9,11},{10,... | collective-permute-start | bytes 5505032 | tf_op jit(solution)/shard_map/ppermute | solution.py:390
  210.5 90.1 %collective-permute-start.15 = (bf16[16,224,256]{2,1,0:T(8,128)(2,1)}, bf16[16,224,256]{2,1,0:T(8,128)(2,1)S(1)}, u32[]{:S(2)}, u32[]{:S(2)}) collective-permute-start(bf16[16,224,256]{2,1,0:T(8,128)(2,1)} %get-tuple-element.83), channel_id=1, source_target_pairs={{0,1},{1,0},{2,3},{3,2},{4,5},{5,4},{6,7},{7,6},{8,9},{9,8},{10,11... | collective-permute-start | bytes 5505032 | tf_op jit(solution)/shard_map/ppermute | solution.py:389
  250.8 49.8 %collective-permute-start.17 = (bf16[16,224,256]{2,1,0:T(8,128)(2,1)}, bf16[16,224,256]{2,1,0:T(8,128)(2,1)}, u32[]{:S(2)}, u32[]{:S(2)}) collective-permute-start(bf16[16,224,256]{2,1,0:T(8,128)(2,1)} %collective-permute-done.16.refs_9_.refs_2_.refs_0_), channel_id=1, source_target_pairs={{0,16},{16,0},{1,17},{17,1},{2,18},{18,2},{3,19},{19,3},{4,20},{20... | collective-permute-start | bytes 5505032 | tf_op jit(solution)/shard_map/ppermute | solution.py:391
  296.7 1.9 copy-start.6
  300.6 6.3 %copy-start.5 = (bf16[16,224,256]{2,1,0:T(8,128)(2,1)}, bf16[16,224,256]{2,1,0:T(8,128)(2,1)S(1)}, u32[]{:S(2)}) copy-start(bf16[16,224,256]{2,1,0:T(8,128)(2,1)S(1)} %collective-permute-done.15.refs_8_.refs_1_) | copy-start | bytes 5505028
  300.9 6.1 %copy-start.7 = (bf16[2048,256]{1,0:T(8,128)(2,1)}, bf16[2048,256]{1,0:T(8,128)(2,1)S(1)}, u32[]{:S(2)}) copy-start(bf16[2048,256]{1,0:T(8,128)(2,1)S(1)} %constant_dynamic-update-slice_fusion.refs_5_.refs_6_) | copy-start | bytes 3145732
  300.9 26.1 %collective-permute-start.18 = (bf16[2048,256]{1,0:T(8,128)(2,1)S(1)}, bf16[2048,256]{1,0:T(8,128)(2,1)S(1)}, u32[]{:S(2)}, u32[]{:S(2)}) collective-permute-start(bf16[2048,256]{1,0:T(8,128)(2,1)S(1)} %constant_dynamic-update-slice_fusion.refs_5_.refs_6_), channel_id=1, source_target_pairs={{0,4},{1,5},{2,6},{3,7},{4,8},{5,9},{6,10},{7,11},{8,12},{9,13},{1... | collective-permute-start | bytes 3145736 | tf_op jit(solution)/shard_map/ppermute | solution.py:467
  304.5 25.8 %collective-permute-start.19 = (bf16[2048,256]{1,0:T(8,128)(2,1)S(1)}, bf16[2048,256]{1,0:T(8,128)(2,1)}, u32[]{:S(2)}, u32[]{:S(2)}) collective-permute-start(bf16[2048,256]{1,0:T(8,128)(2,1)S(1)} %constant_dynamic-update-slice_fusion.refs_5_.refs_6_), channel_id=1, source_target_pairs={{4,0},{5,1},{6,2},{7,3},{8,4},{9,5},{10,6},{11,7},{12,8},{13,9},{1... | collective-permute-start | bytes 3145736 | tf_op jit(solution)/shard_map/ppermute | solution.py:467
  327.0 8.0 %copy-start.10 = (bf16[2048,256]{1,0:T(8,128)(2,1)}, bf16[2048,256]{1,0:T(8,128)(2,1)S(1)}, u32[]{:S(2)}) copy-start(bf16[2048,256]{1,0:T(8,128)(2,1)S(1)} %collective-permute-done.18.up_ref) | copy-start | bytes 3145732
  330.3 22.7 %collective-permute-start.20 = (bf16[2048,256]{1,0:T(8,128)(2,1)S(1)}, bf16[2048,256]{1,0:T(8,128)(2,1)S(1)}, u32[]{:S(2)}, u32[]{:S(2)}) collective-permute-start(bf16[2048,256]{1,0:T(8,128)(2,1)S(1)} %collective-permute-done.18.up_ref), channel_id=1, source_target_pairs={{4,8},{5,9},{6,10},{7,11},{8,12},{9,13},{10,14},{11,15},{20,24},{2... | collective-permute-start | bytes 3145736 | tf_op jit(solution)/shard_map/ppermute | solution.py:467
  332.4 24.8 %collective-permute-start.21 = (bf16[2048,256]{1,0:T(8,128)(2,1)}, bf16[2048,256]{1,0:T(8,128)(2,1)}, u32[]{:S(2)}, u32[]{:S(2)}) collective-permute-start(bf16[2048,256]{1,0:T(8,128)(2,1)} %collective-permute-done.19.down_ref), channel_id=1, source_target_pairs={{4,0},{5,1},{6,2},{7,3},{8,4},{9,5},{10,6},{11,7},{20,16},{21,17},... | collective-permute-start | bytes 3145736 | tf_op jit(solution)/shard_map/ppermute | solution.py:467
  353.0 1.0 copy-start.11
  357.2 39.1 %collective-permute-start.22 = (bf16[2048,256]{1,0:T(8,128)(2,1)}, bf16[2048,256]{1,0:T(8,128)(2,1)S(1)}, u32[]{:S(2)}, u32[]{:S(2)}) collective-permute-start(bf16[2048,256]{1,0:T(8,128)(2,1)} %copy-done.11), channel_id=1, source_target_pairs={{8,12},{9,13},{10,14},{11,15},{24,28},{25,29},{26,30},{27,31}} | collective-permute-start | bytes 3145736 | tf_op jit(solution)/shard_map/ppermute | solution.py:467
  357.9 38.3 %collective-permute-start.23 = (bf16[2048,256]{1,0:T(8,128)(2,1)}, bf16[2048,256]{1,0:T(8,128)(2,1)S(1)}, u32[]{:S(2)}, u32[]{:S(2)}) collective-permute-start(bf16[2048,256]{1,0:T(8,128)(2,1)} %collective-permute-done.21.down_ref), channel_id=1, source_target_pairs={{4,0},{5,1},{6,2},{7,3},{20,16},{21,17},{22,18},{23,19}} | collective-permute-start | bytes 3145736 | tf_op jit(solution)/shard_map/ppermute | solution.py:467
  396.3 1.0 copy-start.8
  396.3 1.4 copy-start.9
  405.0 4.6 %collective-permute-start.24 = (bf16[1024,224]{1,0:T(8,128)(2,1)S(1)}, bf16[1024,224]{1,0:T(8,128)(2,1)S(1)}, u32[]{:S(2)}, u32[]{:S(2)}) collective-permute-start(bf16[1024,224]{1,0:T(8,128)(2,1)S(1)} %slice.59), channel_id=1, source_target_pairs={{0,1},{1,0},{2,3},{3,2},{4,5},{5,4},{6,7},{7,6},{8,9},{9,8},{10,11... | collective-permute-start | bytes 1376264 | tf_op jit(solution)/shard_map/ppermute | solution.py:389
  410.8 14.0 %collective-permute-start.25 = (bf16[1024,224]{1,0:T(8,128)(2,1)S(1)}, bf16[1024,224]{1,0:T(8,128)(2,1)S(1)}, u32[]{:S(2)}, u32[]{:S(2)}) collective-permute-start(bf16[1024,224]{1,0:T(8,128)(2,1)S(1)} %add_convert_fusion), channel_id=1, source_target_pairs={{0,2},{1,3},{2,0},{3,1},{4,6},{5,7},{6,4},{7,5},{8,10},{9,11},{10,... | collective-permute-start | bytes 1376264 | tf_op jit(solution)/shard_map/ppermute | solution.py:390
  424.8 1.9 collective-permute-start.26
Sparse Core Ops, SparseCore 0:
  139.7 77.3 reduce-scatter.2
  219.4 77.2 reduce-scatter.4

commit v10 on v9

--- a/solution.py
+++ b/solution.py
@@ -425,7 +425,7 @@
     far_rows = sort_more(onehot, [far, to_twin(far)])
     scale = lax.dynamic_slice_in_dim(scale, (me // 4) * (rows // places), rows // places, 0)
 
-    crossed = [to_cross(cut(0, cross_quarter)), to_cross(cut(1, cross_quarter))]
+    crossed = [to_cross(cut(0, cross_quarter)), to_cross(after(cut(1, cross_quarter), near[1], base))]
     for n in range(2, 5):
         crossed.append(to_cross(after(cut(n, cross_quarter), far, *crossed[2:n])))
     twin_of = lambda n: to_twin(cut(n, twin_quarter))
@@ -433,7 +433,8 @@
     def sums_of(f, *first):
         rows_in = after(far_rows, *first)
         across_x = crossed[2 * f : 2 * f + 2]
-        beside = [to_plane(after(piece, near_rows)) for piece in across_x]
+        beside = [to_plane(after(across_x[0], near_rows))]
+        beside.append(to_plane(after(across_x[1], *beside)))
         held = [twin_of(2 * f), twin_of(2 * f + 1), *across_x, *beside]
         return partial_sums(f, spans, base, which, near_rows, rows_in, w_gate, w_up, held)
 

time: 458 us -> 448 us (0.978)
  waiting for transfers between devices: 164 us -> 154 us
    ppermute x7, waiting for transfers between devices: 82.4 us -> 76.1 us  [fixed_weights(): to_cross = lambda value: lax.ppermute(value, ('parts', 'ep'), cross)]
  transfers between devices with their start and end apart: 30 -> 30, of which waited for: 18 -> 17; matrix products, arithmetic and copies ran while one was open for 6% -> 6% of each run, Pallas kernels for 35% -> 36%
where the time goes in v10:
time: 448 us; the launch traced here: 446 us
  Pallas kernels  184 us (41%)
  waiting for transfers between devices  154 us (34%)
  starting transfers between devices  33.3 us (7%)
  local copies, waits for them, and re-layouts  29.3 us (7%)
  blocking collectives  17.6 us (4%)
  between operations  13.8 us (3%)
  other arithmetic  13 us (3%)
    pallas_call x6, Pallas kernels, down_and_mix(): pl.pallas_call(kernel, grid_spec=pltpu.PrefetchScalarGridSpec(num_scalar_...  81.9 us
    ppermute x7, waiting for transfers between devices, fixed_weights(): to_cross = lambda value: lax.ppermute(value, ('parts', 'ep'), cross)  76.1 us
    pallas_call x2, Pallas kernels, partial_sums(): pl.pallas_call(partial_kernel, grid_spec=pltpu.PrefetchScalarGridSpec(num...  39.3 us
    ppermute x5, waiting for transfers between devices, fixed_weights(): to_plane = lambda value: lax.ppermute(value, 'parts', [(0, 1), (1, 0)])  38.7 us
    pallas_call x1, Pallas kernels, sort_rows(): pl.pallas_call(functools.partial(sort_kernel, experts), grid_spec=pltpu.P...  27.4 us
    reduce_scatter x2, waiting for transfers between devices, units_of(): lax.psum_scatter(sums, 'ep', scatter_dimension=0, axis_index_groups=line,...  18.7 us
    all_to_all x1, blocking collectives, fixed_weights(): lax.all_to_all(mixed.reshape(size, count, width), 'ep', split_axis=0, con...  17.6 us
    pallas_call x1, Pallas kernels, scatter_rows(): pl.pallas_call(scatter_kernel, grid_spec=pltpu.PrefetchScalarGridSpec(num...  16.7 us
  transfers between devices with their start and end apart: 30, of which 17 were waited for; matrix products, arithmetic and copies ran while one was open for 6% of the time, Pallas kernels for 36%

profile of v10, /device:TPU:15, one launch (start us, length us, event | category | flops | bytes accessed | tf_op | source)
XLA Modules:
  0.0 445.5 jit_solution(12284098152780298123)
XLA Ops:
  8.0 1.8 reshape.60
  11.0 6.6 %all-to-all-start = ((bf16[16,64,256]{2,1,0:T(8,128)(2,1)}), bf16[16,64,256]{2,1,0:T(8,128)(2,1)S(1)}, u32[]{:S(2)}, u32[]{:S(2)}) async-start(bf16[16,64,256]{2,1,0:T(8,128)(2,1)} %pad_maximum_fusion), calls=%async_computation | async-start | bytes 1048576 | tf_op jit(solution)/shard_map/all_to_all | solution.py:406
  17.6 3.8 constant_dynamic-slice_fusion.2
  22.9 2.2 constant_dynamic-slice_fusion
  25.0 6.4 %all-to-all-done = bf16[16,64,256]{2,1,0:T(8,128)(2,1)S(1)} async-done(((bf16[16,64,256]{2,1,0:T(8,128)(2,1)}), bf16[16,64,256]{2,1,0:T(8,128)(2,1)S(1)}, u32[]{:S(2)}, u32[]{:S(2)}) %all-to-all-start) | async-done | bytes 524320 | tf_op jit(solution)/shard_map/all_to_all | solution.py:406
  31.4 3.6 order.1
  37.6 27.4 %sort_rows.1 = (bf16[8192,512]{1,0:T(8,128)(2,1)}, f32[8192,128]{1,0:T(8,128)S(1)}, bf16[8192,1024]{1,0:T(8,128)(2,1)}) custom-call(s32[32]{0:T(128)S(1)} %get-tuple-element.104.low.refs_0_, s32[32]{0:T(128)S(1)} %get-tuple-element.103.high.refs_1_, s32[17]{0:T(128)S(1)} %slice_bitcast_fusion.base.refs_2_, s32[16,8,128]{2,1,0:T(8,128)S(1)} %bitcast.38, ...), custom_call_target="tpu_custom_call" | custom-call | flops 8589934592 | bytes 33554432 | tf_op jit(solution)/shard_map/sort_rows/pallas_call | solution.py:184
  65.0 2.1 copy-done
  68.5 9.0 %collective-permute-done.7.refs_5_ = bf16[16,224,128]{2,1,0:T(8,128)(2,1)S(1)} collective-permute-done((bf16[16,224,128]{2,1,0:T(8,128)(2,1)S(1)}, bf16[16,224,128]{2,1,0:T(8,128)(2,1)S(1)}, u32[]{:S(2)}, u32[]{:S(2)}) %collective-permute-start.7) | collective-permute-done | bytes 917536 | tf_op jit(solution)/shard_map/ppermute | solution.py:390
  78.3 10.3 %collective-permute-done.8.refs_6_ = bf16[16,224,128]{2,1,0:T(8,128)(2,1)S(1)} collective-permute-done((bf16[16,224,128]{2,1,0:T(8,128)(2,1)S(1)}, bf16[16,224,128]{2,1,0:T(8,128)(2,1)S(1)}, u32[]{:S(2)}, u32[]{:S(2)}) %collective-permute-start.8) | collective-permute-done | bytes 917536 | tf_op jit(solution)/shard_map/ppermute | solution.py:391
  88.7 15.3 %sort_more.1.far_ref = bf16[8192,512]{1,0:T(8,128)(2,1)} custom-call(bf16[8192,1024]{1,0:T(8,128)(2,1)} %get-tuple-element.48.onehot_ref, bf16[1024,256]{1,0:T(8,128)(2,1)S(1)} %collective-permute-done.1.refs_0_, bf16[1024,256]{1,0:T(8,128)(2,1)S(1)} %collective-permute-done.2.refs_1_), custom_call_target="tpu_custom_call" | custom-call | flops 8589934592 | bytes 33554432 | tf_op jit(solution)/shard_map/sort_more/pallas_call | solution.py:221
  104.1 5.2 %collective-permute-done.9.refs_7_ = bf16[16,224,128]{2,1,0:T(8,128)(2,1)S(1)} collective-permute-done((bf16[16,224,128]{2,1,0:T(8,128)(2,1)S(1)}, bf16[16,224,128]{2,1,0:T(8,128)(2,1)S(1)}, u32[]{:S(2)}, u32[]{:S(2)}) %collective-permute-start.9) | collective-permute-done | bytes 917536 | tf_op jit(solution)/shard_map/ppermute | solution.py:391
  109.3 19.6 %partial_sums.2 = bf16[8192,256]{1,0:T(8,128)(2,1)} custom-call(s32[32]{0:T(128)S(1)} %get-tuple-element.104.low.refs_0_, s32[32]{0:T(128)S(1)} %get-tuple-element.103.high.refs_1_, s32[17]{0:T(128)S(1)} %slice_bitcast_fusion.base.refs_2_, s32[1]{0:T(128)} %bitcast.8.quarter, bf16[8192,512]{1,0:T(8,128)(2,1)} %get-tuple-element.47.near_ref, ...), custom_call_target="tpu_custom_call" | custom-call | flops 4294967296 | bytes 16777216 | tf_op jit(solution)/shard_map/partial_sums/pallas_call | solution.py:294
  129.1 2.9 collective-permute-start.12
  132.8 20.4 %collective-permute-done.12.refs_5_ = bf16[16,224,128]{2,1,0:T(8,128)(2,1)S(1)} collective-permute-done((bf16[16,224,128]{2,1,0:T(8,128)(2,1)}, bf16[16,224,128]{2,1,0:T(8,128)(2,1)S(1)}, u32[]{:S(2)}, u32[]{:S(2)}) %collective-permute-start.12) | collective-permute-done | bytes 917536 | tf_op jit(solution)/shard_map/ppermute | solution.py:390
  154.3 22.0 %collective-permute-done.14.refs_7_ = bf16[16,224,128]{2,1,0:T(8,128)(2,1)S(1)} collective-permute-done((bf16[16,224,128]{2,1,0:T(8,128)(2,1)S(1)}, bf16[16,224,128]{2,1,0:T(8,128)(2,1)S(1)}, u32[]{:S(2)}, u32[]{:S(2)}) %collective-permute-start.14) | collective-permute-done | bytes 917536 | tf_op jit(solution)/shard_map/ppermute | solution.py:391
  176.3 19.7 %partial_sums.3 = bf16[8192,256]{1,0:T(8,128)(2,1)} custom-call(s32[32]{0:T(128)S(1)} %get-tuple-element.104.low.refs_0_, s32[32]{0:T(128)S(1)} %get-tuple-element.103.high.refs_1_, s32[17]{0:T(128)S(1)} %slice_bitcast_fusion.base.refs_2_, s32[1]{0:T(128)} %bitcast.8.quarter, bf16[8192,512]{1,0:T(8,128)(2,1)} %get-tuple-element.47.near_ref, ...), custom_call_target="tpu_custom_call" | custom-call | flops 4294967296 | bytes 16777216 | tf_op jit(solution)/shard_map/partial_sums/pallas_call | solution.py:294
  196.0 4.8 %dynamic-slice_bitcast_fusion = (bf16[16,224,256]{2,1,0:T(8,128)(2,1)S(1)}, bf16[16,224,256]{2,1,0:T(8,128)(2,1)}, bf16[16,224,256]{2,1,0:T(8,128)(2,1)}) fusion(bf16[16,1024,224]{1,2,0:T(8,128)(2,1)} %param.11, s32[]{:T(128)S(6)} %select_n.50, s32[]{:T(128)S(6)} %select_n.53, s32[]{:T(128)S(6)} %select_n.49), kind=kLoop, calls=%fused_computation | loop fusion | bytes 11010060 | tf_op jit(solution)/shard_map/dynamic_slice | solution.py:416
  200.9 1.4 collective-permute-start.16
  202.3 41.2 %collective-permute-done.16.refs_9_.refs_2_.refs_0_ = bf16[16,224,256]{2,1,0:T(8,128)(2,1)} collective-permute-done((bf16[16,224,256]{2,1,0:T(8,128)(2,1)S(1)}, bf16[16,224,256]{2,1,0:T(8,128)(2,1)}, u32[]{:S(2)}, u32[]{:S(2)}) %collective-permute-start.16) | collective-permute-done | bytes 1835040 | tf_op jit(solution)/shard_map/ppermute | solution.py:390
  243.5 5.6 %broadcast_in_dim.5.place_ref = s32[16,1024,128]{2,1,0:T(8,128)} broadcast(s32[16,1024]{1,0:T(8,128)S(1)} %get-tuple-element.60), dimensions={0,1} | broadcast | bytes 8454144 | tf_op jit(solution)/shard_map/broadcast_in_dim | solution.py:452
  249.1 16.7 %scatter_rows.1.refs_4_.onehot_ref = bf16[1024,8192]{1,0:T(8,128)(2,1)} custom-call(s32[32]{0:T(128)S(1)} %get-tuple-element.104.low.refs_0_, s32[32]{0:T(128)S(1)} %get-tuple-element.103.high.refs_1_, s32[16,1024,128]{2,1,0:T(8,128)} %broadcast_in_dim.5.place_ref), custom_call_target="tpu_custom_call" | custom-call | flops 8388608 | bytes 16777216 | tf_op jit(solution)/shard_map/scatter_rows/pallas_call | solution.py:251
  265.8 2.7 convert_element_type.57
  268.5 18.7 %reduce-scatter.5.cloned.1.call-done = bf16[2048,256]{1,0:T(8,128)(2,1)} async-done(((bf16[8192,256]{1,0:T(8,128)(2,1)}), bf16[2048,256]{1,0:T(8,128)(2,1)}) %reduce-scatter.5.cloned.1.call-update) | async-done | bytes 1048592 | tf_op jit(solution)/shard_map/reduce_scatter | solution.py:442
  287.2 1.5 convert_element_type.59
  289.1 2.0 fusion.3
  291.3 3.6 collective-permute-start.18
  295.0 1.9 collective-permute-start.19
  297.4 16.5 %down_and_mix.6.start = f32[1024,1024]{1,0:T(8,128)} custom-call(s32[32]{0:T(128)} %copy-done.2, s32[32]{0:T(128)} %copy-done.1, s32[17]{0:T(128)} %copy-done.3, s32[3]{0:T(128)} %stack.83.refs_3_, bf16[1024,8192]{1,0:T(8,128)(2,1)} %scatter_rows.1.refs_4_.onehot_ref, bf16[2048,256]{1,0:T(8,128)(2,1)} %copy-done.7, bf16[2048,256]{1,0:T(8,128)(2,1)} %copy-done.7, ...), custom_call_target="tpu_custom_call" | custom-call | flops 4294967296 | bytes 4194304 | tf_op jit(solution)/shard_map/down_and_mix/pallas_call | solution.py:352
  313.9 3.6 collective-permute-done.18.up_ref
  317.4 3.4 collective-permute-done.19.down_ref
  320.8 2.1 collective-permute-start.20
  322.9 1.9 collective-permute-start.21
  325.4 17.3 %down_and_mix.7.start = f32[1024,1024]{1,0:T(8,128)} custom-call(s32[32]{0:T(128)} %copy-done.2, s32[32]{0:T(128)} %copy-done.1, s32[17]{0:T(128)} %copy-done.3, s32[3]{0:T(128)} %pad_add_fusion.1.block, bf16[1024,8192]{1,0:T(8,128)(2,1)} %scatter_rows.1.refs_4_.onehot_ref, bf16[2048,256]{1,0:T(8,128)(2,1)} %copy-done.10, ...), custom_call_target="tpu_custom_call" | custom-call | flops 4294967296 | bytes 4194304 | tf_op jit(solution)/shard_map/down_and_mix/pallas_call | solution.py:352
  344.4 3.2 collective-permute-done.21.down_ref
  348.4 2.5 collective-permute-start.23
  352.1 17.7 %down_and_mix.8.start = f32[1024,1024]{1,0:T(8,128)} custom-call(s32[32]{0:T(128)} %copy-done.2, s32[32]{0:T(128)} %copy-done.1, s32[17]{0:T(128)} %copy-done.3, s32[3]{0:T(128)} %pad_add_fusion.3.block, bf16[1024,8192]{1,0:T(8,128)(2,1)} %scatter_rows.1.refs_4_.onehot_ref, bf16[2048,256]{1,0:T(8,128)(2,1)} %copy-done.10, ...), custom_call_target="tpu_custom_call" | custom-call | flops 4294967296 | bytes 4194304 | tf_op jit(solution)/shard_map/down_and_mix/pallas_call | solution.py:352
  369.8 17.6 %down_and_mix.9.start = f32[1024,1024]{1,0:T(8,128)} custom-call(s32[32]{0:T(128)} %copy-done.2, s32[32]{0:T(128)} %copy-done.1, s32[17]{0:T(128)} %copy-done.3, s32[3]{0:T(128)} %get-tuple-element.106.block, bf16[1024,8192]{1,0:T(8,128)(2,1)} %scatter_rows.1.refs_4_.onehot_ref, bf16[2048,256]{1,0:T(8,128)(2,1)} %copy-done.11, ...), custom_call_target="tpu_custom_call" | custom-call | flops 4294967296 | bytes 4194304 | tf_op jit(solution)/shard_map/down_and_mix/pallas_call | solution.py:352
  388.8 6.2 %down_and_mix.10 = bf16[1024,512]{1,0:T(8,128)(2,1)} custom-call(s32[32]{0:T(128)} %copy-done.2, s32[32]{0:T(128)} %copy-done.1, s32[17]{0:T(128)} %copy-done.3, s32[3]{0:T(128)} %get-tuple-element.105.block, bf16[1024,8192]{1,0:T(8,128)(2,1)} %scatter_rows.1.refs_4_.onehot_ref, bf16[2048,256]{1,0:T(8,128)(2,1)} %copy-done.8, bf16[2048,256]{1,0:T(8,128)(2,1)} %copy-done.9, ...), custom_call_target="tpu_custom_call" | custom-call | flops 2147483648 | bytes 4194304 | tf_op jit(solution)/shard_map/down_and_mix/pallas_call | solution.py:352
  396.1 3.1 collective-permute-start.24
  399.2 1.5 collective-permute-done.24
  402.5 6.7 %down_and_mix.11 = f32[1024,512]{1,0:T(8,128)} custom-call(s32[32]{0:T(128)} %copy-done.2, s32[32]{0:T(128)} %copy-done.1, s32[17]{0:T(128)} %copy-done.3, s32[3]{0:T(128)} %get-tuple-element.105.block, bf16[1024,8192]{1,0:T(8,128)(2,1)} %scatter_rows.1.refs_4_.onehot_ref, bf16[2048,256]{1,0:T(8,128)(2,1)} %copy-done.8, bf16[2048,256]{1,0:T(8,128)(2,1)} %copy-done.9, ...), custom_call_target="tpu_custom_call" | custom-call | flops 2147483648 | bytes 4194304 | tf_op jit(solution)/shard_map/down_and_mix/pallas_call | solution.py:352
  409.1 1.3 slice.85
  410.4 5.5 %collective-permute-done.25 = bf16[1024,224]{1,0:T(8,128)(2,1)S(1)} collective-permute-done((bf16[1024,224]{1,0:T(8,128)(2,1)S(1)}, bf16[1024,224]{1,0:T(8,128)(2,1)S(1)}, u32[]{:S(2)}, u32[]{:S(2)}) %collective-permute-start.25) | collective-permute-done | bytes 458784 | tf_op jit(solution)/shard_map/ppermute | solution.py:390
  416.2 1.5 collective-permute-done.26
  417.8 1.4 fusion.1
  419.1 17.6 %all_to_all.10 = bf16[16,64,224]{2,1,0:T(8,128)(2,1)S(1)} all-to-all(bf16[16,64,224]{2,1,0:T(8,128)(2,1)S(1)} %bitcast.39), channel_id=1, replica_groups=mesh['parts'=2,'ep'=16,'tp'=1] {'ep'}, dimensions={0} | all-to-all | bytes 917504 | tf_op jit(solution)/shard_map/all_to_all | solution.py:503
  437.1 1.6 reshape.65
  (87 shorter events, 21.5 us)
Async XLA Ops:
  11.0 20.4 %all-to-all-start = ((bf16[16,64,256]{2,1,0:T(8,128)(2,1)}), bf16[16,64,256]{2,1,0:T(8,128)(2,1)S(1)}, u32[]{:S(2)}, u32[]{:S(2)}) async-start(bf16[16,64,256]{2,1,0:T(8,128)(2,1)} %pad_maximum_fusion), calls=%async_computation | async-start | bytes 1048576 | tf_op jit(solution)/shard_map/all_to_all | solution.py:406
  17.5 248.3 %reduce-scatter.3.cloned.1.call-start = ((), (), s32[]{:S(2)}) async-start(), calls=%async_computation.4 | async-start | bytes 5242880 | tf_op jit(solution)/shard_map/reduce_scatter | solution.py:442
  17.6 5.2 %copy-start.4 = (bf16[16,224,1024]{2,1,0:T(8,128)(2,1)S(1)}, bf16[16,224,1024]{2,1,0:T(8,128)(2,1)}, u32[]{:S(2)}) copy-start(bf16[16,224,1024]{2,1,0:T(8,128)(2,1)} %refs_1_.3) | copy-start | bytes 22020100
  21.4 45.6 %collective-permute-start.6 = (bf16[16,224,128]{2,1,0:T(8,128)(2,1)}, bf16[16,224,128]{2,1,0:T(8,128)(2,1)S(1)}, u32[]{:S(2)}, u32[]{:S(2)}) collective-permute-start(bf16[16,224,128]{2,1,0:T(8,128)(2,1)} %get-tuple-element.91), channel_id=1, source_target_pairs={{0,2},{1,3},{2,0},{3,1},{4,6},{5,7},{6,4},{7,5},{8,10},{9,11},{10,... | collective-permute-start | bytes 2752520 | tf_op jit(solution)/shard_map/ppermute | solution.py:390
  35.0 1.9 collective-permute-start
  35.0 32.2 %collective-permute-start.1 = (bf16[1024,256]{1,0:T(8,128)(2,1)S(1)}, bf16[1024,256]{1,0:T(8,128)(2,1)S(1)}, u32[]{:S(2)}, u32[]{:S(2)}) collective-permute-start(bf16[1024,256]{1,0:T(8,128)(2,1)S(1)} %bitcast.36), channel_id=1, source_target_pairs={{0,2},{1,3},{2,0},{3,1},{4,6},{5,7},{6,4},{7,5},{8,10},{9,11},{10,... | collective-permute-start | bytes 1572872 | tf_op jit(solution)/shard_map/ppermute | solution.py:390
  36.1 140.2 %copy-start.3 = (s32[17]{0:T(128)}, s32[17]{0:T(128)S(1)}, u32[]{:S(2)}) copy-start(s32[17]{0:T(128)S(1)} %slice_bitcast_fusion.base.refs_2_) | copy-start | bytes 208
  36.3 212.8 %copy-start.1 = (s32[32]{0:T(128)}, s32[32]{0:T(128)S(1)}, u32[]{:S(2)}) copy-start(s32[32]{0:T(128)S(1)} %get-tuple-element.103.high.refs_1_) | copy-start | bytes 388
  36.3 212.8 %copy-start.2 = (s32[32]{0:T(128)}, s32[32]{0:T(128)S(1)}, u32[]{:S(2)}) copy-start(s32[32]{0:T(128)S(1)} %get-tuple-element.104.low.refs_0_) | copy-start | bytes 388
  36.9 40.5 %collective-permute-start.7 = (bf16[16,224,128]{2,1,0:T(8,128)(2,1)S(1)}, bf16[16,224,128]{2,1,0:T(8,128)(2,1)S(1)}, u32[]{:S(2)}, u32[]{:S(2)}) collective-permute-start(bf16[16,224,128]{2,1,0:T(8,128)(2,1)S(1)} %get-tuple-element.52), channel_id=1, source_target_pairs={{0,2},{1,3},{2,0},{3,1},{4,6},{5,7},{6,4},{7,5},{8,10},{9,11},{10,... | collective-permute-start | bytes 2752520 | tf_op jit(solution)/shard_map/ppermute | solution.py:390
  37.6 39.9 %copy-start.12 = (bf16[16,224,128]{2,1,0:T(8,128)(2,1)S(1)}, bf16[16,224,128]{2,1,0:T(8,128)(2,1)}, u32[]{:S(2)}) copy-start(bf16[16,224,128]{2,1,0:T(8,128)(2,1)} %get-tuple-element.50) | copy-start | bytes 2752516
  65.0 2.1 copy-start
  67.0 21.6 %collective-permute-start.8 = (bf16[16,224,128]{2,1,0:T(8,128)(2,1)S(1)}, bf16[16,224,128]{2,1,0:T(8,128)(2,1)S(1)}, u32[]{:S(2)}, u32[]{:S(2)}) collective-permute-start(bf16[16,224,128]{2,1,0:T(8,128)(2,1)S(1)} %collective-permute-done.6.refs_4_), channel_id=1, source_target_pairs={{0,16},{16,0},{1,17},{17,1},{2,18},{18,2},{3,19},{19,3},{4,20},{20... | collective-permute-start | bytes 2752520 | tf_op jit(solution)/shard_map/ppermute | solution.py:391
  67.2 21.5 %collective-permute-start.2 = (bf16[1024,256]{1,0:T(8,128)(2,1)S(1)}, bf16[1024,256]{1,0:T(8,128)(2,1)S(1)}, u32[]{:S(2)}, u32[]{:S(2)}) collective-permute-start(bf16[1024,256]{1,0:T(8,128)(2,1)S(1)} %collective-permute-done.1.refs_0_), channel_id=1, source_target_pairs={{0,1},{1,0},{2,3},{3,2},{4,5},{5,4},{6,7},{7,6},{8,9},{9,8},{10,11... | collective-permute-start | bytes 1572872 | tf_op jit(solution)/shard_map/ppermute | solution.py:389
  68.0 36.1 %collective-permute-start.4 = (bf16[16,224,128]{2,1,0:T(8,128)(2,1)}, bf16[16,224,128]{2,1,0:T(8,128)(2,1)S(1)}, u32[]{:S(2)}, u32[]{:S(2)}) collective-permute-start(bf16[16,224,128]{2,1,0:T(8,128)(2,1)} %get-tuple-element.92), channel_id=1, source_target_pairs={{0,1},{1,0},{2,3},{3,2},{4,5},{5,4},{6,7},{7,6},{8,9},{9,8},{10,11... | collective-permute-start | bytes 2752520 | tf_op jit(solution)/shard_map/ppermute | solution.py:389
  68.0 36.1 %collective-permute-start.5 = (bf16[16,224,128]{2,1,0:T(8,128)(2,1)}, bf16[16,224,128]{2,1,0:T(8,128)(2,1)S(1)}, u32[]{:S(2)}, u32[]{:S(2)}) collective-permute-start(bf16[16,224,128]{2,1,0:T(8,128)(2,1)} %get-tuple-element.89), channel_id=1, source_target_pairs={{0,1},{1,0},{2,3},{3,2},{4,5},{5,4},{6,7},{7,6},{8,9},{9,8},{10,11... | collective-permute-start | bytes 2752520 | tf_op jit(solution)/shard_map/ppermute | solution.py:389
  77.5 26.5 %collective-permute-start.3 = (bf16[16,224,128]{2,1,0:T(8,128)(2,1)S(1)}, bf16[16,224,128]{2,1,0:T(8,128)(2,1)S(1)}, u32[]{:S(2)}, u32[]{:S(2)}) collective-permute-start(bf16[16,224,128]{2,1,0:T(8,128)(2,1)S(1)} %copy-done.12), channel_id=1, source_target_pairs={{0,2},{1,3},{2,0},{3,1},{4,6},{5,7},{6,4},{7,5},{8,10},{9,11},{10,... | collective-permute-start | bytes 2752520 | tf_op jit(solution)/shard_map/ppermute | solution.py:390
  88.6 20.7 %collective-permute-start.9 = (bf16[16,224,128]{2,1,0:T(8,128)(2,1)S(1)}, bf16[16,224,128]{2,1,0:T(8,128)(2,1)S(1)}, u32[]{:S(2)}, u32[]{:S(2)}) collective-permute-start(bf16[16,224,128]{2,1,0:T(8,128)(2,1)S(1)} %collective-permute-done.7.refs_5_), channel_id=1, source_target_pairs={{0,16},{16,0},{1,17},{17,1},{2,18},{18,2},{3,19},{19,3},{4,20},{20... | collective-permute-start | bytes 2752520 | tf_op jit(solution)/shard_map/ppermute | solution.py:391
  128.9 158.3 %reduce-scatter.5.cloned.1.call-start = ((), (), s32[]{:S(2)}) async-start(), calls=%async_computation.5 | async-start | bytes 5242880 | tf_op jit(solution)/shard_map/reduce_scatter | solution.py:442
  129.1 24.1 %collective-permute-start.12 = (bf16[16,224,128]{2,1,0:T(8,128)(2,1)}, bf16[16,224,128]{2,1,0:T(8,128)(2,1)S(1)}, u32[]{:S(2)}, u32[]{:S(2)}) collective-permute-start(bf16[16,224,128]{2,1,0:T(8,128)(2,1)} %get-tuple-element.57), channel_id=1, source_target_pairs={{0,2},{1,3},{2,0},{3,1},{4,6},{5,7},{6,4},{7,5},{8,10},{9,11},{10,... | collective-permute-start | bytes 2752520 | tf_op jit(solution)/shard_map/ppermute | solution.py:390
  132.0 22.3 %collective-permute-start.13 = (bf16[16,224,128]{2,1,0:T(8,128)(2,1)S(1)}, bf16[16,224,128]{2,1,0:T(8,128)(2,1)S(1)}, u32[]{:S(2)}, u32[]{:S(2)}) collective-permute-start(bf16[16,224,128]{2,1,0:T(8,128)(2,1)S(1)} %collective-permute-done.3.refs_4_), channel_id=1, source_target_pairs={{0,16},{16,0},{1,17},{17,1},{2,18},{18,2},{3,19},{19,3},{4,20},{20... | collective-permute-start | bytes 2752520 | tf_op jit(solution)/shard_map/ppermute | solution.py:391
  132.0 22.3 %collective-permute-start.10 = (bf16[16,224,128]{2,1,0:T(8,128)(2,1)S(1)}, bf16[16,224,128]{2,1,0:T(8,128)(2,1)S(1)}, u32[]{:S(2)}, u32[]{:S(2)}) collective-permute-start(bf16[16,224,128]{2,1,0:T(8,128)(2,1)S(1)} %get-tuple-element.90), channel_id=1, source_target_pairs={{0,1},{1,0},{2,3},{3,2},{4,5},{5,4},{6,7},{7,6},{8,9},{9,8},{10,11... | collective-permute-start | bytes 2752520 | tf_op jit(solution)/shard_map/ppermute | solution.py:389
  132.8 21.5 %collective-permute-start.11 = (bf16[16,224,128]{2,1,0:T(8,128)(2,1)}, bf16[16,224,128]{2,1,0:T(8,128)(2,1)S(1)}, u32[]{:S(2)}, u32[]{:S(2)}) collective-permute-start(bf16[16,224,128]{2,1,0:T(8,128)(2,1)} %get-tuple-element.87), channel_id=1, source_target_pairs={{0,1},{1,0},{2,3},{3,2},{4,5},{5,4},{6,7},{7,6},{8,9},{9,8},{10,11... | collective-permute-start | bytes 2752520 | tf_op jit(solution)/shard_map/ppermute | solution.py:389
  154.3 22.0 %collective-permute-start.14 = (bf16[16,224,128]{2,1,0:T(8,128)(2,1)S(1)}, bf16[16,224,128]{2,1,0:T(8,128)(2,1)S(1)}, u32[]{:S(2)}, u32[]{:S(2)}) collective-permute-start(bf16[16,224,128]{2,1,0:T(8,128)(2,1)S(1)} %collective-permute-done.12.refs_5_), channel_id=1, source_target_pairs={{0,16},{16,0},{1,17},{17,1},{2,18},{18,2},{3,19},{19,3},{4,20},{20... | collective-permute-start | bytes 2752520 | tf_op jit(solution)/shard_map/ppermute | solution.py:391
  200.9 42.6 %collective-permute-start.16 = (bf16[16,224,256]{2,1,0:T(8,128)(2,1)S(1)}, bf16[16,224,256]{2,1,0:T(8,128)(2,1)}, u32[]{:S(2)}, u32[]{:S(2)}) collective-permute-start(bf16[16,224,256]{2,1,0:T(8,128)(2,1)S(1)} %get-tuple-element.62), channel_id=1, source_target_pairs={{0,2},{1,3},{2,0},{3,1},{4,6},{5,7},{6,4},{7,5},{8,10},{9,11},{10,... | collective-permute-start | bytes 5505032 | tf_op jit(solution)/shard_map/ppermute | solution.py:390
  202.3 88.8 %collective-permute-start.15 = (bf16[16,224,256]{2,1,0:T(8,128)(2,1)}, bf16[16,224,256]{2,1,0:T(8,128)(2,1)S(1)}, u32[]{:S(2)}, u32[]{:S(2)}) collective-permute-start(bf16[16,224,256]{2,1,0:T(8,128)(2,1)} %get-tuple-element.85), channel_id=1, source_target_pairs={{0,1},{1,0},{2,3},{3,2},{4,5},{5,4},{6,7},{7,6},{8,9},{9,8},{10,11... | collective-permute-start | bytes 5505032 | tf_op jit(solution)/shard_map/ppermute | solution.py:389
  243.5 47.6 %collective-permute-start.17 = (bf16[16,224,256]{2,1,0:T(8,128)(2,1)}, bf16[16,224,256]{2,1,0:T(8,128)(2,1)}, u32[]{:S(2)}, u32[]{:S(2)}) collective-permute-start(bf16[16,224,256]{2,1,0:T(8,128)(2,1)} %collective-permute-done.16.refs_9_.refs_2_.refs_0_), channel_id=1, source_target_pairs={{0,16},{16,0},{1,17},{17,1},{2,18},{18,2},{3,19},{19,3},{4,20},{20... | collective-permute-start | bytes 5505032 | tf_op jit(solution)/shard_map/ppermute | solution.py:391
  287.2 1.9 copy-start.6
  291.1 6.3 %copy-start.5 = (bf16[16,224,256]{2,1,0:T(8,128)(2,1)}, bf16[16,224,256]{2,1,0:T(8,128)(2,1)S(1)}, u32[]{:S(2)}) copy-start(bf16[16,224,256]{2,1,0:T(8,128)(2,1)S(1)} %collective-permute-done.15.refs_8_.refs_1_) | copy-start | bytes 5505028
  291.3 6.1 %copy-start.7 = (bf16[2048,256]{1,0:T(8,128)(2,1)}, bf16[2048,256]{1,0:T(8,128)(2,1)S(1)}, u32[]{:S(2)}) copy-start(bf16[2048,256]{1,0:T(8,128)(2,1)S(1)} %constant_dynamic-update-slice_fusion.refs_5_.refs_6_) | copy-start | bytes 3145732
  291.3 26.1 %collective-permute-start.18 = (bf16[2048,256]{1,0:T(8,128)(2,1)S(1)}, bf16[2048,256]{1,0:T(8,128)(2,1)S(1)}, u32[]{:S(2)}, u32[]{:S(2)}) collective-permute-start(bf16[2048,256]{1,0:T(8,128)(2,1)S(1)} %constant_dynamic-update-slice_fusion.refs_5_.refs_6_), channel_id=1, source_target_pairs={{0,4},{1,5},{2,6},{3,7},{4,8},{5,9},{6,10},{7,11},{8,12},{9,13},{1... | collective-permute-start | bytes 3145736 | tf_op jit(solution)/shard_map/ppermute | solution.py:468
  295.0 25.8 %collective-permute-start.19 = (bf16[2048,256]{1,0:T(8,128)(2,1)S(1)}, bf16[2048,256]{1,0:T(8,128)(2,1)}, u32[]{:S(2)}, u32[]{:S(2)}) collective-permute-start(bf16[2048,256]{1,0:T(8,128)(2,1)S(1)} %constant_dynamic-update-slice_fusion.refs_5_.refs_6_), channel_id=1, source_target_pairs={{4,0},{5,1},{6,2},{7,3},{8,4},{9,5},{10,6},{11,7},{12,8},{13,9},{1... | collective-permute-start | bytes 3145736 | tf_op jit(solution)/shard_map/ppermute | solution.py:468
  317.4 8.0 %copy-start.10 = (bf16[2048,256]{1,0:T(8,128)(2,1)}, bf16[2048,256]{1,0:T(8,128)(2,1)S(1)}, u32[]{:S(2)}) copy-start(bf16[2048,256]{1,0:T(8,128)(2,1)S(1)} %collective-permute-done.18.up_ref) | copy-start | bytes 3145732
  320.8 22.7 %collective-permute-start.20 = (bf16[2048,256]{1,0:T(8,128)(2,1)S(1)}, bf16[2048,256]{1,0:T(8,128)(2,1)S(1)}, u32[]{:S(2)}, u32[]{:S(2)}) collective-permute-start(bf16[2048,256]{1,0:T(8,128)(2,1)S(1)} %collective-permute-done.18.up_ref), channel_id=1, source_target_pairs={{4,8},{5,9},{6,10},{7,11},{8,12},{9,13},{10,14},{11,15},{20,24},{2... | collective-permute-start | bytes 3145736 | tf_op jit(solution)/shard_map/ppermute | solution.py:468
  322.9 24.8 %collective-permute-start.21 = (bf16[2048,256]{1,0:T(8,128)(2,1)}, bf16[2048,256]{1,0:T(8,128)(2,1)}, u32[]{:S(2)}, u32[]{:S(2)}) collective-permute-start(bf16[2048,256]{1,0:T(8,128)(2,1)} %collective-permute-done.19.down_ref), channel_id=1, source_target_pairs={{4,0},{5,1},{6,2},{7,3},{8,4},{9,5},{10,6},{11,7},{20,16},{21,17},... | collective-permute-start | bytes 3145736 | tf_op jit(solution)/shard_map/ppermute | solution.py:468
  343.4 1.0 copy-start.11
  347.7 39.7 %collective-permute-start.22 = (bf16[2048,256]{1,0:T(8,128)(2,1)}, bf16[2048,256]{1,0:T(8,128)(2,1)S(1)}, u32[]{:S(2)}, u32[]{:S(2)}) collective-permute-start(bf16[2048,256]{1,0:T(8,128)(2,1)} %copy-done.11), channel_id=1, source_target_pairs={{8,12},{9,13},{10,14},{11,15},{24,28},{25,29},{26,30},{27,31}} | collective-permute-start | bytes 3145736 | tf_op jit(solution)/shard_map/ppermute | solution.py:468
  348.4 39.0 %collective-permute-start.23 = (bf16[2048,256]{1,0:T(8,128)(2,1)}, bf16[2048,256]{1,0:T(8,128)(2,1)S(1)}, u32[]{:S(2)}, u32[]{:S(2)}) collective-permute-start(bf16[2048,256]{1,0:T(8,128)(2,1)} %collective-permute-done.21.down_ref), channel_id=1, source_target_pairs={{4,0},{5,1},{6,2},{7,3},{20,16},{21,17},{22,18},{23,19}} | collective-permute-start | bytes 3145736 | tf_op jit(solution)/shard_map/ppermute | solution.py:468
  387.4 1.0 copy-start.8
  387.4 1.4 copy-start.9
  396.1 4.6 %collective-permute-start.24 = (bf16[1024,224]{1,0:T(8,128)(2,1)S(1)}, bf16[1024,224]{1,0:T(8,128)(2,1)S(1)}, u32[]{:S(2)}, u32[]{:S(2)}) collective-permute-start(bf16[1024,224]{1,0:T(8,128)(2,1)S(1)} %slice.59), channel_id=1, source_target_pairs={{0,1},{1,0},{2,3},{3,2},{4,5},{5,4},{6,7},{7,6},{8,9},{9,8},{10,11... | collective-permute-start | bytes 1376264 | tf_op jit(solution)/shard_map/ppermute | solution.py:389
  401.9 14.0 %collective-permute-start.25 = (bf16[1024,224]{1,0:T(8,128)(2,1)S(1)}, bf16[1024,224]{1,0:T(8,128)(2,1)S(1)}, u32[]{:S(2)}, u32[]{:S(2)}) collective-permute-start(bf16[1024,224]{1,0:T(8,128)(2,1)S(1)} %add_convert_fusion), channel_id=1, source_target_pairs={{0,2},{1,3},{2,0},{3,1},{4,6},{5,7},{6,4},{7,5},{8,10},{9,11},{10,... | collective-permute-start | bytes 1376264 | tf_op jit(solution)/shard_map/ppermute | solution.py:390
  415.8 1.9 collective-permute-start.26
Sparse Core Ops, SparseCore 0:
  129.0 78.4 reduce-scatter.2
  209.9 77.2 reduce-scatter.4

commit v11 on v9

--- a/solution.py
+++ b/solution.py
@@ -143,7 +143,7 @@
     return (row >= base[e]) & (row < base[e + 1])
 
 
-def sort_kernel(experts, low, high, base, across_ref, gates_ref, *refs):
+def sort_kernel(experts, first, low, high, base, across_ref, gates_ref, *refs):
     slices, (out, scale_out, onehot_ref, name_ref) = refs[:-4], refs[-4:]
     tokens = onehot_ref.shape[1]
     number = lax.broadcasted_iota(jnp.int32, (TILE, 128), 0).astype(F32).astype(BF16)
@@ -151,7 +151,7 @@
 
     @pl.loop(0, BLOCK // TILE)
     def _(part):
-        i = pl.program_id(0) * (BLOCK // TILE) + part
+        i = (first + pl.program_id(0)) * (BLOCK // TILE) + part
         row0 = i * TILE
         here = pl.ds(pl.multiple_of(part * TILE, TILE), TILE)
 
@@ -176,25 +176,30 @@
     scale_out[...] = jnp.broadcast_to(scale, lane.shape)
 
 
-def sort_rows(spans, base, across, gates, slices, rows, experts):
+def sort_rows(spans, base, across, gates, slices, rows, experts, begun=()):
+    first = rows // BLOCK // 2 * bool(begun)
+    kernel = functools.partial(sort_kernel, experts, first)
+    if begun:
+        kernel = lambda *refs: sort_kernel(experts, first, *refs[:-7], *refs[-4:])
     tokens = gates.shape[0]
     across = across[:experts].reshape(experts, tokens // 128, 128)
     whole = lambda i, *_: (0, 0)
     width = len(slices) * LANES
     return pl.pallas_call(
-        functools.partial(sort_kernel, experts),
+        kernel,
         grid_spec=pltpu.PrefetchScalarGridSpec(
             num_scalar_prefetch=3,
-            grid=(rows // BLOCK,),
+            grid=(rows // BLOCK // 2,),
             in_specs=[
                 pl.BlockSpec(across.shape, lambda i, *_: (0, 0, 0)),
                 pl.BlockSpec((tokens, UNITS), whole),
             ]
-            + [pl.BlockSpec((tokens, LANES), whole)] * len(slices),
+            + [pl.BlockSpec((tokens, LANES), whole)] * len(slices)
+            + [pl.BlockSpec(memory_space=pl.ANY)] * len(begun),
             out_specs=[
-                pl.BlockSpec((BLOCK, width), lambda i, *_: (i, 0)),
-                pl.BlockSpec((BLOCK, UNITS), lambda i, *_: (i, 0)),
-                pl.BlockSpec((BLOCK, tokens), lambda i, *_: (i, 0)),
+                pl.BlockSpec((BLOCK, width), lambda i, *_: (first + i, 0)),
+                pl.BlockSpec((BLOCK, UNITS), lambda i, *_: (first + i, 0)),
+                pl.BlockSpec((BLOCK, tokens), lambda i, *_: (first + i, 0)),
             ],
             scratch_shapes=[pltpu.VMEM((BLOCK, UNITS), jnp.int32)],
         ),
@@ -203,10 +208,11 @@
             jax.ShapeDtypeStruct((rows, UNITS), F32),
             jax.ShapeDtypeStruct((rows, tokens), BF16),
         ],
+        input_output_aliases={5 + len(slices) + k: k for k in range(len(begun))},
         compiler_params=params(),
-        cost_estimate=cost(2 * rows * tokens * width, 8 * rows * width),
+        cost_estimate=cost(rows * tokens * width, 4 * rows * width),
         name="sort_rows",
-    )(*spans, base, across, gates, *slices)
+    )(*spans, base, across, gates, *slices, *begun)
 
 
 def sort_more_kernel(onehot_ref, *refs):
@@ -307,22 +313,27 @@
     )(*spans, base, quarter, near, far, w_gate, w_up, *pieces)
 
 
-def down_kernel(low, high, base, block, onehot_ref, up_ref, down_ref, start, *refs):
+def down_kernel(slots, low, high, base, block, onehot_ref, *refs):
+    hidden, start, refs = refs[: 2 * slots], refs[2 * slots], refs[2 * slots + 1 :]
     weights, (out, total_ref, value_ref) = refs[:-3], refs[-3:]
     width = weights[0].shape[1]
     j = pl.program_id(0)
+    slot = j // 2
 
     @pl.when(j == 0)
     def _():
         total_ref[...] = jnp.zeros_like(total_ref) if start is None else start[...]
         value_ref[...] = jnp.zeros_like(value_ref)
 
-    @pl.when(block[2] != 0)
+    @pl.when(block[3 * slot + 2] != 0)
     def _():
         for part in range(BLOCK // TILE):
-            i = (2 * block[0] + j) * (BLOCK // TILE) + part
+            i = (2 * block[3 * slot] + j % 2) * (BLOCK // TILE) + part
             here = slice(part * TILE, (part + 1) * TILE)
-            units = jnp.where(block[1] != 0, up_ref[here, :], down_ref[here, :])
+            source = 2 * slot + 1 - block[3 * slot + 1]
+            units = hidden[0][here, :]
+            for k in range(1, 2 * slots):
+                units = jnp.where(source == k, hidden[k][here, :], units)
 
             @pl.loop(low[i], high[i])
             def _(e):
@@ -343,22 +354,27 @@
 
 def down_and_mix(spans, base, block, onehot, hidden, start, at, weights, dtype):
     rows, units = hidden[0].shape
+    slots = len(hidden) // 2
     count, tokens = len(weights), onehot.shape[0]
-    some = pl.BlockSpec((BLOCK, units), lambda j, *_: (j, 0))
+    some = [
+        pl.BlockSpec((BLOCK, units), lambda j, *_, s=k // 2: (jnp.clip(j - 2 * s, 0, 1), 0))
+        for k in range(2 * slots)
+    ]
     whole = pl.BlockSpec((tokens, count * LANES), lambda j, *_: (0, 0))
-    kernel = down_kernel
+    kernel = functools.partial(down_kernel, slots)
     if start is None:
-        kernel = lambda *refs: down_kernel(*refs[:7], None, *refs[7:])
+        kernel = lambda *refs: down_kernel(slots, *refs[: 5 + 2 * slots], None, *refs[5 + 2 * slots :])
     return pl.pallas_call(
         kernel,
         grid_spec=pltpu.PrefetchScalarGridSpec(
             num_scalar_prefetch=4,
-            grid=(rows // BLOCK,),
+            grid=(2 * slots,),
             in_specs=[
-                pl.BlockSpec((tokens, BLOCK), lambda j, lo, hi, b, k: (0, 2 * k[0] + j)),
-                some,
-                some,
+                pl.BlockSpec(
+                    (tokens, BLOCK), lambda j, lo, hi, b, k: (0, 2 * k[3 * (j // 2)] + j % 2)
+                )
             ]
+            + some
             + [pl.BlockSpec((tokens, count * LANES), lambda j, *_: (0, at // count))]
             * (start is not None)
             + [pl.BlockSpec(w.shape, lambda j, *_: (0, 0, 0)) for w in weights],
@@ -370,7 +386,7 @@
         ),
         out_shape=jax.ShapeDtypeStruct((tokens, count * LANES), dtype),
         compiler_params=params(56),
-        cost_estimate=cost(2 * rows * tokens * LANES * count, 2 * rows * tokens),
+        cost_estimate=cost(2 * slots * rows * tokens * LANES * count, 2 * slots * rows * tokens),
         name="down_and_mix",
     )(*spans, base, block, onehot, *hidden, *([] if start is None else [start]), *weights)
 
@@ -420,28 +436,34 @@
     def after(value, *others):
         return lax.optimization_barrier((value, *others))[0]
 
-    near_rows, scale, onehot = sort_rows(spans, base, across, gates, near, rows, experts)
+    crossed = [to_cross(cut(0, cross_quarter)), to_cross(after(cut(1, cross_quarter), near[1], base))]
+    begun = sort_rows(spans, base, across, gates, near, rows, experts)
+    beside = [to_plane(after(crossed[0], begun[0]))]
+    rest = after(gates, crossed[0])
+    near_rows, scale, onehot = sort_rows(spans, base, across, rest, near, rows, experts, begun)
     far = after(far, near_rows)
     far_rows = sort_more(onehot, [far, to_twin(far)])
     scale = lax.dynamic_slice_in_dim(scale, (me // 4) * (rows // places), rows // places, 0)
 
-    crossed = [to_cross(cut(0, cross_quarter)), to_cross(cut(1, cross_quarter))]
     for n in range(2, 5):
         crossed.append(to_cross(after(cut(n, cross_quarter), far, *crossed[2:n])))
     twin_of = lambda n: to_twin(cut(n, twin_quarter))
 
+    for n in range(1, 4):
+        beside.append(to_plane(after(crossed[n], near_rows, beside[n - 1])))
+
     def sums_of(f, *first):
         rows_in = after(far_rows, *first)
-        across_x = crossed[2 * f : 2 * f + 2]
-        beside = [to_plane(after(piece, near_rows)) for piece in across_x]
-        held = [twin_of(2 * f), twin_of(2 * f + 1), *across_x, *beside]
+        pair = slice(2 * f, 2 * f + 2)
+        held = [twin_of(2 * f), twin_of(2 * f + 1), *crossed[pair], *beside[pair]]
         return partial_sums(f, spans, base, which, near_rows, rows_in, w_gate, w_up, held)
 
     def units_of(sums):
         sums = lax.psum_scatter(
             sums, "ep", scatter_dimension=0, axis_index_groups=line, tiled=True
-        ).astype(F32)
-        return (jax.nn.silu(sums[:, :UNITS]) * sums[:, UNITS:] * scale).astype(BF16)
+        )
+        gate, up = sums[:, :UNITS].astype(F32), sums[:, UNITS:].astype(F32)
+        return (jax.nn.silu(gate) * up * scale).astype(BF16)
 
     sums = sums_of(0, crossed[2])
     later = sums_of(1, sums)
@@ -468,6 +490,7 @@
 
     def mix(flags, hidden, start, at=0, count=4, dtype=F32):
         block = jnp.stack([jnp.asarray(flag, jnp.int32) for flag in flags])
+        hidden = list(hidden)
         return down_and_mix(
             spans, base, block, columns, hidden, start, at, pieces[at : at + count], dtype
         )
@@ -476,8 +499,9 @@
     total, waiting = mix((spot, 1, 1), [units, units], None), []
     for step in range(1, places):
         if step == places - 1:
-            for flags, hidden in waiting:
-                total = mix(flags, hidden, total)
+            if waiting:
+                both = [sum(map(tuple, parts), ()) for parts in zip(*waiting)]
+                total = mix(*both, total)
         *hidden, total = lax.optimization_barrier((*moving, total))
         came_up, came_down = spot >= step, spot < places - step
         above = jnp.minimum(spot + step, places - 1)
@@ -488,7 +512,8 @@
         waiting.append((flags, hidden))
         if 2 * step < places:
             waiting.append(((above, 0, came_up & came_down), hidden))
-        total = mix(*waiting.pop(0), total)
+        if step == 1:
+            total = mix(*waiting.pop(0), total)
     far = mix(flags, hidden, total, 2, 2, BF16)
     near = after(total, far)
     far, far_twin = far[:, :width], far[:, LANES : LANES + width]

time: 458 us -> 429 us (0.937)
  waiting for transfers between devices: 164 us -> 146 us
  Pallas kernels: 183 us -> 177 us
    ppermute x5, waiting for transfers between devices: 40.9 us -> 22.7 us  [fixed_weights(): to_plane = lambda value: lax.ppermute(value, 'parts', [(0, 1), (1, 0)])]
    pallas_call x6 -> x5, Pallas kernels: 81.5 us -> 73.8 us  [down_and_mix(): pl.pallas_call(kernel, grid_spec=pltpu.PrefetchScalarGridSpec(num_scalar_...]
    pallas_call x1 -> x2, Pallas kernels: 27.2 us -> 29.3 us  [sort_rows(): pl.pallas_call(kernel, grid_spec=pltpu.PrefetchScalarGridSpec(num_scalar_...]
  transfers between devices with their start and end apart: 30 -> 30, of which waited for: 18 -> 17; matrix products, arithmetic and copies ran while one was open for 6% -> 5% of each run, Pallas kernels for 35% -> 35%
where the time goes in v11:
time: 429 us; the launch traced here: 426 us
  Pallas kernels  177 us (41%)
  waiting for transfers between devices  146 us (34%)
  starting transfers between devices  32.5 us (8%)
  local copies, waits for them, and re-layouts  30.4 us (7%)
  blocking collectives  17.6 us (4%)
  between operations  13.8 us (3%)
  other arithmetic  8.75 us (2%)
    ppermute x7, waiting for transfers between devices, fixed_weights(): to_cross = lambda value: lax.ppermute(value, ('parts', 'ep'), cross)  80.1 us
    pallas_call x5, Pallas kernels, down_and_mix(): pl.pallas_call(kernel, grid_spec=pltpu.PrefetchScalarGridSpec(num_scalar_...  73.8 us
    pallas_call x2, Pallas kernels, partial_sums(): pl.pallas_call(partial_kernel, grid_spec=pltpu.PrefetchScalarGridSpec(num...  38.7 us
    pallas_call x2, Pallas kernels, sort_rows(): pl.pallas_call(kernel, grid_spec=pltpu.PrefetchScalarGridSpec(num_scalar_...  29.3 us
    ppermute x5, waiting for transfers between devices, fixed_weights(): to_plane = lambda value: lax.ppermute(value, 'parts', [(0, 1), (1, 0)])  22.7 us
    reduce_scatter x2, waiting for transfers between devices, units_of(): lax.psum_scatter(sums, 'ep', scatter_dimension=0, axis_index_groups=line,...  22.4 us
    all_to_all x1, blocking collectives, fixed_weights(): lax.all_to_all(mixed.reshape(size, count, width), 'ep', split_axis=0, con...  17.6 us
    pallas_call x1, Pallas kernels, scatter_rows(): pl.pallas_call(scatter_kernel, grid_spec=pltpu.PrefetchScalarGridSpec(num...  16.2 us
  transfers between devices with their start and end apart: 30, of which 17 were waited for; matrix products, arithmetic and copies ran while one was open for 5% of the time, Pallas kernels for 35%

profile of v11, /device:TPU:15, one launch (start us, length us, event | category | flops | bytes accessed | tf_op | source)
XLA Modules:
  0.0 426.3 jit_solution(9480621009761039980)
XLA Ops:
  8.0 1.8 reshape.61
  11.0 6.6 %all-to-all-start = ((bf16[16,64,256]{2,1,0:T(8,128)(2,1)}), bf16[16,64,256]{2,1,0:T(8,128)(2,1)S(1)}, u32[]{:S(2)}, u32[]{:S(2)}) async-start(bf16[16,64,256]{2,1,0:T(8,128)(2,1)} %pad_maximum_fusion), calls=%async_computation | async-start | bytes 1048576 | tf_op jit(solution)/shard_map/all_to_all | solution.py:422
  17.6 3.8 constant_dynamic-slice_fusion.2
  22.9 2.2 constant_dynamic-slice_fusion
  25.0 6.4 %all-to-all-done = bf16[16,64,256]{2,1,0:T(8,128)(2,1)S(1)} async-done(((bf16[16,64,256]{2,1,0:T(8,128)(2,1)}), bf16[16,64,256]{2,1,0:T(8,128)(2,1)S(1)}, u32[]{:S(2)}, u32[]{:S(2)}) %all-to-all-start) | async-done | bytes 524320 | tf_op jit(solution)/shard_map/all_to_all | solution.py:422
  31.4 3.6 order.1
  37.6 14.1 %sort_rows.2 = (bf16[8192,512]{1,0:T(8,128)(2,1)}, f32[8192,128]{1,0:T(8,128)S(1)}, bf16[8192,1024]{1,0:T(8,128)(2,1)}) custom-call(s32[32]{0:T(128)S(1)} %get-tuple-element.112.low.refs_0_, s32[32]{0:T(128)S(1)} %get-tuple-element.111.high.refs_1_, s32[17]{0:T(128)S(1)} %slice_bitcast_fusion.base.refs_2_, s32[16,8,128]{2,1,0:T(8,128)S(1)} %bitcast.39, ...), custom_call_target="tpu_custom_call" | custom-call | flops 4294967296 | bytes 16777216 | tf_op jit(solution)/shard_map/sort_rows/pallas_call | solution.py:188
  52.2 15.2 %sort_rows.3 = (bf16[8192,512]{1,0:T(8,128)(2,1)}, f32[8192,128]{1,0:T(8,128)S(1)}, bf16[8192,1024]{1,0:T(8,128)(2,1)}) custom-call(s32[32]{0:T(128)S(1)} %get-tuple-element.112.low.refs_0_, s32[32]{0:T(128)S(1)} %get-tuple-element.111.high.refs_1_, ...), custom_call_target="tpu_custom_call", output_to_operand_aliasing={{0}: (7, {}), {1}: (8, {}), {2}: (9, {})} | custom-call | flops 4294967296 | bytes 16777216 | tf_op jit(solution)/shard_map/sort_rows/pallas_call | solution.py:188
  67.3 2.0 copy-done
  70.6 6.9 %collective-permute-done.7.refs_5_ = bf16[16,224,128]{2,1,0:T(8,128)(2,1)S(1)} collective-permute-done((bf16[16,224,128]{2,1,0:T(8,128)(2,1)S(1)}, bf16[16,224,128]{2,1,0:T(8,128)(2,1)S(1)}, u32[]{:S(2)}, u32[]{:S(2)}) %collective-permute-start.7) | collective-permute-done | bytes 917536 | tf_op jit(solution)/shard_map/ppermute | solution.py:406
  78.3 15.3 %sort_more.1.far_ref = bf16[8192,512]{1,0:T(8,128)(2,1)} custom-call(bf16[8192,1024]{1,0:T(8,128)(2,1)} %get-tuple-element.56.onehot_ref, bf16[1024,256]{1,0:T(8,128)(2,1)S(1)} %collective-permute-done.2.refs_0_, bf16[1024,256]{1,0:T(8,128)(2,1)S(1)} %collective-permute-done.3.refs_1_), custom_call_target="tpu_custom_call" | custom-call | flops 8589934592 | bytes 33554432 | tf_op jit(solution)/shard_map/sort_more/pallas_call | solution.py:227
  93.6 6.5 %collective-permute-done.4.refs_4_ = bf16[16,224,128]{2,1,0:T(8,128)(2,1)S(1)} collective-permute-done((bf16[16,224,128]{2,1,0:T(8,128)(2,1)S(1)}, bf16[16,224,128]{2,1,0:T(8,128)(2,1)S(1)}, u32[]{:S(2)}, u32[]{:S(2)}) %collective-permute-start.4) | collective-permute-done | bytes 917536 | tf_op jit(solution)/shard_map/ppermute | solution.py:406
  100.2 19.3 %partial_sums.2 = bf16[8192,256]{1,0:T(8,128)(2,1)} custom-call(s32[32]{0:T(128)S(1)} %get-tuple-element.112.low.refs_0_, s32[32]{0:T(128)S(1)} %get-tuple-element.111.high.refs_1_, s32[17]{0:T(128)S(1)} %slice_bitcast_fusion.base.refs_2_, s32[1]{0:T(128)} %bitcast.8.quarter, bf16[8192,512]{1,0:T(8,128)(2,1)} %get-tuple-element.55.near_ref, ...), custom_call_target="tpu_custom_call" | custom-call | flops 4294967296 | bytes 16777216 | tf_op jit(solution)/shard_map/partial_sums/pallas_call | solution.py:300
  119.8 1.7 collective-permute-start.12
  122.5 20.4 %collective-permute-done.12.refs_5_ = bf16[16,224,128]{2,1,0:T(8,128)(2,1)S(1)} collective-permute-done((bf16[16,224,128]{2,1,0:T(8,128)(2,1)}, bf16[16,224,128]{2,1,0:T(8,128)(2,1)S(1)}, u32[]{:S(2)}, u32[]{:S(2)}) %collective-permute-start.12) | collective-permute-done | bytes 917536 | tf_op jit(solution)/shard_map/ppermute | solution.py:406
  143.9 21.6 %collective-permute-done.14.refs_7_ = bf16[16,224,128]{2,1,0:T(8,128)(2,1)S(1)} collective-permute-done((bf16[16,224,128]{2,1,0:T(8,128)(2,1)S(1)}, bf16[16,224,128]{2,1,0:T(8,128)(2,1)S(1)}, u32[]{:S(2)}, u32[]{:S(2)}) %collective-permute-start.14) | collective-permute-done | bytes 917536 | tf_op jit(solution)/shard_map/ppermute | solution.py:407
  165.5 19.4 %partial_sums.3 = bf16[8192,256]{1,0:T(8,128)(2,1)} custom-call(s32[32]{0:T(128)S(1)} %get-tuple-element.112.low.refs_0_, s32[32]{0:T(128)S(1)} %get-tuple-element.111.high.refs_1_, s32[17]{0:T(128)S(1)} %slice_bitcast_fusion.base.refs_2_, s32[1]{0:T(128)} %bitcast.8.quarter, bf16[8192,512]{1,0:T(8,128)(2,1)} %get-tuple-element.55.near_ref, ...), custom_call_target="tpu_custom_call" | custom-call | flops 4294967296 | bytes 16777216 | tf_op jit(solution)/shard_map/partial_sums/pallas_call | solution.py:300
  185.0 4.9 %dynamic-slice_bitcast_fusion = (bf16[16,224,256]{2,1,0:T(8,128)(2,1)S(1)}, bf16[16,224,256]{2,1,0:T(8,128)(2,1)}, bf16[16,224,256]{2,1,0:T(8,128)(2,1)}) fusion(bf16[16,1024,224]{1,2,0:T(8,128)(2,1)} %param.11, s32[]{:T(128)S(6)} %select_n.48, s32[]{:T(128)S(6)} %select_n.53, s32[]{:T(128)S(6)} %select_n.50), kind=kLoop, calls=%fused_computation | loop fusion | bytes 11010060 | tf_op jit(solution)/shard_map/dynamic_slice | solution.py:432
  189.8 1.5 collective-permute-start.16
  191.3 40.9 %collective-permute-done.16.refs_9_.refs_5_.refs_7_.refs_3_ = bf16[16,224,256]{2,1,0:T(8,128)(2,1)} collective-permute-done((bf16[16,224,256]{2,1,0:T(8,128)(2,1)S(1)}, bf16[16,224,256]{2,1,0:T(8,128)(2,1)}, u32[]{:S(2)}, u32[]{:S(2)}) %collective-permute-start.16) | collective-permute-done | bytes 1835040 | tf_op jit(solution)/shard_map/ppermute | solution.py:406
  232.2 5.7 %broadcast_in_dim.5.place_ref = s32[16,1024,128]{2,1,0:T(8,128)} broadcast(s32[16,1024]{1,0:T(8,128)S(1)} %get-tuple-element.68), dimensions={0,1} | broadcast | bytes 8454144 | tf_op jit(solution)/shard_map/broadcast_in_dim | solution.py:473
  237.9 16.2 %scatter_rows.1.refs_4_.onehot_ref = bf16[1024,8192]{1,0:T(8,128)(2,1)} custom-call(s32[32]{0:T(128)S(1)} %get-tuple-element.112.low.refs_0_, s32[32]{0:T(128)S(1)} %get-tuple-element.111.high.refs_1_, s32[16,1024,128]{2,1,0:T(8,128)} %broadcast_in_dim.5.place_ref), custom_call_target="tpu_custom_call" | custom-call | flops 8388608 | bytes 16777216 | tf_op jit(solution)/shard_map/scatter_rows/pallas_call | solution.py:257
  254.2 22.4 %reduce-scatter.5.cloned.1.call-done = bf16[2048,256]{1,0:T(8,128)(2,1)} async-done(((bf16[8192,256]{1,0:T(8,128)(2,1)}), bf16[2048,256]{1,0:T(8,128)(2,1)}) %reduce-scatter.5.cloned.1.call-update) | async-done | bytes 1048592 | tf_op jit(solution)/shard_map/reduce_scatter | solution.py:462
  276.6 2.5 fusion.12
  279.4 3.6 collective-permute-start.18
  283.0 1.9 collective-permute-start.19
  285.6 16.5 %down_and_mix.5.refs_2_ = f32[1024,1024]{1,0:T(8,128)} custom-call(s32[32]{0:T(128)} %copy-done.2, s32[32]{0:T(128)} %copy-done.1, s32[17]{0:T(128)} %copy-done.3, s32[3]{0:T(128)} %stack.80.refs_3_, bf16[1024,8192]{1,0:T(8,128)(2,1)} %scatter_rows.1.refs_4_.onehot_ref, bf16[2048,256]{1,0:T(8,128)(2,1)} %copy-done.6, bf16[2048,256]{1,0:T(8,128)(2,1)} %copy-done.6, ...), custom_call_target="tpu_custom_call" | custom-call | flops 4294967296 | bytes 4194304 | tf_op jit(solution)/shard_map/down_and_mix/pallas_call | solution.py:367
  302.1 3.4 collective-permute-done.18.refs_0_
  305.4 3.4 collective-permute-done.19.refs_1_
  308.8 2.2 collective-permute-start.20
  311.0 1.9 collective-permute-start.21
  313.5 17.0 %down_and_mix.6.refs_4_ = f32[1024,1024]{1,0:T(8,128)} custom-call(s32[32]{0:T(128)} %copy-done.2, s32[32]{0:T(128)} %copy-done.1, s32[17]{0:T(128)} %copy-done.3, s32[3]{0:T(128)} %pad_add_fusion.1.block, bf16[1024,8192]{1,0:T(8,128)(2,1)} %scatter_rows.1.refs_4_.onehot_ref, bf16[2048,256]{1,0:T(8,128)(2,1)} %copy-done.9, ...), custom_call_target="tpu_custom_call" | custom-call | flops 4294967296 | bytes 4194304 | tf_op jit(solution)/shard_map/down_and_mix/pallas_call | solution.py:367
  330.5 1.1 collective-permute-done.20.refs_2_
  332.5 3.2 collective-permute-done.21.refs_3_
  336.5 2.5 collective-permute-start.23
  340.2 27.2 %down_and_mix.7.refs_2_ = f32[1024,1024]{1,0:T(8,128)} custom-call(s32[32]{0:T(128)} %copy-done.2, s32[32]{0:T(128)} %copy-done.1, s32[17]{0:T(128)} %copy-done.3, s32[6]{0:T(128)} %stack.95.block, bf16[1024,8192]{1,0:T(8,128)(2,1)} %scatter_rows.1.refs_4_.onehot_ref, bf16[2048,256]{1,0:T(8,128)(2,1)} %copy-done.9, ...), custom_call_target="tpu_custom_call" | custom-call | flops 8589934592 | bytes 8388608 | tf_op jit(solution)/shard_map/down_and_mix/pallas_call | solution.py:367
  369.4 6.4 %down_and_mix.8 = bf16[1024,512]{1,0:T(8,128)(2,1)} custom-call(s32[32]{0:T(128)} %copy-done.2, s32[32]{0:T(128)} %copy-done.1, s32[17]{0:T(128)} %copy-done.3, s32[3]{0:T(128)} %pad_add_fusion.block, bf16[1024,8192]{1,0:T(8,128)(2,1)} %scatter_rows.1.refs_4_.onehot_ref, bf16[2048,256]{1,0:T(8,128)(2,1)} %copy-done.7, bf16[2048,256]{1,0:T(8,128)(2,1)} %copy-done.8, ...), custom_call_target="tpu_custom_call" | custom-call | flops 2147483648 | bytes 4194304 | tf_op jit(solution)/shard_map/down_and_mix/pallas_call | solution.py:367
  375.8 1.1 slice.60
  376.9 3.1 collective-permute-start.24
  379.9 1.5 collective-permute-done.24
  381.5 1.2 add_convert_fusion
  383.2 6.7 %down_and_mix.9 = f32[1024,512]{1,0:T(8,128)} custom-call(s32[32]{0:T(128)} %copy-done.2, s32[32]{0:T(128)} %copy-done.1, s32[17]{0:T(128)} %copy-done.3, s32[3]{0:T(128)} %pad_add_fusion.block, bf16[1024,8192]{1,0:T(8,128)(2,1)} %scatter_rows.1.refs_4_.onehot_ref, bf16[2048,256]{1,0:T(8,128)(2,1)} %copy-done.7, bf16[2048,256]{1,0:T(8,128)(2,1)} %copy-done.8, ...), custom_call_target="tpu_custom_call" | custom-call | flops 2147483648 | bytes 4194304 | tf_op jit(solution)/shard_map/down_and_mix/pallas_call | solution.py:367
  390.0 1.3 slice.78
  391.3 5.4 %collective-permute-done.25 = bf16[1024,224]{1,0:T(8,128)(2,1)S(1)} collective-permute-done((bf16[1024,224]{1,0:T(8,128)(2,1)S(1)}, bf16[1024,224]{1,0:T(8,128)(2,1)S(1)}, u32[]{:S(2)}, u32[]{:S(2)}) %collective-permute-start.25) | collective-permute-done | bytes 458784 | tf_op jit(solution)/shard_map/ppermute | solution.py:406
  397.0 1.5 collective-permute-done.26
  398.5 1.4 fusion.11
  399.9 17.6 %all_to_all.10 = bf16[16,64,224]{2,1,0:T(8,128)(2,1)S(1)} all-to-all(bf16[16,64,224]{2,1,0:T(8,128)(2,1)S(1)} %bitcast.41), channel_id=1, replica_groups=mesh['parts'=2,'ep'=16,'tp'=1] {'ep'}, dimensions={0} | all-to-all | bytes 917504 | tf_op jit(solution)/shard_map/all_to_all | solution.py:527
  417.8 1.6 reshape.66
  (83 shorter events, 19.0 us)
Async XLA Ops:
  11.0 20.4 %all-to-all-start = ((bf16[16,64,256]{2,1,0:T(8,128)(2,1)}), bf16[16,64,256]{2,1,0:T(8,128)(2,1)S(1)}, u32[]{:S(2)}, u32[]{:S(2)}) async-start(bf16[16,64,256]{2,1,0:T(8,128)(2,1)} %pad_maximum_fusion), calls=%async_computation | async-start | bytes 1048576 | tf_op jit(solution)/shard_map/all_to_all | solution.py:422
  17.5 236.6 %reduce-scatter.3.cloned.1.call-start = ((), (), s32[]{:S(2)}) async-start(), calls=%async_computation.4 | async-start | bytes 5242880 | tf_op jit(solution)/shard_map/reduce_scatter | solution.py:462
  17.6 5.2 %copy-start.4 = (bf16[16,224,1024]{2,1,0:T(8,128)(2,1)S(1)}, bf16[16,224,1024]{2,1,0:T(8,128)(2,1)}, u32[]{:S(2)}) copy-start(bf16[16,224,1024]{2,1,0:T(8,128)(2,1)} %refs_1_.3) | copy-start | bytes 22020100
  21.5 30.3 %collective-permute-start = (bf16[16,224,128]{2,1,0:T(8,128)(2,1)}, bf16[16,224,128]{2,1,0:T(8,128)(2,1)S(1)}, u32[]{:S(2)}, u32[]{:S(2)}) collective-permute-start(bf16[16,224,128]{2,1,0:T(8,128)(2,1)} %get-tuple-element.101), channel_id=1, source_target_pairs={{0,2},{1,3},{2,0},{3,1},{4,6},{5,7},{6,4},{7,5},{8,10},{9,11},{10,... | collective-permute-start | bytes 2752520 | tf_op jit(solution)/shard_map/ppermute | solution.py:406
  35.0 1.9 collective-permute-start.1
  35.0 34.3 %collective-permute-start.2 = (bf16[1024,256]{1,0:T(8,128)(2,1)S(1)}, bf16[1024,256]{1,0:T(8,128)(2,1)S(1)}, u32[]{:S(2)}, u32[]{:S(2)}) collective-permute-start(bf16[1024,256]{1,0:T(8,128)(2,1)S(1)} %bitcast.36), channel_id=1, source_target_pairs={{0,2},{1,3},{2,0},{3,1},{4,6},{5,7},{6,4},{7,5},{8,10},{9,11},{10,... | collective-permute-start | bytes 1572872 | tf_op jit(solution)/shard_map/ppermute | solution.py:406
  36.3 201.7 %copy-start.1 = (s32[32]{0:T(128)}, s32[32]{0:T(128)S(1)}, u32[]{:S(2)}) copy-start(s32[32]{0:T(128)S(1)} %get-tuple-element.111.high.refs_1_) | copy-start | bytes 388
  36.3 201.7 %copy-start.2 = (s32[32]{0:T(128)}, s32[32]{0:T(128)S(1)}, u32[]{:S(2)}) copy-start(s32[32]{0:T(128)S(1)} %get-tuple-element.112.low.refs_0_) | copy-start | bytes 388
  36.3 129.2 %copy-start.3 = (s32[17]{0:T(128)}, s32[17]{0:T(128)S(1)}, u32[]{:S(2)}) copy-start(s32[17]{0:T(128)S(1)} %slice_bitcast_fusion.base.refs_2_) | copy-start | bytes 208
  37.0 40.5 %collective-permute-start.7 = (bf16[16,224,128]{2,1,0:T(8,128)(2,1)S(1)}, bf16[16,224,128]{2,1,0:T(8,128)(2,1)S(1)}, u32[]{:S(2)}, u32[]{:S(2)}) collective-permute-start(bf16[16,224,128]{2,1,0:T(8,128)(2,1)S(1)} %get-tuple-element.60), channel_id=1, source_target_pairs={{0,2},{1,3},{2,0},{3,1},{4,6},{5,7},{6,4},{7,5},{8,10},{9,11},{10,... | collective-permute-start | bytes 2752520 | tf_op jit(solution)/shard_map/ppermute | solution.py:406
  51.8 26.5 %collective-permute-start.8 = (bf16[16,224,128]{2,1,0:T(8,128)(2,1)S(1)}, bf16[16,224,128]{2,1,0:T(8,128)(2,1)S(1)}, u32[]{:S(2)}, u32[]{:S(2)}) collective-permute-start(bf16[16,224,128]{2,1,0:T(8,128)(2,1)S(1)} %collective-permute-done.refs_4_), channel_id=1, source_target_pairs={{0,16},{16,0},{1,17},{17,1},{2,18},{18,2},{3,19},{19,3},{4,20},{20... | collective-permute-start | bytes 2752520 | tf_op jit(solution)/shard_map/ppermute | solution.py:407
  52.2 25.3 %copy-start.11 = (bf16[16,224,128]{2,1,0:T(8,128)(2,1)S(1)}, bf16[16,224,128]{2,1,0:T(8,128)(2,1)}, u32[]{:S(2)}) copy-start(bf16[16,224,128]{2,1,0:T(8,128)(2,1)} %get-tuple-element.58) | copy-start | bytes 2752516
  67.3 2.1 copy-start
  69.4 8.9 %collective-permute-start.3 = (bf16[1024,256]{1,0:T(8,128)(2,1)S(1)}, bf16[1024,256]{1,0:T(8,128)(2,1)S(1)}, u32[]{:S(2)}, u32[]{:S(2)}) collective-permute-start(bf16[1024,256]{1,0:T(8,128)(2,1)S(1)} %collective-permute-done.2.refs_0_), channel_id=1, source_target_pairs={{0,1},{1,0},{2,3},{3,2},{4,5},{5,4},{6,7},{7,6},{8,9},{9,8},{10,11... | collective-permute-start | bytes 1572872 | tf_op jit(solution)/shard_map/ppermute | solution.py:405
  70.1 30.0 %collective-permute-start.5 = (bf16[16,224,128]{2,1,0:T(8,128)(2,1)}, bf16[16,224,128]{2,1,0:T(8,128)(2,1)S(1)}, u32[]{:S(2)}, u32[]{:S(2)}) collective-permute-start(bf16[16,224,128]{2,1,0:T(8,128)(2,1)} %get-tuple-element.99), channel_id=1, source_target_pairs={{0,1},{1,0},{2,3},{3,2},{4,5},{5,4},{6,7},{7,6},{8,9},{9,8},{10,11... | collective-permute-start | bytes 2752520 | tf_op jit(solution)/shard_map/ppermute | solution.py:405
  70.1 30.0 %collective-permute-start.6 = (bf16[16,224,128]{2,1,0:T(8,128)(2,1)}, bf16[16,224,128]{2,1,0:T(8,128)(2,1)S(1)}, u32[]{:S(2)}, u32[]{:S(2)}) collective-permute-start(bf16[16,224,128]{2,1,0:T(8,128)(2,1)} %get-tuple-element.97), channel_id=1, source_target_pairs={{0,1},{1,0},{2,3},{3,2},{4,5},{5,4},{6,7},{7,6},{8,9},{9,8},{10,11... | collective-permute-start | bytes 2752520 | tf_op jit(solution)/shard_map/ppermute | solution.py:405
  77.5 22.7 %collective-permute-start.4 = (bf16[16,224,128]{2,1,0:T(8,128)(2,1)S(1)}, bf16[16,224,128]{2,1,0:T(8,128)(2,1)S(1)}, u32[]{:S(2)}, u32[]{:S(2)}) collective-permute-start(bf16[16,224,128]{2,1,0:T(8,128)(2,1)S(1)} %copy-done.11), channel_id=1, source_target_pairs={{0,2},{1,3},{2,0},{3,1},{4,6},{5,7},{6,4},{7,5},{8,10},{9,11},{10,... | collective-permute-start | bytes 2752520 | tf_op jit(solution)/shard_map/ppermute | solution.py:406
  78.3 21.9 %collective-permute-start.9 = (bf16[16,224,128]{2,1,0:T(8,128)(2,1)S(1)}, bf16[16,224,128]{2,1,0:T(8,128)(2,1)S(1)}, u32[]{:S(2)}, u32[]{:S(2)}) collective-permute-start(bf16[16,224,128]{2,1,0:T(8,128)(2,1)S(1)} %collective-permute-done.7.refs_5_), channel_id=1, source_target_pairs={{0,16},{16,0},{1,17},{17,1},{2,18},{18,2},{3,19},{19,3},{4,20},{20... | collective-permute-start | bytes 2752520 | tf_op jit(solution)/shard_map/ppermute | solution.py:407
  119.5 157.0 %reduce-scatter.5.cloned.1.call-start = ((), (), s32[]{:S(2)}) async-start(), calls=%async_computation.5 | async-start | bytes 5242880 | tf_op jit(solution)/shard_map/reduce_scatter | solution.py:462
  119.8 23.1 %collective-permute-start.12 = (bf16[16,224,128]{2,1,0:T(8,128)(2,1)}, bf16[16,224,128]{2,1,0:T(8,128)(2,1)S(1)}, u32[]{:S(2)}, u32[]{:S(2)}) collective-permute-start(bf16[16,224,128]{2,1,0:T(8,128)(2,1)} %get-tuple-element.65), channel_id=1, source_target_pairs={{0,2},{1,3},{2,0},{3,1},{4,6},{5,7},{6,4},{7,5},{8,10},{9,11},{10,... | collective-permute-start | bytes 2752520 | tf_op jit(solution)/shard_map/ppermute | solution.py:406
  121.5 22.4 %collective-permute-start.13 = (bf16[16,224,128]{2,1,0:T(8,128)(2,1)S(1)}, bf16[16,224,128]{2,1,0:T(8,128)(2,1)S(1)}, u32[]{:S(2)}, u32[]{:S(2)}) collective-permute-start(bf16[16,224,128]{2,1,0:T(8,128)(2,1)S(1)} %collective-permute-done.4.refs_4_), channel_id=1, source_target_pairs={{0,16},{16,0},{1,17},{17,1},{2,18},{18,2},{3,19},{19,3},{4,20},{20... | collective-permute-start | bytes 2752520 | tf_op jit(solution)/shard_map/ppermute | solution.py:407
  121.5 22.4 %collective-permute-start.10 = (bf16[16,224,128]{2,1,0:T(8,128)(2,1)S(1)}, bf16[16,224,128]{2,1,0:T(8,128)(2,1)S(1)}, u32[]{:S(2)}, u32[]{:S(2)}) collective-permute-start(bf16[16,224,128]{2,1,0:T(8,128)(2,1)S(1)} %get-tuple-element.98), channel_id=1, source_target_pairs={{0,1},{1,0},{2,3},{3,2},{4,5},{5,4},{6,7},{7,6},{8,9},{9,8},{10,11... | collective-permute-start | bytes 2752520 | tf_op jit(solution)/shard_map/ppermute | solution.py:405
  122.5 21.4 %collective-permute-start.11 = (bf16[16,224,128]{2,1,0:T(8,128)(2,1)}, bf16[16,224,128]{2,1,0:T(8,128)(2,1)S(1)}, u32[]{:S(2)}, u32[]{:S(2)}) collective-permute-start(bf16[16,224,128]{2,1,0:T(8,128)(2,1)} %get-tuple-element.95), channel_id=1, source_target_pairs={{0,1},{1,0},{2,3},{3,2},{4,5},{5,4},{6,7},{7,6},{8,9},{9,8},{10,11... | collective-permute-start | bytes 2752520 | tf_op jit(solution)/shard_map/ppermute | solution.py:405
  143.9 21.6 %collective-permute-start.14 = (bf16[16,224,128]{2,1,0:T(8,128)(2,1)S(1)}, bf16[16,224,128]{2,1,0:T(8,128)(2,1)S(1)}, u32[]{:S(2)}, u32[]{:S(2)}) collective-permute-start(bf16[16,224,128]{2,1,0:T(8,128)(2,1)S(1)} %collective-permute-done.12.refs_5_), channel_id=1, source_target_pairs={{0,16},{16,0},{1,17},{17,1},{2,18},{18,2},{3,19},{19,3},{4,20},{20... | collective-permute-start | bytes 2752520 | tf_op jit(solution)/shard_map/ppermute | solution.py:407
  189.8 42.4 %collective-permute-start.16 = (bf16[16,224,256]{2,1,0:T(8,128)(2,1)S(1)}, bf16[16,224,256]{2,1,0:T(8,128)(2,1)}, u32[]{:S(2)}, u32[]{:S(2)}) collective-permute-start(bf16[16,224,256]{2,1,0:T(8,128)(2,1)S(1)} %get-tuple-element.70), channel_id=1, source_target_pairs={{0,2},{1,3},{2,0},{3,1},{4,6},{5,7},{6,4},{7,5},{8,10},{9,11},{10,... | collective-permute-start | bytes 5505032 | tf_op jit(solution)/shard_map/ppermute | solution.py:406
  191.3 87.8 %collective-permute-start.15 = (bf16[16,224,256]{2,1,0:T(8,128)(2,1)}, bf16[16,224,256]{2,1,0:T(8,128)(2,1)S(1)}, u32[]{:S(2)}, u32[]{:S(2)}) collective-permute-start(bf16[16,224,256]{2,1,0:T(8,128)(2,1)} %get-tuple-element.93), channel_id=1, source_target_pairs={{0,1},{1,0},{2,3},{3,2},{4,5},{5,4},{6,7},{7,6},{8,9},{9,8},{10,11... | collective-permute-start | bytes 5505032 | tf_op jit(solution)/shard_map/ppermute | solution.py:405
  232.2 46.9 %collective-permute-start.17 = (bf16[16,224,256]{2,1,0:T(8,128)(2,1)}, bf16[16,224,256]{2,1,0:T(8,128)(2,1)}, u32[]{:S(2)}, u32[]{:S(2)}) collective-permute-start(bf16[16,224,256]{2,1,0:T(8,128)(2,1)} %collective-permute-done.16.refs_9_.refs_5_.refs_7_.refs_3_), channel_id=1, source_target_pairs={{0,16},{16,0},{1,17},{17,1},{2,18},{18,2},{3,19},{19,3},{4,20},{20... | collective-permute-start | bytes 5505032 | tf_op jit(solution)/shard_map/ppermute | solution.py:407
  279.1 6.5 %copy-start.5 = (bf16[16,224,256]{2,1,0:T(8,128)(2,1)}, bf16[16,224,256]{2,1,0:T(8,128)(2,1)S(1)}, u32[]{:S(2)}) copy-start(bf16[16,224,256]{2,1,0:T(8,128)(2,1)S(1)} %collective-permute-done.15.refs_8_.refs_4_.refs_6_) | copy-start | bytes 5505028
  279.4 6.2 %copy-start.6 = (bf16[2048,256]{1,0:T(8,128)(2,1)}, bf16[2048,256]{1,0:T(8,128)(2,1)S(1)}, u32[]{:S(2)}) copy-start(bf16[2048,256]{1,0:T(8,128)(2,1)S(1)} %constant_dynamic-update-slice_fusion.refs_5_.refs_6_) | copy-start | bytes 3145732
  279.4 26.1 %collective-permute-start.18 = (bf16[2048,256]{1,0:T(8,128)(2,1)S(1)}, bf16[2048,256]{1,0:T(8,128)(2,1)S(1)}, u32[]{:S(2)}, u32[]{:S(2)}) collective-permute-start(bf16[2048,256]{1,0:T(8,128)(2,1)S(1)} %constant_dynamic-update-slice_fusion.refs_5_.refs_6_), channel_id=1, source_target_pairs={{0,4},{1,5},{2,6},{3,7},{4,8},{5,9},{6,10},{7,11},{8,12},{9,13},{1... | collective-permute-start | bytes 3145736 | tf_op jit(solution)/shard_map/ppermute | solution.py:489
  283.0 25.8 %collective-permute-start.19 = (bf16[2048,256]{1,0:T(8,128)(2,1)S(1)}, bf16[2048,256]{1,0:T(8,128)(2,1)}, u32[]{:S(2)}, u32[]{:S(2)}) collective-permute-start(bf16[2048,256]{1,0:T(8,128)(2,1)S(1)} %constant_dynamic-update-slice_fusion.refs_5_.refs_6_), channel_id=1, source_target_pairs={{4,0},{5,1},{6,2},{7,3},{8,4},{9,5},{10,6},{11,7},{12,8},{13,9},{1... | collective-permute-start | bytes 3145736 | tf_op jit(solution)/shard_map/ppermute | solution.py:489
  305.4 8.1 %copy-start.9 = (bf16[2048,256]{1,0:T(8,128)(2,1)}, bf16[2048,256]{1,0:T(8,128)(2,1)S(1)}, u32[]{:S(2)}) copy-start(bf16[2048,256]{1,0:T(8,128)(2,1)S(1)} %collective-permute-done.18.refs_0_) | copy-start | bytes 3145732
  308.8 22.7 %collective-permute-start.20 = (bf16[2048,256]{1,0:T(8,128)(2,1)S(1)}, bf16[2048,256]{1,0:T(8,128)(2,1)S(1)}, u32[]{:S(2)}, u32[]{:S(2)}) collective-permute-start(bf16[2048,256]{1,0:T(8,128)(2,1)S(1)} %collective-permute-done.18.refs_0_), channel_id=1, source_target_pairs={{4,8},{5,9},{6,10},{7,11},{8,12},{9,13},{10,14},{11,15},{20,24},{2... | collective-permute-start | bytes 3145736 | tf_op jit(solution)/shard_map/ppermute | solution.py:489
  311.0 24.8 %collective-permute-start.21 = (bf16[2048,256]{1,0:T(8,128)(2,1)}, bf16[2048,256]{1,0:T(8,128)(2,1)}, u32[]{:S(2)}, u32[]{:S(2)}) collective-permute-start(bf16[2048,256]{1,0:T(8,128)(2,1)} %collective-permute-done.19.refs_1_), channel_id=1, source_target_pairs={{4,0},{5,1},{6,2},{7,3},{8,4},{9,5},{10,6},{11,7},{20,16},{21,17},... | collective-permute-start | bytes 3145736 | tf_op jit(solution)/shard_map/ppermute | solution.py:489
  331.5 1.0 copy-start.10
  335.8 31.7 %collective-permute-start.22 = (bf16[2048,256]{1,0:T(8,128)(2,1)}, bf16[2048,256]{1,0:T(8,128)(2,1)S(1)}, u32[]{:S(2)}, u32[]{:S(2)}) collective-permute-start(bf16[2048,256]{1,0:T(8,128)(2,1)} %copy-done.10), channel_id=1, source_target_pairs={{8,12},{9,13},{10,14},{11,15},{24,28},{25,29},{26,30},{27,31}} | collective-permute-start | bytes 3145736 | tf_op jit(solution)/shard_map/ppermute | solution.py:489
  336.5 31.0 %collective-permute-start.23 = (bf16[2048,256]{1,0:T(8,128)(2,1)}, bf16[2048,256]{1,0:T(8,128)(2,1)S(1)}, u32[]{:S(2)}, u32[]{:S(2)}) collective-permute-start(bf16[2048,256]{1,0:T(8,128)(2,1)} %collective-permute-done.21.refs_3_), channel_id=1, source_target_pairs={{4,0},{5,1},{6,2},{7,3},{20,16},{21,17},{22,18},{23,19}} | collective-permute-start | bytes 3145736 | tf_op jit(solution)/shard_map/ppermute | solution.py:489
  367.4 1.0 copy-start.7
  368.5 1.0 copy-start.8
  376.9 4.6 %collective-permute-start.24 = (bf16[1024,224]{1,0:T(8,128)(2,1)S(1)}, bf16[1024,224]{1,0:T(8,128)(2,1)S(1)}, u32[]{:S(2)}, u32[]{:S(2)}) collective-permute-start(bf16[1024,224]{1,0:T(8,128)(2,1)S(1)} %slice.60), channel_id=1, source_target_pairs={{0,1},{1,0},{2,3},{3,2},{4,5},{5,4},{6,7},{7,6},{8,9},{9,8},{10,11... | collective-permute-start | bytes 1376264 | tf_op jit(solution)/shard_map/ppermute | solution.py:405
  382.6 14.0 %collective-permute-start.25 = (bf16[1024,224]{1,0:T(8,128)(2,1)S(1)}, bf16[1024,224]{1,0:T(8,128)(2,1)S(1)}, u32[]{:S(2)}, u32[]{:S(2)}) collective-permute-start(bf16[1024,224]{1,0:T(8,128)(2,1)S(1)} %add_convert_fusion), channel_id=1, source_target_pairs={{0,2},{1,3},{2,0},{3,1},{4,6},{5,7},{6,4},{7,5},{8,10},{9,11},{10,... | collective-permute-start | bytes 1376264 | tf_op jit(solution)/shard_map/ppermute | solution.py:406
  396.6 1.9 collective-permute-start.26
Sparse Core Ops, SparseCore 0:
  119.7 77.1 reduce-scatter.2
  199.3 77.2 reduce-scatter.4

commit v12 on v11

--- a/solution.py
+++ b/solution.py
@@ -11,6 +11,7 @@
 BF16 = jnp.bfloat16
 F32 = jnp.float32
 TILE = 256
+STEP = 512
 BLOCK = 1024
 LANES = 256
 UNITS = 128
@@ -138,8 +139,8 @@
     )
 
 
-def mine_of(base, e, row0):
-    row = row0 + lax.broadcasted_iota(jnp.int32, (TILE, 1), 0)
+def mine_of(base, e, row0, rows=TILE):
+    row = row0 + lax.broadcasted_iota(jnp.int32, (rows, 1), 0)
     return (row >= base[e]) & (row < base[e + 1])
 
 
@@ -273,10 +274,10 @@
     pairs, out = [refs[j : j + 2] for j in range(0, 8, 2)], refs[-1]
     width = pairs[0][0].shape[1]
 
-    @pl.loop(0, BLOCK // TILE)
+    @pl.loop(0, BLOCK // STEP)
     def _(part):
-        i = pl.program_id(0) * (BLOCK // TILE) + part
-        here = pl.ds(pl.multiple_of(part * TILE, TILE), TILE)
+        i = pl.program_id(0) * (BLOCK // STEP) + part
+        here = pl.ds(pl.multiple_of(part * STEP, STEP), STEP)
 
         def add(e, kept):
             total = 0.0
@@ -285,10 +286,13 @@
                 rows_ref, at = (near_ref, far_ref)[k // 2], k % 2 * LANES
                 rows = rows_ref[here, at : at + width]
                 total += dot(rows, weight, ((1,), (0,)))
-            return jnp.where(mine_of(base, e, i * TILE), total, kept)
+            return jnp.where(mine_of(base, e, i * STEP, STEP), total, kept)
 
         out[here, :] = lax.fori_loop(
-            low[i], high[i], add, jnp.zeros((TILE, out.shape[1]), F32)
+            low[STEP // TILE * i],
+            high[STEP // TILE * (i + 1) - 1],
+            add,
+            jnp.zeros((STEP, out.shape[1]), F32),
         ).astype(BF16)
 
 
@@ -327,17 +331,17 @@
 
     @pl.when(block[3 * slot + 2] != 0)
     def _():
-        for part in range(BLOCK // TILE):
-            i = (2 * block[3 * slot] + j % 2) * (BLOCK // TILE) + part
-            here = slice(part * TILE, (part + 1) * TILE)
+        for part in range(BLOCK // STEP):
+            i = (2 * block[3 * slot] + j % 2) * (BLOCK // STEP) + part
+            here = slice(part * STEP, (part + 1) * STEP)
             source = 2 * slot + 1 - block[3 * slot + 1]
             units = hidden[0][here, :]
             for k in range(1, 2 * slots):
                 units = jnp.where(source == k, hidden[k][here, :], units)
 
-            @pl.loop(low[i], high[i])
+            @pl.loop(low[STEP // TILE * i], high[STEP // TILE * (i + 1) - 1])
             def _(e):
-                mine = mine_of(base, e, i * TILE)
+                mine = mine_of(base, e, i * STEP, STEP)
                 for k, weight in enumerate(weights):
                     value = dot(units, weight[e], ((1,), (1,)))
                     at = slice(k * LANES, k * LANES + width)

time: 429 us -> 430 us (level)
  transfers between devices with their start and end apart: 30 -> 30, of which waited for: 17 -> 17; matrix products, arithmetic and copies ran while one was open for 5% -> 5% of each run, Pallas kernels for 35% -> 36%
where the time goes in v12:
time: 430 us; the launch traced here: 427 us
  Pallas kernels  179 us (42%)
  waiting for transfers between devices  145 us (34%)
  starting transfers between devices  32.1 us (7%)
  local copies, waits for them, and re-layouts  30.3 us (7%)
  blocking collectives  17.6 us (4%)
  between operations  13.8 us (3%)
  other arithmetic  8.75 us (2%)
    ppermute x7, waiting for transfers between devices, fixed_weights(): to_cross = lambda value: lax.ppermute(value, ('parts', 'ep'), cross)  80.2 us
    pallas_call x5, Pallas kernels, down_and_mix(): pl.pallas_call(kernel, grid_spec=pltpu.PrefetchScalarGridSpec(num_scalar_...  73.6 us
    pallas_call x2, Pallas kernels, partial_sums(): pl.pallas_call(partial_kernel, grid_spec=pltpu.PrefetchScalarGridSpec(num...  40.4 us
    pallas_call x2, Pallas kernels, sort_rows(): pl.pallas_call(kernel, grid_spec=pltpu.PrefetchScalarGridSpec(num_scalar_...  29.5 us
    ppermute x5, waiting for transfers between devices, fixed_weights(): to_plane = lambda value: lax.ppermute(value, 'parts', [(0, 1), (1, 0)])  22.7 us
    reduce_scatter x2, waiting for transfers between devices, units_of(): lax.psum_scatter(sums, 'ep', scatter_dimension=0, axis_index_groups=line,...  21.1 us
    all_to_all x1, blocking collectives, fixed_weights(): lax.all_to_all(mixed.reshape(size, count, width), 'ep', split_axis=0, con...  17.6 us
    pallas_call x1, Pallas kernels, scatter_rows(): pl.pallas_call(scatter_kernel, grid_spec=pltpu.PrefetchScalarGridSpec(num...  16.8 us
  transfers between devices with their start and end apart: 30, of which 17 were waited for; matrix products, arithmetic and copies ran while one was open for 5% of the time, Pallas kernels for 36%

profile of v12, /device:TPU:15, one launch (start us, length us, event | category | flops | bytes accessed | tf_op | source)
XLA Modules:
  0.0 427.0 jit_solution(3613730375636746523)
XLA Ops:
  8.0 1.8 reshape.61
  11.0 6.6 %all-to-all-start = ((bf16[16,64,256]{2,1,0:T(8,128)(2,1)}), bf16[16,64,256]{2,1,0:T(8,128)(2,1)S(1)}, u32[]{:S(2)}, u32[]{:S(2)}) async-start(bf16[16,64,256]{2,1,0:T(8,128)(2,1)} %pad_maximum_fusion), calls=%async_computation | async-start | bytes 1048576 | tf_op jit(solution)/shard_map/all_to_all | solution.py:426
  17.6 3.8 constant_dynamic-slice_fusion.2
  22.9 2.2 constant_dynamic-slice_fusion
  25.0 6.4 %all-to-all-done = bf16[16,64,256]{2,1,0:T(8,128)(2,1)S(1)} async-done(((bf16[16,64,256]{2,1,0:T(8,128)(2,1)}), bf16[16,64,256]{2,1,0:T(8,128)(2,1)S(1)}, u32[]{:S(2)}, u32[]{:S(2)}) %all-to-all-start) | async-done | bytes 524320 | tf_op jit(solution)/shard_map/all_to_all | solution.py:426
  31.4 3.6 order.1
  35.0 1.0 collective-permute-start.2
  37.6 14.3 %sort_rows.2 = (bf16[8192,512]{1,0:T(8,128)(2,1)}, f32[8192,128]{1,0:T(8,128)S(1)}, bf16[8192,1024]{1,0:T(8,128)(2,1)}) custom-call(s32[32]{0:T(128)S(1)} %get-tuple-element.112.low.refs_0_, s32[32]{0:T(128)S(1)} %get-tuple-element.111.high.refs_1_, s32[17]{0:T(128)S(1)} %slice_bitcast_fusion.base.refs_2_, s32[16,8,128]{2,1,0:T(8,128)S(1)} %bitcast.39, ...), custom_call_target="tpu_custom_call" | custom-call | flops 4294967296 | bytes 16777216 | tf_op jit(solution)/shard_map/sort_rows/pallas_call | solution.py:189
  52.2 15.2 %sort_rows.3 = (bf16[8192,512]{1,0:T(8,128)(2,1)}, f32[8192,128]{1,0:T(8,128)S(1)}, bf16[8192,1024]{1,0:T(8,128)(2,1)}) custom-call(s32[32]{0:T(128)S(1)} %get-tuple-element.112.low.refs_0_, s32[32]{0:T(128)S(1)} %get-tuple-element.111.high.refs_1_, ...), custom_call_target="tpu_custom_call", output_to_operand_aliasing={{0}: (7, {}), {1}: (8, {}), {2}: (9, {})} | custom-call | flops 4294967296 | bytes 16777216 | tf_op jit(solution)/shard_map/sort_rows/pallas_call | solution.py:189
  67.3 2.0 copy-done
  70.6 6.9 %collective-permute-done.7.refs_5_ = bf16[16,224,128]{2,1,0:T(8,128)(2,1)S(1)} collective-permute-done((bf16[16,224,128]{2,1,0:T(8,128)(2,1)S(1)}, bf16[16,224,128]{2,1,0:T(8,128)(2,1)S(1)}, u32[]{:S(2)}, u32[]{:S(2)}) %collective-permute-start.7) | collective-permute-done | bytes 917536 | tf_op jit(solution)/shard_map/ppermute | solution.py:410
  78.3 15.3 %sort_more.1.far_ref = bf16[8192,512]{1,0:T(8,128)(2,1)} custom-call(bf16[8192,1024]{1,0:T(8,128)(2,1)} %get-tuple-element.56.onehot_ref, bf16[1024,256]{1,0:T(8,128)(2,1)S(1)} %collective-permute-done.2.refs_0_, bf16[1024,256]{1,0:T(8,128)(2,1)S(1)} %collective-permute-done.3.refs_1_), custom_call_target="tpu_custom_call" | custom-call | flops 8589934592 | bytes 33554432 | tf_op jit(solution)/shard_map/sort_more/pallas_call | solution.py:228
  93.6 6.5 %collective-permute-done.4.refs_4_ = bf16[16,224,128]{2,1,0:T(8,128)(2,1)S(1)} collective-permute-done((bf16[16,224,128]{2,1,0:T(8,128)(2,1)S(1)}, bf16[16,224,128]{2,1,0:T(8,128)(2,1)S(1)}, u32[]{:S(2)}, u32[]{:S(2)}) %collective-permute-start.4) | collective-permute-done | bytes 917536 | tf_op jit(solution)/shard_map/ppermute | solution.py:410
  100.2 20.2 %partial_sums.2 = bf16[8192,256]{1,0:T(8,128)(2,1)} custom-call(s32[32]{0:T(128)S(1)} %get-tuple-element.112.low.refs_0_, s32[32]{0:T(128)S(1)} %get-tuple-element.111.high.refs_1_, s32[17]{0:T(128)S(1)} %slice_bitcast_fusion.base.refs_2_, s32[1]{0:T(128)} %bitcast.8.quarter, bf16[8192,512]{1,0:T(8,128)(2,1)} %get-tuple-element.55.near_ref, ...), custom_call_target="tpu_custom_call" | custom-call | flops 4294967296 | bytes 16777216 | tf_op jit(solution)/shard_map/partial_sums/pallas_call | solution.py:304
  120.7 1.7 collective-permute-start.12
  123.1 20.7 %collective-permute-done.12.refs_5_ = bf16[16,224,128]{2,1,0:T(8,128)(2,1)S(1)} collective-permute-done((bf16[16,224,128]{2,1,0:T(8,128)(2,1)}, bf16[16,224,128]{2,1,0:T(8,128)(2,1)S(1)}, u32[]{:S(2)}, u32[]{:S(2)}) %collective-permute-start.12) | collective-permute-done | bytes 917536 | tf_op jit(solution)/shard_map/ppermute | solution.py:410
  144.8 21.6 %collective-permute-done.14.refs_7_ = bf16[16,224,128]{2,1,0:T(8,128)(2,1)S(1)} collective-permute-done((bf16[16,224,128]{2,1,0:T(8,128)(2,1)S(1)}, bf16[16,224,128]{2,1,0:T(8,128)(2,1)S(1)}, u32[]{:S(2)}, u32[]{:S(2)}) %collective-permute-start.14) | collective-permute-done | bytes 917536 | tf_op jit(solution)/shard_map/ppermute | solution.py:411
  166.4 20.2 %partial_sums.3 = bf16[8192,256]{1,0:T(8,128)(2,1)} custom-call(s32[32]{0:T(128)S(1)} %get-tuple-element.112.low.refs_0_, s32[32]{0:T(128)S(1)} %get-tuple-element.111.high.refs_1_, s32[17]{0:T(128)S(1)} %slice_bitcast_fusion.base.refs_2_, s32[1]{0:T(128)} %bitcast.8.quarter, bf16[8192,512]{1,0:T(8,128)(2,1)} %get-tuple-element.55.near_ref, ...), custom_call_target="tpu_custom_call" | custom-call | flops 4294967296 | bytes 16777216 | tf_op jit(solution)/shard_map/partial_sums/pallas_call | solution.py:304
  186.7 4.8 %dynamic-slice_bitcast_fusion = (bf16[16,224,256]{2,1,0:T(8,128)(2,1)S(1)}, bf16[16,224,256]{2,1,0:T(8,128)(2,1)}, bf16[16,224,256]{2,1,0:T(8,128)(2,1)}) fusion(bf16[16,1024,224]{1,2,0:T(8,128)(2,1)} %param.11, s32[]{:T(128)S(6)} %select_n.48, s32[]{:T(128)S(6)} %select_n.53, s32[]{:T(128)S(6)} %select_n.50), kind=kLoop, calls=%fused_computation | loop fusion | bytes 11010060 | tf_op jit(solution)/shard_map/dynamic_slice | solution.py:436
  191.5 1.6 collective-permute-start.16
  193.1 40.8 %collective-permute-done.16.refs_9_.refs_5_.refs_7_.refs_3_ = bf16[16,224,256]{2,1,0:T(8,128)(2,1)} collective-permute-done((bf16[16,224,256]{2,1,0:T(8,128)(2,1)S(1)}, bf16[16,224,256]{2,1,0:T(8,128)(2,1)}, u32[]{:S(2)}, u32[]{:S(2)}) %collective-permute-start.16) | collective-permute-done | bytes 1835040 | tf_op jit(solution)/shard_map/ppermute | solution.py:410
  233.9 5.7 %broadcast_in_dim.5.place_ref = s32[16,1024,128]{2,1,0:T(8,128)} broadcast(s32[16,1024]{1,0:T(8,128)S(1)} %get-tuple-element.68), dimensions={0,1} | broadcast | bytes 8454144 | tf_op jit(solution)/shard_map/broadcast_in_dim | solution.py:477
  239.6 16.8 %scatter_rows.1.refs_4_.onehot_ref = bf16[1024,8192]{1,0:T(8,128)(2,1)} custom-call(s32[32]{0:T(128)S(1)} %get-tuple-element.112.low.refs_0_, s32[32]{0:T(128)S(1)} %get-tuple-element.111.high.refs_1_, s32[16,1024,128]{2,1,0:T(8,128)} %broadcast_in_dim.5.place_ref), custom_call_target="tpu_custom_call" | custom-call | flops 8388608 | bytes 16777216 | tf_op jit(solution)/shard_map/scatter_rows/pallas_call | solution.py:258
  256.4 21.1 %reduce-scatter.5.cloned.1.call-done = bf16[2048,256]{1,0:T(8,128)(2,1)} async-done(((bf16[8192,256]{1,0:T(8,128)(2,1)}), bf16[2048,256]{1,0:T(8,128)(2,1)}) %reduce-scatter.5.cloned.1.call-update) | async-done | bytes 1048592 | tf_op jit(solution)/shard_map/reduce_scatter | solution.py:466
  277.5 2.5 fusion.12
  280.3 3.6 collective-permute-start.18
  283.9 1.9 collective-permute-start.19
  286.5 16.4 %down_and_mix.5.refs_2_ = f32[1024,1024]{1,0:T(8,128)} custom-call(s32[32]{0:T(128)} %copy-done.2, s32[32]{0:T(128)} %copy-done.1, s32[17]{0:T(128)} %copy-done.3, s32[3]{0:T(128)} %stack.80.refs_3_, bf16[1024,8192]{1,0:T(8,128)(2,1)} %scatter_rows.1.refs_4_.onehot_ref, bf16[2048,256]{1,0:T(8,128)(2,1)} %copy-done.6, bf16[2048,256]{1,0:T(8,128)(2,1)} %copy-done.6, ...), custom_call_target="tpu_custom_call" | custom-call | flops 4294967296 | bytes 4194304 | tf_op jit(solution)/shard_map/down_and_mix/pallas_call | solution.py:371
  302.8 3.5 collective-permute-done.18.refs_0_
  306.4 3.4 collective-permute-done.19.refs_1_
  309.7 2.1 collective-permute-start.20
  311.8 1.9 collective-permute-start.21
  314.4 17.0 %down_and_mix.6.refs_4_ = f32[1024,1024]{1,0:T(8,128)} custom-call(s32[32]{0:T(128)} %copy-done.2, s32[32]{0:T(128)} %copy-done.1, s32[17]{0:T(128)} %copy-done.3, s32[3]{0:T(128)} %pad_add_fusion.1.block, bf16[1024,8192]{1,0:T(8,128)(2,1)} %scatter_rows.1.refs_4_.onehot_ref, bf16[2048,256]{1,0:T(8,128)(2,1)} %copy-done.9, ...), custom_call_target="tpu_custom_call" | custom-call | flops 4294967296 | bytes 4194304 | tf_op jit(solution)/shard_map/down_and_mix/pallas_call | solution.py:371
  333.4 3.2 collective-permute-done.21.refs_3_
  337.3 2.5 collective-permute-start.23
  341.1 27.1 %down_and_mix.7.refs_2_ = f32[1024,1024]{1,0:T(8,128)} custom-call(s32[32]{0:T(128)} %copy-done.2, s32[32]{0:T(128)} %copy-done.1, s32[17]{0:T(128)} %copy-done.3, s32[6]{0:T(128)} %stack.95.block, bf16[1024,8192]{1,0:T(8,128)(2,1)} %scatter_rows.1.refs_4_.onehot_ref, bf16[2048,256]{1,0:T(8,128)(2,1)} %copy-done.9, ...), custom_call_target="tpu_custom_call" | custom-call | flops 8589934592 | bytes 8388608 | tf_op jit(solution)/shard_map/down_and_mix/pallas_call | solution.py:371
  370.2 6.4 %down_and_mix.8 = bf16[1024,512]{1,0:T(8,128)(2,1)} custom-call(s32[32]{0:T(128)} %copy-done.2, s32[32]{0:T(128)} %copy-done.1, s32[17]{0:T(128)} %copy-done.3, s32[3]{0:T(128)} %pad_add_fusion.block, bf16[1024,8192]{1,0:T(8,128)(2,1)} %scatter_rows.1.refs_4_.onehot_ref, bf16[2048,256]{1,0:T(8,128)(2,1)} %copy-done.7, bf16[2048,256]{1,0:T(8,128)(2,1)} %copy-done.8, ...), custom_call_target="tpu_custom_call" | custom-call | flops 2147483648 | bytes 4194304 | tf_op jit(solution)/shard_map/down_and_mix/pallas_call | solution.py:371
  376.5 1.1 slice.60
  377.6 3.1 collective-permute-start.24
  380.7 1.5 collective-permute-done.24
  382.2 1.2 add_convert_fusion
  384.0 6.7 %down_and_mix.9 = f32[1024,512]{1,0:T(8,128)} custom-call(s32[32]{0:T(128)} %copy-done.2, s32[32]{0:T(128)} %copy-done.1, s32[17]{0:T(128)} %copy-done.3, s32[3]{0:T(128)} %pad_add_fusion.block, bf16[1024,8192]{1,0:T(8,128)(2,1)} %scatter_rows.1.refs_4_.onehot_ref, bf16[2048,256]{1,0:T(8,128)(2,1)} %copy-done.7, bf16[2048,256]{1,0:T(8,128)(2,1)} %copy-done.8, ...), custom_call_target="tpu_custom_call" | custom-call | flops 2147483648 | bytes 4194304 | tf_op jit(solution)/shard_map/down_and_mix/pallas_call | solution.py:371
  390.8 1.3 slice.78
  392.0 5.3 %collective-permute-done.25 = bf16[1024,224]{1,0:T(8,128)(2,1)S(1)} collective-permute-done((bf16[1024,224]{1,0:T(8,128)(2,1)S(1)}, bf16[1024,224]{1,0:T(8,128)(2,1)S(1)}, u32[]{:S(2)}, u32[]{:S(2)}) %collective-permute-start.25) | collective-permute-done | bytes 458784 | tf_op jit(solution)/shard_map/ppermute | solution.py:410
  397.8 1.5 collective-permute-done.26
  399.3 1.4 fusion.11
  400.7 17.6 %all_to_all.10 = bf16[16,64,224]{2,1,0:T(8,128)(2,1)S(1)} all-to-all(bf16[16,64,224]{2,1,0:T(8,128)(2,1)S(1)} %bitcast.41), channel_id=1, replica_groups=mesh['parts'=2,'ep'=16,'tp'=1] {'ep'}, dimensions={0} | all-to-all | bytes 917504 | tf_op jit(solution)/shard_map/all_to_all | solution.py:531
  418.6 1.6 reshape.66
  (83 shorter events, 18.5 us)
Async XLA Ops:
  11.0 20.4 %all-to-all-start = ((bf16[16,64,256]{2,1,0:T(8,128)(2,1)}), bf16[16,64,256]{2,1,0:T(8,128)(2,1)S(1)}, u32[]{:S(2)}, u32[]{:S(2)}) async-start(bf16[16,64,256]{2,1,0:T(8,128)(2,1)} %pad_maximum_fusion), calls=%async_computation | async-start | bytes 1048576 | tf_op jit(solution)/shard_map/all_to_all | solution.py:426
  17.5 238.8 %reduce-scatter.3.cloned.1.call-start = ((), (), s32[]{:S(2)}) async-start(), calls=%async_computation.4 | async-start | bytes 5242880 | tf_op jit(solution)/shard_map/reduce_scatter | solution.py:466
  17.6 5.2 %copy-start.4 = (bf16[16,224,1024]{2,1,0:T(8,128)(2,1)S(1)}, bf16[16,224,1024]{2,1,0:T(8,128)(2,1)}, u32[]{:S(2)}) copy-start(bf16[16,224,1024]{2,1,0:T(8,128)(2,1)} %refs_1_.3) | copy-start | bytes 22020100
  21.5 30.5 %collective-permute-start = (bf16[16,224,128]{2,1,0:T(8,128)(2,1)}, bf16[16,224,128]{2,1,0:T(8,128)(2,1)S(1)}, u32[]{:S(2)}, u32[]{:S(2)}) collective-permute-start(bf16[16,224,128]{2,1,0:T(8,128)(2,1)} %get-tuple-element.101), channel_id=1, source_target_pairs={{0,2},{1,3},{2,0},{3,1},{4,6},{5,7},{6,4},{7,5},{8,10},{9,11},{10,... | collective-permute-start | bytes 2752520 | tf_op jit(solution)/shard_map/ppermute | solution.py:410
  35.0 1.9 collective-permute-start.1
  35.0 34.3 %collective-permute-start.2 = (bf16[1024,256]{1,0:T(8,128)(2,1)S(1)}, bf16[1024,256]{1,0:T(8,128)(2,1)S(1)}, u32[]{:S(2)}, u32[]{:S(2)}) collective-permute-start(bf16[1024,256]{1,0:T(8,128)(2,1)S(1)} %bitcast.36), channel_id=1, source_target_pairs={{0,2},{1,3},{2,0},{3,1},{4,6},{5,7},{6,4},{7,5},{8,10},{9,11},{10,... | collective-permute-start | bytes 1572872 | tf_op jit(solution)/shard_map/ppermute | solution.py:410
  36.3 203.3 %copy-start.1 = (s32[32]{0:T(128)}, s32[32]{0:T(128)S(1)}, u32[]{:S(2)}) copy-start(s32[32]{0:T(128)S(1)} %get-tuple-element.111.high.refs_1_) | copy-start | bytes 388
  36.3 203.3 %copy-start.2 = (s32[32]{0:T(128)}, s32[32]{0:T(128)S(1)}, u32[]{:S(2)}) copy-start(s32[32]{0:T(128)S(1)} %get-tuple-element.112.low.refs_0_) | copy-start | bytes 388
  36.3 130.1 %copy-start.3 = (s32[17]{0:T(128)}, s32[17]{0:T(128)S(1)}, u32[]{:S(2)}) copy-start(s32[17]{0:T(128)S(1)} %slice_bitcast_fusion.base.refs_2_) | copy-start | bytes 208
  37.0 40.5 %collective-permute-start.7 = (bf16[16,224,128]{2,1,0:T(8,128)(2,1)S(1)}, bf16[16,224,128]{2,1,0:T(8,128)(2,1)S(1)}, u32[]{:S(2)}, u32[]{:S(2)}) collective-permute-start(bf16[16,224,128]{2,1,0:T(8,128)(2,1)S(1)} %get-tuple-element.60), channel_id=1, source_target_pairs={{0,2},{1,3},{2,0},{3,1},{4,6},{5,7},{6,4},{7,5},{8,10},{9,11},{10,... | collective-permute-start | bytes 2752520 | tf_op jit(solution)/shard_map/ppermute | solution.py:410
  52.0 26.3 %collective-permute-start.8 = (bf16[16,224,128]{2,1,0:T(8,128)(2,1)S(1)}, bf16[16,224,128]{2,1,0:T(8,128)(2,1)S(1)}, u32[]{:S(2)}, u32[]{:S(2)}) collective-permute-start(bf16[16,224,128]{2,1,0:T(8,128)(2,1)S(1)} %collective-permute-done.refs_4_), channel_id=1, source_target_pairs={{0,16},{16,0},{1,17},{17,1},{2,18},{18,2},{3,19},{19,3},{4,20},{20... | collective-permute-start | bytes 2752520 | tf_op jit(solution)/shard_map/ppermute | solution.py:411
  52.2 25.3 %copy-start.11 = (bf16[16,224,128]{2,1,0:T(8,128)(2,1)S(1)}, bf16[16,224,128]{2,1,0:T(8,128)(2,1)}, u32[]{:S(2)}) copy-start(bf16[16,224,128]{2,1,0:T(8,128)(2,1)} %get-tuple-element.58) | copy-start | bytes 2752516
  67.3 2.1 copy-start
  69.4 8.9 %collective-permute-start.3 = (bf16[1024,256]{1,0:T(8,128)(2,1)S(1)}, bf16[1024,256]{1,0:T(8,128)(2,1)S(1)}, u32[]{:S(2)}, u32[]{:S(2)}) collective-permute-start(bf16[1024,256]{1,0:T(8,128)(2,1)S(1)} %collective-permute-done.2.refs_0_), channel_id=1, source_target_pairs={{0,1},{1,0},{2,3},{3,2},{4,5},{5,4},{6,7},{7,6},{8,9},{9,8},{10,11... | collective-permute-start | bytes 1572872 | tf_op jit(solution)/shard_map/ppermute | solution.py:409
  70.1 30.0 %collective-permute-start.5 = (bf16[16,224,128]{2,1,0:T(8,128)(2,1)}, bf16[16,224,128]{2,1,0:T(8,128)(2,1)S(1)}, u32[]{:S(2)}, u32[]{:S(2)}) collective-permute-start(bf16[16,224,128]{2,1,0:T(8,128)(2,1)} %get-tuple-element.99), channel_id=1, source_target_pairs={{0,1},{1,0},{2,3},{3,2},{4,5},{5,4},{6,7},{7,6},{8,9},{9,8},{10,11... | collective-permute-start | bytes 2752520 | tf_op jit(solution)/shard_map/ppermute | solution.py:409
  70.1 30.0 %collective-permute-start.6 = (bf16[16,224,128]{2,1,0:T(8,128)(2,1)}, bf16[16,224,128]{2,1,0:T(8,128)(2,1)S(1)}, u32[]{:S(2)}, u32[]{:S(2)}) collective-permute-start(bf16[16,224,128]{2,1,0:T(8,128)(2,1)} %get-tuple-element.97), channel_id=1, source_target_pairs={{0,1},{1,0},{2,3},{3,2},{4,5},{5,4},{6,7},{7,6},{8,9},{9,8},{10,11... | collective-permute-start | bytes 2752520 | tf_op jit(solution)/shard_map/ppermute | solution.py:409
  77.5 22.7 %collective-permute-start.4 = (bf16[16,224,128]{2,1,0:T(8,128)(2,1)S(1)}, bf16[16,224,128]{2,1,0:T(8,128)(2,1)S(1)}, u32[]{:S(2)}, u32[]{:S(2)}) collective-permute-start(bf16[16,224,128]{2,1,0:T(8,128)(2,1)S(1)} %copy-done.11), channel_id=1, source_target_pairs={{0,2},{1,3},{2,0},{3,1},{4,6},{5,7},{6,4},{7,5},{8,10},{9,11},{10,... | collective-permute-start | bytes 2752520 | tf_op jit(solution)/shard_map/ppermute | solution.py:410
  78.3 21.9 %collective-permute-start.9 = (bf16[16,224,128]{2,1,0:T(8,128)(2,1)S(1)}, bf16[16,224,128]{2,1,0:T(8,128)(2,1)S(1)}, u32[]{:S(2)}, u32[]{:S(2)}) collective-permute-start(bf16[16,224,128]{2,1,0:T(8,128)(2,1)S(1)} %collective-permute-done.7.refs_5_), channel_id=1, source_target_pairs={{0,16},{16,0},{1,17},{17,1},{2,18},{18,2},{3,19},{19,3},{4,20},{20... | collective-permute-start | bytes 2752520 | tf_op jit(solution)/shard_map/ppermute | solution.py:411
  120.4 157.0 %reduce-scatter.5.cloned.1.call-start = ((), (), s32[]{:S(2)}) async-start(), calls=%async_computation.5 | async-start | bytes 5242880 | tf_op jit(solution)/shard_map/reduce_scatter | solution.py:466
  120.7 23.1 %collective-permute-start.12 = (bf16[16,224,128]{2,1,0:T(8,128)(2,1)}, bf16[16,224,128]{2,1,0:T(8,128)(2,1)S(1)}, u32[]{:S(2)}, u32[]{:S(2)}) collective-permute-start(bf16[16,224,128]{2,1,0:T(8,128)(2,1)} %get-tuple-element.65), channel_id=1, source_target_pairs={{0,2},{1,3},{2,0},{3,1},{4,6},{5,7},{6,4},{7,5},{8,10},{9,11},{10,... | collective-permute-start | bytes 2752520 | tf_op jit(solution)/shard_map/ppermute | solution.py:410
  122.4 22.4 %collective-permute-start.13 = (bf16[16,224,128]{2,1,0:T(8,128)(2,1)S(1)}, bf16[16,224,128]{2,1,0:T(8,128)(2,1)S(1)}, u32[]{:S(2)}, u32[]{:S(2)}) collective-permute-start(bf16[16,224,128]{2,1,0:T(8,128)(2,1)S(1)} %collective-permute-done.4.refs_4_), channel_id=1, source_target_pairs={{0,16},{16,0},{1,17},{17,1},{2,18},{18,2},{3,19},{19,3},{4,20},{20... | collective-permute-start | bytes 2752520 | tf_op jit(solution)/shard_map/ppermute | solution.py:411
  122.4 22.4 %collective-permute-start.10 = (bf16[16,224,128]{2,1,0:T(8,128)(2,1)S(1)}, bf16[16,224,128]{2,1,0:T(8,128)(2,1)S(1)}, u32[]{:S(2)}, u32[]{:S(2)}) collective-permute-start(bf16[16,224,128]{2,1,0:T(8,128)(2,1)S(1)} %get-tuple-element.98), channel_id=1, source_target_pairs={{0,1},{1,0},{2,3},{3,2},{4,5},{5,4},{6,7},{7,6},{8,9},{9,8},{10,11... | collective-permute-start | bytes 2752520 | tf_op jit(solution)/shard_map/ppermute | solution.py:409
  123.1 21.7 %collective-permute-start.11 = (bf16[16,224,128]{2,1,0:T(8,128)(2,1)}, bf16[16,224,128]{2,1,0:T(8,128)(2,1)S(1)}, u32[]{:S(2)}, u32[]{:S(2)}) collective-permute-start(bf16[16,224,128]{2,1,0:T(8,128)(2,1)} %get-tuple-element.95), channel_id=1, source_target_pairs={{0,1},{1,0},{2,3},{3,2},{4,5},{5,4},{6,7},{7,6},{8,9},{9,8},{10,11... | collective-permute-start | bytes 2752520 | tf_op jit(solution)/shard_map/ppermute | solution.py:409
  144.8 21.6 %collective-permute-start.14 = (bf16[16,224,128]{2,1,0:T(8,128)(2,1)S(1)}, bf16[16,224,128]{2,1,0:T(8,128)(2,1)S(1)}, u32[]{:S(2)}, u32[]{:S(2)}) collective-permute-start(bf16[16,224,128]{2,1,0:T(8,128)(2,1)S(1)} %collective-permute-done.12.refs_5_), channel_id=1, source_target_pairs={{0,16},{16,0},{1,17},{17,1},{2,18},{18,2},{3,19},{19,3},{4,20},{20... | collective-permute-start | bytes 2752520 | tf_op jit(solution)/shard_map/ppermute | solution.py:411
  191.5 42.4 %collective-permute-start.16 = (bf16[16,224,256]{2,1,0:T(8,128)(2,1)S(1)}, bf16[16,224,256]{2,1,0:T(8,128)(2,1)}, u32[]{:S(2)}, u32[]{:S(2)}) collective-permute-start(bf16[16,224,256]{2,1,0:T(8,128)(2,1)S(1)} %get-tuple-element.70), channel_id=1, source_target_pairs={{0,2},{1,3},{2,0},{3,1},{4,6},{5,7},{6,4},{7,5},{8,10},{9,11},{10,... | collective-permute-start | bytes 5505032 | tf_op jit(solution)/shard_map/ppermute | solution.py:410
  193.1 86.9 %collective-permute-start.15 = (bf16[16,224,256]{2,1,0:T(8,128)(2,1)}, bf16[16,224,256]{2,1,0:T(8,128)(2,1)S(1)}, u32[]{:S(2)}, u32[]{:S(2)}) collective-permute-start(bf16[16,224,256]{2,1,0:T(8,128)(2,1)} %get-tuple-element.93), channel_id=1, source_target_pairs={{0,1},{1,0},{2,3},{3,2},{4,5},{5,4},{6,7},{7,6},{8,9},{9,8},{10,11... | collective-permute-start | bytes 5505032 | tf_op jit(solution)/shard_map/ppermute | solution.py:409
  233.9 46.1 %collective-permute-start.17 = (bf16[16,224,256]{2,1,0:T(8,128)(2,1)}, bf16[16,224,256]{2,1,0:T(8,128)(2,1)}, u32[]{:S(2)}, u32[]{:S(2)}) collective-permute-start(bf16[16,224,256]{2,1,0:T(8,128)(2,1)} %collective-permute-done.16.refs_9_.refs_5_.refs_7_.refs_3_), channel_id=1, source_target_pairs={{0,16},{16,0},{1,17},{17,1},{2,18},{18,2},{3,19},{19,3},{4,20},{20... | collective-permute-start | bytes 5505032 | tf_op jit(solution)/shard_map/ppermute | solution.py:411
  280.0 6.4 %copy-start.5 = (bf16[16,224,256]{2,1,0:T(8,128)(2,1)}, bf16[16,224,256]{2,1,0:T(8,128)(2,1)S(1)}, u32[]{:S(2)}) copy-start(bf16[16,224,256]{2,1,0:T(8,128)(2,1)S(1)} %collective-permute-done.15.refs_8_.refs_4_.refs_6_) | copy-start | bytes 5505028
  280.3 6.2 %copy-start.6 = (bf16[2048,256]{1,0:T(8,128)(2,1)}, bf16[2048,256]{1,0:T(8,128)(2,1)S(1)}, u32[]{:S(2)}) copy-start(bf16[2048,256]{1,0:T(8,128)(2,1)S(1)} %constant_dynamic-update-slice_fusion.refs_5_.refs_6_) | copy-start | bytes 3145732
  280.3 26.1 %collective-permute-start.18 = (bf16[2048,256]{1,0:T(8,128)(2,1)S(1)}, bf16[2048,256]{1,0:T(8,128)(2,1)S(1)}, u32[]{:S(2)}, u32[]{:S(2)}) collective-permute-start(bf16[2048,256]{1,0:T(8,128)(2,1)S(1)} %constant_dynamic-update-slice_fusion.refs_5_.refs_6_), channel_id=1, source_target_pairs={{0,4},{1,5},{2,6},{3,7},{4,8},{5,9},{6,10},{7,11},{8,12},{9,13},{1... | collective-permute-start | bytes 3145736 | tf_op jit(solution)/shard_map/ppermute | solution.py:493
  283.9 25.8 %collective-permute-start.19 = (bf16[2048,256]{1,0:T(8,128)(2,1)S(1)}, bf16[2048,256]{1,0:T(8,128)(2,1)}, u32[]{:S(2)}, u32[]{:S(2)}) collective-permute-start(bf16[2048,256]{1,0:T(8,128)(2,1)S(1)} %constant_dynamic-update-slice_fusion.refs_5_.refs_6_), channel_id=1, source_target_pairs={{4,0},{5,1},{6,2},{7,3},{8,4},{9,5},{10,6},{11,7},{12,8},{13,9},{1... | collective-permute-start | bytes 3145736 | tf_op jit(solution)/shard_map/ppermute | solution.py:493
  306.4 8.0 %copy-start.9 = (bf16[2048,256]{1,0:T(8,128)(2,1)}, bf16[2048,256]{1,0:T(8,128)(2,1)S(1)}, u32[]{:S(2)}) copy-start(bf16[2048,256]{1,0:T(8,128)(2,1)S(1)} %collective-permute-done.18.refs_0_) | copy-start | bytes 3145732
  309.7 22.6 %collective-permute-start.20 = (bf16[2048,256]{1,0:T(8,128)(2,1)S(1)}, bf16[2048,256]{1,0:T(8,128)(2,1)S(1)}, u32[]{:S(2)}, u32[]{:S(2)}) collective-permute-start(bf16[2048,256]{1,0:T(8,128)(2,1)S(1)} %collective-permute-done.18.refs_0_), channel_id=1, source_target_pairs={{4,8},{5,9},{6,10},{7,11},{8,12},{9,13},{10,14},{11,15},{20,24},{2... | collective-permute-start | bytes 3145736 | tf_op jit(solution)/shard_map/ppermute | solution.py:493
  311.8 24.8 %collective-permute-start.21 = (bf16[2048,256]{1,0:T(8,128)(2,1)}, bf16[2048,256]{1,0:T(8,128)(2,1)}, u32[]{:S(2)}, u32[]{:S(2)}) collective-permute-start(bf16[2048,256]{1,0:T(8,128)(2,1)} %collective-permute-done.19.refs_1_), channel_id=1, source_target_pairs={{4,0},{5,1},{6,2},{7,3},{8,4},{9,5},{10,6},{11,7},{20,16},{21,17},... | collective-permute-start | bytes 3145736 | tf_op jit(solution)/shard_map/ppermute | solution.py:493
  332.4 1.0 copy-start.10
  336.6 31.6 %collective-permute-start.22 = (bf16[2048,256]{1,0:T(8,128)(2,1)}, bf16[2048,256]{1,0:T(8,128)(2,1)S(1)}, u32[]{:S(2)}, u32[]{:S(2)}) collective-permute-start(bf16[2048,256]{1,0:T(8,128)(2,1)} %copy-done.10), channel_id=1, source_target_pairs={{8,12},{9,13},{10,14},{11,15},{24,28},{25,29},{26,30},{27,31}} | collective-permute-start | bytes 3145736 | tf_op jit(solution)/shard_map/ppermute | solution.py:493
  337.3 30.9 %collective-permute-start.23 = (bf16[2048,256]{1,0:T(8,128)(2,1)}, bf16[2048,256]{1,0:T(8,128)(2,1)S(1)}, u32[]{:S(2)}, u32[]{:S(2)}) collective-permute-start(bf16[2048,256]{1,0:T(8,128)(2,1)} %collective-permute-done.21.refs_3_), channel_id=1, source_target_pairs={{4,0},{5,1},{6,2},{7,3},{20,16},{21,17},{22,18},{23,19}} | collective-permute-start | bytes 3145736 | tf_op jit(solution)/shard_map/ppermute | solution.py:493
  368.2 1.0 copy-start.7
  369.2 1.0 copy-start.8
  377.6 4.6 %collective-permute-start.24 = (bf16[1024,224]{1,0:T(8,128)(2,1)S(1)}, bf16[1024,224]{1,0:T(8,128)(2,1)S(1)}, u32[]{:S(2)}, u32[]{:S(2)}) collective-permute-start(bf16[1024,224]{1,0:T(8,128)(2,1)S(1)} %slice.60), channel_id=1, source_target_pairs={{0,1},{1,0},{2,3},{3,2},{4,5},{5,4},{6,7},{7,6},{8,9},{9,8},{10,11... | collective-permute-start | bytes 1376264 | tf_op jit(solution)/shard_map/ppermute | solution.py:409
  383.4 14.0 %collective-permute-start.25 = (bf16[1024,224]{1,0:T(8,128)(2,1)S(1)}, bf16[1024,224]{1,0:T(8,128)(2,1)S(1)}, u32[]{:S(2)}, u32[]{:S(2)}) collective-permute-start(bf16[1024,224]{1,0:T(8,128)(2,1)S(1)} %add_convert_fusion), channel_id=1, source_target_pairs={{0,2},{1,3},{2,0},{3,1},{4,6},{5,7},{6,4},{7,5},{8,10},{9,11},{10,... | collective-permute-start | bytes 1376264 | tf_op jit(solution)/shard_map/ppermute | solution.py:410
  397.4 1.9 collective-permute-start.26
Sparse Core Ops, SparseCore 0:
  120.6 77.1 reduce-scatter.2
  200.2 77.2 reduce-scatter.4

commit v13 on v11

--- a/solution.py
+++ b/solution.py
@@ -314,7 +314,7 @@
 
 
 def down_kernel(slots, low, high, base, block, onehot_ref, *refs):
-    hidden, start, refs = refs[: 2 * slots], refs[2 * slots], refs[2 * slots + 1 :]
+    hidden, start, refs = refs[: 4 * slots], refs[4 * slots], refs[4 * slots + 1 :]
     weights, (out, total_ref, value_ref) = refs[:-3], refs[-3:]
     width = weights[0].shape[1]
     j = pl.program_id(0)
@@ -330,9 +330,9 @@
         for part in range(BLOCK // TILE):
             i = (2 * block[3 * slot] + j % 2) * (BLOCK // TILE) + part
             here = slice(part * TILE, (part + 1) * TILE)
-            source = 2 * slot + 1 - block[3 * slot + 1]
+            source = 4 * slot + 2 - 2 * block[3 * slot + 1] + j % 2
             units = hidden[0][here, :]
-            for k in range(1, 2 * slots):
+            for k in range(1, 4 * slots):
                 units = jnp.where(source == k, hidden[k][here, :], units)
 
             @pl.loop(low[i], high[i])
@@ -354,16 +354,13 @@
 
 def down_and_mix(spans, base, block, onehot, hidden, start, at, weights, dtype):
     rows, units = hidden[0].shape
-    slots = len(hidden) // 2
+    slots = len(hidden) // 4
     count, tokens = len(weights), onehot.shape[0]
-    some = [
-        pl.BlockSpec((BLOCK, units), lambda j, *_, s=k // 2: (jnp.clip(j - 2 * s, 0, 1), 0))
-        for k in range(2 * slots)
-    ]
+    some = [pl.BlockSpec((rows, units), lambda j, *_: (0, 0))] * (4 * slots)
     whole = pl.BlockSpec((tokens, count * LANES), lambda j, *_: (0, 0))
     kernel = functools.partial(down_kernel, slots)
     if start is None:
-        kernel = lambda *refs: down_kernel(slots, *refs[: 5 + 2 * slots], None, *refs[5 + 2 * slots :])
+        kernel = lambda *refs: down_kernel(slots, *refs[: 5 + 4 * slots], None, *refs[5 + 4 * slots :])
     return pl.pallas_call(
         kernel,
         grid_spec=pltpu.PrefetchScalarGridSpec(
@@ -386,7 +383,7 @@
         ),
         out_shape=jax.ShapeDtypeStruct((tokens, count * LANES), dtype),
         compiler_params=params(56),
-        cost_estimate=cost(2 * slots * rows * tokens * LANES * count, 2 * slots * rows * tokens),
+        cost_estimate=cost(4 * slots * rows * tokens * LANES * count, 4 * slots * rows * tokens),
         name="down_and_mix",
     )(*spans, base, block, onehot, *hidden, *([] if start is None else [start]), *weights)
 
@@ -495,20 +492,25 @@
             spans, base, block, columns, hidden, start, at, pieces[at : at + count], dtype
         )
 
-    moving = [steps(units, 1, True), steps(units, 1, False)]
-    total, waiting = mix((spot, 1, 1), [units, units], None), []
+    halves = [units[:BLOCK], units[BLOCK:]]
+    moving = [[steps(half, 1, up) for up in (True, False)] for half in halves]
+    total, waiting = mix((spot, 1, 1), halves + halves, None), []
     for step in range(1, places):
-        if step == places - 1:
-            if waiting:
-                both = [sum(map(tuple, parts), ()) for parts in zip(*waiting)]
-                total = mix(*both, total)
-        *hidden, total = lax.optimization_barrier((*moving, total))
+        if step == places - 1 and waiting:
+            both = [sum(map(tuple, parts), ()) for parts in zip(*waiting)]
+            total = mix(*both, total)
+        arrived = []
+        for n in range(2):
+            *half, total = lax.optimization_barrier((*moving[n], total))
+            arrived.append(half)
+            if step < places - 1:
+                moving[n] = [steps(half[k], step + 1, k == 0) for k in range(2)]
+        hidden = [arrived[n][k] for k in range(2) for n in range(2)]
         came_up, came_down = spot >= step, spot < places - step
         above = jnp.minimum(spot + step, places - 1)
         flags = (jnp.where(came_up, spot - step, above), came_up, came_up | came_down)
         if step == places - 1:
             break
-        moving = [steps(hidden[0], step + 1, True), steps(hidden[1], step + 1, False)]
         waiting.append((flags, hidden))
         if 2 * step < places:
             waiting.append(((above, 0, came_up & came_down), hidden))

time: 429 us -> 434 us (1.012)
  starting transfers between devices: 32.5 us -> 44.2 us
  waiting for transfers between devices: 146 us -> 135 us
    ppermute x6 -> x12, starting transfers between devices: 12.8 us -> 25.4 us  [steps(): return lax.ppermute(value, 'ep', links)]
    ppermute x6 -> x12, waiting for transfers between devices: 11 us -> 0.03 us  [steps(): return lax.ppermute(value, 'ep', links)]
  transfers between devices with their start and end apart: 30 -> 36, of which waited for: 17 -> 13; matrix products, arithmetic and copies ran while one was open for 5% -> 5% of each run, Pallas kernels for 35% -> 36%
where the time goes in v13:
time: 434 us; the launch traced here: 431 us
  Pallas kernels  180 us (41%)
  waiting for transfers between devices  135 us (31%)
  starting transfers between devices  44.2 us (10%)
  local copies, waits for them, and re-layouts  29.6 us (7%)
  blocking collectives  19.4 us (4%)
  between operations  13.9 us (3%)
  other arithmetic  8.71 us (2%)
    ppermute x7, waiting for transfers between devices, fixed_weights(): to_cross = lambda value: lax.ppermute(value, ('parts', 'ep'), cross)  80.4 us
    pallas_call x5, Pallas kernels, down_and_mix(): pl.pallas_call(kernel, grid_spec=pltpu.PrefetchScalarGridSpec(num_scalar_...  75.5 us
    pallas_call x2, Pallas kernels, partial_sums(): pl.pallas_call(partial_kernel, grid_spec=pltpu.PrefetchScalarGridSpec(num...  39.3 us
    pallas_call x2, Pallas kernels, sort_rows(): pl.pallas_call(kernel, grid_spec=pltpu.PrefetchScalarGridSpec(num_scalar_...  29.5 us
    ppermute x12, starting transfers between devices, steps(): return lax.ppermute(value, 'ep', links)  25.4 us
    ppermute x5, waiting for transfers between devices, fixed_weights(): to_plane = lambda value: lax.ppermute(value, 'parts', [(0, 1), (1, 0)])  22.7 us
    reduce_scatter x2, waiting for transfers between devices, units_of(): lax.psum_scatter(sums, 'ep', scatter_dimension=0, axis_index_groups=line,...  21.9 us
    all_to_all x1, blocking collectives, fixed_weights(): lax.all_to_all(mixed.reshape(size, count, width), 'ep', split_axis=0, con...  19.4 us
  transfers between devices with their start and end apart: 36, of which 13 were waited for; matrix products, arithmetic and copies ran while one was open for 5% of the time, Pallas kernels for 36%

profile of v13, /device:TPU:15, one launch (start us, length us, event | category | flops | bytes accessed | tf_op | source)
XLA Modules:
  0.0 430.7 jit_solution(13938714099802635636)
XLA Ops:
  8.0 1.8 reshape.61
  11.0 6.6 %all-to-all-start = ((bf16[16,64,256]{2,1,0:T(8,128)(2,1)}), bf16[16,64,256]{2,1,0:T(8,128)(2,1)S(1)}, u32[]{:S(2)}, u32[]{:S(2)}) async-start(bf16[16,64,256]{2,1,0:T(8,128)(2,1)} %pad_maximum_fusion), calls=%async_computation | async-start | bytes 1048576 | tf_op jit(solution)/shard_map/all_to_all | solution.py:419
  17.6 3.8 constant_dynamic-slice_fusion.2
  22.9 2.2 constant_dynamic-slice_fusion
  25.0 6.4 %all-to-all-done = bf16[16,64,256]{2,1,0:T(8,128)(2,1)S(1)} async-done(((bf16[16,64,256]{2,1,0:T(8,128)(2,1)}), bf16[16,64,256]{2,1,0:T(8,128)(2,1)S(1)}, u32[]{:S(2)}, u32[]{:S(2)}) %all-to-all-start) | async-done | bytes 524320 | tf_op jit(solution)/shard_map/all_to_all | solution.py:419
  31.4 3.6 order.1
  37.6 14.5 %sort_rows.2 = (bf16[8192,512]{1,0:T(8,128)(2,1)}, f32[8192,128]{1,0:T(8,128)S(1)}, bf16[8192,1024]{1,0:T(8,128)(2,1)}) custom-call(s32[32]{0:T(128)S(1)} %get-tuple-element.132.low.refs_0_, s32[32]{0:T(128)S(1)} %get-tuple-element.131.high.refs_1_, s32[17]{0:T(128)S(1)} %slice_bitcast_fusion.base.refs_2_, s32[16,8,128]{2,1,0:T(8,128)S(1)} %bitcast.39, ...), custom_call_target="tpu_custom_call" | custom-call | flops 4294967296 | bytes 16777216 | tf_op jit(solution)/shard_map/sort_rows/pallas_call | solution.py:188
  52.3 14.9 %sort_rows.3 = (bf16[8192,512]{1,0:T(8,128)(2,1)}, f32[8192,128]{1,0:T(8,128)S(1)}, bf16[8192,1024]{1,0:T(8,128)(2,1)}) custom-call(s32[32]{0:T(128)S(1)} %get-tuple-element.132.low.refs_0_, s32[32]{0:T(128)S(1)} %get-tuple-element.131.high.refs_1_, ...), custom_call_target="tpu_custom_call", output_to_operand_aliasing={{0}: (7, {}), {1}: (8, {}), {2}: (9, {})} | custom-call | flops 4294967296 | bytes 16777216 | tf_op jit(solution)/shard_map/sort_rows/pallas_call | solution.py:188
  67.3 2.1 copy-done
  70.6 6.9 %collective-permute-done.7.refs_5_ = bf16[16,224,128]{2,1,0:T(8,128)(2,1)S(1)} collective-permute-done((bf16[16,224,128]{2,1,0:T(8,128)(2,1)S(1)}, bf16[16,224,128]{2,1,0:T(8,128)(2,1)S(1)}, u32[]{:S(2)}, u32[]{:S(2)}) %collective-permute-start.7) | collective-permute-done | bytes 917536 | tf_op jit(solution)/shard_map/ppermute | solution.py:403
  78.3 15.4 %sort_more.1.far_ref = bf16[8192,512]{1,0:T(8,128)(2,1)} custom-call(bf16[8192,1024]{1,0:T(8,128)(2,1)} %get-tuple-element.65.onehot_ref, bf16[1024,256]{1,0:T(8,128)(2,1)S(1)} %collective-permute-done.2.refs_0_, bf16[1024,256]{1,0:T(8,128)(2,1)S(1)} %collective-permute-done.3.refs_1_), custom_call_target="tpu_custom_call" | custom-call | flops 8589934592 | bytes 33554432 | tf_op jit(solution)/shard_map/sort_more/pallas_call | solution.py:227
  93.6 6.5 %collective-permute-done.4.refs_4_ = bf16[16,224,128]{2,1,0:T(8,128)(2,1)S(1)} collective-permute-done((bf16[16,224,128]{2,1,0:T(8,128)(2,1)S(1)}, bf16[16,224,128]{2,1,0:T(8,128)(2,1)S(1)}, u32[]{:S(2)}, u32[]{:S(2)}) %collective-permute-start.4) | collective-permute-done | bytes 917536 | tf_op jit(solution)/shard_map/ppermute | solution.py:403
  100.2 19.6 %partial_sums.2 = bf16[8192,256]{1,0:T(8,128)(2,1)} custom-call(s32[32]{0:T(128)S(1)} %get-tuple-element.132.low.refs_0_, s32[32]{0:T(128)S(1)} %get-tuple-element.131.high.refs_1_, s32[17]{0:T(128)S(1)} %slice_bitcast_fusion.base.refs_2_, s32[1]{0:T(128)} %bitcast.8.quarter, bf16[8192,512]{1,0:T(8,128)(2,1)} %get-tuple-element.64.near_ref, ...), custom_call_target="tpu_custom_call" | custom-call | flops 4294967296 | bytes 16777216 | tf_op jit(solution)/shard_map/partial_sums/pallas_call | solution.py:300
  120.0 1.8 collective-permute-start.12
  122.4 20.8 %collective-permute-done.12.refs_5_ = bf16[16,224,128]{2,1,0:T(8,128)(2,1)S(1)} collective-permute-done((bf16[16,224,128]{2,1,0:T(8,128)(2,1)}, bf16[16,224,128]{2,1,0:T(8,128)(2,1)S(1)}, u32[]{:S(2)}, u32[]{:S(2)}) %collective-permute-start.12) | collective-permute-done | bytes 917536 | tf_op jit(solution)/shard_map/ppermute | solution.py:403
  144.2 21.7 %collective-permute-done.14.refs_7_ = bf16[16,224,128]{2,1,0:T(8,128)(2,1)S(1)} collective-permute-done((bf16[16,224,128]{2,1,0:T(8,128)(2,1)S(1)}, bf16[16,224,128]{2,1,0:T(8,128)(2,1)S(1)}, u32[]{:S(2)}, u32[]{:S(2)}) %collective-permute-start.14) | collective-permute-done | bytes 917536 | tf_op jit(solution)/shard_map/ppermute | solution.py:404
  165.9 19.7 %partial_sums.3 = bf16[8192,256]{1,0:T(8,128)(2,1)} custom-call(s32[32]{0:T(128)S(1)} %get-tuple-element.132.low.refs_0_, s32[32]{0:T(128)S(1)} %get-tuple-element.131.high.refs_1_, s32[17]{0:T(128)S(1)} %slice_bitcast_fusion.base.refs_2_, s32[1]{0:T(128)} %bitcast.8.quarter, bf16[8192,512]{1,0:T(8,128)(2,1)} %get-tuple-element.64.near_ref, ...), custom_call_target="tpu_custom_call" | custom-call | flops 4294967296 | bytes 16777216 | tf_op jit(solution)/shard_map/partial_sums/pallas_call | solution.py:300
  185.6 4.8 %dynamic-slice_bitcast_fusion = (bf16[16,224,256]{2,1,0:T(8,128)(2,1)S(1)}, bf16[16,224,256]{2,1,0:T(8,128)(2,1)}, bf16[16,224,256]{2,1,0:T(8,128)(2,1)}) fusion(bf16[16,1024,224]{1,2,0:T(8,128)(2,1)} %param.11, s32[]{:T(128)S(6)} %select_n.48, s32[]{:T(128)S(6)} %select_n.53, s32[]{:T(128)S(6)} %select_n.50), kind=kLoop, calls=%fused_computation | loop fusion | bytes 11010060 | tf_op jit(solution)/shard_map/dynamic_slice | solution.py:429
  190.4 1.5 collective-permute-start.16
  191.9 40.9 %collective-permute-done.16.refs_11_.refs_7_.refs_5_ = bf16[16,224,256]{2,1,0:T(8,128)(2,1)} collective-permute-done((bf16[16,224,256]{2,1,0:T(8,128)(2,1)S(1)}, bf16[16,224,256]{2,1,0:T(8,128)(2,1)}, u32[]{:S(2)}, u32[]{:S(2)}) %collective-permute-start.16) | collective-permute-done | bytes 1835040 | tf_op jit(solution)/shard_map/ppermute | solution.py:403
  232.8 5.7 %broadcast_in_dim.5.place_ref = s32[16,1024,128]{2,1,0:T(8,128)} broadcast(s32[16,1024]{1,0:T(8,128)S(1)} %get-tuple-element.77), dimensions={0,1} | broadcast | bytes 8454144 | tf_op jit(solution)/shard_map/broadcast_in_dim | solution.py:470
  238.6 16.4 %scatter_rows.1.refs_4_.onehot_ref = bf16[1024,8192]{1,0:T(8,128)(2,1)} custom-call(s32[32]{0:T(128)S(1)} %get-tuple-element.132.low.refs_0_, s32[32]{0:T(128)S(1)} %get-tuple-element.131.high.refs_1_, s32[16,1024,128]{2,1,0:T(8,128)} %broadcast_in_dim.5.place_ref), custom_call_target="tpu_custom_call" | custom-call | flops 8388608 | bytes 16777216 | tf_op jit(solution)/shard_map/scatter_rows/pallas_call | solution.py:257
  255.0 21.9 %reduce-scatter.5.cloned.1.call-done = bf16[2048,256]{1,0:T(8,128)(2,1)} async-done(((bf16[8192,256]{1,0:T(8,128)(2,1)}), bf16[2048,256]{1,0:T(8,128)(2,1)}) %reduce-scatter.5.cloned.1.call-update) | async-done | bytes 1048592 | tf_op jit(solution)/shard_map/reduce_scatter | solution.py:459
  276.8 2.5 fusion.12
  279.7 3.6 collective-permute-start.18
  283.4 1.9 collective-permute-start.19
  285.3 3.4 collective-permute-start.22
  288.7 2.7 collective-permute-start.23
  292.0 16.7 %down_and_mix.5.refs_4_ = f32[1024,1024]{1,0:T(8,128)} custom-call(s32[32]{0:T(128)} %copy-done.2, s32[32]{0:T(128)} %copy-done.1, s32[17]{0:T(128)} %copy-done.3, s32[3]{0:T(128)} %stack.80.refs_3_, bf16[1024,8192]{1,0:T(8,128)(2,1)} %scatter_rows.1.refs_4_.onehot_ref, bf16[1024,256]{1,0:T(8,128)(2,1)} %copy-done.7, bf16[1024,256]{1,0:T(8,128)(2,1)} %copy-done.6, ...), custom_call_target="tpu_custom_call" | custom-call | flops 4294967296 | bytes 4194304 | tf_op jit(solution)/shard_map/down_and_mix/pallas_call | solution.py:364
  308.7 2.3 collective-permute-start.20
  311.0 1.9 collective-permute-start.21
  313.0 3.4 collective-permute-start.26
  316.4 1.9 collective-permute-start.27
  320.2 17.9 %down_and_mix.6.refs_8_ = f32[1024,1024]{1,0:T(8,128)} custom-call(s32[32]{0:T(128)} %copy-done.2, s32[32]{0:T(128)} %copy-done.1, s32[17]{0:T(128)} %copy-done.3, s32[3]{0:T(128)} %pad_add_fusion.1.block, bf16[1024,8192]{1,0:T(8,128)(2,1)} %scatter_rows.1.refs_4_.onehot_ref, bf16[1024,256]{1,0:T(8,128)(2,1)} %copy-done.8, ...), custom_call_target="tpu_custom_call" | custom-call | flops 4294967296 | bytes 4194304 | tf_op jit(solution)/shard_map/down_and_mix/pallas_call | solution.py:364
  338.8 1.3 collective-permute-start.25
  340.9 1.5 collective-permute-start.29
  342.5 27.8 %down_and_mix.7.refs_4_ = f32[1024,1024]{1,0:T(8,128)} custom-call(s32[32]{0:T(128)} %copy-done.2, s32[32]{0:T(128)} %copy-done.1, s32[17]{0:T(128)} %copy-done.3, s32[6]{0:T(128)} %stack.95.block, bf16[1024,8192]{1,0:T(8,128)(2,1)} %scatter_rows.1.refs_4_.onehot_ref, bf16[1024,256]{1,0:T(8,128)(2,1)} %copy-done.8, ...), custom_call_target="tpu_custom_call" | custom-call | flops 8589934592 | bytes 8388608 | tf_op jit(solution)/shard_map/down_and_mix/pallas_call | solution.py:364
  372.4 6.4 %down_and_mix.8 = bf16[1024,512]{1,0:T(8,128)(2,1)} custom-call(s32[32]{0:T(128)} %copy-done.2, s32[32]{0:T(128)} %copy-done.1, s32[17]{0:T(128)} %copy-done.3, s32[3]{0:T(128)} %pad_add_fusion.block, bf16[1024,8192]{1,0:T(8,128)(2,1)} %scatter_rows.1.refs_4_.onehot_ref, bf16[1024,256]{1,0:T(8,128)(2,1)} %copy-done.9, bf16[1024,256]{1,0:T(8,128)(2,1)} %copy-done.11, ...), custom_call_target="tpu_custom_call" | custom-call | flops 2147483648 | bytes 4194304 | tf_op jit(solution)/shard_map/down_and_mix/pallas_call | solution.py:364
  379.8 2.6 collective-permute-start.30
  382.5 1.5 collective-permute-done.30
  384.0 1.2 add_convert_fusion
  385.8 6.7 %down_and_mix.9 = f32[1024,512]{1,0:T(8,128)} custom-call(s32[32]{0:T(128)} %copy-done.2, s32[32]{0:T(128)} %copy-done.1, s32[17]{0:T(128)} %copy-done.3, s32[3]{0:T(128)} %pad_add_fusion.block, bf16[1024,8192]{1,0:T(8,128)(2,1)} %scatter_rows.1.refs_4_.onehot_ref, bf16[1024,256]{1,0:T(8,128)(2,1)} %copy-done.9, bf16[1024,256]{1,0:T(8,128)(2,1)} %copy-done.11, ...), custom_call_target="tpu_custom_call" | custom-call | flops 2147483648 | bytes 4194304 | tf_op jit(solution)/shard_map/down_and_mix/pallas_call | solution.py:364
  392.5 1.3 slice.88
  393.8 5.3 %collective-permute-done.31 = bf16[1024,224]{1,0:T(8,128)(2,1)S(1)} collective-permute-done((bf16[1024,224]{1,0:T(8,128)(2,1)S(1)}, bf16[1024,224]{1,0:T(8,128)(2,1)S(1)}, u32[]{:S(2)}, u32[]{:S(2)}) %collective-permute-start.31) | collective-permute-done | bytes 458784 | tf_op jit(solution)/shard_map/ppermute | solution.py:403
  399.5 1.5 collective-permute-done.32
  401.1 1.4 fusion.11
  402.5 19.4 %all_to_all.10 = bf16[16,64,224]{2,1,0:T(8,128)(2,1)S(1)} all-to-all(bf16[16,64,224]{2,1,0:T(8,128)(2,1)S(1)} %bitcast.41), channel_id=1, replica_groups=mesh['parts'=2,'ep'=16,'tp'=1] {'ep'}, dimensions={0} | all-to-all | bytes 917504 | tf_op jit(solution)/shard_map/all_to_all | solution.py:529
  422.2 1.6 reshape.66
  (108 shorter events, 19.5 us)
Async XLA Ops:
  11.0 20.4 %all-to-all-start = ((bf16[16,64,256]{2,1,0:T(8,128)(2,1)}), bf16[16,64,256]{2,1,0:T(8,128)(2,1)S(1)}, u32[]{:S(2)}, u32[]{:S(2)}) async-start(bf16[16,64,256]{2,1,0:T(8,128)(2,1)} %pad_maximum_fusion), calls=%async_computation | async-start | bytes 1048576 | tf_op jit(solution)/shard_map/all_to_all | solution.py:419
  17.5 237.4 %reduce-scatter.3.cloned.1.call-start = ((), (), s32[]{:S(2)}) async-start(), calls=%async_computation.4 | async-start | bytes 5242880 | tf_op jit(solution)/shard_map/reduce_scatter | solution.py:459
  17.6 5.2 %copy-start.4 = (bf16[16,224,1024]{2,1,0:T(8,128)(2,1)S(1)}, bf16[16,224,1024]{2,1,0:T(8,128)(2,1)}, u32[]{:S(2)}) copy-start(bf16[16,224,1024]{2,1,0:T(8,128)(2,1)} %refs_1_.3) | copy-start | bytes 22020100
  21.5 30.7 %collective-permute-start = (bf16[16,224,128]{2,1,0:T(8,128)(2,1)}, bf16[16,224,128]{2,1,0:T(8,128)(2,1)S(1)}, u32[]{:S(2)}, u32[]{:S(2)}) collective-permute-start(bf16[16,224,128]{2,1,0:T(8,128)(2,1)} %get-tuple-element.119), channel_id=1, source_target_pairs={{0,2},{1,3},{2,0},{3,1},{4,6},{5,7},{6,4},{7,5},{8,10},{9,11},{10,... | collective-permute-start | bytes 2752520 | tf_op jit(solution)/shard_map/ppermute | solution.py:403
  35.0 1.9 collective-permute-start.1
  35.0 34.3 %collective-permute-start.2 = (bf16[1024,256]{1,0:T(8,128)(2,1)S(1)}, bf16[1024,256]{1,0:T(8,128)(2,1)S(1)}, u32[]{:S(2)}, u32[]{:S(2)}) collective-permute-start(bf16[1024,256]{1,0:T(8,128)(2,1)S(1)} %bitcast.36), channel_id=1, source_target_pairs={{0,2},{1,3},{2,0},{3,1},{4,6},{5,7},{6,4},{7,5},{8,10},{9,11},{10,... | collective-permute-start | bytes 1572872 | tf_op jit(solution)/shard_map/ppermute | solution.py:403
  36.2 202.3 %copy-start.1 = (s32[32]{0:T(128)}, s32[32]{0:T(128)S(1)}, u32[]{:S(2)}) copy-start(s32[32]{0:T(128)S(1)} %get-tuple-element.131.high.refs_1_) | copy-start | bytes 388
  36.2 202.3 %copy-start.2 = (s32[32]{0:T(128)}, s32[32]{0:T(128)S(1)}, u32[]{:S(2)}) copy-start(s32[32]{0:T(128)S(1)} %get-tuple-element.132.low.refs_0_) | copy-start | bytes 388
  36.3 129.6 %copy-start.3 = (s32[17]{0:T(128)}, s32[17]{0:T(128)S(1)}, u32[]{:S(2)}) copy-start(s32[17]{0:T(128)S(1)} %slice_bitcast_fusion.base.refs_2_) | copy-start | bytes 208
  36.9 40.5 %collective-permute-start.7 = (bf16[16,224,128]{2,1,0:T(8,128)(2,1)S(1)}, bf16[16,224,128]{2,1,0:T(8,128)(2,1)S(1)}, u32[]{:S(2)}, u32[]{:S(2)}) collective-permute-start(bf16[16,224,128]{2,1,0:T(8,128)(2,1)S(1)} %get-tuple-element.69), channel_id=1, source_target_pairs={{0,2},{1,3},{2,0},{3,1},{4,6},{5,7},{6,4},{7,5},{8,10},{9,11},{10,... | collective-permute-start | bytes 2752520 | tf_op jit(solution)/shard_map/ppermute | solution.py:403
  52.1 26.1 %collective-permute-start.8 = (bf16[16,224,128]{2,1,0:T(8,128)(2,1)S(1)}, bf16[16,224,128]{2,1,0:T(8,128)(2,1)S(1)}, u32[]{:S(2)}, u32[]{:S(2)}) collective-permute-start(bf16[16,224,128]{2,1,0:T(8,128)(2,1)S(1)} %collective-permute-done.refs_4_), channel_id=1, source_target_pairs={{0,16},{16,0},{1,17},{17,1},{2,18},{18,2},{3,19},{19,3},{4,20},{20... | collective-permute-start | bytes 2752520 | tf_op jit(solution)/shard_map/ppermute | solution.py:404
  52.3 25.1 %copy-start.13 = (bf16[16,224,128]{2,1,0:T(8,128)(2,1)S(1)}, bf16[16,224,128]{2,1,0:T(8,128)(2,1)}, u32[]{:S(2)}) copy-start(bf16[16,224,128]{2,1,0:T(8,128)(2,1)} %get-tuple-element.67) | copy-start | bytes 2752516
  69.3 8.9 %collective-permute-start.3 = (bf16[1024,256]{1,0:T(8,128)(2,1)S(1)}, bf16[1024,256]{1,0:T(8,128)(2,1)S(1)}, u32[]{:S(2)}, u32[]{:S(2)}) collective-permute-start(bf16[1024,256]{1,0:T(8,128)(2,1)S(1)} %collective-permute-done.2.refs_0_), channel_id=1, source_target_pairs={{0,1},{1,0},{2,3},{3,2},{4,5},{5,4},{6,7},{7,6},{8,9},{9,8},{10,11... | collective-permute-start | bytes 1572872 | tf_op jit(solution)/shard_map/ppermute | solution.py:402
  70.1 30.1 %collective-permute-start.5 = (bf16[16,224,128]{2,1,0:T(8,128)(2,1)}, bf16[16,224,128]{2,1,0:T(8,128)(2,1)S(1)}, u32[]{:S(2)}, u32[]{:S(2)}) collective-permute-start(bf16[16,224,128]{2,1,0:T(8,128)(2,1)} %get-tuple-element.117), channel_id=1, source_target_pairs={{0,1},{1,0},{2,3},{3,2},{4,5},{5,4},{6,7},{7,6},{8,9},{9,8},{10,11... | collective-permute-start | bytes 2752520 | tf_op jit(solution)/shard_map/ppermute | solution.py:402
  70.1 30.1 %collective-permute-start.6 = (bf16[16,224,128]{2,1,0:T(8,128)(2,1)}, bf16[16,224,128]{2,1,0:T(8,128)(2,1)S(1)}, u32[]{:S(2)}, u32[]{:S(2)}) collective-permute-start(bf16[16,224,128]{2,1,0:T(8,128)(2,1)} %get-tuple-element.115), channel_id=1, source_target_pairs={{0,1},{1,0},{2,3},{3,2},{4,5},{5,4},{6,7},{7,6},{8,9},{9,8},{10,11... | collective-permute-start | bytes 2752520 | tf_op jit(solution)/shard_map/ppermute | solution.py:402
  77.5 22.7 %collective-permute-start.4 = (bf16[16,224,128]{2,1,0:T(8,128)(2,1)S(1)}, bf16[16,224,128]{2,1,0:T(8,128)(2,1)S(1)}, u32[]{:S(2)}, u32[]{:S(2)}) collective-permute-start(bf16[16,224,128]{2,1,0:T(8,128)(2,1)S(1)} %copy-done.13), channel_id=1, source_target_pairs={{0,2},{1,3},{2,0},{3,1},{4,6},{5,7},{6,4},{7,5},{8,10},{9,11},{10,... | collective-permute-start | bytes 2752520 | tf_op jit(solution)/shard_map/ppermute | solution.py:403
  78.3 21.9 %collective-permute-start.9 = (bf16[16,224,128]{2,1,0:T(8,128)(2,1)S(1)}, bf16[16,224,128]{2,1,0:T(8,128)(2,1)S(1)}, u32[]{:S(2)}, u32[]{:S(2)}) collective-permute-start(bf16[16,224,128]{2,1,0:T(8,128)(2,1)S(1)} %collective-permute-done.7.refs_5_), channel_id=1, source_target_pairs={{0,16},{16,0},{1,17},{17,1},{2,18},{18,2},{3,19},{19,3},{4,20},{20... | collective-permute-start | bytes 2752520 | tf_op jit(solution)/shard_map/ppermute | solution.py:404
  119.8 157.0 %reduce-scatter.5.cloned.1.call-start = ((), (), s32[]{:S(2)}) async-start(), calls=%async_computation.5 | async-start | bytes 5242880 | tf_op jit(solution)/shard_map/reduce_scatter | solution.py:459
  120.0 23.1 %collective-permute-start.12 = (bf16[16,224,128]{2,1,0:T(8,128)(2,1)}, bf16[16,224,128]{2,1,0:T(8,128)(2,1)S(1)}, u32[]{:S(2)}, u32[]{:S(2)}) collective-permute-start(bf16[16,224,128]{2,1,0:T(8,128)(2,1)} %get-tuple-element.74), channel_id=1, source_target_pairs={{0,2},{1,3},{2,0},{3,1},{4,6},{5,7},{6,4},{7,5},{8,10},{9,11},{10,... | collective-permute-start | bytes 2752520 | tf_op jit(solution)/shard_map/ppermute | solution.py:403
  121.8 22.4 %collective-permute-start.13 = (bf16[16,224,128]{2,1,0:T(8,128)(2,1)S(1)}, bf16[16,224,128]{2,1,0:T(8,128)(2,1)S(1)}, u32[]{:S(2)}, u32[]{:S(2)}) collective-permute-start(bf16[16,224,128]{2,1,0:T(8,128)(2,1)S(1)} %collective-permute-done.4.refs_4_), channel_id=1, source_target_pairs={{0,16},{16,0},{1,17},{17,1},{2,18},{18,2},{3,19},{19,3},{4,20},{20... | collective-permute-start | bytes 2752520 | tf_op jit(solution)/shard_map/ppermute | solution.py:404
  121.8 22.4 %collective-permute-start.10 = (bf16[16,224,128]{2,1,0:T(8,128)(2,1)S(1)}, bf16[16,224,128]{2,1,0:T(8,128)(2,1)S(1)}, u32[]{:S(2)}, u32[]{:S(2)}) collective-permute-start(bf16[16,224,128]{2,1,0:T(8,128)(2,1)S(1)} %get-tuple-element.116), channel_id=1, source_target_pairs={{0,1},{1,0},{2,3},{3,2},{4,5},{5,4},{6,7},{7,6},{8,9},{9,8},{10,11... | collective-permute-start | bytes 2752520 | tf_op jit(solution)/shard_map/ppermute | solution.py:402
  122.4 21.8 %collective-permute-start.11 = (bf16[16,224,128]{2,1,0:T(8,128)(2,1)}, bf16[16,224,128]{2,1,0:T(8,128)(2,1)S(1)}, u32[]{:S(2)}, u32[]{:S(2)}) collective-permute-start(bf16[16,224,128]{2,1,0:T(8,128)(2,1)} %get-tuple-element.113), channel_id=1, source_target_pairs={{0,1},{1,0},{2,3},{3,2},{4,5},{5,4},{6,7},{7,6},{8,9},{9,8},{10,11... | collective-permute-start | bytes 2752520 | tf_op jit(solution)/shard_map/ppermute | solution.py:402
  144.2 21.7 %collective-permute-start.14 = (bf16[16,224,128]{2,1,0:T(8,128)(2,1)S(1)}, bf16[16,224,128]{2,1,0:T(8,128)(2,1)S(1)}, u32[]{:S(2)}, u32[]{:S(2)}) collective-permute-start(bf16[16,224,128]{2,1,0:T(8,128)(2,1)S(1)} %collective-permute-done.12.refs_5_), channel_id=1, source_target_pairs={{0,16},{16,0},{1,17},{17,1},{2,18},{18,2},{3,19},{19,3},{4,20},{20... | collective-permute-start | bytes 2752520 | tf_op jit(solution)/shard_map/ppermute | solution.py:404
  190.4 42.4 %collective-permute-start.16 = (bf16[16,224,256]{2,1,0:T(8,128)(2,1)S(1)}, bf16[16,224,256]{2,1,0:T(8,128)(2,1)}, u32[]{:S(2)}, u32[]{:S(2)}) collective-permute-start(bf16[16,224,256]{2,1,0:T(8,128)(2,1)S(1)} %get-tuple-element.79), channel_id=1, source_target_pairs={{0,2},{1,3},{2,0},{3,1},{4,6},{5,7},{6,4},{7,5},{8,10},{9,11},{10,... | collective-permute-start | bytes 5505032 | tf_op jit(solution)/shard_map/ppermute | solution.py:403
  191.9 87.5 %collective-permute-start.15 = (bf16[16,224,256]{2,1,0:T(8,128)(2,1)}, bf16[16,224,256]{2,1,0:T(8,128)(2,1)S(1)}, u32[]{:S(2)}, u32[]{:S(2)}) collective-permute-start(bf16[16,224,256]{2,1,0:T(8,128)(2,1)} %get-tuple-element.111), channel_id=1, source_target_pairs={{0,1},{1,0},{2,3},{3,2},{4,5},{5,4},{6,7},{7,6},{8,9},{9,8},{10,11... | collective-permute-start | bytes 5505032 | tf_op jit(solution)/shard_map/ppermute | solution.py:402
  232.8 46.6 %collective-permute-start.17 = (bf16[16,224,256]{2,1,0:T(8,128)(2,1)}, bf16[16,224,256]{2,1,0:T(8,128)(2,1)}, u32[]{:S(2)}, u32[]{:S(2)}) collective-permute-start(bf16[16,224,256]{2,1,0:T(8,128)(2,1)} %collective-permute-done.16.refs_11_.refs_7_.refs_5_), channel_id=1, source_target_pairs={{0,16},{16,0},{1,17},{17,1},{2,18},{18,2},{3,19},{19,3},{4,20},{20... | collective-permute-start | bytes 5505032 | tf_op jit(solution)/shard_map/ppermute | solution.py:404
  279.4 12.6 %copy-start.5 = (bf16[16,224,256]{2,1,0:T(8,128)(2,1)}, bf16[16,224,256]{2,1,0:T(8,128)(2,1)S(1)}, u32[]{:S(2)}) copy-start(bf16[16,224,256]{2,1,0:T(8,128)(2,1)S(1)} %collective-permute-done.15.refs_10_.refs_6_) | copy-start | bytes 5505028
  279.7 12.3 %copy-start.6 = (bf16[1024,256]{1,0:T(8,128)(2,1)}, bf16[1024,256]{1,0:T(8,128)(2,1)S(1)}, u32[]{:S(2)}) copy-start(bf16[1024,256]{1,0:T(8,128)(2,1)S(1)} %get-tuple-element.122.refs_6_.refs_8_) | copy-start | bytes 1572868
  279.7 12.3 %copy-start.7 = (bf16[1024,256]{1,0:T(8,128)(2,1)}, bf16[1024,256]{1,0:T(8,128)(2,1)S(1)}, u32[]{:S(2)}) copy-start(bf16[1024,256]{1,0:T(8,128)(2,1)S(1)} %get-tuple-element.123.refs_5_.refs_7_) | copy-start | bytes 1572868
  279.7 29.0 %collective-permute-start.18 = (bf16[1024,256]{1,0:T(8,128)(2,1)S(1)}, bf16[1024,256]{1,0:T(8,128)(2,1)S(1)}, u32[]{:S(2)}, u32[]{:S(2)}) collective-permute-start(bf16[1024,256]{1,0:T(8,128)(2,1)S(1)} %get-tuple-element.123.refs_5_.refs_7_), channel_id=1, source_target_pairs={{0,4},{1,5},{2,6},{3,7},{4,8},{5,9},{6,10},{7,11},{8,12},{9,13},{1... | collective-permute-start | bytes 1572872 | tf_op jit(solution)/shard_map/ppermute | solution.py:486
  283.4 25.4 %collective-permute-start.19 = (bf16[1024,256]{1,0:T(8,128)(2,1)S(1)}, bf16[1024,256]{1,0:T(8,128)(2,1)}, u32[]{:S(2)}, u32[]{:S(2)}) collective-permute-start(bf16[1024,256]{1,0:T(8,128)(2,1)S(1)} %get-tuple-element.123.refs_5_.refs_7_), channel_id=1, source_target_pairs={{4,0},{5,1},{6,2},{7,3},{8,4},{9,5},{10,6},{11,7},{12,8},{13,9},{1... | collective-permute-start | bytes 1572872 | tf_op jit(solution)/shard_map/ppermute | solution.py:486
  285.3 27.6 %collective-permute-start.22 = (bf16[1024,256]{1,0:T(8,128)(2,1)S(1)}, bf16[1024,256]{1,0:T(8,128)(2,1)}, u32[]{:S(2)}, u32[]{:S(2)}) collective-permute-start(bf16[1024,256]{1,0:T(8,128)(2,1)S(1)} %get-tuple-element.122.refs_6_.refs_8_), channel_id=1, source_target_pairs={{0,4},{1,5},{2,6},{3,7},{4,8},{5,9},{6,10},{7,11},{8,12},{9,13},{1... | collective-permute-start | bytes 1572872 | tf_op jit(solution)/shard_map/ppermute | solution.py:486
  288.7 24.3 %collective-permute-start.23 = (bf16[1024,256]{1,0:T(8,128)(2,1)S(1)}, bf16[1024,256]{1,0:T(8,128)(2,1)}, u32[]{:S(2)}, u32[]{:S(2)}) collective-permute-start(bf16[1024,256]{1,0:T(8,128)(2,1)S(1)} %get-tuple-element.122.refs_6_.refs_8_), channel_id=1, source_target_pairs={{4,0},{5,1},{6,2},{7,3},{8,4},{9,5},{10,6},{11,7},{12,8},{13,9},{1... | collective-permute-start | bytes 1572872 | tf_op jit(solution)/shard_map/ppermute | solution.py:486
  308.7 11.5 %copy-start.8 = (bf16[1024,256]{1,0:T(8,128)(2,1)}, bf16[1024,256]{1,0:T(8,128)(2,1)S(1)}, u32[]{:S(2)}) copy-start(bf16[1024,256]{1,0:T(8,128)(2,1)S(1)} %collective-permute-done.18.refs_0_) | copy-start | bytes 1572868
  308.7 29.4 %collective-permute-start.20 = (bf16[1024,256]{1,0:T(8,128)(2,1)S(1)}, bf16[1024,256]{1,0:T(8,128)(2,1)S(1)}, u32[]{:S(2)}, u32[]{:S(2)}) collective-permute-start(bf16[1024,256]{1,0:T(8,128)(2,1)S(1)} %collective-permute-done.18.refs_0_), channel_id=1, source_target_pairs={{4,8},{5,9},{6,10},{7,11},{8,12},{9,13},{10,14},{11,15},{20,24},{2... | collective-permute-start | bytes 1572872 | tf_op jit(solution)/shard_map/ppermute | solution.py:486
  311.0 27.1 %collective-permute-start.21 = (bf16[1024,256]{1,0:T(8,128)(2,1)}, bf16[1024,256]{1,0:T(8,128)(2,1)S(1)}, u32[]{:S(2)}, u32[]{:S(2)}) collective-permute-start(bf16[1024,256]{1,0:T(8,128)(2,1)} %collective-permute-done.19.refs_2_), channel_id=1, source_target_pairs={{4,0},{5,1},{6,2},{7,3},{8,4},{9,5},{10,6},{11,7},{20,16},{21,17},... | collective-permute-start | bytes 1572872 | tf_op jit(solution)/shard_map/ppermute | solution.py:486
  313.0 27.2 %collective-permute-start.26 = (bf16[1024,256]{1,0:T(8,128)(2,1)}, bf16[1024,256]{1,0:T(8,128)(2,1)S(1)}, u32[]{:S(2)}, u32[]{:S(2)}) collective-permute-start(bf16[1024,256]{1,0:T(8,128)(2,1)} %collective-permute-done.22.refs_1_), channel_id=1, source_target_pairs={{4,8},{5,9},{6,10},{7,11},{8,12},{9,13},{10,14},{11,15},{20,24},{2... | collective-permute-start | bytes 1572872 | tf_op jit(solution)/shard_map/ppermute | solution.py:486
  316.4 23.8 %collective-permute-start.27 = (bf16[1024,256]{1,0:T(8,128)(2,1)}, bf16[1024,256]{1,0:T(8,128)(2,1)S(1)}, u32[]{:S(2)}, u32[]{:S(2)}) collective-permute-start(bf16[1024,256]{1,0:T(8,128)(2,1)} %collective-permute-done.23.refs_3_), channel_id=1, source_target_pairs={{4,0},{5,1},{6,2},{7,3},{8,4},{9,5},{10,6},{11,7},{20,16},{21,17},... | collective-permute-start | bytes 1572872 | tf_op jit(solution)/shard_map/ppermute | solution.py:486
  338.1 4.4 %copy-start.14 = (bf16[1024,256]{1,0:T(8,128)(2,1)}, bf16[1024,256]{1,0:T(8,128)(2,1)S(1)}, u32[]{:S(2)}) copy-start(bf16[1024,256]{1,0:T(8,128)(2,1)S(1)} %collective-permute-done.20.refs_4_) | copy-start | bytes 1572868
  338.1 4.3 %copy-start.15 = (bf16[1024,256]{1,0:T(8,128)(2,1)}, bf16[1024,256]{1,0:T(8,128)(2,1)S(1)}, u32[]{:S(2)}) copy-start(bf16[1024,256]{1,0:T(8,128)(2,1)S(1)} %collective-permute-done.21.refs_6_) | copy-start | bytes 1572868
  338.1 32.2 %collective-permute-start.24 = (bf16[1024,256]{1,0:T(8,128)(2,1)S(1)}, bf16[1024,256]{1,0:T(8,128)(2,1)S(1)}, u32[]{:S(2)}, u32[]{:S(2)}) collective-permute-start(bf16[1024,256]{1,0:T(8,128)(2,1)S(1)} %collective-permute-done.20.refs_4_), channel_id=1, source_target_pairs={{8,12},{9,13},{10,14},{11,15},{24,28},{25,29},{26,30},{27,31}} | collective-permute-start | bytes 1572872 | tf_op jit(solution)/shard_map/ppermute | solution.py:486
  338.8 31.5 %collective-permute-start.25 = (bf16[1024,256]{1,0:T(8,128)(2,1)S(1)}, bf16[1024,256]{1,0:T(8,128)(2,1)S(1)}, u32[]{:S(2)}, u32[]{:S(2)}) collective-permute-start(bf16[1024,256]{1,0:T(8,128)(2,1)S(1)} %collective-permute-done.21.refs_6_), channel_id=1, source_target_pairs={{4,0},{5,1},{6,2},{7,3},{20,16},{21,17},{22,18},{23,19}} | collective-permute-start | bytes 1572872 | tf_op jit(solution)/shard_map/ppermute | solution.py:486
  340.2 2.3 copy-start.16
  340.2 30.1 %collective-permute-start.28 = (bf16[1024,256]{1,0:T(8,128)(2,1)S(1)}, bf16[1024,256]{1,0:T(8,128)(2,1)S(1)}, u32[]{:S(2)}, u32[]{:S(2)}) collective-permute-start(bf16[1024,256]{1,0:T(8,128)(2,1)S(1)} %collective-permute-done.26.refs_5_), channel_id=1, source_target_pairs={{8,12},{9,13},{10,14},{11,15},{24,28},{25,29},{26,30},{27,31}} | collective-permute-start | bytes 1572872 | tf_op jit(solution)/shard_map/ppermute | solution.py:486
  340.9 29.4 %collective-permute-start.29 = (bf16[1024,256]{1,0:T(8,128)(2,1)S(1)}, bf16[1024,256]{1,0:T(8,128)(2,1)S(1)}, u32[]{:S(2)}, u32[]{:S(2)}) collective-permute-start(bf16[1024,256]{1,0:T(8,128)(2,1)S(1)} %collective-permute-done.27.refs_7_), channel_id=1, source_target_pairs={{4,0},{5,1},{6,2},{7,3},{20,16},{21,17},{22,18},{23,19}} | collective-permute-start | bytes 1572872 | tf_op jit(solution)/shard_map/ppermute | solution.py:486
  379.8 4.2 collective-permute-start.30
  385.2 14.0 %collective-permute-start.31 = (bf16[1024,224]{1,0:T(8,128)(2,1)S(1)}, bf16[1024,224]{1,0:T(8,128)(2,1)S(1)}, u32[]{:S(2)}, u32[]{:S(2)}) collective-permute-start(bf16[1024,224]{1,0:T(8,128)(2,1)S(1)} %add_convert_fusion), channel_id=1, source_target_pairs={{0,2},{1,3},{2,0},{3,1},{4,6},{5,7},{6,4},{7,5},{8,10},{9,11},{10,... | collective-permute-start | bytes 1376264 | tf_op jit(solution)/shard_map/ppermute | solution.py:403
  399.2 1.9 collective-permute-start.32
  (6 other events, 8.3 us)
Sparse Core Ops, SparseCore 0:
  119.9 77.1 reduce-scatter.2
  199.5 77.2 reduce-scatter.4

commit v14 on v11

--- a/solution.py
+++ b/solution.py
@@ -385,7 +385,7 @@
             ],
         ),
         out_shape=jax.ShapeDtypeStruct((tokens, count * LANES), dtype),
-        compiler_params=params(56),
+        compiler_params=params(32),
         cost_estimate=cost(2 * slots * rows * tokens * LANES * count, 2 * slots * rows * tokens),
         name="down_and_mix",
     )(*spans, base, block, onehot, *hidden, *([] if start is None else [start]), *weights)

time: 429 us -> 422 us (0.984)
  Pallas kernels: 177 us -> 162 us
  waiting for transfers between devices: 146 us -> 153 us
    pallas_call x5, Pallas kernels: 73.8 us -> 58 us  [down_and_mix(): pl.pallas_call(kernel, grid_spec=pltpu.PrefetchScalarGridSpec(num_scalar_...]
    unnamed x26 -> x22, local copies, waits for them, and re-layouts: 6.02 us -> 12.6 us
    ppermute x7, waiting for transfers between devices: 80.1 us -> 84.7 us  [fixed_weights(): to_cross = lambda value: lax.ppermute(value, ('parts', 'ep'), cross)]
  transfers between devices with their start and end apart: 30 -> 30, of which waited for: 17 -> 16; matrix products, arithmetic and copies ran while one was open for 5% -> 5% of each run, Pallas kernels for 35% -> 33%
where the time goes in v14:
time: 422 us; the launch traced here: 419 us
  Pallas kernels  162 us (38%)
  waiting for transfers between devices  153 us (36%)
  starting transfers between devices  33.4 us (8%)
  local copies, waits for them, and re-layouts  33.2 us (8%)
  blocking collectives  17.6 us (4%)
  between operations  13.8 us (3%)
  other arithmetic  5.5 us (1%)
    ppermute x7, waiting for transfers between devices, fixed_weights(): to_cross = lambda value: lax.ppermute(value, ('parts', 'ep'), cross)  84.7 us
    pallas_call x5, Pallas kernels, down_and_mix(): pl.pallas_call(kernel, grid_spec=pltpu.PrefetchScalarGridSpec(num_scalar_...  58 us
    pallas_call x2, Pallas kernels, partial_sums(): pl.pallas_call(partial_kernel, grid_spec=pltpu.PrefetchScalarGridSpec(num...  39.2 us
    pallas_call x2, Pallas kernels, sort_rows(): pl.pallas_call(kernel, grid_spec=pltpu.PrefetchScalarGridSpec(num_scalar_...  29.5 us
    ppermute x5, waiting for transfers between devices, fixed_weights(): to_plane = lambda value: lax.ppermute(value, 'parts', [(0, 1), (1, 0)])  22.7 us
    reduce_scatter x2, waiting for transfers between devices, units_of(): lax.psum_scatter(sums, 'ep', scatter_dimension=0, axis_index_groups=line,...  22.2 us
    all_to_all x1, blocking collectives, fixed_weights(): lax.all_to_all(mixed.reshape(size, count, width), 'ep', split_axis=0, con...  17.6 us
    pallas_call x1, Pallas kernels, scatter_rows(): pl.pallas_call(scatter_kernel, grid_spec=pltpu.PrefetchScalarGridSpec(num...  16.7 us
  transfers between devices with their start and end apart: 30, of which 16 were waited for; matrix products, arithmetic and copies ran while one was open for 5% of the time, Pallas kernels for 33%

profile of v14, /device:TPU:15, one launch (start us, length us, event | category | flops | bytes accessed | tf_op | source)
XLA Modules:
  0.0 418.9 jit_solution(7564153963732140319)
XLA Ops:
  8.0 1.8 reshape.61
  11.0 6.6 %all-to-all-start = ((bf16[16,64,256]{2,1,0:T(8,128)(2,1)}), bf16[16,64,256]{2,1,0:T(8,128)(2,1)S(1)}, u32[]{:S(2)}, u32[]{:S(2)}) async-start(bf16[16,64,256]{2,1,0:T(8,128)(2,1)} %pad_maximum_fusion), calls=%async_computation | async-start | bytes 1048576 | tf_op jit(solution)/shard_map/all_to_all | solution.py:422
  17.6 3.8 constant_dynamic-slice_fusion.2
  22.9 2.2 constant_dynamic-slice_fusion
  25.1 6.4 %all-to-all-done = bf16[16,64,256]{2,1,0:T(8,128)(2,1)S(1)} async-done(((bf16[16,64,256]{2,1,0:T(8,128)(2,1)}), bf16[16,64,256]{2,1,0:T(8,128)(2,1)S(1)}, u32[]{:S(2)}, u32[]{:S(2)}) %all-to-all-start) | async-done | bytes 524320 | tf_op jit(solution)/shard_map/all_to_all | solution.py:422
  31.4 3.6 order.1
  37.7 14.5 %sort_rows.2 = (bf16[8192,512]{1,0:T(8,128)(2,1)}, f32[8192,128]{1,0:T(8,128)S(1)}, bf16[8192,1024]{1,0:T(8,128)(2,1)}) custom-call(s32[32]{0:T(128)S(1)} %get-tuple-element.112.low.refs_0_, s32[32]{0:T(128)S(1)} %get-tuple-element.111.high.refs_1_, s32[17]{0:T(128)S(1)} %slice_bitcast_fusion.base.refs_2_, s32[16,8,128]{2,1,0:T(8,128)S(1)} %bitcast.39, ...), custom_call_target="tpu_custom_call" | custom-call | flops 4294967296 | bytes 16777216 | tf_op jit(solution)/shard_map/sort_rows/pallas_call | solution.py:188
  52.2 14.9 %sort_rows.3 = (bf16[8192,512]{1,0:T(8,128)(2,1)}, f32[8192,128]{1,0:T(8,128)S(1)}, bf16[8192,1024]{1,0:T(8,128)(2,1)}) custom-call(s32[32]{0:T(128)S(1)} %get-tuple-element.112.low.refs_0_, s32[32]{0:T(128)S(1)} %get-tuple-element.111.high.refs_1_, ...), custom_call_target="tpu_custom_call", output_to_operand_aliasing={{0}: (7, {}), {1}: (8, {}), {2}: (9, {})} | custom-call | flops 4294967296 | bytes 16777216 | tf_op jit(solution)/shard_map/sort_rows/pallas_call | solution.py:188
  67.1 2.1 copy-done.4
  70.4 7.1 %collective-permute-done.7.refs_5_ = bf16[16,224,128]{2,1,0:T(8,128)(2,1)S(1)} collective-permute-done((bf16[16,224,128]{2,1,0:T(8,128)(2,1)S(1)}, bf16[16,224,128]{2,1,0:T(8,128)(2,1)S(1)}, u32[]{:S(2)}, u32[]{:S(2)}) %collective-permute-start.7) | collective-permute-done | bytes 917536 | tf_op jit(solution)/shard_map/ppermute | solution.py:406
  78.3 15.3 %sort_more.1.far_ref = bf16[8192,512]{1,0:T(8,128)(2,1)} custom-call(bf16[8192,1024]{1,0:T(8,128)(2,1)} %get-tuple-element.56.onehot_ref, bf16[1024,256]{1,0:T(8,128)(2,1)S(1)} %collective-permute-done.2.refs_0_, bf16[1024,256]{1,0:T(8,128)(2,1)S(1)} %collective-permute-done.3.refs_1_), custom_call_target="tpu_custom_call" | custom-call | flops 8589934592 | bytes 33554432 | tf_op jit(solution)/shard_map/sort_more/pallas_call | solution.py:227
  93.6 6.5 %collective-permute-done.4.refs_4_ = bf16[16,224,128]{2,1,0:T(8,128)(2,1)S(1)} collective-permute-done((bf16[16,224,128]{2,1,0:T(8,128)(2,1)S(1)}, bf16[16,224,128]{2,1,0:T(8,128)(2,1)S(1)}, u32[]{:S(2)}, u32[]{:S(2)}) %collective-permute-start.4) | collective-permute-done | bytes 917536 | tf_op jit(solution)/shard_map/ppermute | solution.py:406
  100.3 19.6 %partial_sums.2 = bf16[8192,256]{1,0:T(8,128)(2,1)} custom-call(s32[32]{0:T(128)S(1)} %get-tuple-element.112.low.refs_0_, s32[32]{0:T(128)S(1)} %get-tuple-element.111.high.refs_1_, s32[17]{0:T(128)S(1)} %slice_bitcast_fusion.base.refs_2_, s32[1]{0:T(128)} %bitcast.8.quarter, bf16[8192,512]{1,0:T(8,128)(2,1)} %get-tuple-element.55.near_ref, ...), custom_call_target="tpu_custom_call" | custom-call | flops 4294967296 | bytes 16777216 | tf_op jit(solution)/shard_map/partial_sums/pallas_call | solution.py:300
  120.1 1.7 collective-permute-start.12
  122.4 20.9 %collective-permute-done.12.refs_5_ = bf16[16,224,128]{2,1,0:T(8,128)(2,1)S(1)} collective-permute-done((bf16[16,224,128]{2,1,0:T(8,128)(2,1)}, bf16[16,224,128]{2,1,0:T(8,128)(2,1)S(1)}, u32[]{:S(2)}, u32[]{:S(2)}) %collective-permute-start.12) | collective-permute-done | bytes 917536 | tf_op jit(solution)/shard_map/ppermute | solution.py:406
  144.2 21.6 %collective-permute-done.14.refs_7_ = bf16[16,224,128]{2,1,0:T(8,128)(2,1)S(1)} collective-permute-done((bf16[16,224,128]{2,1,0:T(8,128)(2,1)S(1)}, bf16[16,224,128]{2,1,0:T(8,128)(2,1)S(1)}, u32[]{:S(2)}, u32[]{:S(2)}) %collective-permute-start.14) | collective-permute-done | bytes 917536 | tf_op jit(solution)/shard_map/ppermute | solution.py:407
  165.8 19.6 %partial_sums.3 = bf16[8192,256]{1,0:T(8,128)(2,1)} custom-call(s32[32]{0:T(128)S(1)} %get-tuple-element.112.low.refs_0_, s32[32]{0:T(128)S(1)} %get-tuple-element.111.high.refs_1_, s32[17]{0:T(128)S(1)} %slice_bitcast_fusion.base.refs_2_, s32[1]{0:T(128)} %bitcast.8.quarter, bf16[8192,512]{1,0:T(8,128)(2,1)} %get-tuple-element.55.near_ref, ...), custom_call_target="tpu_custom_call" | custom-call | flops 4294967296 | bytes 16777216 | tf_op jit(solution)/shard_map/partial_sums/pallas_call | solution.py:300
  185.5 4.4 %dynamic-slice_bitcast_fusion = (bf16[16,224,256]{2,1,0:T(8,128)(2,1)S(1)}, bf16[16,224,256]{2,1,0:T(8,128)(2,1)S(1)}, bf16[16,224,256]{2,1,0:T(8,128)(2,1)}) fusion(bf16[16,1024,224]{1,2,0:T(8,128)(2,1)} %param.11, s32[]{:T(128)S(6)} %select_n.48, s32[]{:T(128)S(6)} %select_n.53, s32[]{:T(128)S(6)} %select_n.50), kind=kLoop, calls=%fused_computation | loop fusion | bytes 11010060 | tf_op jit(solution)/shard_map/dynamic_slice | solution.py:432
  189.9 1.6 collective-permute-start.16
  191.4 40.8 %collective-permute-done.16.refs_9_.refs_5_.refs_7_.refs_3_ = bf16[16,224,256]{2,1,0:T(8,128)(2,1)} collective-permute-done((bf16[16,224,256]{2,1,0:T(8,128)(2,1)S(1)}, bf16[16,224,256]{2,1,0:T(8,128)(2,1)}, u32[]{:S(2)}, u32[]{:S(2)}) %collective-permute-start.16) | collective-permute-done | bytes 1835040 | tf_op jit(solution)/shard_map/ppermute | solution.py:406
  232.2 5.8 %broadcast_in_dim.5.place_ref = s32[16,1024,128]{2,1,0:T(8,128)} broadcast(s32[16,1024]{1,0:T(8,128)S(1)} %get-tuple-element.68), dimensions={0,1} | broadcast | bytes 8454144 | tf_op jit(solution)/shard_map/broadcast_in_dim | solution.py:473
  238.0 16.7 %scatter_rows.1.refs_4_.onehot_ref = bf16[1024,8192]{1,0:T(8,128)(2,1)} custom-call(s32[32]{0:T(128)S(1)} %get-tuple-element.112.low.refs_0_, s32[32]{0:T(128)S(1)} %get-tuple-element.111.high.refs_1_, s32[16,1024,128]{2,1,0:T(8,128)} %broadcast_in_dim.5.place_ref), custom_call_target="tpu_custom_call" | custom-call | flops 8388608 | bytes 16777216 | tf_op jit(solution)/shard_map/scatter_rows/pallas_call | solution.py:257
  254.7 22.2 %reduce-scatter.5.cloned.1.call-done = bf16[2048,256]{1,0:T(8,128)(2,1)} async-done(((bf16[8192,256]{1,0:T(8,128)(2,1)}), bf16[2048,256]{1,0:T(8,128)(2,1)}) %reduce-scatter.5.cloned.1.call-update) | async-done | bytes 1048592 | tf_op jit(solution)/shard_map/reduce_scatter | solution.py:462
  276.9 2.5 fusion.12
  279.7 3.6 collective-permute-start.18
  283.3 1.9 collective-permute-start.19
  285.3 13.4 %down_and_mix.5.refs_2_ = f32[1024,1024]{1,0:T(8,128)S(1)} custom-call(s32[32]{0:T(128)S(1)} %get-tuple-element.112.low.refs_0_, s32[32]{0:T(128)S(1)} %get-tuple-element.111.high.refs_1_, s32[17]{0:T(128)S(1)} %slice_bitcast_fusion.base.refs_2_, s32[3]{0:T(128)S(1)} %stack.80.refs_3_, bf16[1024,8192]{1,0:T(8,128)(2,1)} %scatter_rows.1.refs_4_.onehot_ref, ...), custom_call_target="tpu_custom_call" | custom-call | flops 4294967296 | bytes 4194304 | tf_op jit(solution)/shard_map/down_and_mix/pallas_call | solution.py:367
  298.7 2.0 copy-done.2
  300.6 5.1 %collective-permute-done.18.refs_0_ = bf16[2048,256]{1,0:T(8,128)(2,1)S(1)} collective-permute-done((bf16[2048,256]{1,0:T(8,128)(2,1)S(1)}, bf16[2048,256]{1,0:T(8,128)(2,1)S(1)}, u32[]{:S(2)}, u32[]{:S(2)}) %collective-permute-start.18) | collective-permute-done | bytes 1048608 | tf_op jit(solution)/shard_map/ppermute | solution.py:489
  305.7 3.4 collective-permute-done.19.refs_1_
  309.1 3.0 collective-permute-start.20
  312.1 1.9 collective-permute-start.21
  314.2 2.2 copy-done.3
  316.3 13.6 %down_and_mix.6.refs_4_ = f32[1024,1024]{1,0:T(8,128)S(1)} custom-call(s32[32]{0:T(128)S(1)} %get-tuple-element.112.low.refs_0_, s32[32]{0:T(128)S(1)} %get-tuple-element.111.high.refs_1_, s32[17]{0:T(128)S(1)} %slice_bitcast_fusion.base.refs_2_, s32[3]{0:T(128)S(1)} %pad_add_fusion.1.block, bf16[1024,8192]{1,0:T(8,128)(2,1)} %scatter_rows.1.refs_4_.onehot_ref, ...), custom_call_target="tpu_custom_call" | custom-call | flops 4294967296 | bytes 4194304 | tf_op jit(solution)/shard_map/down_and_mix/pallas_call | solution.py:367
  329.9 2.0 copy-done
  331.9 5.0 %collective-permute-done.21.refs_3_ = bf16[2048,256]{1,0:T(8,128)(2,1)} collective-permute-done((bf16[2048,256]{1,0:T(8,128)(2,1)}, bf16[2048,256]{1,0:T(8,128)(2,1)}, u32[]{:S(2)}, u32[]{:S(2)}) %collective-permute-start.21) | collective-permute-done | bytes 1048608 | tf_op jit(solution)/shard_map/ppermute | solution.py:489
  337.6 3.2 collective-permute-start.23
  341.0 2.2 copy-done.1
  343.2 1.2 copy-done.6
  344.4 22.9 %down_and_mix.7.refs_2_ = f32[1024,1024]{1,0:T(8,128)S(1)} custom-call(s32[32]{0:T(128)S(1)} %get-tuple-element.112.low.refs_0_, s32[32]{0:T(128)S(1)} %get-tuple-element.111.high.refs_1_, s32[17]{0:T(128)S(1)} %slice_bitcast_fusion.base.refs_2_, s32[6]{0:T(128)S(1)} %stack.95.block, bf16[1024,8192]{1,0:T(8,128)(2,1)} %scatter_rows.1.refs_4_.onehot_ref, ...), custom_call_target="tpu_custom_call" | custom-call | flops 8589934592 | bytes 8388608 | tf_op jit(solution)/shard_map/down_and_mix/pallas_call | solution.py:367
  367.3 4.3 %down_and_mix.8 = bf16[1024,512]{1,0:T(8,128)(2,1)S(1)} custom-call(s32[32]{0:T(128)S(1)} %get-tuple-element.112.low.refs_0_, s32[32]{0:T(128)S(1)} %get-tuple-element.111.high.refs_1_, s32[17]{0:T(128)S(1)} %slice_bitcast_fusion.base.refs_2_, s32[3]{0:T(128)S(1)} %pad_add_fusion.block, bf16[1024,8192]{1,0:T(8,128)(2,1)} %scatter_rows.1.refs_4_.onehot_ref, ...), custom_call_target="tpu_custom_call" | custom-call | flops 2147483648 | bytes 4194304 | tf_op jit(solution)/shard_map/down_and_mix/pallas_call | solution.py:367
  371.7 3.1 collective-permute-start.24
  374.8 1.5 collective-permute-done.24
  377.1 3.8 down_and_mix.9
  381.0 9.5 %collective-permute-done.25 = bf16[1024,224]{1,0:T(8,128)(2,1)S(1)} collective-permute-done((bf16[1024,224]{1,0:T(8,128)(2,1)S(1)}, bf16[1024,224]{1,0:T(8,128)(2,1)S(1)}, u32[]{:S(2)}, u32[]{:S(2)}) %collective-permute-start.25) | collective-permute-done | bytes 458784 | tf_op jit(solution)/shard_map/ppermute | solution.py:406
  390.8 1.5 collective-permute-done.26
  392.5 17.6 %all_to_all.10 = bf16[16,64,224]{2,1,0:T(8,128)(2,1)S(1)} all-to-all(bf16[16,64,224]{2,1,0:T(8,128)(2,1)S(1)} %bitcast.41), channel_id=1, replica_groups=mesh['parts'=2,'ep'=16,'tp'=1] {'ep'}, dimensions={0} | all-to-all | bytes 917504 | tf_op jit(solution)/shard_map/all_to_all | solution.py:527
  410.5 1.6 reshape.66
  (79 shorter events, 13.6 us)
Async XLA Ops:
  11.0 20.4 %all-to-all-start = ((bf16[16,64,256]{2,1,0:T(8,128)(2,1)}), bf16[16,64,256]{2,1,0:T(8,128)(2,1)S(1)}, u32[]{:S(2)}, u32[]{:S(2)}) async-start(bf16[16,64,256]{2,1,0:T(8,128)(2,1)} %pad_maximum_fusion), calls=%async_computation | async-start | bytes 1048576 | tf_op jit(solution)/shard_map/all_to_all | solution.py:422
  17.5 237.2 %reduce-scatter.3.cloned.1.call-start = ((), (), s32[]{:S(2)}) async-start(), calls=%async_computation.4 | async-start | bytes 5242880 | tf_op jit(solution)/shard_map/reduce_scatter | solution.py:462
  17.6 5.2 %copy-start.7 = (bf16[16,224,1024]{2,1,0:T(8,128)(2,1)S(1)}, bf16[16,224,1024]{2,1,0:T(8,128)(2,1)}, u32[]{:S(2)}) copy-start(bf16[16,224,1024]{2,1,0:T(8,128)(2,1)} %refs_1_.3) | copy-start | bytes 22020100
  21.5 30.7 %collective-permute-start = (bf16[16,224,128]{2,1,0:T(8,128)(2,1)}, bf16[16,224,128]{2,1,0:T(8,128)(2,1)S(1)}, u32[]{:S(2)}, u32[]{:S(2)}) collective-permute-start(bf16[16,224,128]{2,1,0:T(8,128)(2,1)} %get-tuple-element.101), channel_id=1, source_target_pairs={{0,2},{1,3},{2,0},{3,1},{4,6},{5,7},{6,4},{7,5},{8,10},{9,11},{10,... | collective-permute-start | bytes 2752520 | tf_op jit(solution)/shard_map/ppermute | solution.py:406
  35.1 1.9 collective-permute-start.1
  35.1 34.1 %collective-permute-start.2 = (bf16[1024,256]{1,0:T(8,128)(2,1)S(1)}, bf16[1024,256]{1,0:T(8,128)(2,1)S(1)}, u32[]{:S(2)}, u32[]{:S(2)}) collective-permute-start(bf16[1024,256]{1,0:T(8,128)(2,1)S(1)} %bitcast.36), channel_id=1, source_target_pairs={{0,2},{1,3},{2,0},{3,1},{4,6},{5,7},{6,4},{7,5},{8,10},{9,11},{10,... | collective-permute-start | bytes 1572872 | tf_op jit(solution)/shard_map/ppermute | solution.py:406
  37.0 40.5 %collective-permute-start.7 = (bf16[16,224,128]{2,1,0:T(8,128)(2,1)S(1)}, bf16[16,224,128]{2,1,0:T(8,128)(2,1)S(1)}, u32[]{:S(2)}, u32[]{:S(2)}) collective-permute-start(bf16[16,224,128]{2,1,0:T(8,128)(2,1)S(1)} %get-tuple-element.60), channel_id=1, source_target_pairs={{0,2},{1,3},{2,0},{3,1},{4,6},{5,7},{6,4},{7,5},{8,10},{9,11},{10,... | collective-permute-start | bytes 2752520 | tf_op jit(solution)/shard_map/ppermute | solution.py:406
  52.2 26.1 %collective-permute-start.8 = (bf16[16,224,128]{2,1,0:T(8,128)(2,1)S(1)}, bf16[16,224,128]{2,1,0:T(8,128)(2,1)S(1)}, u32[]{:S(2)}, u32[]{:S(2)}) collective-permute-start(bf16[16,224,128]{2,1,0:T(8,128)(2,1)S(1)} %collective-permute-done.refs_4_), channel_id=1, source_target_pairs={{0,16},{16,0},{1,17},{17,1},{2,18},{18,2},{3,19},{19,3},{4,20},{20... | collective-permute-start | bytes 2752520 | tf_op jit(solution)/shard_map/ppermute | solution.py:407
  52.2 25.3 %copy-start.9 = (bf16[16,224,128]{2,1,0:T(8,128)(2,1)S(1)}, bf16[16,224,128]{2,1,0:T(8,128)(2,1)}, u32[]{:S(2)}) copy-start(bf16[16,224,128]{2,1,0:T(8,128)(2,1)} %get-tuple-element.58) | copy-start | bytes 2752516
  67.1 2.1 copy-start.4
  69.2 9.1 %collective-permute-start.3 = (bf16[1024,256]{1,0:T(8,128)(2,1)S(1)}, bf16[1024,256]{1,0:T(8,128)(2,1)S(1)}, u32[]{:S(2)}, u32[]{:S(2)}) collective-permute-start(bf16[1024,256]{1,0:T(8,128)(2,1)S(1)} %collective-permute-done.2.refs_0_), channel_id=1, source_target_pairs={{0,1},{1,0},{2,3},{3,2},{4,5},{5,4},{6,7},{7,6},{8,9},{9,8},{10,11... | collective-permute-start | bytes 1572872 | tf_op jit(solution)/shard_map/ppermute | solution.py:405
  69.9 30.2 %collective-permute-start.5 = (bf16[16,224,128]{2,1,0:T(8,128)(2,1)}, bf16[16,224,128]{2,1,0:T(8,128)(2,1)S(1)}, u32[]{:S(2)}, u32[]{:S(2)}) collective-permute-start(bf16[16,224,128]{2,1,0:T(8,128)(2,1)} %get-tuple-element.99), channel_id=1, source_target_pairs={{0,1},{1,0},{2,3},{3,2},{4,5},{5,4},{6,7},{7,6},{8,9},{9,8},{10,11... | collective-permute-start | bytes 2752520 | tf_op jit(solution)/shard_map/ppermute | solution.py:405
  69.9 30.2 %collective-permute-start.6 = (bf16[16,224,128]{2,1,0:T(8,128)(2,1)}, bf16[16,224,128]{2,1,0:T(8,128)(2,1)S(1)}, u32[]{:S(2)}, u32[]{:S(2)}) collective-permute-start(bf16[16,224,128]{2,1,0:T(8,128)(2,1)} %get-tuple-element.97), channel_id=1, source_target_pairs={{0,1},{1,0},{2,3},{3,2},{4,5},{5,4},{6,7},{7,6},{8,9},{9,8},{10,11... | collective-permute-start | bytes 2752520 | tf_op jit(solution)/shard_map/ppermute | solution.py:405
  77.5 22.7 %collective-permute-start.4 = (bf16[16,224,128]{2,1,0:T(8,128)(2,1)S(1)}, bf16[16,224,128]{2,1,0:T(8,128)(2,1)S(1)}, u32[]{:S(2)}, u32[]{:S(2)}) collective-permute-start(bf16[16,224,128]{2,1,0:T(8,128)(2,1)S(1)} %copy-done.9), channel_id=1, source_target_pairs={{0,2},{1,3},{2,0},{3,1},{4,6},{5,7},{6,4},{7,5},{8,10},{9,11},{10,... | collective-permute-start | bytes 2752520 | tf_op jit(solution)/shard_map/ppermute | solution.py:406
  78.3 21.9 %collective-permute-start.9 = (bf16[16,224,128]{2,1,0:T(8,128)(2,1)S(1)}, bf16[16,224,128]{2,1,0:T(8,128)(2,1)S(1)}, u32[]{:S(2)}, u32[]{:S(2)}) collective-permute-start(bf16[16,224,128]{2,1,0:T(8,128)(2,1)S(1)} %collective-permute-done.7.refs_5_), channel_id=1, source_target_pairs={{0,16},{16,0},{1,17},{17,1},{2,18},{18,2},{3,19},{19,3},{4,20},{20... | collective-permute-start | bytes 2752520 | tf_op jit(solution)/shard_map/ppermute | solution.py:407
  119.8 2.3 copy-start.8
  119.9 157.0 %reduce-scatter.5.cloned.1.call-start = ((), (), s32[]{:S(2)}) async-start(), calls=%async_computation.5 | async-start | bytes 5242880 | tf_op jit(solution)/shard_map/reduce_scatter | solution.py:462
  120.1 23.1 %collective-permute-start.12 = (bf16[16,224,128]{2,1,0:T(8,128)(2,1)}, bf16[16,224,128]{2,1,0:T(8,128)(2,1)S(1)}, u32[]{:S(2)}, u32[]{:S(2)}) collective-permute-start(bf16[16,224,128]{2,1,0:T(8,128)(2,1)} %get-tuple-element.65), channel_id=1, source_target_pairs={{0,2},{1,3},{2,0},{3,1},{4,6},{5,7},{6,4},{7,5},{8,10},{9,11},{10,... | collective-permute-start | bytes 2752520 | tf_op jit(solution)/shard_map/ppermute | solution.py:406
  121.8 22.4 %collective-permute-start.13 = (bf16[16,224,128]{2,1,0:T(8,128)(2,1)S(1)}, bf16[16,224,128]{2,1,0:T(8,128)(2,1)S(1)}, u32[]{:S(2)}, u32[]{:S(2)}) collective-permute-start(bf16[16,224,128]{2,1,0:T(8,128)(2,1)S(1)} %collective-permute-done.4.refs_4_), channel_id=1, source_target_pairs={{0,16},{16,0},{1,17},{17,1},{2,18},{18,2},{3,19},{19,3},{4,20},{20... | collective-permute-start | bytes 2752520 | tf_op jit(solution)/shard_map/ppermute | solution.py:407
  121.8 22.4 %collective-permute-start.10 = (bf16[16,224,128]{2,1,0:T(8,128)(2,1)S(1)}, bf16[16,224,128]{2,1,0:T(8,128)(2,1)S(1)}, u32[]{:S(2)}, u32[]{:S(2)}) collective-permute-start(bf16[16,224,128]{2,1,0:T(8,128)(2,1)S(1)} %get-tuple-element.98), channel_id=1, source_target_pairs={{0,1},{1,0},{2,3},{3,2},{4,5},{5,4},{6,7},{7,6},{8,9},{9,8},{10,11... | collective-permute-start | bytes 2752520 | tf_op jit(solution)/shard_map/ppermute | solution.py:405
  122.2 22.1 %collective-permute-start.11 = (bf16[16,224,128]{2,1,0:T(8,128)(2,1)S(1)}, bf16[16,224,128]{2,1,0:T(8,128)(2,1)S(1)}, u32[]{:S(2)}, u32[]{:S(2)}) collective-permute-start(bf16[16,224,128]{2,1,0:T(8,128)(2,1)S(1)} %copy-done.8), channel_id=1, source_target_pairs={{0,1},{1,0},{2,3},{3,2},{4,5},{5,4},{6,7},{7,6},{8,9},{9,8},{10,11... | collective-permute-start | bytes 2752520 | tf_op jit(solution)/shard_map/ppermute | solution.py:405
  144.2 21.6 %collective-permute-start.14 = (bf16[16,224,128]{2,1,0:T(8,128)(2,1)S(1)}, bf16[16,224,128]{2,1,0:T(8,128)(2,1)S(1)}, u32[]{:S(2)}, u32[]{:S(2)}) collective-permute-start(bf16[16,224,128]{2,1,0:T(8,128)(2,1)S(1)} %collective-permute-done.12.refs_5_), channel_id=1, source_target_pairs={{0,16},{16,0},{1,17},{17,1},{2,18},{18,2},{3,19},{19,3},{4,20},{20... | collective-permute-start | bytes 2752520 | tf_op jit(solution)/shard_map/ppermute | solution.py:407
  189.9 42.3 %collective-permute-start.16 = (bf16[16,224,256]{2,1,0:T(8,128)(2,1)S(1)}, bf16[16,224,256]{2,1,0:T(8,128)(2,1)}, u32[]{:S(2)}, u32[]{:S(2)}) collective-permute-start(bf16[16,224,256]{2,1,0:T(8,128)(2,1)S(1)} %get-tuple-element.70), channel_id=1, source_target_pairs={{0,2},{1,3},{2,0},{3,1},{4,6},{5,7},{6,4},{7,5},{8,10},{9,11},{10,... | collective-permute-start | bytes 5505032 | tf_op jit(solution)/shard_map/ppermute | solution.py:406
  191.4 88.0 %collective-permute-start.15 = (bf16[16,224,256]{2,1,0:T(8,128)(2,1)}, bf16[16,224,256]{2,1,0:T(8,128)(2,1)}, u32[]{:S(2)}, u32[]{:S(2)}) collective-permute-start(bf16[16,224,256]{2,1,0:T(8,128)(2,1)} %get-tuple-element.93), channel_id=1, source_target_pairs={{0,1},{1,0},{2,3},{3,2},{4,5},{5,4},{6,7},{7,6},{8,9},{9,8},{10,11... | collective-permute-start | bytes 5505032 | tf_op jit(solution)/shard_map/ppermute | solution.py:405
  232.2 47.2 %collective-permute-start.17 = (bf16[16,224,256]{2,1,0:T(8,128)(2,1)}, bf16[16,224,256]{2,1,0:T(8,128)(2,1)}, u32[]{:S(2)}, u32[]{:S(2)}) collective-permute-start(bf16[16,224,256]{2,1,0:T(8,128)(2,1)} %collective-permute-done.16.refs_9_.refs_5_.refs_7_.refs_3_), channel_id=1, source_target_pairs={{0,16},{16,0},{1,17},{17,1},{2,18},{18,2},{3,19},{19,3},{4,20},{20... | collective-permute-start | bytes 5505032 | tf_op jit(solution)/shard_map/ppermute | solution.py:407
  279.7 26.1 %collective-permute-start.18 = (bf16[2048,256]{1,0:T(8,128)(2,1)S(1)}, bf16[2048,256]{1,0:T(8,128)(2,1)S(1)}, u32[]{:S(2)}, u32[]{:S(2)}) collective-permute-start(bf16[2048,256]{1,0:T(8,128)(2,1)S(1)} %constant_dynamic-update-slice_fusion.refs_5_.refs_6_), channel_id=1, source_target_pairs={{0,4},{1,5},{2,6},{3,7},{4,8},{5,9},{6,10},{7,11},{8,12},{9,13},{1... | collective-permute-start | bytes 3145736 | tf_op jit(solution)/shard_map/ppermute | solution.py:489
  283.3 25.8 %collective-permute-start.19 = (bf16[2048,256]{1,0:T(8,128)(2,1)S(1)}, bf16[2048,256]{1,0:T(8,128)(2,1)}, u32[]{:S(2)}, u32[]{:S(2)}) collective-permute-start(bf16[2048,256]{1,0:T(8,128)(2,1)S(1)} %constant_dynamic-update-slice_fusion.refs_5_.refs_6_), channel_id=1, source_target_pairs={{4,0},{5,1},{6,2},{7,3},{8,4},{9,5},{10,6},{11,7},{12,8},{13,9},{1... | collective-permute-start | bytes 3145736 | tf_op jit(solution)/shard_map/ppermute | solution.py:489
  298.7 2.0 copy-start.2
  305.7 24.2 %copy-start.5 = (bf16[2048,256]{1,0:T(8,128)(2,1)}, bf16[2048,256]{1,0:T(8,128)(2,1)S(1)}, u32[]{:S(2)}) copy-start(bf16[2048,256]{1,0:T(8,128)(2,1)S(1)} %collective-permute-done.18.refs_0_) | copy-start | bytes 3145732
  309.1 22.8 %collective-permute-start.20 = (bf16[2048,256]{1,0:T(8,128)(2,1)S(1)}, bf16[2048,256]{1,0:T(8,128)(2,1)}, u32[]{:S(2)}, u32[]{:S(2)}) collective-permute-start(bf16[2048,256]{1,0:T(8,128)(2,1)S(1)} %collective-permute-done.18.refs_0_), channel_id=1, source_target_pairs={{4,8},{5,9},{6,10},{7,11},{8,12},{9,13},{10,14},{11,15},{20,24},{2... | collective-permute-start | bytes 3145736 | tf_op jit(solution)/shard_map/ppermute | solution.py:489
  312.1 24.8 %collective-permute-start.21 = (bf16[2048,256]{1,0:T(8,128)(2,1)}, bf16[2048,256]{1,0:T(8,128)(2,1)}, u32[]{:S(2)}, u32[]{:S(2)}) collective-permute-start(bf16[2048,256]{1,0:T(8,128)(2,1)} %collective-permute-done.19.refs_1_), channel_id=1, source_target_pairs={{4,0},{5,1},{6,2},{7,3},{8,4},{9,5},{10,6},{11,7},{20,16},{21,17},... | collective-permute-start | bytes 3145736 | tf_op jit(solution)/shard_map/ppermute | solution.py:489
  314.1 2.2 copy-start.3
  329.9 2.0 copy-start
  336.9 30.4 %collective-permute-start.22 = (bf16[2048,256]{1,0:T(8,128)(2,1)}, bf16[2048,256]{1,0:T(8,128)(2,1)S(1)}, u32[]{:S(2)}, u32[]{:S(2)}) collective-permute-start(bf16[2048,256]{1,0:T(8,128)(2,1)} %collective-permute-done.20.refs_2_), channel_id=1, source_target_pairs={{8,12},{9,13},{10,14},{11,15},{24,28},{25,29},{26,30},{27,31}} | collective-permute-start | bytes 3145736 | tf_op jit(solution)/shard_map/ppermute | solution.py:489
  337.6 29.7 %collective-permute-start.23 = (bf16[2048,256]{1,0:T(8,128)(2,1)}, bf16[2048,256]{1,0:T(8,128)(2,1)}, u32[]{:S(2)}, u32[]{:S(2)}) collective-permute-start(bf16[2048,256]{1,0:T(8,128)(2,1)} %collective-permute-done.21.refs_3_), channel_id=1, source_target_pairs={{4,0},{5,1},{6,2},{7,3},{20,16},{21,17},{22,18},{23,19}} | collective-permute-start | bytes 3145736 | tf_op jit(solution)/shard_map/ppermute | solution.py:489
  341.0 2.2 copy-start.1
  343.2 1.2 copy-start.6
  371.7 4.6 %collective-permute-start.24 = (bf16[1024,224]{1,0:T(8,128)(2,1)S(1)}, bf16[1024,224]{1,0:T(8,128)(2,1)S(1)}, u32[]{:S(2)}, u32[]{:S(2)}) collective-permute-start(bf16[1024,224]{1,0:T(8,128)(2,1)S(1)} %slice.60), channel_id=1, source_target_pairs={{0,1},{1,0},{2,3},{3,2},{4,5},{5,4},{6,7},{7,6},{8,9},{9,8},{10,11... | collective-permute-start | bytes 1376264 | tf_op jit(solution)/shard_map/ppermute | solution.py:405
  376.4 14.0 %collective-permute-start.25 = (bf16[1024,224]{1,0:T(8,128)(2,1)S(1)}, bf16[1024,224]{1,0:T(8,128)(2,1)S(1)}, u32[]{:S(2)}, u32[]{:S(2)}) collective-permute-start(bf16[1024,224]{1,0:T(8,128)(2,1)S(1)} %add_convert_fusion), channel_id=1, source_target_pairs={{0,2},{1,3},{2,0},{3,1},{4,6},{5,7},{6,4},{7,5},{8,10},{9,11},{10,... | collective-permute-start | bytes 1376264 | tf_op jit(solution)/shard_map/ppermute | solution.py:406
  390.4 1.9 collective-permute-start.26
Sparse Core Ops, SparseCore 0:
  120.0 77.1 reduce-scatter.2
  199.6 77.2 reduce-scatter.4

commit v15 on v14

--- a/solution.py
+++ b/solution.py
@@ -60,7 +60,7 @@
     return lax.dot_general(a, b, ((contract[0], contract[1]), ((), ())), preferred_element_type=F32)
 
 
-def params(mib=48):
+def params(mib=24):
     return pltpu.CompilerParams(vmem_limit_bytes=mib << 20)
 
 

time: 422 us -> 429 us (1.017)
  local copies, waits for them, and re-layouts: 33.2 us -> 57.7 us
  Pallas kernels: 162 us -> 147 us
    unnamed x22 -> x44, local copies, waits for them, and re-layouts: 12.6 us -> 40.3 us
    pallas_call x1, Pallas kernels: 15.3 us -> 10 us  [sort_more(): pl.pallas_call(sort_more_kernel, grid=(rows // BLOCK,), in_specs=[pl.Bloc...]
    pallas_call x1, Pallas kernels: 16.7 us -> 11.9 us  [scatter_rows(): pl.pallas_call(scatter_kernel, grid_spec=pltpu.PrefetchScalarGridSpec(num...]
  transfers between devices with their start and end apart: 30 -> 30, of which waited for: 16 -> 17; matrix products, arithmetic and copies ran while one was open for 5% -> 4% of each run, Pallas kernels for 33% -> 29%
where the time goes in v15:
time: 429 us; the launch traced here: 426 us
  waiting for transfers between devices  149 us (35%)
  Pallas kernels  147 us (34%)
  local copies, waits for them, and re-layouts  57.7 us (13%)
  starting transfers between devices  35.8 us (8%)
  blocking collectives  17.9 us (4%)
  between operations  13.9 us (3%)
  other arithmetic  5.53 us (1%)
    ppermute x7, waiting for transfers between devices, fixed_weights(): to_cross = lambda value: lax.ppermute(value, ('parts', 'ep'), cross)  85.7 us
    pallas_call x5, Pallas kernels, down_and_mix(): pl.pallas_call(kernel, grid_spec=pltpu.PrefetchScalarGridSpec(num_scalar_...  58 us
    unnamed x44, local copies, waits for them, and re-layouts  40.3 us
    pallas_call x2, Pallas kernels, partial_sums(): pl.pallas_call(partial_kernel, grid_spec=pltpu.PrefetchScalarGridSpec(num...  36.3 us
    pallas_call x2, Pallas kernels, sort_rows(): pl.pallas_call(kernel, grid_spec=pltpu.PrefetchScalarGridSpec(num_scalar_...  26.7 us
    ppermute x5, waiting for transfers between devices, fixed_weights(): to_plane = lambda value: lax.ppermute(value, 'parts', [(0, 1), (1, 0)])  23 us
    reduce_scatter x2, waiting for transfers between devices, units_of(): lax.psum_scatter(sums, 'ep', scatter_dimension=0, axis_index_groups=line,...  18.1 us
    all_to_all x1, blocking collectives, fixed_weights(): lax.all_to_all(mixed.reshape(size, count, width), 'ep', split_axis=0, con...  17.9 us
  transfers between devices with their start and end apart: 30, of which 17 were waited for; matrix products, arithmetic and copies ran while one was open for 4% of the time, Pallas kernels for 29%

profile of v15, /device:TPU:15, one launch (start us, length us, event | category | flops | bytes accessed | tf_op | source)
XLA Modules:
  0.0 426.0 jit_solution(1286428975198255754)
XLA Ops:
  11.0 6.6 %all-to-all-start = ((bf16[16,64,256]{2,1,0:T(8,128)(2,1)}), bf16[16,64,256]{2,1,0:T(8,128)(2,1)S(1)}, u32[]{:S(2)}, u32[]{:S(2)}) async-start(bf16[16,64,256]{2,1,0:T(8,128)(2,1)} %pad_maximum_fusion), calls=%async_computation | async-start | bytes 1048576 | tf_op jit(solution)/shard_map/all_to_all | solution.py:422
  17.7 4.2 constant_dynamic-slice_fusion.2
  23.3 2.2 constant_dynamic-slice_fusion
  25.4 6.1 %all-to-all-done = bf16[16,64,256]{2,1,0:T(8,128)(2,1)S(1)} async-done(((bf16[16,64,256]{2,1,0:T(8,128)(2,1)}), bf16[16,64,256]{2,1,0:T(8,128)(2,1)S(1)}, u32[]{:S(2)}, u32[]{:S(2)}) %all-to-all-start) | async-done | bytes 524320 | tf_op jit(solution)/shard_map/all_to_all | solution.py:422
  31.5 3.7 order.1
  37.7 13.5 %sort_rows.2 = (bf16[8192,512]{1,0:T(8,128)(2,1)S(1)}, f32[8192,128]{1,0:T(8,128)S(1)}, bf16[8192,1024]{1,0:T(8,128)(2,1)S(1)}) custom-call(s32[32]{0:T(128)S(1)} %get-tuple-element.112.low.refs_0_, s32[32]{0:T(128)S(1)} %get-tuple-element.111.high.refs_1_, s32[17]{0:T(128)S(1)} %slice_bitcast_fusion.base.refs_2_, s32[16,8,128]{2,1,0:T(8,128)S(1)} %bitcast.39, ...), custom_call_target="tpu_custom_call" | custom-call | flops 4294967296 | bytes 16777216 | tf_op jit(solution)/shard_map/sort_rows/pallas_call | solution.py:188
  51.3 13.3 %sort_rows.3 = (bf16[8192,512]{1,0:T(8,128)(2,1)S(1)}, f32[8192,128]{1,0:T(8,128)S(1)}, bf16[8192,1024]{1,0:T(8,128)(2,1)S(1)}) custom-call(s32[32]{0:T(128)S(1)} %get-tuple-element.112.low.refs_0_, s32[32]{0:T(128)S(1)} %get-tuple-element.111.high.refs_1_, ...), custom_call_target="tpu_custom_call", output_to_operand_aliasing={{0}: (7, {}), {1}: (8, {}), {2}: (9, {})} | custom-call | flops 4294967296 | bytes 16777216 | tf_op jit(solution)/shard_map/sort_rows/pallas_call | solution.py:188
  64.6 2.0 copy-done.14
  69.0 8.3 %collective-permute-done.7.refs_5_ = bf16[16,224,128]{2,1,0:T(8,128)(2,1)S(1)} collective-permute-done((bf16[16,224,128]{2,1,0:T(8,128)(2,1)S(1)}, bf16[16,224,128]{2,1,0:T(8,128)(2,1)S(1)}, u32[]{:S(2)}, u32[]{:S(2)}) %collective-permute-start.7) | collective-permute-done | bytes 917536 | tf_op jit(solution)/shard_map/ppermute | solution.py:406
  79.4 10.0 %sort_more.1.far_ref = bf16[8192,512]{1,0:T(8,128)(2,1)S(1)} custom-call(bf16[8192,1024]{1,0:T(8,128)(2,1)S(1)} %get-tuple-element.56.onehot_ref, bf16[1024,256]{1,0:T(8,128)(2,1)S(1)} %copy-done.18, bf16[1024,256]{1,0:T(8,128)(2,1)S(1)} %collective-permute-done.3.refs_1_), custom_call_target="tpu_custom_call" | custom-call | flops 8589934592 | bytes 33554432 | tf_op jit(solution)/shard_map/sort_more/pallas_call | solution.py:227
  89.4 3.3 copy-done.7
  92.7 7.5 %collective-permute-done.4.refs_4_ = bf16[16,224,128]{2,1,0:T(8,128)(2,1)S(1)} collective-permute-done((bf16[16,224,128]{2,1,0:T(8,128)(2,1)}, bf16[16,224,128]{2,1,0:T(8,128)(2,1)S(1)}, u32[]{:S(2)}, u32[]{:S(2)}) %collective-permute-start.4) | collective-permute-done | bytes 917536 | tf_op jit(solution)/shard_map/ppermute | solution.py:406
  100.3 3.1 copy-done.2
  103.3 3.1 copy-done.5
  106.4 18.2 %partial_sums.2 = bf16[8192,256]{1,0:T(8,128)(2,1)S(1)} custom-call(s32[32]{0:T(128)S(1)} %get-tuple-element.112.low.refs_0_, s32[32]{0:T(128)S(1)} %get-tuple-element.111.high.refs_1_, s32[17]{0:T(128)S(1)} %slice_bitcast_fusion.base.refs_2_, s32[1]{0:T(128)} %bitcast.8.quarter, bf16[8192,512]{1,0:T(8,128)(2,1)} %copy-done.1, bf16[8192,512]{1,0:T(8,128)(2,1)} %copy-done.7, ...), custom_call_target="tpu_custom_call" | custom-call | flops 4294967296 | bytes 16777216 | tf_op jit(solution)/shard_map/partial_sums/pallas_call | solution.py:300
  124.6 2.0 copy-done.10
  129.1 20.9 %collective-permute-done.12.refs_5_ = bf16[16,224,128]{2,1,0:T(8,128)(2,1)S(1)} collective-permute-done((bf16[16,224,128]{2,1,0:T(8,128)(2,1)}, bf16[16,224,128]{2,1,0:T(8,128)(2,1)S(1)}, u32[]{:S(2)}, u32[]{:S(2)}) %collective-permute-start.12) | collective-permute-done | bytes 917536 | tf_op jit(solution)/shard_map/ppermute | solution.py:406
  150.8 21.6 %collective-permute-done.14.refs_7_ = bf16[16,224,128]{2,1,0:T(8,128)(2,1)S(1)} collective-permute-done((bf16[16,224,128]{2,1,0:T(8,128)(2,1)S(1)}, bf16[16,224,128]{2,1,0:T(8,128)(2,1)S(1)}, u32[]{:S(2)}, u32[]{:S(2)}) %collective-permute-start.14) | collective-permute-done | bytes 917536 | tf_op jit(solution)/shard_map/ppermute | solution.py:407
  172.4 3.1 copy-done.3
  175.5 3.2 copy-done.6
  178.7 18.2 %partial_sums.3 = bf16[8192,256]{1,0:T(8,128)(2,1)S(1)} custom-call(s32[32]{0:T(128)S(1)} %get-tuple-element.112.low.refs_0_, s32[32]{0:T(128)S(1)} %get-tuple-element.111.high.refs_1_, s32[17]{0:T(128)S(1)} %slice_bitcast_fusion.base.refs_2_, s32[1]{0:T(128)} %bitcast.8.quarter, bf16[8192,512]{1,0:T(8,128)(2,1)} %copy-done.1, bf16[8192,512]{1,0:T(8,128)(2,1)} %copy-done.7, ...), custom_call_target="tpu_custom_call" | custom-call | flops 4294967296 | bytes 16777216 | tf_op jit(solution)/shard_map/partial_sums/pallas_call | solution.py:300
  196.9 2.1 copy-done.11
  199.0 4.4 %dynamic-slice_bitcast_fusion = (bf16[16,224,256]{2,1,0:T(8,128)(2,1)S(1)}, bf16[16,224,256]{2,1,0:T(8,128)(2,1)S(1)}, bf16[16,224,256]{2,1,0:T(8,128)(2,1)}) fusion(bf16[16,1024,224]{1,2,0:T(8,128)(2,1)} %param.11, s32[]{:T(128)S(6)} %select_n.48, s32[]{:T(128)S(6)} %select_n.53, s32[]{:T(128)S(6)} %select_n.50), kind=kLoop, calls=%fused_computation | loop fusion | bytes 11010060 | tf_op jit(solution)/shard_map/dynamic_slice | solution.py:432
  205.1 40.7 %collective-permute-done.16.refs_9_.refs_5_.refs_7_.refs_3_ = bf16[16,224,256]{2,1,0:T(8,128)(2,1)} collective-permute-done((bf16[16,224,256]{2,1,0:T(8,128)(2,1)S(1)}, bf16[16,224,256]{2,1,0:T(8,128)(2,1)}, u32[]{:S(2)}, u32[]{:S(2)}) %collective-permute-start.16) | collective-permute-done | bytes 1835040 | tf_op jit(solution)/shard_map/ppermute | solution.py:406
  245.7 2.3 broadcast_in_dim.5.place_ref
  248.0 11.9 %scatter_rows.1.refs_4_.onehot_ref = bf16[1024,8192]{1,0:T(8,128)(2,1)S(1)} custom-call(s32[32]{0:T(128)S(1)} %get-tuple-element.112.low.refs_0_, s32[32]{0:T(128)S(1)} %get-tuple-element.111.high.refs_1_, s32[16,1024,128]{2,1,0:T(8,128)S(1)} %broadcast_in_dim.5.place_ref), custom_call_target="tpu_custom_call" | custom-call | flops 8388608 | bytes 16777216 | tf_op jit(solution)/shard_map/scatter_rows/pallas_call | solution.py:257
  259.9 5.8 %copy-done = bf16[1024,8192]{1,0:T(8,128)(2,1)} copy-done((bf16[1024,8192]{1,0:T(8,128)(2,1)}, bf16[1024,8192]{1,0:T(8,128)(2,1)S(1)}, u32[]{:S(2)}) %copy-start) | copy-done | bytes 16777240
  265.7 18.1 %reduce-scatter.5.cloned.1.call-done = bf16[2048,256]{1,0:T(8,128)(2,1)} async-done(((bf16[8192,256]{1,0:T(8,128)(2,1)}), bf16[2048,256]{1,0:T(8,128)(2,1)}) %reduce-scatter.5.cloned.1.call-update) | async-done | bytes 1048592 | tf_op jit(solution)/shard_map/reduce_scatter | solution.py:462
  283.8 2.5 fusion.12
  287.1 4.0 collective-permute-start.18
  291.2 1.9 collective-permute-start.19
  293.1 13.7 %down_and_mix.5.refs_2_ = f32[1024,1024]{1,0:T(8,128)S(1)} custom-call(s32[32]{0:T(128)S(1)} %get-tuple-element.112.low.refs_0_, s32[32]{0:T(128)S(1)} %get-tuple-element.111.high.refs_1_, s32[17]{0:T(128)S(1)} %slice_bitcast_fusion.base.refs_2_, s32[3]{0:T(128)S(1)} %stack.80.refs_3_, bf16[1024,8192]{1,0:T(8,128)(2,1)} %copy-done, ...), custom_call_target="tpu_custom_call" | custom-call | flops 4294967296 | bytes 4194304 | tf_op jit(solution)/shard_map/down_and_mix/pallas_call | solution.py:367
  306.9 2.0 copy-done.12
  308.8 3.6 collective-permute-done.18.refs_0_
  312.5 3.9 collective-permute-done.19.refs_1_
  316.4 2.5 collective-permute-start.20
  321.0 2.2 copy-done.13
  323.2 13.2 %down_and_mix.6.refs_4_ = f32[1024,1024]{1,0:T(8,128)S(1)} custom-call(s32[32]{0:T(128)S(1)} %get-tuple-element.112.low.refs_0_, s32[32]{0:T(128)S(1)} %get-tuple-element.111.high.refs_1_, s32[17]{0:T(128)S(1)} %slice_bitcast_fusion.base.refs_2_, s32[3]{0:T(128)S(1)} %pad_add_fusion.1.block, bf16[1024,8192]{1,0:T(8,128)(2,1)} %copy-done, ...), custom_call_target="tpu_custom_call" | custom-call | flops 4294967296 | bytes 4194304 | tf_op jit(solution)/shard_map/down_and_mix/pallas_call | solution.py:367
  336.4 2.0 copy-done.8
  338.4 4.4 %collective-permute-done.21.refs_3_ = bf16[2048,256]{1,0:T(8,128)(2,1)} collective-permute-done((bf16[2048,256]{1,0:T(8,128)(2,1)}, bf16[2048,256]{1,0:T(8,128)(2,1)}, u32[]{:S(2)}, u32[]{:S(2)}) %collective-permute-start.21) | collective-permute-done | bytes 1048608 | tf_op jit(solution)/shard_map/ppermute | solution.py:489
  343.5 3.2 collective-permute-start.23
  346.8 2.2 copy-done.9
  350.2 22.9 %down_and_mix.7.refs_2_ = f32[1024,1024]{1,0:T(8,128)S(1)} custom-call(s32[32]{0:T(128)S(1)} %get-tuple-element.112.low.refs_0_, s32[32]{0:T(128)S(1)} %get-tuple-element.111.high.refs_1_, s32[17]{0:T(128)S(1)} %slice_bitcast_fusion.base.refs_2_, s32[6]{0:T(128)S(1)} %stack.95.block, bf16[1024,8192]{1,0:T(8,128)(2,1)} %copy-done, ...), custom_call_target="tpu_custom_call" | custom-call | flops 8589934592 | bytes 8388608 | tf_op jit(solution)/shard_map/down_and_mix/pallas_call | solution.py:367
  373.2 4.3 %down_and_mix.8 = bf16[1024,512]{1,0:T(8,128)(2,1)S(1)} custom-call(s32[32]{0:T(128)S(1)} %get-tuple-element.112.low.refs_0_, s32[32]{0:T(128)S(1)} %get-tuple-element.111.high.refs_1_, s32[17]{0:T(128)S(1)} %slice_bitcast_fusion.base.refs_2_, s32[3]{0:T(128)S(1)} %pad_add_fusion.block, bf16[1024,8192]{1,0:T(8,128)(2,1)} %copy-done, ...), custom_call_target="tpu_custom_call" | custom-call | flops 2147483648 | bytes 4194304 | tf_op jit(solution)/shard_map/down_and_mix/pallas_call | solution.py:367
  377.5 4.0 collective-permute-start.24
  385.0 3.8 down_and_mix.9
  388.9 8.3 %collective-permute-done.25 = bf16[1024,224]{1,0:T(8,128)(2,1)S(1)} collective-permute-done((bf16[1024,224]{1,0:T(8,128)(2,1)S(1)}, bf16[1024,224]{1,0:T(8,128)(2,1)S(1)}, u32[]{:S(2)}, u32[]{:S(2)}) %collective-permute-start.25) | collective-permute-done | bytes 458784 | tf_op jit(solution)/shard_map/ppermute | solution.py:406
  399.3 17.9 %all_to_all.10 = bf16[16,64,224]{2,1,0:T(8,128)(2,1)S(1)} all-to-all(bf16[16,64,224]{2,1,0:T(8,128)(2,1)S(1)} %bitcast.41), channel_id=1, replica_groups=mesh['parts'=2,'ep'=16,'tp'=1] {'ep'}, dimensions={0} | all-to-all | bytes 917504 | tf_op jit(solution)/shard_map/all_to_all | solution.py:527
  (101 shorter events, 30.6 us)
Async XLA Ops:
  11.0 20.4 %all-to-all-start = ((bf16[16,64,256]{2,1,0:T(8,128)(2,1)}), bf16[16,64,256]{2,1,0:T(8,128)(2,1)S(1)}, u32[]{:S(2)}, u32[]{:S(2)}) async-start(bf16[16,64,256]{2,1,0:T(8,128)(2,1)} %pad_maximum_fusion), calls=%async_computation | async-start | bytes 1048576 | tf_op jit(solution)/shard_map/all_to_all | solution.py:422
  17.6 248.1 %reduce-scatter.3.cloned.1.call-start = ((), (), s32[]{:S(2)}) async-start(), calls=%async_computation.4 | async-start | bytes 5242880 | tf_op jit(solution)/shard_map/reduce_scatter | solution.py:462
  17.7 5.6 %copy-start.4 = (bf16[16,224,1024]{2,1,0:T(8,128)(2,1)S(1)}, bf16[16,224,1024]{2,1,0:T(8,128)(2,1)}, u32[]{:S(2)}) copy-start(bf16[16,224,1024]{2,1,0:T(8,128)(2,1)} %refs_1_.3) | copy-start | bytes 22020100
  21.9 29.4 %collective-permute-start = (bf16[16,224,128]{2,1,0:T(8,128)(2,1)}, bf16[16,224,128]{2,1,0:T(8,128)(2,1)S(1)}, u32[]{:S(2)}, u32[]{:S(2)}) collective-permute-start(bf16[16,224,128]{2,1,0:T(8,128)(2,1)} %get-tuple-element.101), channel_id=1, source_target_pairs={{0,2},{1,3},{2,0},{3,1},{4,6},{5,7},{6,4},{7,5},{8,10},{9,11},{10,... | collective-permute-start | bytes 2752520 | tf_op jit(solution)/shard_map/ppermute | solution.py:406
  35.1 1.9 collective-permute-start.1
  35.1 31.4 %collective-permute-start.2 = (bf16[1024,256]{1,0:T(8,128)(2,1)S(1)}, bf16[1024,256]{1,0:T(8,128)(2,1)S(1)}, u32[]{:S(2)}, u32[]{:S(2)}) collective-permute-start(bf16[1024,256]{1,0:T(8,128)(2,1)S(1)} %bitcast.36), channel_id=1, source_target_pairs={{0,2},{1,3},{2,0},{3,1},{4,6},{5,7},{6,4},{7,5},{8,10},{9,11},{10,... | collective-permute-start | bytes 1572872 | tf_op jit(solution)/shard_map/ppermute | solution.py:406
  37.0 40.3 %collective-permute-start.7 = (bf16[16,224,128]{2,1,0:T(8,128)(2,1)S(1)}, bf16[16,224,128]{2,1,0:T(8,128)(2,1)S(1)}, u32[]{:S(2)}, u32[]{:S(2)}) collective-permute-start(bf16[16,224,128]{2,1,0:T(8,128)(2,1)S(1)} %get-tuple-element.60), channel_id=1, source_target_pairs={{0,2},{1,3},{2,0},{3,1},{4,6},{5,7},{6,4},{7,5},{8,10},{9,11},{10,... | collective-permute-start | bytes 2752520 | tf_op jit(solution)/shard_map/ppermute | solution.py:406
  51.2 27.1 %collective-permute-start.8 = (bf16[16,224,128]{2,1,0:T(8,128)(2,1)S(1)}, bf16[16,224,128]{2,1,0:T(8,128)(2,1)S(1)}, u32[]{:S(2)}, u32[]{:S(2)}) collective-permute-start(bf16[16,224,128]{2,1,0:T(8,128)(2,1)S(1)} %collective-permute-done.refs_4_), channel_id=1, source_target_pairs={{0,16},{16,0},{1,17},{17,1},{2,18},{18,2},{3,19},{19,3},{4,20},{20... | collective-permute-start | bytes 2752520 | tf_op jit(solution)/shard_map/ppermute | solution.py:407
  64.6 2.0 copy-start.14
  66.6 22.8 %copy-start.1 = (bf16[8192,512]{1,0:T(8,128)(2,1)}, bf16[8192,512]{1,0:T(8,128)(2,1)S(1)}, u32[]{:S(2)}) copy-start(bf16[8192,512]{1,0:T(8,128)(2,1)S(1)} %get-tuple-element.55.near_ref) | copy-start | bytes 25165828
  66.6 11.8 %collective-permute-start.3 = (bf16[1024,256]{1,0:T(8,128)(2,1)S(1)}, bf16[1024,256]{1,0:T(8,128)(2,1)S(1)}, u32[]{:S(2)}, u32[]{:S(2)}) collective-permute-start(bf16[1024,256]{1,0:T(8,128)(2,1)S(1)} %collective-permute-done.2.refs_0_), channel_id=1, source_target_pairs={{0,1},{1,0},{2,3},{3,2},{4,5},{5,4},{6,7},{7,6},{8,9},{9,8},{10,11... | collective-permute-start | bytes 1572872 | tf_op jit(solution)/shard_map/ppermute | solution.py:405
  68.5 31.7 %collective-permute-start.5 = (bf16[16,224,128]{2,1,0:T(8,128)(2,1)}, bf16[16,224,128]{2,1,0:T(8,128)(2,1)S(1)}, u32[]{:S(2)}, u32[]{:S(2)}) collective-permute-start(bf16[16,224,128]{2,1,0:T(8,128)(2,1)} %get-tuple-element.99), channel_id=1, source_target_pairs={{0,1},{1,0},{2,3},{3,2},{4,5},{5,4},{6,7},{7,6},{8,9},{9,8},{10,11... | collective-permute-start | bytes 2752520 | tf_op jit(solution)/shard_map/ppermute | solution.py:405
  68.5 31.7 %collective-permute-start.6 = (bf16[16,224,128]{2,1,0:T(8,128)(2,1)}, bf16[16,224,128]{2,1,0:T(8,128)(2,1)S(1)}, u32[]{:S(2)}, u32[]{:S(2)}) collective-permute-start(bf16[16,224,128]{2,1,0:T(8,128)(2,1)} %get-tuple-element.97), channel_id=1, source_target_pairs={{0,1},{1,0},{2,3},{3,2},{4,5},{5,4},{6,7},{7,6},{8,9},{9,8},{10,11... | collective-permute-start | bytes 2752520 | tf_op jit(solution)/shard_map/ppermute | solution.py:405
  77.3 22.9 %collective-permute-start.4 = (bf16[16,224,128]{2,1,0:T(8,128)(2,1)}, bf16[16,224,128]{2,1,0:T(8,128)(2,1)S(1)}, u32[]{:S(2)}, u32[]{:S(2)}) collective-permute-start(bf16[16,224,128]{2,1,0:T(8,128)(2,1)} %get-tuple-element.58), channel_id=1, source_target_pairs={{0,2},{1,3},{2,0},{3,1},{4,6},{5,7},{6,4},{7,5},{8,10},{9,11},{10,... | collective-permute-start | bytes 2752520 | tf_op jit(solution)/shard_map/ppermute | solution.py:406
  78.3 21.9 %collective-permute-start.9 = (bf16[16,224,128]{2,1,0:T(8,128)(2,1)S(1)}, bf16[16,224,128]{2,1,0:T(8,128)(2,1)S(1)}, u32[]{:S(2)}, u32[]{:S(2)}) collective-permute-start(bf16[16,224,128]{2,1,0:T(8,128)(2,1)S(1)} %collective-permute-done.7.refs_5_), channel_id=1, source_target_pairs={{0,16},{16,0},{1,17},{17,1},{2,18},{18,2},{3,19},{19,3},{4,20},{20... | collective-permute-start | bytes 2752520 | tf_op jit(solution)/shard_map/ppermute | solution.py:407
  89.4 3.3 copy-start.7
  100.3 3.1 copy-start.2
  103.3 3.1 copy-start.5
  124.6 2.0 copy-start.10
  126.6 1.8 copy-start.19
  126.6 2.5 copy-start.20
  126.6 157.2 %reduce-scatter.5.cloned.1.call-start = ((), (), s32[]{:S(2)}) async-start(), calls=%async_computation.5 | async-start | bytes 5242880 | tf_op jit(solution)/shard_map/reduce_scatter | solution.py:462
  126.9 23.1 %collective-permute-start.12 = (bf16[16,224,128]{2,1,0:T(8,128)(2,1)}, bf16[16,224,128]{2,1,0:T(8,128)(2,1)S(1)}, u32[]{:S(2)}, u32[]{:S(2)}) collective-permute-start(bf16[16,224,128]{2,1,0:T(8,128)(2,1)} %get-tuple-element.65), channel_id=1, source_target_pairs={{0,2},{1,3},{2,0},{3,1},{4,6},{5,7},{6,4},{7,5},{8,10},{9,11},{10,... | collective-permute-start | bytes 2752520 | tf_op jit(solution)/shard_map/ppermute | solution.py:406
  128.4 22.4 %collective-permute-start.13 = (bf16[16,224,128]{2,1,0:T(8,128)(2,1)S(1)}, bf16[16,224,128]{2,1,0:T(8,128)(2,1)S(1)}, u32[]{:S(2)}, u32[]{:S(2)}) collective-permute-start(bf16[16,224,128]{2,1,0:T(8,128)(2,1)S(1)} %collective-permute-done.4.refs_4_), channel_id=1, source_target_pairs={{0,16},{16,0},{1,17},{17,1},{2,18},{18,2},{3,19},{19,3},{4,20},{20... | collective-permute-start | bytes 2752520 | tf_op jit(solution)/shard_map/ppermute | solution.py:407
  128.4 22.4 %collective-permute-start.10 = (bf16[16,224,128]{2,1,0:T(8,128)(2,1)S(1)}, bf16[16,224,128]{2,1,0:T(8,128)(2,1)S(1)}, u32[]{:S(2)}, u32[]{:S(2)}) collective-permute-start(bf16[16,224,128]{2,1,0:T(8,128)(2,1)S(1)} %copy-done.19), channel_id=1, source_target_pairs={{0,1},{1,0},{2,3},{3,2},{4,5},{5,4},{6,7},{7,6},{8,9},{9,8},{10,11... | collective-permute-start | bytes 2752520 | tf_op jit(solution)/shard_map/ppermute | solution.py:405
  129.1 21.7 %collective-permute-start.11 = (bf16[16,224,128]{2,1,0:T(8,128)(2,1)S(1)}, bf16[16,224,128]{2,1,0:T(8,128)(2,1)S(1)}, u32[]{:S(2)}, u32[]{:S(2)}) collective-permute-start(bf16[16,224,128]{2,1,0:T(8,128)(2,1)S(1)} %copy-done.20), channel_id=1, source_target_pairs={{0,1},{1,0},{2,3},{3,2},{4,5},{5,4},{6,7},{7,6},{8,9},{9,8},{10,11... | collective-permute-start | bytes 2752520 | tf_op jit(solution)/shard_map/ppermute | solution.py:405
  150.8 21.6 %collective-permute-start.14 = (bf16[16,224,128]{2,1,0:T(8,128)(2,1)S(1)}, bf16[16,224,128]{2,1,0:T(8,128)(2,1)S(1)}, u32[]{:S(2)}, u32[]{:S(2)}) collective-permute-start(bf16[16,224,128]{2,1,0:T(8,128)(2,1)S(1)} %collective-permute-done.12.refs_5_), channel_id=1, source_target_pairs={{0,16},{16,0},{1,17},{17,1},{2,18},{18,2},{3,19},{19,3},{4,20},{20... | collective-permute-start | bytes 2752520 | tf_op jit(solution)/shard_map/ppermute | solution.py:407
  172.4 3.1 copy-start.3
  175.5 3.2 copy-start.6
  196.9 2.1 copy-start.11
  203.3 42.4 %collective-permute-start.16 = (bf16[16,224,256]{2,1,0:T(8,128)(2,1)S(1)}, bf16[16,224,256]{2,1,0:T(8,128)(2,1)}, u32[]{:S(2)}, u32[]{:S(2)}) collective-permute-start(bf16[16,224,256]{2,1,0:T(8,128)(2,1)S(1)} %get-tuple-element.70), channel_id=1, source_target_pairs={{0,2},{1,3},{2,0},{3,1},{4,6},{5,7},{6,4},{7,5},{8,10},{9,11},{10,... | collective-permute-start | bytes 5505032 | tf_op jit(solution)/shard_map/ppermute | solution.py:406
  205.0 81.3 %collective-permute-start.15 = (bf16[16,224,256]{2,1,0:T(8,128)(2,1)}, bf16[16,224,256]{2,1,0:T(8,128)(2,1)}, u32[]{:S(2)}, u32[]{:S(2)}) collective-permute-start(bf16[16,224,256]{2,1,0:T(8,128)(2,1)} %get-tuple-element.93), channel_id=1, source_target_pairs={{0,1},{1,0},{2,3},{3,2},{4,5},{5,4},{6,7},{7,6},{8,9},{9,8},{10,11... | collective-permute-start | bytes 5505032 | tf_op jit(solution)/shard_map/ppermute | solution.py:405
  245.7 41.2 %collective-permute-start.17 = (bf16[16,224,256]{2,1,0:T(8,128)(2,1)}, bf16[16,224,256]{2,1,0:T(8,128)(2,1)}, u32[]{:S(2)}, u32[]{:S(2)}) collective-permute-start(bf16[16,224,256]{2,1,0:T(8,128)(2,1)} %collective-permute-done.16.refs_9_.refs_5_.refs_7_.refs_3_), channel_id=1, source_target_pairs={{0,16},{16,0},{1,17},{17,1},{2,18},{18,2},{3,19},{19,3},{4,20},{20... | collective-permute-start | bytes 5505032 | tf_op jit(solution)/shard_map/ppermute | solution.py:407
  259.9 5.8 %copy-start = (bf16[1024,8192]{1,0:T(8,128)(2,1)}, bf16[1024,8192]{1,0:T(8,128)(2,1)S(1)}, u32[]{:S(2)}) copy-start(bf16[1024,8192]{1,0:T(8,128)(2,1)S(1)} %scatter_rows.1.refs_4_.onehot_ref) | copy-start | bytes 50331652
  287.1 25.3 %collective-permute-start.18 = (bf16[2048,256]{1,0:T(8,128)(2,1)S(1)}, bf16[2048,256]{1,0:T(8,128)(2,1)S(1)}, u32[]{:S(2)}, u32[]{:S(2)}) collective-permute-start(bf16[2048,256]{1,0:T(8,128)(2,1)S(1)} %constant_dynamic-update-slice_fusion.refs_5_.refs_6_), channel_id=1, source_target_pairs={{0,4},{1,5},{2,6},{3,7},{4,8},{5,9},{6,10},{7,11},{8,12},{9,13},{1... | collective-permute-start | bytes 3145736 | tf_op jit(solution)/shard_map/ppermute | solution.py:489
  291.2 25.2 %collective-permute-start.19 = (bf16[2048,256]{1,0:T(8,128)(2,1)S(1)}, bf16[2048,256]{1,0:T(8,128)(2,1)}, u32[]{:S(2)}, u32[]{:S(2)}) collective-permute-start(bf16[2048,256]{1,0:T(8,128)(2,1)S(1)} %constant_dynamic-update-slice_fusion.refs_5_.refs_6_), channel_id=1, source_target_pairs={{4,0},{5,1},{6,2},{7,3},{8,4},{9,5},{10,6},{11,7},{12,8},{13,9},{1... | collective-permute-start | bytes 3145736 | tf_op jit(solution)/shard_map/ppermute | solution.py:489
  306.8 2.0 copy-start.12
  312.5 23.9 %copy-start.15 = (bf16[2048,256]{1,0:T(8,128)(2,1)}, bf16[2048,256]{1,0:T(8,128)(2,1)S(1)}, u32[]{:S(2)}) copy-start(bf16[2048,256]{1,0:T(8,128)(2,1)S(1)} %collective-permute-done.18.refs_0_) | copy-start | bytes 3145732
  316.4 22.0 %collective-permute-start.20 = (bf16[2048,256]{1,0:T(8,128)(2,1)S(1)}, bf16[2048,256]{1,0:T(8,128)(2,1)}, u32[]{:S(2)}, u32[]{:S(2)}) collective-permute-start(bf16[2048,256]{1,0:T(8,128)(2,1)S(1)} %collective-permute-done.18.refs_0_), channel_id=1, source_target_pairs={{4,8},{5,9},{6,10},{7,11},{8,12},{9,13},{10,14},{11,15},{20,24},{2... | collective-permute-start | bytes 3145736 | tf_op jit(solution)/shard_map/ppermute | solution.py:489
  319.0 23.8 %collective-permute-start.21 = (bf16[2048,256]{1,0:T(8,128)(2,1)}, bf16[2048,256]{1,0:T(8,128)(2,1)}, u32[]{:S(2)}, u32[]{:S(2)}) collective-permute-start(bf16[2048,256]{1,0:T(8,128)(2,1)} %collective-permute-done.19.refs_1_), channel_id=1, source_target_pairs={{4,0},{5,1},{6,2},{7,3},{8,4},{9,5},{10,6},{11,7},{20,16},{21,17},... | collective-permute-start | bytes 3145736 | tf_op jit(solution)/shard_map/ppermute | solution.py:489
  321.0 2.2 copy-start.13
  336.4 2.0 copy-start.8
  342.7 30.4 %collective-permute-start.22 = (bf16[2048,256]{1,0:T(8,128)(2,1)}, bf16[2048,256]{1,0:T(8,128)(2,1)S(1)}, u32[]{:S(2)}, u32[]{:S(2)}) collective-permute-start(bf16[2048,256]{1,0:T(8,128)(2,1)} %collective-permute-done.20.refs_2_), channel_id=1, source_target_pairs={{8,12},{9,13},{10,14},{11,15},{24,28},{25,29},{26,30},{27,31}} | collective-permute-start | bytes 3145736 | tf_op jit(solution)/shard_map/ppermute | solution.py:489
  343.5 29.7 %collective-permute-start.23 = (bf16[2048,256]{1,0:T(8,128)(2,1)}, bf16[2048,256]{1,0:T(8,128)(2,1)}, u32[]{:S(2)}, u32[]{:S(2)}) collective-permute-start(bf16[2048,256]{1,0:T(8,128)(2,1)} %collective-permute-done.21.refs_3_), channel_id=1, source_target_pairs={{4,0},{5,1},{6,2},{7,3},{20,16},{21,17},{22,18},{23,19}} | collective-permute-start | bytes 3145736 | tf_op jit(solution)/shard_map/ppermute | solution.py:489
  346.8 2.2 copy-start.9
  377.5 5.6 %collective-permute-start.24 = (bf16[1024,224]{1,0:T(8,128)(2,1)S(1)}, bf16[1024,224]{1,0:T(8,128)(2,1)S(1)}, u32[]{:S(2)}, u32[]{:S(2)}) collective-permute-start(bf16[1024,224]{1,0:T(8,128)(2,1)S(1)} %slice.60), channel_id=1, source_target_pairs={{0,1},{1,0},{2,3},{3,2},{4,5},{5,4},{6,7},{7,6},{8,9},{9,8},{10,11... | collective-permute-start | bytes 1376264 | tf_op jit(solution)/shard_map/ppermute | solution.py:405
  383.2 14.0 %collective-permute-start.25 = (bf16[1024,224]{1,0:T(8,128)(2,1)S(1)}, bf16[1024,224]{1,0:T(8,128)(2,1)S(1)}, u32[]{:S(2)}, u32[]{:S(2)}) collective-permute-start(bf16[1024,224]{1,0:T(8,128)(2,1)S(1)} %add_convert_fusion), channel_id=1, source_target_pairs={{0,2},{1,3},{2,0},{3,1},{4,6},{5,7},{6,4},{7,5},{8,10},{9,11},{10,... | collective-permute-start | bytes 1376264 | tf_op jit(solution)/shard_map/ppermute | solution.py:406
  397.2 1.9 collective-permute-start.26
  (3 other events, 3.5 us)
Sparse Core Ops, SparseCore 0:
  126.8 77.3 reduce-scatter.2
  206.5 77.2 reduce-scatter.4
